TPU v7x, 32 devices: a whole 2x2x4 slice. The times are simulated.
32 devices in a mesh: gx: 8 (over z, core), gy: 2 (over y), gz: 2 (over x).
Axes of the slice: x: 2, y: 2, z: 4, core: 2. Of those that a mesh axis runs over, the one named last changes fastest.
Arguments:
- fields: float32 [2, 4, 3, 16, 128, 256], P(None, None, None, 'gz', 'gx', 'gy'), may hold values from -6 to 6
- material: int32 [16, 128, 256], P('gz', 'gx', 'gy'), may hold values from 0 to 3
- pml_width: int32 [6], replicated, may hold values from 2 to 4
- eps_real: float32 [4], replicated, may hold values from 1 to 12
- eps_loss: float32 [4], replicated, may hold values from 0.05 to 1
- coeffs: float32 [2, 4, 4], replicated, may hold values from -3 to 3
- ritz: float32 [2, 4], replicated, may hold values from -4 to 4
Outputs:
- basis_new: float32 [2, 4, 3, 16, 128, 256], P(None, None, None, 'gz', 'gx', 'gy')
- residual: float32 [2, 4, 3, 16, 128, 256], P(None, None, None, 'gz', 'gx', 'gy')
- gram_out: float32 [2, 4, 4], replicated
All inputs are finite; a program needn't handle non-finite values.
Results may differ from a plain program's by a relative error of at most 0.000078.
Values sent between devices are 32-bit elements; how exact they have to be, the bound alone decides.
No kernel may reach another device: no remote copies, remote signals or barrier semaphores. Data moves between devices by JAX's collectives and lax.ppermute only.
A program may use at most 64 MiB of HBM per device.

v0:
```python
import functools

import jax
import jax.numpy as jnp
from jax import lax
from jax.experimental import pallas as pl
from jax.experimental.pallas import tpu as pltpu
from jax.sharding import PartitionSpec as P

OMEGA_SQ = 0.36
SIGMA_TOP = 3.0
BOUNDS = ((4, 5), (0, 1), (2, 3))
AXES = ("gz", "gx", "gy")

VMEM = pl.BlockSpec(memory_space=pltpu.VMEM)
SMEM = pl.BlockSpec(memory_space=pltpu.SMEM)
HIGH = lax.Precision.HIGHEST


def passed_along(value, axis, steps):
    count = lax.axis_size(axis)
    leading, last = (max(0, -steps), min(count, count - steps))
    return lax.ppermute(value, axis, [(source, source + steps) for source in range(leading, last)])


def inverse_stretch(places, length, low_width, high_width):
    inside_depth = jnp.clip((low_width - places) / low_width, 0.0, 1.0) + jnp.clip(
        (places + 1.0 - length + high_width) / high_width, 0.0, 1.0
    )
    absorb = SIGMA_TOP * inside_depth * inside_depth
    scaled = 1.0 / (1.0 + absorb * absorb)
    return scaled, -absorb * scaled


def cmul(left, right):
    return (left[0] * right[0] - left[1] * right[1], left[0] * right[1] + left[1] * right[0])


def add(left, right):
    return (left[0] + right[0], left[1] + right[1])


def sub(left, right):
    return (left[0] - right[0], left[1] - right[1])


def axis_stretch(pml_ref, direction, count, places):
    total = count * lax.axis_size(AXES[direction])
    low_slot, high_slot = BOUNDS[direction]
    low = jnp.full(places.shape, pml_ref[low_slot], jnp.int32).astype(jnp.float32)
    high = jnp.full(places.shape, pml_ref[high_slot], jnp.int32).astype(jnp.float32)
    return inverse_stretch(places, jnp.float32(total), low, high)


def local_places(direction, count, shape, dim):
    start = lax.axis_index(AXES[direction]) * count
    return (lax.broadcasted_iota(jnp.int32, shape, dim) + start).astype(jnp.float32)


def one_place(direction, count, offset, shape):
    start = lax.axis_index(AXES[direction]) * count + offset
    return jnp.full(shape, start, jnp.int32).astype(jnp.float32)


def packed_lane(slot, part, vector, vectors):
    return (slot * 2 + part) * vectors + vector


def rotate_kernel(coeffs_ref, fields_ref, basis_ref, zf_ref, xf_ref, yf_ref):
    _, vectors, _, nz, nx, ny = fields_ref.shape
    lanes = lax.broadcasted_iota(jnp.int32, (nx, ny), 1)

    @pl.loop(0, nz)
    def _(z):
        packed = jnp.zeros((nx, ny), jnp.float32)
        for comp in range(3):
            old = [(fields_ref[0, a, comp, z], fields_ref[1, a, comp, z]) for a in range(vectors)]
            for b in range(vectors):
                new = None
                for a in range(vectors):
                    term = cmul((coeffs_ref[0, a, b], coeffs_ref[1, a, b]), old[a])
                    new = term if new is None else add(new, term)
                for part in range(2):
                    basis_ref[part, b, comp, z] = new[part]
                    if comp != 1:
                        lane = packed_lane(comp // 2, part, b, vectors)
                        packed = jnp.where(lanes == lane, pltpu.roll(new[part], lane, 1), packed)
                    if comp != 0:
                        xf_ref[part, b, comp - 1, pl.ds(z, 1)] = new[part][0:1]
        yf_ref[z] = packed

    for part in range(2):
        for b in range(vectors):
            for comp in range(2):
                zf_ref[part, b, comp] = basis_ref[part, b, comp, 0]


def image_kernel(
    pml_ref, eps_real_ref, eps_loss_ref, ritz_ref,
    basis_ref, material_ref, zf_ref, xf_ref, yf_ref,
    residual_ref, gram_ref, hzf_ref, hxf_ref, hyf_ref,
    eps_ref, sz_ref, acc_ref, lift_ref,
):
    _, vectors, _, nz, nx, ny = basis_ref.shape
    plane = (nx, ny)
    rows = lax.broadcasted_iota(jnp.int32, plane, 0)
    lanes = lax.broadcasted_iota(jnp.int32, plane, 1)
    shx = axis_stretch(pml_ref, 1, nx, local_places(1, nx, plane, 0) + 0.5)
    sex = axis_stretch(pml_ref, 1, nx, local_places(1, nx, plane, 0))
    shy = axis_stretch(pml_ref, 2, ny, local_places(2, ny, plane, 1) + 0.5)
    sey = axis_stretch(pml_ref, 2, ny, local_places(2, ny, plane, 1))
    table = (nz, ny)
    sez_rows = axis_stretch(pml_ref, 0, nz, local_places(0, nz, table, 0))
    shz_rows = axis_stretch(pml_ref, 0, nz, local_places(0, nz, table, 0) + 0.5)
    for part in range(2):
        sz_ref[part] = sez_rows[part]
        sz_ref[2 + part] = shz_rows[part]
    sz_next = axis_stretch(pml_ref, 0, nz, one_place(0, nz, nz, (1, ny)))
    sx_next = axis_stretch(pml_ref, 1, nx, one_place(1, nx, nx, (1, ny)))
    sy_next = axis_stretch(pml_ref, 2, ny, one_place(2, ny, ny, (1, ny)))

    material = material_ref[...]
    for part, source in enumerate((eps_real_ref, eps_loss_ref)):
        value = jnp.zeros(material.shape, jnp.float32)
        for number in range(source.shape[0]):
            value = jnp.where(material == number, -OMEGA_SQ * source[number], value)
        eps_ref[part] = value

    for a in range(vectors):
        for comp in range(2):
            scaled = cmul(sz_next, (zf_ref[0, a, comp], zf_ref[1, a, comp]))
            for part in range(2):
                lift_ref[part, a, comp] = scaled[part]

    def field(b, comp, z):
        return (basis_ref[0, b, comp, z], basis_ref[1, b, comp, z])

    def ahead_x(value, b, comp, z):
        return tuple(
            jnp.where(rows == nx - 1, xf_ref[part, b, comp - 1, pl.ds(z, 1)], pltpu.roll(value[part], nx - 1, 0))
            for part in range(2)
        )

    def ahead_y(value, b, comp, z):
        out = []
        for part in range(2):
            lane = packed_lane(comp // 2, part, b, vectors)
            edge = pltpu.roll(yf_ref[z], ny - 1 - lane, 1)
            out.append(jnp.where(lanes == ny - 1, edge, pltpu.roll(value[part], ny - 1, 1)))
        return tuple(out)

    def behind(value, axis):
        places = rows if axis == 0 else lanes
        return tuple(jnp.where(places == 0, 0.0, pltpu.roll(value[part], 1, axis)) for part in range(2))

    def fold(value):
        return functools.reduce(jnp.add, [value[row:row + 8] for row in range(0, value.shape[0], 8)])

    @pl.loop(0, nz)
    def _(z):
        hyf_ref[z] = jnp.zeros(plane, jnp.float32)

    for b in range(vectors):
        factor = (ritz_ref[0, b], ritz_ref[1, b])

        def step(z, carry, last, b=b, factor=factor):
            hx_before, hy_before, sums = carry
            sez = (sz_ref[0, pl.ds(z, 1)], sz_ref[1, pl.ds(z, 1)])
            shz = (sz_ref[2, pl.ds(z, 1)], sz_ref[3, pl.ds(z, 1)])
            u = [field(b, comp, z) for comp in range(3)]
            if last:
                up = [(zf_ref[0, b, comp], zf_ref[1, b, comp]) for comp in range(2)]
            else:
                up = [field(b, comp, z + 1) for comp in range(2)]
            dzx, dzy = (cmul(shz, sub(up[comp], u[comp])) for comp in range(2))
            dxy, dxz = (cmul(shx, sub(ahead_x(u[comp], b, comp, z), u[comp])) for comp in (1, 2))
            dyx, dyz = (cmul(shy, sub(ahead_y(u[comp], b, comp, z), u[comp])) for comp in (0, 2))
            hx, hy, hz = sub(dyz, dzy), sub(dzx, dxz), sub(dxy, dyx)
            byz, byx = (cmul(sey, sub(h, behind(h, 1))) for h in (hz, hx))
            bxz, bxy = (cmul(sex, sub(h, behind(h, 0))) for h in (hz, hy))
            bzy = cmul(sez, sub(hy, hy_before))
            bzx = cmul(sez, sub(hx, hx_before))
            eps = (eps_ref[0, z], eps_ref[1, z])
            w = [
                add(curl, cmul(eps, u[comp]))
                for comp, curl in enumerate((sub(byz, bzy), sub(bzx, bxz), sub(bxy, byx)))
            ]
            for comp in range(3):
                left = sub(w[comp], cmul(factor, u[comp]))
                for part in range(2):
                    residual_ref[part, b, comp, z] = left[part]
            for part in range(2):
                hxf_ref[part, b, 0, pl.ds(z, 1)] = hy[part][nx - 1:nx]
                hxf_ref[part, b, 1, pl.ds(z, 1)] = hz[part][nx - 1:nx]
            packed = hyf_ref[z]
            for slot, value in enumerate((hz, hx)):
                for part in range(2):
                    lane = packed_lane(slot, part, b, vectors)
                    packed = jnp.where(lanes == lane, pltpu.roll(value[part], (lane + 1) % ny, 1), packed)
            hyf_ref[z] = packed
            new_sums = []
            for a in range(vectors):
                total = None
                for comp in range(3):
                    term = cmul(field(a, comp, z), w[comp])
                    total = term if total is None else add(total, term)
                if last:
                    total = add(total, cmul((lift_ref[0, a, 0], lift_ref[1, a, 0]), hy))
                    total = sub(total, cmul((lift_ref[0, a, 1], lift_ref[1, a, 1]), hx))
                new_sums.append((sums[a][0] + fold(total[0]), sums[a][1] + fold(total[1])))
            if last:
                for part in range(2):
                    hzf_ref[part, b, 0] = hx[part]
                    hzf_ref[part, b, 1] = hy[part]
            return hx, hy, tuple(new_sums)

        zero = jnp.zeros(plane, jnp.float32)
        none = jnp.zeros((8, ny), jnp.float32)
        carry = ((zero, zero), (zero, zero), tuple((none, none) for _ in range(vectors)))
        carry = lax.fori_loop(0, nz - 1, lambda z, c: step(z, c, False), carry)
        _, _, sums = step(nz - 1, carry, True)
        h_y = (hxf_ref[0, b, 0], hxf_ref[1, b, 0])
        h_z = (hxf_ref[0, b, 1], hxf_ref[1, b, 1])
        for a in range(vectors):
            over = cmul((xf_ref[0, a, 0], xf_ref[1, a, 0]), h_z)
            over = sub(over, cmul((xf_ref[0, a, 1], xf_ref[1, a, 1]), h_y))
            over = cmul(sx_next, over)
            for part in range(2):
                acc_ref[b, part * vectors + a] = sums[a][part] + fold(over[part])

    pairs = lax.dot_general(
        yf_ref[...].reshape(nz * nx, ny), hyf_ref[...].reshape(nz * nx, ny),
        (((0,), (0,)), ((), ())), precision=HIGH, preferred_element_type=jnp.float32,
    )
    both = 2 * vectors
    block = pairs[both:2 * both, both:2 * both] - pairs[0:both, 0:both]
    side = cmul(
        (sy_next[0][:, :vectors], sy_next[1][:, :vectors]),
        (
            block[:vectors, :vectors] - block[vectors:, vectors:],
            block[:vectors, vectors:] + block[vectors:, :vectors],
        ),
    )
    totals = jnp.sum(jnp.sum(acc_ref[...], axis=2), axis=2, keepdims=True)
    columns = lax.broadcasted_iota(jnp.int32, (both, ny), 1)
    body_sum = jnp.zeros((both, ny), jnp.float32)
    for b in range(vectors):
        body_sum = jnp.where(columns == b, totals[b], body_sum)
    cells = 3.0 * nz * nx * ny
    for axis in AXES:
        cells = cells * lax.axis_size(axis)
    for part in range(2):
        whole = body_sum[part * vectors:(part + 1) * vectors, :vectors] + side[part]
        gram_ref[part] = whole * (1.0 / cells)


def rim_kernel(pml_ref, partial_ref, hzf_ref, hxf_ref, hyf_ref, residual_ref):
    _, vectors, _, nz, nx, ny = partial_ref.shape
    plane = (nx, ny)
    rows = lax.broadcasted_iota(jnp.int32, plane, 0)
    lanes = lax.broadcasted_iota(jnp.int32, plane, 1)
    sez = axis_stretch(pml_ref, 0, nz, one_place(0, nz, 0, plane))
    sex = axis_stretch(pml_ref, 1, nx, one_place(1, nx, 0, (1, ny)))
    sey = axis_stretch(pml_ref, 2, ny, one_place(2, ny, 0, plane))
    none = jnp.zeros(plane, jnp.float32)
    sex = tuple(jnp.where(rows == 0, part, none) for part in sex)
    sey = tuple(jnp.where(lanes == 0, part, none) for part in sey)

    def step(z, first):
        packed = hyf_ref[z]
        for b in range(vectors):

            def column(slot, b=b):
                return tuple(
                    pltpu.roll(packed, (ny - packed_lane(slot, part, b, vectors)) % ny, 1) for part in range(2)
                )

            def row(slot, b=b):
                return tuple(hxf_ref[part, b, slot, pl.ds(z, 1)] for part in range(2))

            left = [(partial_ref[0, b, comp, z], partial_ref[1, b, comp, z]) for comp in range(3)]
            left[0] = sub(left[0], cmul(sey, column(0)))
            left[2] = add(left[2], cmul(sey, column(1)))
            left[1] = add(left[1], cmul(sex, row(1)))
            left[2] = sub(left[2], cmul(sex, row(0)))
            if first:
                left[0] = add(left[0], cmul(sez, (hzf_ref[0, b, 1], hzf_ref[1, b, 1])))
                left[1] = sub(left[1], cmul(sez, (hzf_ref[0, b, 0], hzf_ref[1, b, 0])))
            for comp in range(3):
                for part in range(2):
                    residual_ref[part, b, comp, z] = left[comp][part]

    step(0, True)

    @pl.loop(1, nz)
    def _(z):
        step(z, False)


def summed_everywhere(value):
    for axis in ("gz", "gy", "gx"):
        count = lax.axis_size(axis)
        if count & (count - 1):
            value = lax.psum(value, axis)
            continue
        reach = 1
        while reach < count:
            value = value + lax.ppermute(value, axis, [(source, source ^ reach) for source in range(count)])
            reach *= 2
    return value


def body(fields, material, pml_width, eps_real, eps_loss, coeffs, ritz):
    _, vectors, _, nz, nx, ny = fields.shape
    f32 = lambda *shape: jax.ShapeDtypeStruct(shape, jnp.float32)
    params = pltpu.CompilerParams(vmem_limit_bytes=40 * 1024 * 1024)
    zf_shape = (2, vectors, 2, nx, ny)
    xf_shape = (2, vectors, 2, nz, ny)
    yf_shape = (nz, nx, ny)
    basis, zf, xf, yf = pl.pallas_call(
        rotate_kernel,
        out_shape=(f32(*fields.shape), f32(*zf_shape), f32(*xf_shape), f32(*yf_shape)),
        in_specs=[SMEM, VMEM],
        out_specs=(VMEM,) * 4,
        compiler_params=params,
        name="rotate_vectors",
    )(coeffs, fields)
    zf = passed_along(zf, "gz", -1)
    xf = passed_along(xf, "gx", -1)
    yf = passed_along(yf, "gy", -1)
    partial, gram, hzf, hxf, hyf = pl.pallas_call(
        image_kernel,
        out_shape=(
            f32(*fields.shape), f32(2, vectors, vectors), f32(*zf_shape), f32(*xf_shape), f32(*yf_shape),
        ),
        in_specs=[SMEM] * 4 + [VMEM] * 5,
        out_specs=(VMEM,) * 5,
        scratch_shapes=[
            pltpu.VMEM((2, nz, nx, ny), jnp.float32),
            pltpu.VMEM((4, nz, ny), jnp.float32),
            pltpu.VMEM((vectors, 2 * vectors, 8, ny), jnp.float32),
            pltpu.VMEM(zf_shape, jnp.float32),
        ],
        compiler_params=params,
        name="apply_operator",
    )(pml_width, eps_real, eps_loss, ritz, basis, material, zf, xf, yf)
    hzf = passed_along(hzf, "gz", 1)
    hxf = passed_along(hxf, "gx", 1)
    hyf = passed_along(hyf, "gy", 1)
    gram = summed_everywhere(gram)
    residual = pl.pallas_call(
        rim_kernel,
        out_shape=f32(*fields.shape),
        in_specs=[SMEM] + [VMEM] * 4,
        out_specs=VMEM,
        compiler_params=params,
        name="add_rims",
    )(pml_width, partial, hzf, hxf, hyf)
    return basis, residual, gram


def solution(mesh):
    in_specs = (P(None, None, None, "gz", "gx", "gy"), P("gz", "gx", "gy"), P(), P(), P(), P(), P())
    out_specs = (P(None, None, None, "gz", "gx", "gy"), P(None, None, None, "gz", "gx", "gy"), P())
    return jax.shard_map(body, mesh=mesh, in_specs=in_specs, out_specs=out_specs, check_vma=False)
```

profile of v0, /device:TPU:0, one launch (start us, length us, event | category | flops | bytes accessed | tf_op | source)
XLA Modules:
  0.0 52.9 jit_solution(3452431627733462066)
XLA Ops:
  0.6 1.4 %copy-done = f32[2,4,3,8,16,128]{5,4,3,2,1,0:T(8,128)S(1)} copy-done((f32[2,4,3,8,16,128]{5,4,3,2,1,0:T(8,128)S(1)}, f32[2,4,3,8,16,128]{5,4,3,2,1,0:T(8,128)}, u32[]{:S(2)}) %copy-start) | copy-done | bytes 1572888
  2.0 0.7 %copy-done.3 = f32[2,4,4]{2,1,0:T(4,128)S(1)} copy-done((f32[2,4,4]{2,1,0:T(4,128)S(1)}, f32[2,4,4]{2,1,0:T(4,128)}, u32[]{:S(2)}) %copy-start.3) | copy-done | bytes 152
  2.8 3.1 %rotate_vectors.1 = (f32[2,4,3,8,16,128]{5,4,3,2,1,0:T(8,128)}, f32[2,4,2,16,128]{4,3,2,1,0:T(8,128)S(1)}, f32[2,4,2,8,128]{4,3,2,1,0:T(8,128)S(1)}, f32[8,16,128]{2,1,0:T(8,128)S(1)}) custom-call(f32[2,4,4]{2,1,0:T(4,128)S(1)} %copy-done.3, f32[2,4,3,8,16,128]{5,4,3,2,1,0:T(8,128)S(1)} %copy-done), custom_call_target="tpu_custom_call" | custom-call | tf_op jit(solution)/shard_map/rotate_vectors/pallas_call | solution.py:320
  5.8 1.3 %collective-permute-start = (f32[2,4,2,16,128]{4,3,2,1,0:T(8,128)S(1)}, f32[2,4,2,16,128]{4,3,2,1,0:T(8,128)S(1)}, u32[]{:S(2)}, u32[]{:S(2)}) collective-permute-start(f32[2,4,2,16,128]{4,3,2,1,0:T(8,128)S(1)} %get-tuple-element.13), channel_id=1, source_target_pairs={{1,0},{3,2},{5,4},{7,6},{9,8},{11,10},{13,12},{15,14},{17,16},{19,... | collective-permute-start | bytes 393224 | tf_op jit(solution)/shard_map/ppermute | solution.py:23
  7.1 1.3 %collective-permute-start.1 = (f32[2,4,2,8,128]{4,3,2,1,0:T(8,128)S(1)}, f32[2,4,2,8,128]{4,3,2,1,0:T(8,128)S(1)}, u32[]{:S(2)}, u32[]{:S(2)}) collective-permute-start(f32[2,4,2,8,128]{4,3,2,1,0:T(8,128)S(1)} %get-tuple-element.14), channel_id=1, source_target_pairs={{4,0},{8,4},{12,8},{16,12},{20,16},{24,20},{28,24},{5,1},{9,5},{13... | collective-permute-start | bytes 196616 | tf_op jit(solution)/shard_map/ppermute | solution.py:23
  8.4 1.3 %collective-permute-start.2 = (f32[8,16,128]{2,1,0:T(8,128)S(1)}, f32[8,16,128]{2,1,0:T(8,128)S(1)}, u32[]{:S(2)}, u32[]{:S(2)}) collective-permute-start(f32[8,16,128]{2,1,0:T(8,128)S(1)} %get-tuple-element.15), channel_id=1, source_target_pairs={{2,0},{3,1},{6,4},{7,5},{10,8},{11,9},{14,12},{15,13},{18,16},{19,... | collective-permute-start | bytes 196616 | tf_op jit(solution)/shard_map/ppermute | solution.py:23
  9.7 0.5 %collective-permute-done.1.xf_ref = f32[2,4,2,8,128]{4,3,2,1,0:T(8,128)S(1)} collective-permute-done((f32[2,4,2,8,128]{4,3,2,1,0:T(8,128)S(1)}, f32[2,4,2,8,128]{4,3,2,1,0:T(8,128)S(1)}, u32[]{:S(2)}, u32[]{:S(2)}) %collective-permute-start.1) | collective-permute-done | bytes 65568 | tf_op jit(solution)/shard_map/ppermute | solution.py:23
  10.3 5.0 %collective-permute-done.2.yf_ref = f32[8,16,128]{2,1,0:T(8,128)S(1)} collective-permute-done((f32[8,16,128]{2,1,0:T(8,128)S(1)}, f32[8,16,128]{2,1,0:T(8,128)S(1)}, u32[]{:S(2)}, u32[]{:S(2)}) %collective-permute-start.2) | collective-permute-done | bytes 65568 | tf_op jit(solution)/shard_map/ppermute | solution.py:23
  15.3 1.4 %copy-done.1 = f32[2,4,3,8,16,128]{5,4,3,2,1,0:T(8,128)S(1)} copy-done((f32[2,4,3,8,16,128]{5,4,3,2,1,0:T(8,128)S(1)}, f32[2,4,3,8,16,128]{5,4,3,2,1,0:T(8,128)}, u32[]{:S(2)}) %copy-start.1) | copy-done | bytes 1572888
  16.7 7.2 %apply_operator.1 = (f32[2,4,3,8,16,128]{5,4,3,2,1,0:T(8,128)S(1)}, f32[2,4,4]{2,1,0:T(4,128)S(1)}, f32[2,4,2,16,128]{4,3,2,1,0:T(8,128)S(1)}, f32[2,4,2,8,128]{4,3,2,1,0:T(8,128)S(1)}, f32[8,16,128]{2,1,0:T(8,128)S(1)}) custom-call(s32[6]{0:T(128)S(1)} %copy-done.4, f32[4]{0:T(128)S(1)} %copy-done.6, f32[4]{0:T(128)S(1)} %copy-done.7, ...), custom_call_target="tpu_custom_call" | custom-call | tf_op jit(solution)/shard_map/apply_operator/pallas_call | solution.py:331
  23.9 4.6 %collective-permute-start.3 = (f32[2,4,2,16,128]{4,3,2,1,0:T(8,128)S(1)}, f32[2,4,2,16,128]{4,3,2,1,0:T(8,128)S(1)}, u32[]{:S(2)}, u32[]{:S(2)}) collective-permute-start(f32[2,4,2,16,128]{4,3,2,1,0:T(8,128)S(1)} %get-tuple-element.17), channel_id=1, source_target_pairs={{0,1},{2,3},{4,5},{6,7},{8,9},{10,11},{12,13},{14,15},{16,17},{18,... | collective-permute-start | bytes 393224 | tf_op jit(solution)/shard_map/ppermute | solution.py:23
  28.5 1.8 %collective-permute-start.4 = (f32[2,4,2,8,128]{4,3,2,1,0:T(8,128)S(1)}, f32[2,4,2,8,128]{4,3,2,1,0:T(8,128)S(1)}, u32[]{:S(2)}, u32[]{:S(2)}) collective-permute-start(f32[2,4,2,8,128]{4,3,2,1,0:T(8,128)S(1)} %get-tuple-element.18), channel_id=1, source_target_pairs={{0,4},{4,8},{8,12},{12,16},{16,20},{20,24},{24,28},{1,5},{5,9},{9,... | collective-permute-start | bytes 196616 | tf_op jit(solution)/shard_map/ppermute | solution.py:23
  30.3 2.1 %collective-permute-start.5 = (f32[8,16,128]{2,1,0:T(8,128)S(1)}, f32[8,16,128]{2,1,0:T(8,128)S(1)}, u32[]{:S(2)}, u32[]{:S(2)}) collective-permute-start(f32[8,16,128]{2,1,0:T(8,128)S(1)} %get-tuple-element.19), channel_id=1, source_target_pairs={{0,2},{1,3},{4,6},{5,7},{8,10},{9,11},{12,14},{13,15},{16,18},{17,... | collective-permute-start | bytes 196616 | tf_op jit(solution)/shard_map/ppermute | solution.py:23
  32.4 0.1 collective-permute-start.6
  32.5 3.6 %collective-permute-done.6 = f32[2,4,4]{2,1,0:T(4,128)S(1)} collective-permute-done((f32[2,4,4]{2,1,0:T(4,128)S(1)}, f32[2,4,4]{2,1,0:T(4,128)S(1)}, u32[]{:S(2)}, u32[]{:S(2)}) %collective-permute-start.6) | collective-permute-done | bytes 160 | tf_op jit(solution)/shard_map/ppermute | solution.py:308
  36.1 3.6 %collective-permute-done.7 = f32[2,4,4]{2,1,0:T(4,128)S(1)} collective-permute-done((f32[2,4,4]{2,1,0:T(4,128)S(1)}, f32[2,4,4]{2,1,0:T(4,128)S(1)}, u32[]{:S(2)}, u32[]{:S(2)}) %collective-permute-start.7) | collective-permute-done | bytes 160 | tf_op jit(solution)/shard_map/ppermute | solution.py:308
  39.7 0.3 collective-permute-start.8
  40.0 0.9 %collective-permute-done.8 = f32[2,4,4]{2,1,0:T(4,128)S(1)} collective-permute-done((f32[2,4,4]{2,1,0:T(4,128)S(1)}, f32[2,4,4]{2,1,0:T(4,128)S(1)}, u32[]{:S(2)}, u32[]{:S(2)}) %collective-permute-start.8) | collective-permute-done | bytes 160 | tf_op jit(solution)/shard_map/ppermute | solution.py:308
  40.9 2.7 %collective-permute-start.9 = (f32[2,4,4]{2,1,0:T(4,128)S(1)}, f32[2,4,4]{2,1,0:T(4,128)S(1)}, u32[]{:S(2)}, u32[]{:S(2)}) collective-permute-start(f32[2,4,4]{2,1,0:T(4,128)S(1)} %add.17), channel_id=1, source_target_pairs={{0,8},{4,12},{8,0},{12,4},{16,24},{20,28},{24,16},{28,20},{1,9},{5... | collective-permute-start | bytes 392 | tf_op jit(solution)/shard_map/ppermute | solution.py:308
  43.6 1.6 %collective-permute-done.9 = f32[2,4,4]{2,1,0:T(4,128)S(1)} collective-permute-done((f32[2,4,4]{2,1,0:T(4,128)S(1)}, f32[2,4,4]{2,1,0:T(4,128)S(1)}, u32[]{:S(2)}, u32[]{:S(2)}) %collective-permute-start.9) | collective-permute-done | bytes 160 | tf_op jit(solution)/shard_map/ppermute | solution.py:308
  45.1 3.0 %collective-permute-start.10 = (f32[2,4,4]{2,1,0:T(4,128)S(1)}, f32[2,4,4]{2,1,0:T(4,128)S(1)}, u32[]{:S(2)}, u32[]{:S(2)}) collective-permute-start(f32[2,4,4]{2,1,0:T(4,128)S(1)} %add.18), channel_id=1, source_target_pairs={{0,16},{4,20},{8,24},{12,28},{16,0},{20,4},{24,8},{28,12},{1,17},{... | collective-permute-start | bytes 392 | tf_op jit(solution)/shard_map/ppermute | solution.py:308
  48.2 1.6 %collective-permute-done.10 = f32[2,4,4]{2,1,0:T(4,128)S(1)} collective-permute-done((f32[2,4,4]{2,1,0:T(4,128)S(1)}, f32[2,4,4]{2,1,0:T(4,128)S(1)}, u32[]{:S(2)}, u32[]{:S(2)}) %collective-permute-start.10) | collective-permute-done | bytes 160 | tf_op jit(solution)/shard_map/ppermute | solution.py:308
  49.8 0.6 %add.19 = f32[2,4,4]{2,1,0:T(4,128)} add(f32[2,4,4]{2,1,0:T(4,128)S(1)} %add.18, f32[2,4,4]{2,1,0:T(4,128)S(1)} %collective-permute-done.10) | non-fusion elementwise | flops 32 | bytes 384 | tf_op jit(solution)/shard_map/add | solution.py:308
  50.4 2.5 %add_rims.1 = f32[2,4,3,8,16,128]{5,4,3,2,1,0:T(8,128)} custom-call(s32[6]{0:T(128)S(1)} %copy-done.4, f32[2,4,3,8,16,128]{5,4,3,2,1,0:T(8,128)S(1)} %get-tuple-element.16.partial_ref, f32[2,4,2,16,128]{4,3,2,1,0:T(8,128)S(1)} %collective-permute-done.3.hzf_ref, f32[2,4,2,8,128]{4,3,2,1,0:T(8,128)S(1)} %collective-permute-done.4.hxf_ref, ...), custom_call_target="tpu_custom_call" | custom-call | tf_op jit(solution)/shard_map/add_rims/pallas_call | solution.py:351
  (22 shorter events, 0.1 us)
Async XLA Ops:
  0.6 1.4 %copy-start = (f32[2,4,3,8,16,128]{5,4,3,2,1,0:T(8,128)S(1)}, f32[2,4,3,8,16,128]{5,4,3,2,1,0:T(8,128)}, u32[]{:S(2)}) copy-start(f32[2,4,3,8,16,128]{5,4,3,2,1,0:T(8,128)} %fields_ref.1) | copy-start | bytes 4718596
  2.0 0.7 %copy-start.3 = (f32[2,4,4]{2,1,0:T(4,128)S(1)}, f32[2,4,4]{2,1,0:T(4,128)}, u32[]{:S(2)}) copy-start(f32[2,4,4]{2,1,0:T(4,128)} %coeffs_ref.1) | copy-start | bytes 388
  2.7 12.5 %copy-start.2 = (s32[8,16,128]{2,1,0:T(8,128)S(1)}, s32[8,16,128]{2,1,0:T(8,128)}, u32[]{:S(2)}) copy-start(s32[8,16,128]{2,1,0:T(8,128)} %material_ref.1) | copy-start | bytes 196612
  2.7 12.5 %copy-start.4 = (s32[6]{0:T(128)S(1)}, s32[6]{0:T(128)}, u32[]{:S(2)}) copy-start(s32[6]{0:T(128)} %pml_ref.3) | copy-start | bytes 76
  2.7 12.5 %copy-start.5 = (f32[2,4]{1,0:T(2,128)S(1)}, f32[2,4]{1,0:T(2,128)}, u32[]{:S(2)}) copy-start(f32[2,4]{1,0:T(2,128)} %ritz_ref.1) | copy-start | bytes 100
  2.7 12.6 %copy-start.6 = (f32[4]{0:T(128)S(1)}, f32[4]{0:T(128)}, u32[]{:S(2)}) copy-start(f32[4]{0:T(128)} %eps_real_ref.1) | copy-start | bytes 52
  2.7 12.6 %copy-start.7 = (f32[4]{0:T(128)S(1)}, f32[4]{0:T(128)}, u32[]{:S(2)}) copy-start(f32[4]{0:T(128)} %eps_loss_ref.1) | copy-start | bytes 52
  5.8 9.4 %collective-permute-start = (f32[2,4,2,16,128]{4,3,2,1,0:T(8,128)S(1)}, f32[2,4,2,16,128]{4,3,2,1,0:T(8,128)S(1)}, u32[]{:S(2)}, u32[]{:S(2)}) collective-permute-start(f32[2,4,2,16,128]{4,3,2,1,0:T(8,128)S(1)} %get-tuple-element.13), channel_id=1, source_target_pairs={{1,0},{3,2},{5,4},{7,6},{9,8},{11,10},{13,12},{15,14},{17,16},{19,... | collective-permute-start | bytes 393224 | tf_op jit(solution)/shard_map/ppermute | solution.py:23
  7.1 3.1 %collective-permute-start.1 = (f32[2,4,2,8,128]{4,3,2,1,0:T(8,128)S(1)}, f32[2,4,2,8,128]{4,3,2,1,0:T(8,128)S(1)}, u32[]{:S(2)}, u32[]{:S(2)}) collective-permute-start(f32[2,4,2,8,128]{4,3,2,1,0:T(8,128)S(1)} %get-tuple-element.14), channel_id=1, source_target_pairs={{4,0},{8,4},{12,8},{16,12},{20,16},{24,20},{28,24},{5,1},{9,5},{13... | collective-permute-start | bytes 196616 | tf_op jit(solution)/shard_map/ppermute | solution.py:23
  8.4 6.8 %collective-permute-start.2 = (f32[8,16,128]{2,1,0:T(8,128)S(1)}, f32[8,16,128]{2,1,0:T(8,128)S(1)}, u32[]{:S(2)}, u32[]{:S(2)}) collective-permute-start(f32[8,16,128]{2,1,0:T(8,128)S(1)} %get-tuple-element.15), channel_id=1, source_target_pairs={{2,0},{3,1},{6,4},{7,5},{10,8},{11,9},{14,12},{15,13},{18,16},{19,... | collective-permute-start | bytes 196616 | tf_op jit(solution)/shard_map/ppermute | solution.py:23
  15.3 1.4 %copy-start.1 = (f32[2,4,3,8,16,128]{5,4,3,2,1,0:T(8,128)S(1)}, f32[2,4,3,8,16,128]{5,4,3,2,1,0:T(8,128)}, u32[]{:S(2)}) copy-start(f32[2,4,3,8,16,128]{5,4,3,2,1,0:T(8,128)} %get-tuple-element.9.basis_ref) | copy-start | bytes 4718596
  23.9 26.4 %collective-permute-start.3 = (f32[2,4,2,16,128]{4,3,2,1,0:T(8,128)S(1)}, f32[2,4,2,16,128]{4,3,2,1,0:T(8,128)S(1)}, u32[]{:S(2)}, u32[]{:S(2)}) collective-permute-start(f32[2,4,2,16,128]{4,3,2,1,0:T(8,128)S(1)} %get-tuple-element.17), channel_id=1, source_target_pairs={{0,1},{2,3},{4,5},{6,7},{8,9},{10,11},{12,13},{14,15},{16,17},{18,... | collective-permute-start | bytes 393224 | tf_op jit(solution)/shard_map/ppermute | solution.py:23
  28.5 21.9 %collective-permute-start.4 = (f32[2,4,2,8,128]{4,3,2,1,0:T(8,128)S(1)}, f32[2,4,2,8,128]{4,3,2,1,0:T(8,128)S(1)}, u32[]{:S(2)}, u32[]{:S(2)}) collective-permute-start(f32[2,4,2,8,128]{4,3,2,1,0:T(8,128)S(1)} %get-tuple-element.18), channel_id=1, source_target_pairs={{0,4},{4,8},{8,12},{12,16},{16,20},{20,24},{24,28},{1,5},{5,9},{9,... | collective-permute-start | bytes 196616 | tf_op jit(solution)/shard_map/ppermute | solution.py:23
  30.3 20.1 %collective-permute-start.5 = (f32[8,16,128]{2,1,0:T(8,128)S(1)}, f32[8,16,128]{2,1,0:T(8,128)S(1)}, u32[]{:S(2)}, u32[]{:S(2)}) collective-permute-start(f32[8,16,128]{2,1,0:T(8,128)S(1)} %get-tuple-element.19), channel_id=1, source_target_pairs={{0,2},{1,3},{4,6},{5,7},{8,10},{9,11},{12,14},{13,15},{16,18},{17,... | collective-permute-start | bytes 196616 | tf_op jit(solution)/shard_map/ppermute | solution.py:23
  32.4 3.7 %collective-permute-start.6 = (f32[2,4,4]{2,1,0:T(4,128)S(1)}, f32[2,4,4]{2,1,0:T(4,128)S(1)}, u32[]{:S(2)}, u32[]{:S(2)}) collective-permute-start(f32[2,4,4]{2,1,0:T(4,128)S(1)} %get-tuple-element.20), channel_id=1, source_target_pairs={{0,1},{1,0},{2,3},{3,2},{4,5},{5,4},{6,7},{7,6},{8,9},{9,8},{10,11... | collective-permute-start | bytes 392 | tf_op jit(solution)/shard_map/ppermute | solution.py:308
  36.1 3.6 %collective-permute-start.7 = (f32[2,4,4]{2,1,0:T(4,128)S(1)}, f32[2,4,4]{2,1,0:T(4,128)S(1)}, u32[]{:S(2)}, u32[]{:S(2)}) collective-permute-start(f32[2,4,4]{2,1,0:T(4,128)S(1)} %add.15), channel_id=1, source_target_pairs={{0,2},{2,0},{1,3},{3,1},{4,6},{6,4},{5,7},{7,5},{8,10},{10,8},{9,1... | collective-permute-start | bytes 392 | tf_op jit(solution)/shard_map/ppermute | solution.py:308
  39.7 1.2 %collective-permute-start.8 = (f32[2,4,4]{2,1,0:T(4,128)S(1)}, f32[2,4,4]{2,1,0:T(4,128)S(1)}, u32[]{:S(2)}, u32[]{:S(2)}) collective-permute-start(f32[2,4,4]{2,1,0:T(4,128)S(1)} %add.16), channel_id=1, source_target_pairs={{0,4},{4,0},{8,12},{12,8},{16,20},{20,16},{24,28},{28,24},{1,5},{5... | collective-permute-start | bytes 392 | tf_op jit(solution)/shard_map/ppermute | solution.py:308
  40.9 4.3 %collective-permute-start.9 = (f32[2,4,4]{2,1,0:T(4,128)S(1)}, f32[2,4,4]{2,1,0:T(4,128)S(1)}, u32[]{:S(2)}, u32[]{:S(2)}) collective-permute-start(f32[2,4,4]{2,1,0:T(4,128)S(1)} %add.17), channel_id=1, source_target_pairs={{0,8},{4,12},{8,0},{12,4},{16,24},{20,28},{24,16},{28,20},{1,9},{5... | collective-permute-start | bytes 392 | tf_op jit(solution)/shard_map/ppermute | solution.py:308
  45.1 4.6 %collective-permute-start.10 = (f32[2,4,4]{2,1,0:T(4,128)S(1)}, f32[2,4,4]{2,1,0:T(4,128)S(1)}, u32[]{:S(2)}, u32[]{:S(2)}) collective-permute-start(f32[2,4,4]{2,1,0:T(4,128)S(1)} %add.18), channel_id=1, source_target_pairs={{0,16},{4,20},{8,24},{12,28},{16,0},{20,4},{24,8},{28,12},{1,17},{... | collective-permute-start | bytes 392 | tf_op jit(solution)/shard_map/ppermute | solution.py:308
where the time goes:
time: 53.2 us; the launch traced here: 52.9 us
  starting transfers between devices  18.4 us (35%)
  waiting for transfers between devices  16.8 us (32%)
  Pallas kernels  12.8 us (24%)
  local copies, waits for them, and re-layouts  3.51 us (7%)
  between operations  0.76 us (1%)
  other arithmetic  0.61 us (1%)
    ppermute x6, starting transfers between devices, passed_along(): lax.ppermute(value, axis, [(source, source + steps) for source in range(l...  12.3 us
    ppermute x5, waiting for transfers between devices, summed_everywhere(): lax.ppermute(value, axis, [(source, source ^ reach) for source in range(c...  11.2 us
    pallas_call x1, Pallas kernels, body(): pl.pallas_call(image_kernel, out_shape=(f32(*fields.shape), f32(2, vector...  7.2 us
    ppermute x5, starting transfers between devices, summed_everywhere(): lax.ppermute(value, axis, [(source, source ^ reach) for source in range(c...  6.08 us
    ppermute x6, waiting for transfers between devices, passed_along(): lax.ppermute(value, axis, [(source, source + steps) for source in range(l...  5.54 us
    unnamed x16, local copies, waits for them, and re-layouts  3.51 us
    pallas_call x1, Pallas kernels, body(): pl.pallas_call(rotate_kernel, out_shape=(f32(*fields.shape), f32(*zf_shap...  3.09 us
    pallas_call x1, Pallas kernels, body(): pl.pallas_call(rim_kernel, out_shape=f32(*fields.shape), in_specs=[SMEM]...  2.53 us
  transfers between devices with their start and end apart: 11, of which 7 were waited for; matrix products, arithmetic and copies ran while one was open for 1% of the time, Pallas kernels for 0%

commit v1 on v0

--- a/solution.py
+++ b/solution.py
@@ -14,13 +14,13 @@
 
 VMEM = pl.BlockSpec(memory_space=pltpu.VMEM)
 SMEM = pl.BlockSpec(memory_space=pltpu.SMEM)
+HBM = pl.BlockSpec(memory_space=pltpu.HBM)
 HIGH = lax.Precision.HIGHEST
 
 
-def passed_along(value, axis, steps):
+def passed_round(value, axis, steps):
     count = lax.axis_size(axis)
-    leading, last = (max(0, -steps), min(count, count - steps))
-    return lax.ppermute(value, axis, [(source, source + steps) for source in range(leading, last)])
+    return lax.ppermute(value, axis, [(source, (source + steps) % count) for source in range(count)])
 
 
 def inverse_stretch(places, length, low_width, high_width):
@@ -62,46 +62,75 @@
     return jnp.full(shape, start, jnp.int32).astype(jnp.float32)
 
 
-def packed_lane(slot, part, vector, vectors):
+def packed_row(slot, part, vector, vectors):
     return (slot * 2 + part) * vectors + vector
 
 
-def rotate_kernel(coeffs_ref, fields_ref, basis_ref, zf_ref, xf_ref, yf_ref):
+def has_neighbour(direction, steps):
+    place = lax.axis_index(AXES[direction]) + steps
+    inside = (place >= 0) & (place < lax.axis_size(AXES[direction]))
+    return jnp.where(inside, 1.0, 0.0).astype(jnp.float32)
+
+
+def face_kernel(fields_hbm, fields_ref, zf_ref, xf_ref, yf_ref, sems):
     _, vectors, _, nz, nx, ny = fields_ref.shape
     lanes = lax.broadcasted_iota(jnp.int32, (nx, ny), 1)
+    copies = [
+        pltpu.make_async_copy(fields_hbm.at[part, :, comp], fields_ref.at[part, :, comp], sems.at[part, comp])
+        for comp in (0, 2, 1) for part in range(2)
+    ]
+    for copy in copies:
+        copy.start()
+    for copy in copies:
+        copy.wait()
+
+    packed = [jnp.zeros((nx, ny), jnp.float32)] * nz
+    for comp in (0, 2):
+        for part in range(2):
+            for a in range(vectors):
+                row = packed_row(comp // 2, part, a, vectors)
+                for z in range(nz):
+                    value = fields_ref[part, a, comp, z]
+                    packed[z] = jnp.where(lanes == row, pltpu.roll(value, row, 1) if row else value, packed[z])
+    turned = jnp.concatenate(packed, axis=0).T
+    yf_ref[...] = turned[:yf_ref.shape[0]]
+    for part in range(2):
+        for a in range(vectors):
+            for slot in range(2):
+                zf_ref[part, a, slot] = fields_ref[part, a, slot, 0]
+                xf_ref[part, a, slot] = fields_ref[part, a, slot + 1, :, 0, :]
+
+
+def rotated(coeffs_ref, old, b):
+    new = None
+    for a, value in enumerate(old):
+        term = cmul((coeffs_ref[0, a, b], coeffs_ref[1, a, b]), value)
+        new = term if new is None else add(new, term)
+    return new
+
+
+def rotate_kernel(coeffs_ref, fields_ref, basis_ref):
+    _, vectors, _, nz, nx, ny = fields_ref.shape
 
     @pl.loop(0, nz)
     def _(z):
-        packed = jnp.zeros((nx, ny), jnp.float32)
         for comp in range(3):
             old = [(fields_ref[0, a, comp, z], fields_ref[1, a, comp, z]) for a in range(vectors)]
             for b in range(vectors):
-                new = None
-                for a in range(vectors):
-                    term = cmul((coeffs_ref[0, a, b], coeffs_ref[1, a, b]), old[a])
-                    new = term if new is None else add(new, term)
+                new = rotated(coeffs_ref, old, b)
                 for part in range(2):
                     basis_ref[part, b, comp, z] = new[part]
-                    if comp != 1:
-                        lane = packed_lane(comp // 2, part, b, vectors)
-                        packed = jnp.where(lanes == lane, pltpu.roll(new[part], lane, 1), packed)
-                    if comp != 0:
-                        xf_ref[part, b, comp - 1, pl.ds(z, 1)] = new[part][0:1]
-        yf_ref[z] = packed
-
-    for part in range(2):
-        for b in range(vectors):
-            for comp in range(2):
-                zf_ref[part, b, comp] = basis_ref[part, b, comp, 0]
 
 
 def image_kernel(
-    pml_ref, eps_real_ref, eps_loss_ref, ritz_ref,
-    basis_ref, material_ref, zf_ref, xf_ref, yf_ref,
-    residual_ref, gram_ref, hzf_ref, hxf_ref, hyf_ref,
-    eps_ref, sz_ref, acc_ref, lift_ref,
+    pml_ref, eps_real_ref, eps_loss_ref, coeffs_ref,
+    basis_ref, material_ref, raw_zf_ref, raw_xf_ref, raw_yf_ref,
+    image_ref, gram_ref, hzf_ref, hxf_ref, hyf_ref, basis_hbm,
+    eps_ref, sz_ref, acc_ref, lift_ref, zf_ref, xf_ref, yt_ref, yf_ref, packed_ref, sem,
 ):
     _, vectors, _, nz, nx, ny = basis_ref.shape
+    keep = pltpu.make_async_copy(basis_ref, basis_hbm, sem)
+    keep.start()
     plane = (nx, ny)
     rows = lax.broadcasted_iota(jnp.int32, plane, 0)
     lanes = lax.broadcasted_iota(jnp.int32, plane, 1)
@@ -126,6 +155,36 @@
             value = jnp.where(material == number, -OMEGA_SQ * source[number], value)
         eps_ref[part] = value
 
+    for direction, raw_ref, face_ref in ((0, raw_zf_ref, zf_ref), (1, raw_xf_ref, xf_ref)):
+        inside = has_neighbour(direction, 1)
+        for slot in range(2):
+            old = [(raw_ref[0, a, slot] * inside, raw_ref[1, a, slot] * inside) for a in range(vectors)]
+            for b in range(vectors):
+                new = rotated(coeffs_ref, old, b)
+                for part in range(2):
+                    face_ref[part, b, slot] = new[part]
+    inside = has_neighbour(2, 1)
+    both = 2 * vectors
+    cells = nz * nx
+    which = lax.broadcasted_iota(jnp.int32, (both, cells), 0)
+    turned = [jnp.zeros((both, cells), jnp.float32)] * 2
+    for part in range(2):
+        for a in range(vectors):
+            column = jnp.zeros((both, cells), jnp.float32)
+            for b in range(vectors):
+                first, second = coeffs_ref[0, a, b] * inside, coeffs_ref[1, a, b] * inside
+                if part:
+                    first, second = -second, first
+                column = jnp.where(which == b, first, column)
+                column = jnp.where(which == vectors + b, second, column)
+            for slot in range(2):
+                row = packed_row(slot, part, a, vectors)
+                turned[slot] = turned[slot] + column * raw_yf_ref[row:row + 1]
+    yt_ref[...] = jnp.zeros(yt_ref.shape, jnp.float32)
+    for slot in range(2):
+        yt_ref[slot * both:(slot + 1) * both] = turned[slot]
+    yf_ref[...] = yt_ref[...].T.reshape(nz, nx, ny)
+
     for a in range(vectors):
         for comp in range(2):
             scaled = cmul(sz_next, (zf_ref[0, a, comp], zf_ref[1, a, comp]))
@@ -144,8 +203,8 @@
     def ahead_y(value, b, comp, z):
         out = []
         for part in range(2):
-            lane = packed_lane(comp // 2, part, b, vectors)
-            edge = pltpu.roll(yf_ref[z], ny - 1 - lane, 1)
+            row = packed_row(comp // 2, part, b, vectors)
+            edge = pltpu.roll(yf_ref[z], ny - 1 - row, 1)
             out.append(jnp.where(lanes == ny - 1, edge, pltpu.roll(value[part], ny - 1, 1)))
         return tuple(out)
 
@@ -158,12 +217,11 @@
 
     @pl.loop(0, nz)
     def _(z):
-        hyf_ref[z] = jnp.zeros(plane, jnp.float32)
+        packed_ref[z] = jnp.zeros(plane, jnp.float32)
 
     for b in range(vectors):
-        factor = (ritz_ref[0, b], ritz_ref[1, b])
-
-        def step(z, carry, last, b=b, factor=factor):
+
+        def step(z, carry, last, b=b):
             hx_before, hy_before, sums = carry
             sez = (sz_ref[0, pl.ds(z, 1)], sz_ref[1, pl.ds(z, 1)])
             shz = (sz_ref[2, pl.ds(z, 1)], sz_ref[3, pl.ds(z, 1)])
@@ -186,18 +244,17 @@
                 for comp, curl in enumerate((sub(byz, bzy), sub(bzx, bxz), sub(bxy, byx)))
             ]
             for comp in range(3):
-                left = sub(w[comp], cmul(factor, u[comp]))
-                for part in range(2):
-                    residual_ref[part, b, comp, z] = left[part]
+                for part in range(2):
+                    image_ref[part, b, comp, z] = w[comp][part]
             for part in range(2):
                 hxf_ref[part, b, 0, pl.ds(z, 1)] = hy[part][nx - 1:nx]
                 hxf_ref[part, b, 1, pl.ds(z, 1)] = hz[part][nx - 1:nx]
-            packed = hyf_ref[z]
+            packed = packed_ref[z]
             for slot, value in enumerate((hz, hx)):
                 for part in range(2):
-                    lane = packed_lane(slot, part, b, vectors)
-                    packed = jnp.where(lanes == lane, pltpu.roll(value[part], (lane + 1) % ny, 1), packed)
-            hyf_ref[z] = packed
+                    row = packed_row(slot, part, b, vectors)
+                    packed = jnp.where(lanes == row, pltpu.roll(value[part], (row + 1) % ny, 1), packed)
+            packed_ref[z] = packed
             new_sums = []
             for a in range(vectors):
                 total = None
@@ -228,11 +285,11 @@
             for part in range(2):
                 acc_ref[b, part * vectors + a] = sums[a][part] + fold(over[part])
 
+    hyf_ref[...] = packed_ref[...].reshape(cells, ny).T[:2 * both]
     pairs = lax.dot_general(
-        yf_ref[...].reshape(nz * nx, ny), hyf_ref[...].reshape(nz * nx, ny),
-        (((0,), (0,)), ((), ())), precision=HIGH, preferred_element_type=jnp.float32,
+        yt_ref[0:2 * both], hyf_ref[...], (((1,), (1,)), ((), ())),
+        precision=HIGH, preferred_element_type=jnp.float32,
     )
-    both = 2 * vectors
     block = pairs[both:2 * both, both:2 * both] - pairs[0:both, 0:both]
     side = cmul(
         (sy_next[0][:, :vectors], sy_next[1][:, :vectors]),
@@ -246,16 +303,19 @@
     body_sum = jnp.zeros((both, ny), jnp.float32)
     for b in range(vectors):
         body_sum = jnp.where(columns == b, totals[b], body_sum)
-    cells = 3.0 * nz * nx * ny
+    everywhere = 3.0 * nz * nx * ny
     for axis in AXES:
-        cells = cells * lax.axis_size(axis)
+        everywhere = everywhere * lax.axis_size(axis)
     for part in range(2):
         whole = body_sum[part * vectors:(part + 1) * vectors, :vectors] + side[part]
-        gram_ref[part] = whole * (1.0 / cells)
-
-
-def rim_kernel(pml_ref, partial_ref, hzf_ref, hxf_ref, hyf_ref, residual_ref):
-    _, vectors, _, nz, nx, ny = partial_ref.shape
+        gram_ref[part] = whole * (1.0 / everywhere)
+    keep.wait()
+
+
+def rim_kernel(
+    pml_ref, ritz_ref, basis_ref, image_ref, hzf_ref, hxf_ref, hyf_ref, residual_ref, yt_ref, packed_ref
+):
+    _, vectors, _, nz, nx, ny = basis_ref.shape
     plane = (nx, ny)
     rows = lax.broadcasted_iota(jnp.int32, plane, 0)
     lanes = lax.broadcasted_iota(jnp.int32, plane, 1)
@@ -263,22 +323,31 @@
     sex = axis_stretch(pml_ref, 1, nx, one_place(1, nx, 0, (1, ny)))
     sey = axis_stretch(pml_ref, 2, ny, one_place(2, ny, 0, plane))
     none = jnp.zeros(plane, jnp.float32)
-    sex = tuple(jnp.where(rows == 0, part, none) for part in sex)
-    sey = tuple(jnp.where(lanes == 0, part, none) for part in sey)
+    sez = tuple(part * has_neighbour(0, -1) for part in sez)
+    sex = tuple(jnp.where(rows == 0, part * has_neighbour(1, -1), none) for part in sex)
+    sey = tuple(jnp.where(lanes == 0, part * has_neighbour(2, -1), none) for part in sey)
+    yt_ref[...] = jnp.zeros(yt_ref.shape, jnp.float32)
+    yt_ref[:hyf_ref.shape[0]] = hyf_ref[...]
+    packed_ref[...] = yt_ref[...].T.reshape(nz, nx, ny)
 
     def step(z, first):
-        packed = hyf_ref[z]
+        packed = packed_ref[z]
         for b in range(vectors):
 
             def column(slot, b=b):
                 return tuple(
-                    pltpu.roll(packed, (ny - packed_lane(slot, part, b, vectors)) % ny, 1) for part in range(2)
+                    pltpu.roll(packed, (ny - packed_row(slot, part, b, vectors)) % ny, 1) for part in range(2)
                 )
 
             def row(slot, b=b):
                 return tuple(hxf_ref[part, b, slot, pl.ds(z, 1)] for part in range(2))
 
-            left = [(partial_ref[0, b, comp, z], partial_ref[1, b, comp, z]) for comp in range(3)]
+            factor = (ritz_ref[0, b], ritz_ref[1, b])
+            left = []
+            for comp in range(3):
+                u = (basis_ref[0, b, comp, z], basis_ref[1, b, comp, z])
+                w = (image_ref[0, b, comp, z], image_ref[1, b, comp, z])
+                left.append(sub(w, cmul(factor, u)))
             left[0] = sub(left[0], cmul(sey, column(0)))
             left[2] = add(left[2], cmul(sey, column(1)))
             left[1] = add(left[1], cmul(sex, row(1)))
@@ -297,66 +366,95 @@
         step(z, False)
 
 
-def summed_everywhere(value):
-    for axis in ("gz", "gy", "gx"):
+def sum_steps(axes):
+    steps = []
+    for axis in axes:
         count = lax.axis_size(axis)
         if count & (count - 1):
-            value = lax.psum(value, axis)
+            steps.append(lambda value, axis=axis: lax.psum(value, axis) - value)
             continue
         reach = 1
         while reach < count:
-            value = value + lax.ppermute(value, axis, [(source, source ^ reach) for source in range(count)])
+            pairs = [(source, source ^ reach) for source in range(count)]
+            steps.append(functools.partial(lax.ppermute, axis_name=axis, perm=pairs))
             reach *= 2
-    return value
+    return steps
 
 
 def body(fields, material, pml_width, eps_real, eps_loss, coeffs, ritz):
     _, vectors, _, nz, nx, ny = fields.shape
     f32 = lambda *shape: jax.ShapeDtypeStruct(shape, jnp.float32)
+    scratch = lambda *shape: pltpu.VMEM(shape, jnp.float32)
     params = pltpu.CompilerParams(vmem_limit_bytes=40 * 1024 * 1024)
+    whole = f32(*fields.shape)
     zf_shape = (2, vectors, 2, nx, ny)
     xf_shape = (2, vectors, 2, nz, ny)
-    yf_shape = (nz, nx, ny)
-    basis, zf, xf, yf = pl.pallas_call(
+    yf_shape = (4 * vectors, nz * nx)
+    faces = (f32(*zf_shape), f32(*xf_shape), f32(*yf_shape))
+    near, zf, xf, yf = pl.pallas_call(
+        face_kernel,
+        out_shape=(whole,) + faces,
+        in_specs=[HBM],
+        out_specs=(VMEM,) * 4,
+        scratch_shapes=[pltpu.SemaphoreType.DMA((2, 3))],
+        compiler_params=params,
+        name="take_faces",
+    )(pltpu.with_memory_space_constraint(fields, pltpu.HBM))
+    zf = passed_round(zf, "gz", -1)
+    xf = passed_round(xf, "gx", -1)
+    yf = passed_round(yf, "gy", -1)
+    cells = fields.size // 6 // vectors
+    basis = pl.pallas_call(
         rotate_kernel,
-        out_shape=(f32(*fields.shape), f32(*zf_shape), f32(*xf_shape), f32(*yf_shape)),
+        out_shape=whole,
         in_specs=[SMEM, VMEM],
-        out_specs=(VMEM,) * 4,
+        out_specs=VMEM,
         compiler_params=params,
+        cost_estimate=pl.CostEstimate(flops=400 * cells, bytes_accessed=8 * fields.size, transcendentals=0),
         name="rotate_vectors",
-    )(coeffs, fields)
-    zf = passed_along(zf, "gz", -1)
-    xf = passed_along(xf, "gx", -1)
-    yf = passed_along(yf, "gy", -1)
-    partial, gram, hzf, hxf, hyf = pl.pallas_call(
+    )(coeffs, near)
+    image, gram, hzf, hxf, hyf, basis_new = pl.pallas_call(
         image_kernel,
-        out_shape=(
-            f32(*fields.shape), f32(2, vectors, vectors), f32(*zf_shape), f32(*xf_shape), f32(*yf_shape),
-        ),
+        out_shape=(whole, f32(2, vectors, vectors)) + faces + (whole,),
         in_specs=[SMEM] * 4 + [VMEM] * 5,
-        out_specs=(VMEM,) * 5,
+        out_specs=(VMEM,) * 5 + (HBM,),
         scratch_shapes=[
-            pltpu.VMEM((2, nz, nx, ny), jnp.float32),
-            pltpu.VMEM((4, nz, ny), jnp.float32),
-            pltpu.VMEM((vectors, 2 * vectors, 8, ny), jnp.float32),
-            pltpu.VMEM(zf_shape, jnp.float32),
+            scratch(2, nz, nx, ny),
+            scratch(4, nz, ny),
+            scratch(vectors, 2 * vectors, 8, ny),
+            scratch(*zf_shape),
+            scratch(*zf_shape),
+            scratch(*xf_shape),
+            scratch(ny, nz * nx),
+            scratch(nz, nx, ny),
+            scratch(nz, nx, ny),
+            pltpu.SemaphoreType.DMA,
         ],
         compiler_params=params,
+        cost_estimate=pl.CostEstimate(flops=1200 * cells, bytes_accessed=8 * fields.size, transcendentals=0),
         name="apply_operator",
-    )(pml_width, eps_real, eps_loss, ritz, basis, material, zf, xf, yf)
-    hzf = passed_along(hzf, "gz", 1)
-    hxf = passed_along(hxf, "gx", 1)
-    hyf = passed_along(hyf, "gy", 1)
-    gram = summed_everywhere(gram)
+    )(pml_width, eps_real, eps_loss, coeffs, basis, material, zf, xf, yf)
+    hzf = passed_round(hzf, "gz", 1)
+    hxf = passed_round(hxf, "gx", 1)
+    hyf = passed_round(hyf, "gy", 1)
+    steps = sum_steps(("gx", "gy", "gz"))
+    for step in steps[:-2]:
+        gram = gram + step(gram)
+    gram, image = lax.optimization_barrier((gram, image))
+    other = steps[-2](gram)
     residual = pl.pallas_call(
         rim_kernel,
-        out_shape=f32(*fields.shape),
-        in_specs=[SMEM] + [VMEM] * 4,
+        out_shape=whole,
+        in_specs=[SMEM] * 2 + [VMEM] * 5,
         out_specs=VMEM,
+        scratch_shapes=[scratch(ny, nz * nx), scratch(nz, nx, ny)],
         compiler_params=params,
+        cost_estimate=pl.CostEstimate(flops=200 * cells, bytes_accessed=12 * fields.size, transcendentals=0),
         name="add_rims",
-    )(pml_width, partial, hzf, hxf, hyf)
-    return basis, residual, gram
+    )(pml_width, ritz, basis, image, hzf, hxf, hyf)
+    other, residual = lax.optimization_barrier((other, residual))
+    gram = gram + other
+    return basis_new, residual, gram + steps[-1](gram)
 
 
 def solution(mesh):

time: 53.2 us -> 38.8 us (0.73)
  waiting for transfers between devices: 16.8 us -> 9.39 us
  starting transfers between devices: 18.4 us -> 14.5 us
  local copies, waits for them, and re-layouts: 3.51 us -> 0.03 us
  Pallas kernels: 12.8 us -> 13.4 us
    ppermute x11, waiting for transfers between devices: 16.8 us -> 9.39 us  [the longest x3 6.44 us: body(): gram = gram + step(gram)]
    ppermute x11, starting transfers between devices: 18.4 us -> 14.5 us  [the longest x6 9.41 us: passed_round(): lax.ppermute(value, axis, [(source, (source + steps) % count) for source...]
    unnamed x16 -> x12, local copies, waits for them, and re-layouts: 3.51 us -> 0.03 us
    pallas_call x3 -> x4, Pallas kernels: 12.8 us -> 13.4 us  [the longest x1 7.46 us: body(): pl.pallas_call(image_kernel, out_shape=(whole, f32(2, vectors, vectors))...]
  transfers between devices with their start and end apart: 11 -> 11, of which waited for: 7 -> 6; matrix products, arithmetic and copies ran while one was open for 1% -> 0% of each run, Pallas kernels for 0% -> 11%
where the time goes in v1:
time: 38.8 us; the launch traced here: 38.6 us
  starting transfers between devices  14.5 us (37%)
  Pallas kernels  13.4 us (35%)
  waiting for transfers between devices  9.39 us (24%)
  between operations  0.73 us (2%)
  other arithmetic  0.61 us (2%)
    ppermute x6, starting transfers between devices, passed_round(): lax.ppermute(value, axis, [(source, (source + steps) % count) for source...  9.41 us
    pallas_call x1, Pallas kernels, body(): pl.pallas_call(image_kernel, out_shape=(whole, f32(2, vectors, vectors))...  7.46 us
    ppermute x3, waiting for transfers between devices, body(): gram = gram + step(gram)  6.44 us
    ppermute x3, starting transfers between devices, body(): gram = gram + step(gram)  2.84 us
    pallas_call x1, Pallas kernels, body(): pl.pallas_call(rim_kernel, out_shape=whole, in_specs=[SMEM] * 2 + [VMEM]...  2.62 us
    ppermute x1, waiting for transfers between devices, body(): return (basis_new, residual, gram + steps[-1](gram))  2.12 us
    pallas_call x1, Pallas kernels, body(): pl.pallas_call(face_kernel, out_shape=(whole,) + faces, in_specs=[HBM], o...  1.8 us
    ppermute x1, starting transfers between devices, body(): return (basis_new, residual, gram + steps[-1](gram))  1.49 us
  transfers between devices with their start and end apart: 11, of which 6 were waited for; matrix products, arithmetic and copies ran while one was open for 0% of the time, Pallas kernels for 11%

profile of v1, /device:TPU:0, one launch (start us, length us, event | category | flops | bytes accessed | tf_op | source)
XLA Modules:
  0.0 38.6 jit_solution(5763820095151400184)
XLA Ops:
  0.6 1.8 %take_faces.1 = (f32[2,4,3,8,16,128]{5,4,3,2,1,0:T(8,128)S(1)}, f32[2,4,2,16,128]{4,3,2,1,0:T(8,128)S(1)}, f32[2,4,2,8,128]{4,3,2,1,0:T(8,128)S(1)}, f32[16,128]{1,0:T(8,128)S(1)}) custom-call(f32[2,4,3,8,16,128]{5,4,3,2,1,0:T(8,128)} %fields_hbm.1), custom_call_target="tpu_custom_call" | custom-call | tf_op jit(solution)/shard_map/take_faces/pallas_call | solution.py:394
  2.4 3.0 %collective-permute-start = (f32[2,4,2,16,128]{4,3,2,1,0:T(8,128)S(1)}, f32[2,4,2,16,128]{4,3,2,1,0:T(8,128)S(1)}, u32[]{:S(2)}, u32[]{:S(2)}) collective-permute-start(f32[2,4,2,16,128]{4,3,2,1,0:T(8,128)S(1)} %get-tuple-element.18), channel_id=1, source_target_pairs={{0,1},{1,0},{2,3},{3,2},{4,5},{5,4},{6,7},{7,6},{8,9},{9,8},{10,11... | collective-permute-start | bytes 393224 | tf_op jit(solution)/shard_map/ppermute | solution.py:23
  5.4 2.8 %collective-permute-start.1 = (f32[2,4,2,8,128]{4,3,2,1,0:T(8,128)S(1)}, f32[2,4,2,8,128]{4,3,2,1,0:T(8,128)S(1)}, u32[]{:S(2)}, u32[]{:S(2)}) collective-permute-start(f32[2,4,2,8,128]{4,3,2,1,0:T(8,128)S(1)} %get-tuple-element.19), channel_id=1, source_target_pairs={{0,28},{4,0},{8,4},{12,8},{16,12},{20,16},{24,20},{28,24},{1,29},{... | collective-permute-start | bytes 196616 | tf_op jit(solution)/shard_map/ppermute | solution.py:23
  8.2 1.5 %collective-permute-start.2 = (f32[16,128]{1,0:T(8,128)S(1)}, f32[16,128]{1,0:T(8,128)S(1)}, u32[]{:S(2)}, u32[]{:S(2)}) collective-permute-start(f32[16,128]{1,0:T(8,128)S(1)} %get-tuple-element.20), channel_id=1, source_target_pairs={{0,2},{2,0},{1,3},{3,1},{4,6},{6,4},{5,7},{7,5},{8,10},{10,8},{9,1... | collective-permute-start | bytes 24584 | tf_op jit(solution)/shard_map/ppermute | solution.py:23
  9.7 0.0 copy-start.5
  9.8 1.5 %rotate_vectors.1.basis_ref = f32[2,4,3,8,16,128]{5,4,3,2,1,0:T(8,128)S(1)} custom-call(f32[2,4,4]{2,1,0:T(4,128)S(1)} %copy-done.1, f32[2,4,3,8,16,128]{5,4,3,2,1,0:T(8,128)S(1)} %get-tuple-element.17.fields_ref), custom_call_target="tpu_custom_call" | custom-call | flops 6553600 | bytes 3145728 | tf_op jit(solution)/shard_map/rotate_vectors/pallas_call | solution.py:407
  11.2 0.0 copy-start.3
  11.3 0.6 %collective-permute-done.2.raw_yf_ref = f32[16,128]{1,0:T(8,128)S(1)} collective-permute-done((f32[16,128]{1,0:T(8,128)S(1)}, f32[16,128]{1,0:T(8,128)S(1)}, u32[]{:S(2)}, u32[]{:S(2)}) %collective-permute-start.2) | collective-permute-done | bytes 8224 | tf_op jit(solution)/shard_map/ppermute | solution.py:23
  11.9 0.0 collective-permute-done.1.raw_xf_ref
  11.9 0.0 collective-permute-done.raw_zf_ref
  11.9 7.5 %apply_operator.1 = (f32[2,4,3,8,16,128]{5,4,3,2,1,0:T(8,128)S(1)}, f32[2,4,4]{2,1,0:T(4,128)S(1)}, f32[2,4,2,16,128]{4,3,2,1,0:T(8,128)S(1)}, f32[2,4,2,8,128]{...) custom-call(s32[6]{0:T(128)S(1)} %copy-done.2, f32[4]{0:T(128)S(1)} %copy-done.4, ...), custom_call_target="tpu_custom_call" | custom-call | flops 19660800 | bytes 3145728 | tf_op jit(solution)/shard_map/apply_operator/pallas_call | solution.py:416
  19.4 0.6 %collective-permute-start.7 = (f32[2,4,2,16,128]{4,3,2,1,0:T(8,128)S(1)}, f32[2,4,2,16,128]{4,3,2,1,0:T(8,128)S(1)}, u32[]{:S(2)}, u32[]{:S(2)}) collective-permute-start(f32[2,4,2,16,128]{4,3,2,1,0:T(8,128)S(1)} %get-tuple-element.26), channel_id=1, source_target_pairs={{0,1},{1,0},{2,3},{3,2},{4,5},{5,4},{6,7},{7,6},{8,9},{9,8},{10,11... | collective-permute-start | bytes 393224 | tf_op jit(solution)/shard_map/ppermute | solution.py:23
  20.0 1.5 %collective-permute-start.9 = (f32[16,128]{1,0:T(8,128)S(1)}, f32[16,128]{1,0:T(8,128)S(1)}, u32[]{:S(2)}, u32[]{:S(2)}) collective-permute-start(f32[16,128]{1,0:T(8,128)S(1)} %get-tuple-element.28), channel_id=1, source_target_pairs={{0,2},{2,0},{1,3},{3,1},{4,6},{6,4},{5,7},{7,5},{8,10},{10,8},{9,1... | collective-permute-start | bytes 24584 | tf_op jit(solution)/shard_map/ppermute | solution.py:23
  21.5 1.2 %collective-permute-done.3 = f32[2,4,4]{2,1,0:T(4,128)S(1)} collective-permute-done((f32[2,4,4]{2,1,0:T(4,128)S(1)}, f32[2,4,4]{2,1,0:T(4,128)S(1)}, u32[]{:S(2)}, u32[]{:S(2)}) %collective-permute-start.3) | collective-permute-done | bytes 160 | tf_op jit(solution)/shard_map/ppermute | solution.py:442
  22.7 0.9 %collective-permute-start.4 = (f32[2,4,4]{2,1,0:T(4,128)S(1)}, f32[2,4,4]{2,1,0:T(4,128)S(1)}, u32[]{:S(2)}, u32[]{:S(2)}) collective-permute-start(f32[2,4,4]{2,1,0:T(4,128)S(1)} %add.15), channel_id=1, source_target_pairs={{0,8},{4,12},{8,0},{12,4},{16,24},{20,28},{24,16},{28,20},{1,9},{5... | collective-permute-start | bytes 392 | tf_op jit(solution)/shard_map/ppermute | solution.py:442
  23.6 2.7 %collective-permute-done.4 = f32[2,4,4]{2,1,0:T(4,128)S(1)} collective-permute-done((f32[2,4,4]{2,1,0:T(4,128)S(1)}, f32[2,4,4]{2,1,0:T(4,128)S(1)}, u32[]{:S(2)}, u32[]{:S(2)}) %collective-permute-start.4) | collective-permute-done | bytes 160 | tf_op jit(solution)/shard_map/ppermute | solution.py:442
  26.3 1.9 %collective-permute-start.5 = (f32[2,4,4]{2,1,0:T(4,128)S(1)}, f32[2,4,4]{2,1,0:T(4,128)S(1)}, u32[]{:S(2)}, u32[]{:S(2)}) collective-permute-start(f32[2,4,4]{2,1,0:T(4,128)S(1)} %add.16), channel_id=1, source_target_pairs={{0,16},{4,20},{8,24},{12,28},{16,0},{20,4},{24,8},{28,12},{1,17},{... | collective-permute-start | bytes 392 | tf_op jit(solution)/shard_map/ppermute | solution.py:442
  28.2 2.6 %collective-permute-done.5 = f32[2,4,4]{2,1,0:T(4,128)S(1)} collective-permute-done((f32[2,4,4]{2,1,0:T(4,128)S(1)}, f32[2,4,4]{2,1,0:T(4,128)S(1)}, u32[]{:S(2)}, u32[]{:S(2)}) %collective-permute-start.5) | collective-permute-done | bytes 160 | tf_op jit(solution)/shard_map/ppermute | solution.py:442
  30.8 0.8 %collective-permute-start.6 = (f32[2,4,4]{2,1,0:T(4,128)S(1)}, f32[2,4,4]{2,1,0:T(4,128)S(1)}, u32[]{:S(2)}, u32[]{:S(2)}) collective-permute-start(f32[2,4,4]{2,1,0:T(4,128)S(1)} %add.17), channel_id=1, source_target_pairs={{0,2},{2,0},{1,3},{3,1},{4,6},{6,4},{5,7},{7,5},{8,10},{10,8},{9,1... | collective-permute-start | bytes 392 | tf_op jit(solution)/shard_map/ppermute | solution.py:444
  31.6 2.6 %add_rims.1 = f32[2,4,3,8,16,128]{5,4,3,2,1,0:T(8,128)} custom-call(s32[6]{0:T(128)S(1)} %copy-done.2, f32[2,4]{1,0:T(2,128)S(1)} %copy-done.3, f32[2,4,3,8,16,128]{5,4,3,2,1,0:T(8,128)S(1)} %rotate_vectors.1.basis_ref, f32[2,4,3,8,16,128]{5,4,3,2,1,0:T(8,128)S(1)} %get-tuple-element.25.image_ref, f32[2,4,2,16,128]{4,3,2,1,0:T(8,128)S(1)} %collective-permute-done.7.hzf_ref, ...), custom_call_target="tpu_custom_call" | custom-call | flops 3276800 | bytes 4718592 | tf_op jit(solution)/shard_map/add_rims/pallas_call | solution.py:445
  34.2 0.2 collective-permute-done.6
  34.4 1.5 %collective-permute-start.10 = (f32[2,4,4]{2,1,0:T(4,128)S(1)}, f32[2,4,4]{2,1,0:T(4,128)S(1)}, u32[]{:S(2)}, u32[]{:S(2)}) collective-permute-start(f32[2,4,4]{2,1,0:T(4,128)S(1)} %add.18), channel_id=1, source_target_pairs={{0,1},{1,0},{2,3},{3,2},{4,5},{5,4},{6,7},{7,6},{8,9},{9,8},{10,11... | collective-permute-start | bytes 392 | tf_op jit(solution)/shard_map/ppermute | solution.py:457
  35.9 2.1 %collective-permute-done.10 = f32[2,4,4]{2,1,0:T(4,128)S(1)} collective-permute-done((f32[2,4,4]{2,1,0:T(4,128)S(1)}, f32[2,4,4]{2,1,0:T(4,128)S(1)}, u32[]{:S(2)}, u32[]{:S(2)}) %collective-permute-start.10) | collective-permute-done | bytes 160 | tf_op jit(solution)/shard_map/ppermute | solution.py:457
  38.0 0.6 %add.19 = f32[2,4,4]{2,1,0:T(4,128)} add(f32[2,4,4]{2,1,0:T(4,128)S(1)} %add.18, f32[2,4,4]{2,1,0:T(4,128)S(1)} %collective-permute-done.10) | non-fusion elementwise | flops 32 | bytes 384 | tf_op jit(solution)/shard_map/add | solution.py:457
  (19 shorter events, 0.0 us)
Async XLA Ops:
  0.6 9.1 %copy-start.1 = (f32[2,4,4]{2,1,0:T(4,128)S(1)}, f32[2,4,4]{2,1,0:T(4,128)}, u32[]{:S(2)}) copy-start(f32[2,4,4]{2,1,0:T(4,128)} %coeffs_ref.3) | copy-start | bytes 388
  2.4 9.4 %collective-permute-start = (f32[2,4,2,16,128]{4,3,2,1,0:T(8,128)S(1)}, f32[2,4,2,16,128]{4,3,2,1,0:T(8,128)S(1)}, u32[]{:S(2)}, u32[]{:S(2)}) collective-permute-start(f32[2,4,2,16,128]{4,3,2,1,0:T(8,128)S(1)} %get-tuple-element.18), channel_id=1, source_target_pairs={{0,1},{1,0},{2,3},{3,2},{4,5},{5,4},{6,7},{7,6},{8,9},{9,8},{10,11... | collective-permute-start | bytes 393224 | tf_op jit(solution)/shard_map/ppermute | solution.py:23
  5.4 6.4 %collective-permute-start.1 = (f32[2,4,2,8,128]{4,3,2,1,0:T(8,128)S(1)}, f32[2,4,2,8,128]{4,3,2,1,0:T(8,128)S(1)}, u32[]{:S(2)}, u32[]{:S(2)}) collective-permute-start(f32[2,4,2,8,128]{4,3,2,1,0:T(8,128)S(1)} %get-tuple-element.19), channel_id=1, source_target_pairs={{0,28},{4,0},{8,4},{12,8},{16,12},{20,16},{24,20},{28,24},{1,29},{... | collective-permute-start | bytes 196616 | tf_op jit(solution)/shard_map/ppermute | solution.py:23
  8.2 3.7 %collective-permute-start.2 = (f32[16,128]{1,0:T(8,128)S(1)}, f32[16,128]{1,0:T(8,128)S(1)}, u32[]{:S(2)}, u32[]{:S(2)}) collective-permute-start(f32[16,128]{1,0:T(8,128)S(1)} %get-tuple-element.20), channel_id=1, source_target_pairs={{0,2},{2,0},{1,3},{3,1},{4,6},{6,4},{5,7},{7,5},{8,10},{10,8},{9,1... | collective-permute-start | bytes 24584 | tf_op jit(solution)/shard_map/ppermute | solution.py:23
  9.7 2.1 %copy-start = (s32[8,16,128]{2,1,0:T(8,128)S(1)}, s32[8,16,128]{2,1,0:T(8,128)}, u32[]{:S(2)}) copy-start(s32[8,16,128]{2,1,0:T(8,128)} %material_ref.1) | copy-start | bytes 196612
  9.7 2.1 %copy-start.2 = (s32[6]{0:T(128)S(1)}, s32[6]{0:T(128)}, u32[]{:S(2)}) copy-start(s32[6]{0:T(128)} %pml_ref.3) | copy-start | bytes 76
  9.7 2.1 %copy-start.4 = (f32[4]{0:T(128)S(1)}, f32[4]{0:T(128)}, u32[]{:S(2)}) copy-start(f32[4]{0:T(128)} %eps_real_ref.1) | copy-start | bytes 52
  9.7 2.2 %copy-start.5 = (f32[4]{0:T(128)S(1)}, f32[4]{0:T(128)}, u32[]{:S(2)}) copy-start(f32[4]{0:T(128)} %eps_loss_ref.1) | copy-start | bytes 52
  11.2 20.3 %copy-start.3 = (f32[2,4]{1,0:T(2,128)S(1)}, f32[2,4]{1,0:T(2,128)}, u32[]{:S(2)}) copy-start(f32[2,4]{1,0:T(2,128)} %ritz_ref.1) | copy-start | bytes 100
  19.4 12.2 %collective-permute-start.7 = (f32[2,4,2,16,128]{4,3,2,1,0:T(8,128)S(1)}, f32[2,4,2,16,128]{4,3,2,1,0:T(8,128)S(1)}, u32[]{:S(2)}, u32[]{:S(2)}) collective-permute-start(f32[2,4,2,16,128]{4,3,2,1,0:T(8,128)S(1)} %get-tuple-element.26), channel_id=1, source_target_pairs={{0,1},{1,0},{2,3},{3,2},{4,5},{5,4},{6,7},{7,6},{8,9},{9,8},{10,11... | collective-permute-start | bytes 393224 | tf_op jit(solution)/shard_map/ppermute | solution.py:23
  20.0 11.6 %collective-permute-start.8 = (f32[2,4,2,8,128]{4,3,2,1,0:T(8,128)S(1)}, f32[2,4,2,8,128]{4,3,2,1,0:T(8,128)S(1)}, u32[]{:S(2)}, u32[]{:S(2)}) collective-permute-start(f32[2,4,2,8,128]{4,3,2,1,0:T(8,128)S(1)} %get-tuple-element.27), channel_id=1, source_target_pairs={{0,4},{4,8},{8,12},{12,16},{16,20},{20,24},{24,28},{28,0},{1,5},{5... | collective-permute-start | bytes 196616 | tf_op jit(solution)/shard_map/ppermute | solution.py:23
  20.0 11.6 %collective-permute-start.9 = (f32[16,128]{1,0:T(8,128)S(1)}, f32[16,128]{1,0:T(8,128)S(1)}, u32[]{:S(2)}, u32[]{:S(2)}) collective-permute-start(f32[16,128]{1,0:T(8,128)S(1)} %get-tuple-element.28), channel_id=1, source_target_pairs={{0,2},{2,0},{1,3},{3,1},{4,6},{6,4},{5,7},{7,5},{8,10},{10,8},{9,1... | collective-permute-start | bytes 24584 | tf_op jit(solution)/shard_map/ppermute | solution.py:23
  21.5 1.2 %collective-permute-start.3 = (f32[2,4,4]{2,1,0:T(4,128)S(1)}, f32[2,4,4]{2,1,0:T(4,128)S(1)}, u32[]{:S(2)}, u32[]{:S(2)}) collective-permute-start(f32[2,4,4]{2,1,0:T(4,128)S(1)} %get-tuple-element.22), channel_id=1, source_target_pairs={{0,4},{4,0},{8,12},{12,8},{16,20},{20,16},{24,28},{28,24},{1,5},{5... | collective-permute-start | bytes 392 | tf_op jit(solution)/shard_map/ppermute | solution.py:442
  22.7 3.6 %collective-permute-start.4 = (f32[2,4,4]{2,1,0:T(4,128)S(1)}, f32[2,4,4]{2,1,0:T(4,128)S(1)}, u32[]{:S(2)}, u32[]{:S(2)}) collective-permute-start(f32[2,4,4]{2,1,0:T(4,128)S(1)} %add.15), channel_id=1, source_target_pairs={{0,8},{4,12},{8,0},{12,4},{16,24},{20,28},{24,16},{28,20},{1,9},{5... | collective-permute-start | bytes 392 | tf_op jit(solution)/shard_map/ppermute | solution.py:442
  26.3 4.5 %collective-permute-start.5 = (f32[2,4,4]{2,1,0:T(4,128)S(1)}, f32[2,4,4]{2,1,0:T(4,128)S(1)}, u32[]{:S(2)}, u32[]{:S(2)}) collective-permute-start(f32[2,4,4]{2,1,0:T(4,128)S(1)} %add.16), channel_id=1, source_target_pairs={{0,16},{4,20},{8,24},{12,28},{16,0},{20,4},{24,8},{28,12},{1,17},{... | collective-permute-start | bytes 392 | tf_op jit(solution)/shard_map/ppermute | solution.py:442
  30.8 3.6 %collective-permute-start.6 = (f32[2,4,4]{2,1,0:T(4,128)S(1)}, f32[2,4,4]{2,1,0:T(4,128)S(1)}, u32[]{:S(2)}, u32[]{:S(2)}) collective-permute-start(f32[2,4,4]{2,1,0:T(4,128)S(1)} %add.17), channel_id=1, source_target_pairs={{0,2},{2,0},{1,3},{3,1},{4,6},{6,4},{5,7},{7,5},{8,10},{10,8},{9,1... | collective-permute-start | bytes 392 | tf_op jit(solution)/shard_map/ppermute | solution.py:444
  34.4 3.6 %collective-permute-start.10 = (f32[2,4,4]{2,1,0:T(4,128)S(1)}, f32[2,4,4]{2,1,0:T(4,128)S(1)}, u32[]{:S(2)}, u32[]{:S(2)}) collective-permute-start(f32[2,4,4]{2,1,0:T(4,128)S(1)} %add.18), channel_id=1, source_target_pairs={{0,1},{1,0},{2,3},{3,2},{4,5},{5,4},{6,7},{7,6},{8,9},{9,8},{10,11... | collective-permute-start | bytes 392 | tf_op jit(solution)/shard_map/ppermute | solution.py:457

commit v2 on v1

--- a/solution.py
+++ b/solution.py
@@ -366,19 +366,35 @@
         step(z, False)
 
 
-def sum_steps(axes):
-    steps = []
+def sum_phases():
+    sizes = [lax.axis_size(axis) for axis in ("gx", "gy", "gz")]
+    if any(size & (size - 1) for size in sizes):
+        return None
+    across = sizes[1] * sizes[2]
+    masks = [1 << bit for bit in range((sizes[0] * across).bit_length() - 1)]
+    along = [mask for mask in masks if mask >= across]
+    rest = [mask for mask in masks if mask < across]
+    phases = [along[place:place + 2] for place in range(1, len(along), 2)] + [along[:1]]
+    phases += [rest[place:place + 2] for place in range(0, len(rest), 2)]
+    return [phase for phase in phases if phase]
+
+
+def from_partners(value, phase):
+    axes = ("gx", "gy", "gz")
+    count = 1
     for axis in axes:
-        count = lax.axis_size(axis)
-        if count & (count - 1):
-            steps.append(lambda value, axis=axis: lax.psum(value, axis) - value)
-            continue
-        reach = 1
-        while reach < count:
-            pairs = [(source, source ^ reach) for source in range(count)]
-            steps.append(functools.partial(lax.ppermute, axis_name=axis, perm=pairs))
-            reach *= 2
-    return steps
+        count *= lax.axis_size(axis)
+    first, second = phase[0], phase[-1]
+    distances = [first] if len(phase) == 1 else [first, second, first ^ second]
+    return [
+        lax.ppermute(value, axes, [(source, source ^ distance) for source in range(count)])
+        for distance in distances
+    ]
+
+
+def joined(value, others):
+    value = value + others[0]
+    return value + (others[1] + others[2]) if others[1:] else value
 
 
 def body(fields, material, pml_width, eps_real, eps_loss, coeffs, ritz):
@@ -434,14 +450,16 @@
         cost_estimate=pl.CostEstimate(flops=1200 * cells, bytes_accessed=8 * fields.size, transcendentals=0),
         name="apply_operator",
     )(pml_width, eps_real, eps_loss, coeffs, basis, material, zf, xf, yf)
+    phases = sum_phases()
+    others = from_partners(gram, phases[0])
     hzf = passed_round(hzf, "gz", 1)
     hxf = passed_round(hxf, "gx", 1)
     hyf = passed_round(hyf, "gy", 1)
-    steps = sum_steps(("gx", "gy", "gz"))
-    for step in steps[:-2]:
-        gram = gram + step(gram)
-    gram, image = lax.optimization_barrier((gram, image))
-    other = steps[-2](gram)
+    for phase in phases[1:]:
+        gram = joined(gram, others)
+        if phase is phases[-1]:
+            gram, image = lax.optimization_barrier((gram, image))
+        others = from_partners(gram, phase)
     residual = pl.pallas_call(
         rim_kernel,
         out_shape=whole,
@@ -452,9 +470,8 @@
         cost_estimate=pl.CostEstimate(flops=200 * cells, bytes_accessed=12 * fields.size, transcendentals=0),
         name="add_rims",
     )(pml_width, ritz, basis, image, hzf, hxf, hyf)
-    other, residual = lax.optimization_barrier((other, residual))
-    gram = gram + other
-    return basis_new, residual, gram + steps[-1](gram)
+    others, residual = lax.optimization_barrier((others, residual))
+    return basis_new, residual, joined(gram, others)
 
 
 def solution(mesh):

time: 38.8 us -> 34.3 us (0.88)
  waiting for transfers between devices: 9.39 us -> 2.84 us
  starting transfers between devices: 14.5 us -> 16.5 us
    ppermute x5 -> x7, waiting for transfers between devices: 8.77 us -> 2.22 us  [from_partners(): lax.ppermute(value, axes, [(source, source ^ distance) for source in rang...]
    ppermute x5 -> x7, starting transfers between devices: 5.08 us -> 7.18 us  [from_partners(): lax.ppermute(value, axes, [(source, source ^ distance) for source in rang...]
  transfers between devices with their start and end apart: 11 -> 13, of which waited for: 6 -> 4; matrix products, arithmetic and copies ran while one was open for 0% -> 0% of each run, Pallas kernels for 11% -> 12%
where the time goes in v2:
time: 34.3 us; the launch traced here: 34.1 us
  starting transfers between devices  16.5 us (48%)
  Pallas kernels  13.4 us (39%)
  waiting for transfers between devices  2.84 us (8%)
  between operations  0.74 us (2%)
  other arithmetic  0.61 us (2%)
    ppermute x6, starting transfers between devices, passed_round(): lax.ppermute(value, axis, [(source, (source + steps) % count) for source...  9.36 us
    pallas_call x1, Pallas kernels, body(): pl.pallas_call(image_kernel, out_shape=(whole, f32(2, vectors, vectors))...  7.46 us
    ppermute x7, starting transfers between devices, from_partners(): lax.ppermute(value, axes, [(source, source ^ distance) for source in rang...  7.18 us
    pallas_call x1, Pallas kernels, body(): pl.pallas_call(rim_kernel, out_shape=whole, in_specs=[SMEM] * 2 + [VMEM]...  2.62 us
    ppermute x7, waiting for transfers between devices, from_partners(): lax.ppermute(value, axes, [(source, source ^ distance) for source in rang...  2.22 us
    pallas_call x1, Pallas kernels, body(): pl.pallas_call(face_kernel, out_shape=(whole,) + faces, in_specs=[HBM], o...  1.8 us
    pallas_call x1, Pallas kernels, body(): pl.pallas_call(rotate_kernel, out_shape=whole, in_specs=[SMEM, VMEM], out...  1.48 us
  transfers between devices with their start and end apart: 13, of which 4 were waited for; matrix products, arithmetic and copies ran while one was open for 0% of the time, Pallas kernels for 12%

profile of v2, /device:TPU:0, one launch (start us, length us, event | category | flops | bytes accessed | tf_op | source)
XLA Modules:
  0.0 34.1 jit_solution(12218209337794100907)
XLA Ops:
  0.6 1.8 %take_faces.1 = (f32[2,4,3,8,16,128]{5,4,3,2,1,0:T(8,128)S(1)}, f32[2,4,2,16,128]{4,3,2,1,0:T(8,128)S(1)}, f32[2,4,2,8,128]{4,3,2,1,0:T(8,128)S(1)}, f32[16,128]{1,0:T(8,128)S(1)}) custom-call(f32[2,4,3,8,16,128]{5,4,3,2,1,0:T(8,128)} %fields_hbm.1), custom_call_target="tpu_custom_call" | custom-call | tf_op jit(solution)/shard_map/take_faces/pallas_call | solution.py:410
  2.4 3.0 %collective-permute-start = (f32[2,4,2,16,128]{4,3,2,1,0:T(8,128)S(1)}, f32[2,4,2,16,128]{4,3,2,1,0:T(8,128)S(1)}, u32[]{:S(2)}, u32[]{:S(2)}) collective-permute-start(f32[2,4,2,16,128]{4,3,2,1,0:T(8,128)S(1)} %get-tuple-element.20), channel_id=1, source_target_pairs={{0,1},{1,0},{2,3},{3,2},{4,5},{5,4},{6,7},{7,6},{8,9},{9,8},{10,11... | collective-permute-start | bytes 393224 | tf_op jit(solution)/shard_map/ppermute | solution.py:23
  5.4 2.8 %collective-permute-start.1 = (f32[2,4,2,8,128]{4,3,2,1,0:T(8,128)S(1)}, f32[2,4,2,8,128]{4,3,2,1,0:T(8,128)S(1)}, u32[]{:S(2)}, u32[]{:S(2)}) collective-permute-start(f32[2,4,2,8,128]{4,3,2,1,0:T(8,128)S(1)} %get-tuple-element.21), channel_id=1, source_target_pairs={{0,28},{4,0},{8,4},{12,8},{16,12},{20,16},{24,20},{28,24},{1,29},{... | collective-permute-start | bytes 196616 | tf_op jit(solution)/shard_map/ppermute | solution.py:23
  8.2 1.5 %collective-permute-start.2 = (f32[16,128]{1,0:T(8,128)S(1)}, f32[16,128]{1,0:T(8,128)S(1)}, u32[]{:S(2)}, u32[]{:S(2)}) collective-permute-start(f32[16,128]{1,0:T(8,128)S(1)} %get-tuple-element.22), channel_id=1, source_target_pairs={{0,2},{2,0},{1,3},{3,1},{4,6},{6,4},{5,7},{7,5},{8,10},{10,8},{9,1... | collective-permute-start | bytes 24584 | tf_op jit(solution)/shard_map/ppermute | solution.py:23
  9.7 0.0 copy-start.5
  9.8 1.5 %rotate_vectors.1.basis_ref = f32[2,4,3,8,16,128]{5,4,3,2,1,0:T(8,128)S(1)} custom-call(f32[2,4,4]{2,1,0:T(4,128)S(1)} %copy-done.1, f32[2,4,3,8,16,128]{5,4,3,2,1,0:T(8,128)S(1)} %get-tuple-element.19.fields_ref), custom_call_target="tpu_custom_call" | custom-call | flops 6553600 | bytes 3145728 | tf_op jit(solution)/shard_map/rotate_vectors/pallas_call | solution.py:423
  11.2 0.0 copy-start.3
  11.3 0.6 %collective-permute-done.2.raw_yf_ref = f32[16,128]{1,0:T(8,128)S(1)} collective-permute-done((f32[16,128]{1,0:T(8,128)S(1)}, f32[16,128]{1,0:T(8,128)S(1)}, u32[]{:S(2)}, u32[]{:S(2)}) %collective-permute-start.2) | collective-permute-done | bytes 8224 | tf_op jit(solution)/shard_map/ppermute | solution.py:23
  11.9 0.0 collective-permute-done.1.raw_xf_ref
  11.9 7.5 %apply_operator.1 = (f32[2,4,3,8,16,128]{5,4,3,2,1,0:T(8,128)S(1)}, f32[2,4,4]{2,1,0:T(4,128)S(1)}, f32[2,4,2,16,128]{4,3,2,1,0:T(8,128)S(1)}, f32[2,4,2,8,128]{...) custom-call(s32[6]{0:T(128)S(1)} %copy-done.2, f32[4]{0:T(128)S(1)} %copy-done.4, ...), custom_call_target="tpu_custom_call" | custom-call | flops 19660800 | bytes 3145728 | tf_op jit(solution)/shard_map/apply_operator/pallas_call | solution.py:432
  19.4 0.1 collective-permute-start.4
  19.5 1.2 %collective-permute-start.5 = (f32[2,4,4]{2,1,0:T(4,128)S(1)}, f32[2,4,4]{2,1,0:T(4,128)S(1)}, u32[]{:S(2)}, u32[]{:S(2)}) collective-permute-start(f32[2,4,4]{2,1,0:T(4,128)S(1)} %get-tuple-element.24), channel_id=1, source_target_pairs={{0,24},{1,25},{2,26},{3,27},{4,28},{5,29},{6,30},{7,31},{8,16},{9,... | collective-permute-start | bytes 392 | tf_op jit(solution)/shard_map/ppermute | solution.py:390
  20.7 2.2 %collective-permute-start.3 = (f32[2,4,4]{2,1,0:T(4,128)S(1)}, f32[2,4,4]{2,1,0:T(4,128)S(1)}, u32[]{:S(2)}, u32[]{:S(2)}) collective-permute-start(f32[2,4,4]{2,1,0:T(4,128)S(1)} %get-tuple-element.24), channel_id=1, source_target_pairs={{0,8},{1,9},{2,10},{3,11},{4,12},{5,13},{6,14},{7,15},{8,0},{9,1},... | collective-permute-start | bytes 392 | tf_op jit(solution)/shard_map/ppermute | solution.py:390
  22.9 0.5 %collective-permute-start.10 = (f32[2,4,2,16,128]{4,3,2,1,0:T(8,128)S(1)}, f32[2,4,2,16,128]{4,3,2,1,0:T(8,128)S(1)}, u32[]{:S(2)}, u32[]{:S(2)}) collective-permute-start(f32[2,4,2,16,128]{4,3,2,1,0:T(8,128)S(1)} %get-tuple-element.28), channel_id=1, source_target_pairs={{0,1},{1,0},{2,3},{3,2},{4,5},{5,4},{6,7},{7,6},{8,9},{9,8},{10,11... | collective-permute-start | bytes 393224 | tf_op jit(solution)/shard_map/ppermute | solution.py:23
  23.5 0.5 %collective-permute-done.4 = f32[2,4,4]{2,1,0:T(4,128)S(1)} collective-permute-done((f32[2,4,4]{2,1,0:T(4,128)S(1)}, f32[2,4,4]{2,1,0:T(4,128)S(1)}, u32[]{:S(2)}, u32[]{:S(2)}) %collective-permute-start.4) | collective-permute-done | bytes 160 | tf_op jit(solution)/shard_map/ppermute | solution.py:390
  23.9 1.5 %collective-permute-start.12 = (f32[16,128]{1,0:T(8,128)S(1)}, f32[16,128]{1,0:T(8,128)S(1)}, u32[]{:S(2)}, u32[]{:S(2)}) collective-permute-start(f32[16,128]{1,0:T(8,128)S(1)} %get-tuple-element.30), channel_id=1, source_target_pairs={{0,2},{2,0},{1,3},{3,1},{4,6},{6,4},{5,7},{7,5},{8,10},{10,8},{9,1... | collective-permute-start | bytes 24584 | tf_op jit(solution)/shard_map/ppermute | solution.py:23
  25.5 0.1 collective-permute-start.6
  25.6 1.1 %collective-permute-done.6 = f32[2,4,4]{2,1,0:T(4,128)S(1)} collective-permute-done((f32[2,4,4]{2,1,0:T(4,128)S(1)}, f32[2,4,4]{2,1,0:T(4,128)S(1)}, u32[]{:S(2)}, u32[]{:S(2)}) %collective-permute-start.6) | collective-permute-done | bytes 160 | tf_op jit(solution)/shard_map/ppermute | solution.py:390
  26.7 1.0 %collective-permute-start.7 = (f32[2,4,4]{2,1,0:T(4,128)S(1)}, f32[2,4,4]{2,1,0:T(4,128)S(1)}, u32[]{:S(2)}, u32[]{:S(2)}) collective-permute-start(f32[2,4,4]{2,1,0:T(4,128)S(1)} %add.24), channel_id=1, source_target_pairs={{0,1},{1,0},{2,3},{3,2},{4,5},{5,4},{6,7},{7,6},{8,9},{9,8},{10,11... | collective-permute-start | bytes 392 | tf_op jit(solution)/shard_map/ppermute | solution.py:390
  27.7 1.3 %collective-permute-start.8 = (f32[2,4,4]{2,1,0:T(4,128)S(1)}, f32[2,4,4]{2,1,0:T(4,128)S(1)}, u32[]{:S(2)}, u32[]{:S(2)}) collective-permute-start(f32[2,4,4]{2,1,0:T(4,128)S(1)} %add.24), channel_id=1, source_target_pairs={{0,2},{1,3},{2,0},{3,1},{4,6},{5,7},{6,4},{7,5},{8,10},{9,11},{10,... | collective-permute-start | bytes 392 | tf_op jit(solution)/shard_map/ppermute | solution.py:390
  29.0 1.2 %collective-permute-start.9 = (f32[2,4,4]{2,1,0:T(4,128)S(1)}, f32[2,4,4]{2,1,0:T(4,128)S(1)}, u32[]{:S(2)}, u32[]{:S(2)}) collective-permute-start(f32[2,4,4]{2,1,0:T(4,128)S(1)} %add.24), channel_id=1, source_target_pairs={{0,3},{1,2},{2,1},{3,0},{4,7},{5,6},{6,5},{7,4},{8,11},{9,10},{10,... | collective-permute-start | bytes 392 | tf_op jit(solution)/shard_map/ppermute | solution.py:390
  30.2 2.6 %add_rims.1 = f32[2,4,3,8,16,128]{5,4,3,2,1,0:T(8,128)} custom-call(s32[6]{0:T(128)S(1)} %copy-done.2, f32[2,4]{1,0:T(2,128)S(1)} %copy-done.3, f32[2,4,3,8,16,128]{5,4,3,2,1,0:T(8,128)S(1)} %rotate_vectors.1.basis_ref, f32[2,4,3,8,16,128]{5,4,3,2,1,0:T(8,128)S(1)} %get-tuple-element.27.image_ref, f32[2,4,2,16,128]{4,3,2,1,0:T(8,128)S(1)} %collective-permute-done.10.hzf_ref, ...), custom_call_target="tpu_custom_call" | custom-call | flops 3276800 | bytes 4718592 | tf_op jit(solution)/shard_map/add_rims/pallas_call | solution.py:463
  32.9 0.6 %collective-permute-done.9 = f32[2,4,4]{2,1,0:T(4,128)S(1)} collective-permute-done((f32[2,4,4]{2,1,0:T(4,128)S(1)}, f32[2,4,4]{2,1,0:T(4,128)S(1)}, u32[]{:S(2)}, u32[]{:S(2)}) %collective-permute-start.9) | collective-permute-done | bytes 160 | tf_op jit(solution)/shard_map/ppermute | solution.py:390
  33.5 0.6 %add_add_fusion = f32[1,8,4]{2,1,0:T(8,128)} fusion(f32[1,8,4]{2,1,0:T(8,128)S(1)} %bitcast.15, f32[1,8,4]{2,1,0:T(8,128)S(1)} %bitcast.18, f32[1,8,4]{2,1,0:T(8,128)S(1)} %bitcast.11, f32[1,8,4]{2,1,0:T(8,128)S(1)} %bitcast.14), kind=kLoop, calls=%fused_computation | loop fusion | flops 96 | bytes 640 | tf_op jit(solution)/shard_map/add | solution.py:397
  (21 shorter events, 0.1 us)
Async XLA Ops:
  0.6 9.1 %copy-start.1 = (f32[2,4,4]{2,1,0:T(4,128)S(1)}, f32[2,4,4]{2,1,0:T(4,128)}, u32[]{:S(2)}) copy-start(f32[2,4,4]{2,1,0:T(4,128)} %coeffs_ref.3) | copy-start | bytes 388
  2.4 9.4 %collective-permute-start = (f32[2,4,2,16,128]{4,3,2,1,0:T(8,128)S(1)}, f32[2,4,2,16,128]{4,3,2,1,0:T(8,128)S(1)}, u32[]{:S(2)}, u32[]{:S(2)}) collective-permute-start(f32[2,4,2,16,128]{4,3,2,1,0:T(8,128)S(1)} %get-tuple-element.20), channel_id=1, source_target_pairs={{0,1},{1,0},{2,3},{3,2},{4,5},{5,4},{6,7},{7,6},{8,9},{9,8},{10,11... | collective-permute-start | bytes 393224 | tf_op jit(solution)/shard_map/ppermute | solution.py:23
  5.4 6.4 %collective-permute-start.1 = (f32[2,4,2,8,128]{4,3,2,1,0:T(8,128)S(1)}, f32[2,4,2,8,128]{4,3,2,1,0:T(8,128)S(1)}, u32[]{:S(2)}, u32[]{:S(2)}) collective-permute-start(f32[2,4,2,8,128]{4,3,2,1,0:T(8,128)S(1)} %get-tuple-element.21), channel_id=1, source_target_pairs={{0,28},{4,0},{8,4},{12,8},{16,12},{20,16},{24,20},{28,24},{1,29},{... | collective-permute-start | bytes 196616 | tf_op jit(solution)/shard_map/ppermute | solution.py:23
  8.2 3.7 %collective-permute-start.2 = (f32[16,128]{1,0:T(8,128)S(1)}, f32[16,128]{1,0:T(8,128)S(1)}, u32[]{:S(2)}, u32[]{:S(2)}) collective-permute-start(f32[16,128]{1,0:T(8,128)S(1)} %get-tuple-element.22), channel_id=1, source_target_pairs={{0,2},{2,0},{1,3},{3,1},{4,6},{6,4},{5,7},{7,5},{8,10},{10,8},{9,1... | collective-permute-start | bytes 24584 | tf_op jit(solution)/shard_map/ppermute | solution.py:23
  9.7 2.1 %copy-start = (s32[8,16,128]{2,1,0:T(8,128)S(1)}, s32[8,16,128]{2,1,0:T(8,128)}, u32[]{:S(2)}) copy-start(s32[8,16,128]{2,1,0:T(8,128)} %material_ref.1) | copy-start | bytes 196612
  9.7 2.1 %copy-start.2 = (s32[6]{0:T(128)S(1)}, s32[6]{0:T(128)}, u32[]{:S(2)}) copy-start(s32[6]{0:T(128)} %pml_ref.3) | copy-start | bytes 76
  9.7 2.1 %copy-start.4 = (f32[4]{0:T(128)S(1)}, f32[4]{0:T(128)}, u32[]{:S(2)}) copy-start(f32[4]{0:T(128)} %eps_real_ref.1) | copy-start | bytes 52
  9.7 2.2 %copy-start.5 = (f32[4]{0:T(128)S(1)}, f32[4]{0:T(128)}, u32[]{:S(2)}) copy-start(f32[4]{0:T(128)} %eps_loss_ref.1) | copy-start | bytes 52
  11.2 19.0 %copy-start.3 = (f32[2,4]{1,0:T(2,128)S(1)}, f32[2,4]{1,0:T(2,128)}, u32[]{:S(2)}) copy-start(f32[2,4]{1,0:T(2,128)} %ritz_ref.1) | copy-start | bytes 100
  19.4 4.6 %collective-permute-start.4 = (f32[2,4,4]{2,1,0:T(4,128)S(1)}, f32[2,4,4]{2,1,0:T(4,128)S(1)}, u32[]{:S(2)}, u32[]{:S(2)}) collective-permute-start(f32[2,4,4]{2,1,0:T(4,128)S(1)} %get-tuple-element.24), channel_id=1, source_target_pairs={{0,16},{1,17},{2,18},{3,19},{4,20},{5,21},{6,22},{7,23},{8,24},{9,... | collective-permute-start | bytes 392 | tf_op jit(solution)/shard_map/ppermute | solution.py:390
  19.5 6.0 %collective-permute-start.5 = (f32[2,4,4]{2,1,0:T(4,128)S(1)}, f32[2,4,4]{2,1,0:T(4,128)S(1)}, u32[]{:S(2)}, u32[]{:S(2)}) collective-permute-start(f32[2,4,4]{2,1,0:T(4,128)S(1)} %get-tuple-element.24), channel_id=1, source_target_pairs={{0,24},{1,25},{2,26},{3,27},{4,28},{5,29},{6,30},{7,31},{8,16},{9,... | collective-permute-start | bytes 392 | tf_op jit(solution)/shard_map/ppermute | solution.py:390
  20.7 4.8 %collective-permute-start.3 = (f32[2,4,4]{2,1,0:T(4,128)S(1)}, f32[2,4,4]{2,1,0:T(4,128)S(1)}, u32[]{:S(2)}, u32[]{:S(2)}) collective-permute-start(f32[2,4,4]{2,1,0:T(4,128)S(1)} %get-tuple-element.24), channel_id=1, source_target_pairs={{0,8},{1,9},{2,10},{3,11},{4,12},{5,13},{6,14},{7,15},{8,0},{9,1},... | collective-permute-start | bytes 392 | tf_op jit(solution)/shard_map/ppermute | solution.py:390
  22.9 7.3 %collective-permute-start.10 = (f32[2,4,2,16,128]{4,3,2,1,0:T(8,128)S(1)}, f32[2,4,2,16,128]{4,3,2,1,0:T(8,128)S(1)}, u32[]{:S(2)}, u32[]{:S(2)}) collective-permute-start(f32[2,4,2,16,128]{4,3,2,1,0:T(8,128)S(1)} %get-tuple-element.28), channel_id=1, source_target_pairs={{0,1},{1,0},{2,3},{3,2},{4,5},{5,4},{6,7},{7,6},{8,9},{9,8},{10,11... | collective-permute-start | bytes 393224 | tf_op jit(solution)/shard_map/ppermute | solution.py:23
  23.5 6.8 %collective-permute-start.11 = (f32[2,4,2,8,128]{4,3,2,1,0:T(8,128)S(1)}, f32[2,4,2,8,128]{4,3,2,1,0:T(8,128)S(1)}, u32[]{:S(2)}, u32[]{:S(2)}) collective-permute-start(f32[2,4,2,8,128]{4,3,2,1,0:T(8,128)S(1)} %get-tuple-element.29), channel_id=1, source_target_pairs={{0,4},{4,8},{8,12},{12,16},{16,20},{20,24},{24,28},{28,0},{1,5},{5... | collective-permute-start | bytes 196616 | tf_op jit(solution)/shard_map/ppermute | solution.py:23
  23.9 5.1 %collective-permute-start.12 = (f32[16,128]{1,0:T(8,128)S(1)}, f32[16,128]{1,0:T(8,128)S(1)}, u32[]{:S(2)}, u32[]{:S(2)}) collective-permute-start(f32[16,128]{1,0:T(8,128)S(1)} %get-tuple-element.30), channel_id=1, source_target_pairs={{0,2},{2,0},{1,3},{3,1},{4,6},{6,4},{5,7},{7,5},{8,10},{10,8},{9,1... | collective-permute-start | bytes 24584 | tf_op jit(solution)/shard_map/ppermute | solution.py:23
  25.5 1.2 %collective-permute-start.6 = (f32[2,4,4]{2,1,0:T(4,128)S(1)}, f32[2,4,4]{2,1,0:T(4,128)S(1)}, u32[]{:S(2)}, u32[]{:S(2)}) collective-permute-start(f32[2,4,4]{2,1,0:T(4,128)S(1)} %bitcast.12), channel_id=1, source_target_pairs={{0,4},{1,5},{2,6},{3,7},{4,0},{5,1},{6,2},{7,3},{8,12},{9,13},{10,... | collective-permute-start | bytes 392 | tf_op jit(solution)/shard_map/ppermute | solution.py:390
  26.7 6.1 %collective-permute-start.7 = (f32[2,4,4]{2,1,0:T(4,128)S(1)}, f32[2,4,4]{2,1,0:T(4,128)S(1)}, u32[]{:S(2)}, u32[]{:S(2)}) collective-permute-start(f32[2,4,4]{2,1,0:T(4,128)S(1)} %add.24), channel_id=1, source_target_pairs={{0,1},{1,0},{2,3},{3,2},{4,5},{5,4},{6,7},{7,6},{8,9},{9,8},{10,11... | collective-permute-start | bytes 392 | tf_op jit(solution)/shard_map/ppermute | solution.py:390
  27.7 5.1 %collective-permute-start.8 = (f32[2,4,4]{2,1,0:T(4,128)S(1)}, f32[2,4,4]{2,1,0:T(4,128)S(1)}, u32[]{:S(2)}, u32[]{:S(2)}) collective-permute-start(f32[2,4,4]{2,1,0:T(4,128)S(1)} %add.24), channel_id=1, source_target_pairs={{0,2},{1,3},{2,0},{3,1},{4,6},{5,7},{6,4},{7,5},{8,10},{9,11},{10,... | collective-permute-start | bytes 392 | tf_op jit(solution)/shard_map/ppermute | solution.py:390
  29.0 4.5 %collective-permute-start.9 = (f32[2,4,4]{2,1,0:T(4,128)S(1)}, f32[2,4,4]{2,1,0:T(4,128)S(1)}, u32[]{:S(2)}, u32[]{:S(2)}) collective-permute-start(f32[2,4,4]{2,1,0:T(4,128)S(1)} %add.24), channel_id=1, source_target_pairs={{0,3},{1,2},{2,1},{3,0},{4,7},{5,6},{6,5},{7,4},{8,11},{9,10},{10,... | collective-permute-start | bytes 392 | tf_op jit(solution)/shard_map/ppermute | solution.py:390

commit v3 on v1

--- a/solution.py
+++ b/solution.py
@@ -364,21 +364,6 @@
     @pl.loop(1, nz)
     def _(z):
         step(z, False)
-
-
-def sum_steps(axes):
-    steps = []
-    for axis in axes:
-        count = lax.axis_size(axis)
-        if count & (count - 1):
-            steps.append(lambda value, axis=axis: lax.psum(value, axis) - value)
-            continue
-        reach = 1
-        while reach < count:
-            pairs = [(source, source ^ reach) for source in range(count)]
-            steps.append(functools.partial(lax.ppermute, axis_name=axis, perm=pairs))
-            reach *= 2
-    return steps
 
 
 def body(fields, material, pml_width, eps_real, eps_loss, coeffs, ritz):
@@ -434,14 +419,10 @@
         cost_estimate=pl.CostEstimate(flops=1200 * cells, bytes_accessed=8 * fields.size, transcendentals=0),
         name="apply_operator",
     )(pml_width, eps_real, eps_loss, coeffs, basis, material, zf, xf, yf)
+    grams = lax.all_gather(gram, ("gx", "gy", "gz"))
     hzf = passed_round(hzf, "gz", 1)
     hxf = passed_round(hxf, "gx", 1)
     hyf = passed_round(hyf, "gy", 1)
-    steps = sum_steps(("gx", "gy", "gz"))
-    for step in steps[:-2]:
-        gram = gram + step(gram)
-    gram, image = lax.optimization_barrier((gram, image))
-    other = steps[-2](gram)
     residual = pl.pallas_call(
         rim_kernel,
         out_shape=whole,
@@ -452,9 +433,8 @@
         cost_estimate=pl.CostEstimate(flops=200 * cells, bytes_accessed=12 * fields.size, transcendentals=0),
         name="add_rims",
     )(pml_width, ritz, basis, image, hzf, hxf, hyf)
-    other, residual = lax.optimization_barrier((other, residual))
-    gram = gram + other
-    return basis_new, residual, gram + steps[-1](gram)
+    grams, residual = lax.optimization_barrier((grams, residual))
+    return basis_new, residual, jnp.sum(grams, axis=0)
 
 
 def solution(mesh):

time: 38.8 us -> 93.3 us (2.40)
  blocking collectives: 0 us -> 68.3 us
  waiting for transfers between devices: 9.39 us -> 0.62 us
  starting transfers between devices: 14.5 us -> 9.41 us
    all_gather x0 -> x1, blocking collectives: none -> 68.3 us  [body(): grams = lax.all_gather(gram, ('gx', 'gy', 'gz'))]
    ppermute x5 -> x0, waiting for transfers between devices: 8.77 us -> none  [the longest x3 6.44 us: body(): gram = gram + step(gram)]
    ppermute x5 -> x0, starting transfers between devices: 5.08 us -> none  [the longest x3 2.84 us: body(): gram = gram + step(gram)]
  transfers between devices with their start and end apart: 11 -> 6, of which waited for: 6 -> 1; matrix products, arithmetic and copies ran while one was open for 0% -> 0% of each run, Pallas kernels for 11% -> 2%
where the time goes in v3:
time: 93.3 us; the launch traced here: 93.1 us
  blocking collectives  68.3 us (73%)
  Pallas kernels  13.4 us (14%)
  starting transfers between devices  9.41 us (10%)
    all_gather x1, blocking collectives, body(): grams = lax.all_gather(gram, ('gx', 'gy', 'gz'))  68.3 us
    ppermute x6, starting transfers between devices, passed_round(): lax.ppermute(value, axis, [(source, (source + steps) % count) for source...  9.41 us
    pallas_call x1, Pallas kernels, body(): pl.pallas_call(image_kernel, out_shape=(whole, f32(2, vectors, vectors))...  7.46 us
    pallas_call x1, Pallas kernels, body(): pl.pallas_call(rim_kernel, out_shape=whole, in_specs=[SMEM] * 2 + [VMEM]...  2.62 us
  transfers between devices with their start and end apart: 6, of which 1 were waited for; matrix products, arithmetic and copies ran while one was open for 0% of the time, Pallas kernels for 2%

profile of v3, /device:TPU:0, one launch (start us, length us, event | category | flops | bytes accessed | tf_op | source)
XLA Modules:
  0.0 93.1 jit_solution(10836206744542157126)
XLA Ops:
  0.6 0.0 copy-start.1
  0.6 1.8 %take_faces.1 = (f32[2,4,3,8,16,128]{5,4,3,2,1,0:T(8,128)S(1)}, f32[2,4,2,16,128]{4,3,2,1,0:T(8,128)S(1)}, f32[2,4,2,8,128]{4,3,2,1,0:T(8,128)S(1)}, f32[16,128]{1,0:T(8,128)S(1)}) custom-call(f32[2,4,3,8,16,128]{5,4,3,2,1,0:T(8,128)} %fields_hbm.1), custom_call_target="tpu_custom_call" | custom-call | tf_op jit(solution)/shard_map/take_faces/pallas_call | solution.py:379
  2.4 3.0 %collective-permute-start = (f32[2,4,2,16,128]{4,3,2,1,0:T(8,128)S(1)}, f32[2,4,2,16,128]{4,3,2,1,0:T(8,128)S(1)}, u32[]{:S(2)}, u32[]{:S(2)}) collective-permute-start(f32[2,4,2,16,128]{4,3,2,1,0:T(8,128)S(1)} %get-tuple-element.16), channel_id=1, source_target_pairs={{0,1},{1,0},{2,3},{3,2},{4,5},{5,4},{6,7},{7,6},{8,9},{9,8},{10,11... | collective-permute-start | bytes 393224 | tf_op jit(solution)/shard_map/ppermute | solution.py:23
  5.4 2.8 %collective-permute-start.1 = (f32[2,4,2,8,128]{4,3,2,1,0:T(8,128)S(1)}, f32[2,4,2,8,128]{4,3,2,1,0:T(8,128)S(1)}, u32[]{:S(2)}, u32[]{:S(2)}) collective-permute-start(f32[2,4,2,8,128]{4,3,2,1,0:T(8,128)S(1)} %get-tuple-element.17), channel_id=1, source_target_pairs={{0,28},{4,0},{8,4},{12,8},{16,12},{20,16},{24,20},{28,24},{1,29},{... | collective-permute-start | bytes 196616 | tf_op jit(solution)/shard_map/ppermute | solution.py:23
  8.2 1.5 %collective-permute-start.2 = (f32[16,128]{1,0:T(8,128)S(1)}, f32[16,128]{1,0:T(8,128)S(1)}, u32[]{:S(2)}, u32[]{:S(2)}) collective-permute-start(f32[16,128]{1,0:T(8,128)S(1)} %get-tuple-element.18), channel_id=1, source_target_pairs={{0,2},{2,0},{1,3},{3,1},{4,6},{6,4},{5,7},{7,5},{8,10},{10,8},{9,1... | collective-permute-start | bytes 24584 | tf_op jit(solution)/shard_map/ppermute | solution.py:23
  9.7 0.0 copy-done.1
  9.7 0.0 copy-start.5
  9.8 1.5 %rotate_vectors.1.basis_ref = f32[2,4,3,8,16,128]{5,4,3,2,1,0:T(8,128)S(1)} custom-call(f32[2,4,4]{2,1,0:T(4,128)S(1)} %copy-done.1, f32[2,4,3,8,16,128]{5,4,3,2,1,0:T(8,128)S(1)} %get-tuple-element.15.fields_ref), custom_call_target="tpu_custom_call" | custom-call | flops 6553600 | bytes 3145728 | tf_op jit(solution)/shard_map/rotate_vectors/pallas_call | solution.py:392
  11.2 0.0 copy-start.3
  11.3 0.6 collective-permute-done.2.raw_yf_ref
  11.9 0.0 collective-permute-done.1.raw_xf_ref
  11.9 0.0 collective-permute-done.raw_zf_ref
  11.9 0.0 copy-done
  11.9 0.0 copy-done.2
  11.9 7.5 %apply_operator.1 = (f32[2,4,3,8,16,128]{5,4,3,2,1,0:T(8,128)S(1)}, f32[2,4,4]{2,1,0:T(4,128)S(1)}, f32[2,4,2,16,128]{4,3,2,1,0:T(8,128)S(1)}, f32[2,4,2,8,128]{...) custom-call(s32[6]{0:T(128)S(1)} %copy-done.2, f32[4]{0:T(128)S(1)} %copy-done.4, ...), custom_call_target="tpu_custom_call" | custom-call | flops 19660800 | bytes 3145728 | tf_op jit(solution)/shard_map/apply_operator/pallas_call | solution.py:401
  19.4 0.6 collective-permute-start.3
  20.0 0.0 collective-permute-start.4
  20.0 1.5 %collective-permute-start.5 = (f32[16,128]{1,0:T(8,128)S(1)}, f32[16,128]{1,0:T(8,128)S(1)}, u32[]{:S(2)}, u32[]{:S(2)}) collective-permute-start(f32[16,128]{1,0:T(8,128)S(1)} %get-tuple-element.24), channel_id=1, source_target_pairs={{0,2},{2,0},{1,3},{3,1},{4,6},{6,4},{5,7},{7,5},{8,10},{10,8},{9,1... | collective-permute-start | bytes 24584 | tf_op jit(solution)/shard_map/ppermute | solution.py:23
  21.5 68.3 %all-gather = f32[64,4,4]{2,1,0:T(4,128)S(1)} all-gather(f32[2,4,4]{2,1,0:T(4,128)S(1)} %get-tuple-element.20), channel_id=2, replica_groups=mesh['gx'=8,'gy'=2,'gz'=2] {'gx','gy','gz'}, dimensions={0}, use_global_device_ids=true | all-gather | bytes 4224 | tf_op jit(solution)/shard_map/all_gather | solution.py:422
  89.8 0.0 collective-permute-done.5.hyf_ref
  89.8 0.0 collective-permute-done.4.hxf_ref
  89.8 0.0 collective-permute-done.3.hzf_ref
  89.8 2.6 %add_rims.1 = f32[2,4,3,8,16,128]{5,4,3,2,1,0:T(8,128)} custom-call(s32[6]{0:T(128)S(1)} %copy-done.2, f32[2,4]{1,0:T(2,128)S(1)} %copy-done.3, f32[2,4,3,8,16,128]{5,4,3,2,1,0:T(8,128)S(1)} %rotate_vectors.1.basis_ref, f32[2,4,3,8,16,128]{5,4,3,2,1,0:T(8,128)S(1)} %get-tuple-element.21.image_ref, f32[2,4,2,16,128]{4,3,2,1,0:T(8,128)S(1)} %collective-permute-done.3.hzf_ref, ...), custom_call_target="tpu_custom_call" | custom-call | flops 3276800 | bytes 4718592 | tf_op jit(solution)/shard_map/add_rims/pallas_call | solution.py:426
  92.5 0.6 reduce_sum.9
  (6 shorter events, 0.0 us)
Async XLA Ops:
  0.6 9.1 %copy-start.1 = (f32[2,4,4]{2,1,0:T(4,128)S(1)}, f32[2,4,4]{2,1,0:T(4,128)}, u32[]{:S(2)}) copy-start(f32[2,4,4]{2,1,0:T(4,128)} %coeffs_ref.3) | copy-start | bytes 388
  2.4 9.4 %collective-permute-start = (f32[2,4,2,16,128]{4,3,2,1,0:T(8,128)S(1)}, f32[2,4,2,16,128]{4,3,2,1,0:T(8,128)S(1)}, u32[]{:S(2)}, u32[]{:S(2)}) collective-permute-start(f32[2,4,2,16,128]{4,3,2,1,0:T(8,128)S(1)} %get-tuple-element.16), channel_id=1, source_target_pairs={{0,1},{1,0},{2,3},{3,2},{4,5},{5,4},{6,7},{7,6},{8,9},{9,8},{10,11... | collective-permute-start | bytes 393224 | tf_op jit(solution)/shard_map/ppermute | solution.py:23
  5.4 6.4 %collective-permute-start.1 = (f32[2,4,2,8,128]{4,3,2,1,0:T(8,128)S(1)}, f32[2,4,2,8,128]{4,3,2,1,0:T(8,128)S(1)}, u32[]{:S(2)}, u32[]{:S(2)}) collective-permute-start(f32[2,4,2,8,128]{4,3,2,1,0:T(8,128)S(1)} %get-tuple-element.17), channel_id=1, source_target_pairs={{0,28},{4,0},{8,4},{12,8},{16,12},{20,16},{24,20},{28,24},{1,29},{... | collective-permute-start | bytes 196616 | tf_op jit(solution)/shard_map/ppermute | solution.py:23
  8.2 3.7 %collective-permute-start.2 = (f32[16,128]{1,0:T(8,128)S(1)}, f32[16,128]{1,0:T(8,128)S(1)}, u32[]{:S(2)}, u32[]{:S(2)}) collective-permute-start(f32[16,128]{1,0:T(8,128)S(1)} %get-tuple-element.18), channel_id=1, source_target_pairs={{0,2},{2,0},{1,3},{3,1},{4,6},{6,4},{5,7},{7,5},{8,10},{10,8},{9,1... | collective-permute-start | bytes 24584 | tf_op jit(solution)/shard_map/ppermute | solution.py:23
  9.7 2.1 %copy-start = (s32[8,16,128]{2,1,0:T(8,128)S(1)}, s32[8,16,128]{2,1,0:T(8,128)}, u32[]{:S(2)}) copy-start(s32[8,16,128]{2,1,0:T(8,128)} %material_ref.1) | copy-start | bytes 196612
  9.7 2.1 %copy-start.2 = (s32[6]{0:T(128)S(1)}, s32[6]{0:T(128)}, u32[]{:S(2)}) copy-start(s32[6]{0:T(128)} %pml_ref.3) | copy-start | bytes 76
  9.7 2.1 %copy-start.4 = (f32[4]{0:T(128)S(1)}, f32[4]{0:T(128)}, u32[]{:S(2)}) copy-start(f32[4]{0:T(128)} %eps_real_ref.1) | copy-start | bytes 52
  9.7 2.2 %copy-start.5 = (f32[4]{0:T(128)S(1)}, f32[4]{0:T(128)}, u32[]{:S(2)}) copy-start(f32[4]{0:T(128)} %eps_loss_ref.1) | copy-start | bytes 52
  11.2 78.6 %copy-start.3 = (f32[2,4]{1,0:T(2,128)S(1)}, f32[2,4]{1,0:T(2,128)}, u32[]{:S(2)}) copy-start(f32[2,4]{1,0:T(2,128)} %ritz_ref.1) | copy-start | bytes 100
  19.4 70.4 %collective-permute-start.3 = (f32[2,4,2,16,128]{4,3,2,1,0:T(8,128)S(1)}, f32[2,4,2,16,128]{4,3,2,1,0:T(8,128)S(1)}, u32[]{:S(2)}, u32[]{:S(2)}) collective-permute-start(f32[2,4,2,16,128]{4,3,2,1,0:T(8,128)S(1)} %get-tuple-element.22), channel_id=1, source_target_pairs={{0,1},{1,0},{2,3},{3,2},{4,5},{5,4},{6,7},{7,6},{8,9},{9,8},{10,11... | collective-permute-start | bytes 393224 | tf_op jit(solution)/shard_map/ppermute | solution.py:23
  20.0 69.8 %collective-permute-start.4 = (f32[2,4,2,8,128]{4,3,2,1,0:T(8,128)S(1)}, f32[2,4,2,8,128]{4,3,2,1,0:T(8,128)S(1)}, u32[]{:S(2)}, u32[]{:S(2)}) collective-permute-start(f32[2,4,2,8,128]{4,3,2,1,0:T(8,128)S(1)} %get-tuple-element.23), channel_id=1, source_target_pairs={{0,4},{4,8},{8,12},{12,16},{16,20},{20,24},{24,28},{28,0},{1,5},{5... | collective-permute-start | bytes 196616 | tf_op jit(solution)/shard_map/ppermute | solution.py:23
  20.0 69.8 %collective-permute-start.5 = (f32[16,128]{1,0:T(8,128)S(1)}, f32[16,128]{1,0:T(8,128)S(1)}, u32[]{:S(2)}, u32[]{:S(2)}) collective-permute-start(f32[16,128]{1,0:T(8,128)S(1)} %get-tuple-element.24), channel_id=1, source_target_pairs={{0,2},{2,0},{1,3},{3,1},{4,6},{6,4},{5,7},{7,5},{8,10},{10,8},{9,1... | collective-permute-start | bytes 24584 | tf_op jit(solution)/shard_map/ppermute | solution.py:23

commit v4 on v2

v4 whole, which is shorter than its diff:
```python
import functools

import jax
import jax.numpy as jnp
from jax import lax
from jax.experimental import pallas as pl
from jax.experimental.pallas import tpu as pltpu
from jax.sharding import PartitionSpec as P

OMEGA_SQ = 0.36
SIGMA_TOP = 3.0
BOUNDS = ((4, 5), (0, 1), (2, 3))
AXES = ("gz", "gx", "gy")

VMEM = pl.BlockSpec(memory_space=pltpu.VMEM)
SMEM = pl.BlockSpec(memory_space=pltpu.SMEM)
HBM = pl.BlockSpec(memory_space=pltpu.HBM)


def passed_round(value, axis, steps):
    count = lax.axis_size(axis)
    return lax.ppermute(value, axis, [(source, (source + steps) % count) for source in range(count)])


def inverse_stretch(places, length, low_width, high_width):
    inside_depth = jnp.clip((low_width - places) / low_width, 0.0, 1.0) + jnp.clip(
        (places + 1.0 - length + high_width) / high_width, 0.0, 1.0
    )
    absorb = SIGMA_TOP * inside_depth * inside_depth
    scaled = 1.0 / (1.0 + absorb * absorb)
    return scaled, -absorb * scaled


def cmul(left, right):
    return (left[0] * right[0] - left[1] * right[1], left[0] * right[1] + left[1] * right[0])


def add(left, right):
    return (left[0] + right[0], left[1] + right[1])


def sub(left, right):
    return (left[0] - right[0], left[1] - right[1])


def axis_stretch(pml_ref, direction, count, places):
    total = count * lax.axis_size(AXES[direction])
    low_slot, high_slot = BOUNDS[direction]
    low = jnp.full(places.shape, pml_ref[low_slot], jnp.int32).astype(jnp.float32)
    high = jnp.full(places.shape, pml_ref[high_slot], jnp.int32).astype(jnp.float32)
    return inverse_stretch(places, jnp.float32(total), low, high)


def local_places(direction, count, shape, dim):
    start = lax.axis_index(AXES[direction]) * count
    return (lax.broadcasted_iota(jnp.int32, shape, dim) + start).astype(jnp.float32)


def one_place(direction, count, offset, shape):
    start = lax.axis_index(AXES[direction]) * count + offset
    return jnp.full(shape, start, jnp.int32).astype(jnp.float32)


def packed_row(slot, part, vector, vectors):
    return (slot * 2 + part) * vectors + vector


def has_neighbour(direction, steps):
    place = lax.axis_index(AXES[direction]) + steps
    inside = (place >= 0) & (place < lax.axis_size(AXES[direction]))
    return jnp.where(inside, 1.0, 0.0).astype(jnp.float32)


def face_kernel(fields_hbm, fields_ref, zf_ref, xf_ref, yf_ref, sems):
    _, vectors, _, nz, nx, ny = fields_ref.shape
    lanes = lax.broadcasted_iota(jnp.int32, (nx, ny), 1)
    copies = [
        pltpu.make_async_copy(fields_hbm.at[part, :, comp], fields_ref.at[part, :, comp], sems.at[part, comp])
        for comp in (0, 2, 1) for part in range(2)
    ]
    for copy in copies:
        copy.start()
    for copy in copies:
        copy.wait()

    packed = [jnp.zeros((nx, ny), jnp.float32)] * nz
    for comp in (0, 2):
        for part in range(2):
            for a in range(vectors):
                row = packed_row(comp // 2, part, a, vectors)
                for z in range(nz):
                    value = fields_ref[part, a, comp, z]
                    packed[z] = jnp.where(lanes == row, pltpu.roll(value, row, 1) if row else value, packed[z])
    turned = jnp.concatenate(packed, axis=0).T
    yf_ref[...] = turned[:yf_ref.shape[0]]
    for part in range(2):
        for a in range(vectors):
            for slot in range(2):
                zf_ref[part, a, slot] = fields_ref[part, a, slot, 0]
                xf_ref[part, a, slot] = fields_ref[part, a, slot + 1, :, 0, :]


def rotated(coeffs_ref, old, b):
    new = None
    for a, value in enumerate(old):
        term = cmul((coeffs_ref[0, a, b], coeffs_ref[1, a, b]), value)
        new = term if new is None else add(new, term)
    return new


SUB = 8
SHX, SEX, SHY, SEY = range(0, 8, 2)


def prepare_kernel(
    pml_ref, eps_real_ref, eps_loss_ref, coeffs_ref, fields_ref, material_ref,
    basis_ref, eps_ref, table_ref, sz_ref,
):
    _, vectors, _, nz, nx, ny = fields_ref.shape
    plane = (nx, ny)
    for slot, direction, half, count, dim in (
        (SHX, 1, 0.5, nx, 0), (SEX, 1, 0.0, nx, 0), (SHY, 2, 0.5, ny, 1), (SEY, 2, 0.0, ny, 1),
    ):
        values = axis_stretch(pml_ref, direction, count, local_places(direction, count, plane, dim) + half)
        for part in range(2):
            table_ref[slot + part] = values[part]
    for slot, half in ((0, 0.0), (2, 0.5)):
        values = axis_stretch(pml_ref, 0, nz, local_places(0, nz, (nz, ny), 0) + half)
        for part in range(2):
            sz_ref[slot + part] = values[part]

    @pl.loop(0, nz)
    def _(z):
        material = material_ref[z]
        for part, source in enumerate((eps_real_ref, eps_loss_ref)):
            value = jnp.zeros(plane, jnp.float32)
            for number in range(source.shape[0]):
                value = jnp.where(material == number, -OMEGA_SQ * source[number], value)
            eps_ref[part, z] = value
        for comp in range(3):
            old = [(fields_ref[0, a, comp, z], fields_ref[1, a, comp, z]) for a in range(vectors)]
            for b in range(vectors):
                new = rotated(coeffs_ref, old, b)
                for part in range(2):
                    basis_ref[part, b, comp, z] = new[part]


def turn_face(coeffs_ref, direction, raw_ref, face_ref):
    inside = has_neighbour(direction, 1)
    vectors = raw_ref.shape[1]
    for slot in range(2):
        old = [(raw_ref[0, a, slot] * inside, raw_ref[1, a, slot] * inside) for a in range(vectors)]
        for b in range(vectors):
            new = rotated(coeffs_ref, old, b)
            for part in range(2):
                face_ref[part, b, slot] = new[part]


def turn_column(coeffs_ref, raw_ref, rows_ref, cells_ref):
    vectors = coeffs_ref.shape[1]
    nz, nx, ny = cells_ref.shape
    inside = has_neighbour(2, 1)
    both = 2 * vectors
    which = lax.broadcasted_iota(jnp.int32, (both, nz * nx), 0)
    turned = [jnp.zeros((both, nz * nx), jnp.float32)] * 2
    for part in range(2):
        for a in range(vectors):
            column = jnp.zeros((both, nz * nx), jnp.float32)
            for b in range(vectors):
                first, second = coeffs_ref[0, a, b] * inside, coeffs_ref[1, a, b] * inside
                if part:
                    first, second = -second, first
                column = jnp.where(which == b, first, column)
                column = jnp.where(which == vectors + b, second, column)
            for slot in range(2):
                row = packed_row(slot, part, a, vectors)
                turned[slot] = turned[slot] + column * raw_ref[row:row + 1]
    for slot in range(2):
        rows_ref[slot * both:(slot + 1) * both] = turned[slot]
    rest = jnp.zeros((ny - 2 * both, nz * nx), jnp.float32)
    cells_ref[...] = jnp.concatenate(turned + [rest], axis=0).T.reshape(nz, nx, ny)


def plane_step(
    b, z, before, sums, up_of, basis_ref, eps_ref, table_ref, sz_ref, xf_ref, yf_ref, image_ref, hxf_ref, packed_ref
):
    _, vectors, _, _, nx, ny = basis_ref.shape
    tile = (SUB, ny)
    rows = lax.broadcasted_iota(jnp.int32, tile, 0)
    lanes = lax.broadcasted_iota(jnp.int32, tile, 1)
    parts = range(2)
    count = nx // SUB
    cut = [slice(SUB * t, SUB * (t + 1)) for t in range(count)]

    def table(slot, t):
        return tuple(table_ref[slot + part, cut[t]] for part in parts)

    sez = tuple(sz_ref[part, pl.ds(z, 1)] for part in parts)
    shz = tuple(sz_ref[2 + part, pl.ds(z, 1)] for part in parts)
    shy, sey = table(SHY, 0), table(SEY, 0)

    def turned_up(comp, t):
        return tuple(pltpu.roll(basis_ref[part, b, comp, z, cut[t]], SUB - 1, 0) for part in parts)

    sums = list(sums)
    after, behind_y, behind_z = [], None, None
    for t in range(count):
        u = [tuple(basis_ref[part, b, comp, z, cut[t]] for part in parts) for comp in range(3)]
        up = [up_of(comp, t) for comp in range(2)]
        dzx, dzy = (cmul(shz, sub(up[comp], u[comp])) for comp in range(2))

        def ahead_x(comp):
            if t + 1 < count:
                edge = turned_up(comp, t + 1)
            else:
                edge = tuple(xf_ref[part, b, comp - 1, pl.ds(z, 1)] for part in parts)
            here = turned_up(comp, t)
            return tuple(jnp.where(rows == SUB - 1, edge[part], here[part]) for part in parts)

        def ahead_y(comp):
            out = []
            for part in parts:
                row = packed_row(comp // 2, part, b, vectors)
                edge = pltpu.roll(yf_ref[z, cut[t]], ny - 1 - row, 1)
                out.append(jnp.where(lanes == ny - 1, edge, pltpu.roll(u[comp][part], ny - 1, 1)))
            return tuple(out)

        shx, sex = table(SHX, t), table(SEX, t)
        dxy, dxz = (cmul(shx, sub(ahead_x(comp), u[comp])) for comp in (1, 2))
        dyx, dyz = (cmul(shy, sub(ahead_y(comp), u[comp])) for comp in (0, 2))
        hx, hy, hz = sub(dyz, dzy), sub(dzx, dxz), sub(dxy, dyx)

        def behind_x(here, past):
            return tuple(
                jnp.where(rows == 0, 0.0 if past is None else past[part], here[part]) for part in parts
            )

        def back_y(value):
            return tuple(jnp.where(lanes == 0, 0.0, pltpu.roll(value[part], 1, 1)) for part in parts)

        down_y = tuple(pltpu.roll(hy[part], 1, 0) for part in parts)
        down_z = tuple(pltpu.roll(hz[part], 1, 0) for part in parts)
        bxy = cmul(sex, sub(hy, behind_x(down_y, behind_y)))
        bxz = cmul(sex, sub(hz, behind_x(down_z, behind_z)))
        behind_y, behind_z = down_y, down_z
        byz, byx = (cmul(sey, sub(h, back_y(h))) for h in (hz, hx))
        bzx, bzy = (cmul(sez, sub(h, past)) for h, past in zip((hx, hy), before[t]))
        eps = tuple(eps_ref[part, z, cut[t]] for part in parts)
        w = [
            add(curl, cmul(eps, u[comp]))
            for comp, curl in enumerate((sub(byz, bzy), sub(bzx, bxz), sub(bxy, byx)))
        ]
        for comp in range(3):
            for part in parts:
                image_ref[part, b, comp, z, cut[t]] = w[comp][part]
        for a in range(vectors):
            total = sums[a]
            for comp in range(3):
                total = add(total, cmul(tuple(basis_ref[part, a, comp, z, cut[t]] for part in parts), w[comp]))
            sums[a] = total
        packed = packed_ref[z, cut[t]]
        for slot, value in enumerate((hz, hx)):
            for part in parts:
                row = packed_row(slot, part, b, vectors)
                packed = jnp.where(lanes == row, pltpu.roll(value[part], (row + 1) % ny, 1), packed)
        packed_ref[z, cut[t]] = packed
        after.append((hx, hy))
    for part in parts:
        hxf_ref[part, b, 0, pl.ds(z, 1)] = hy[part][SUB - 1:]
        hxf_ref[part, b, 1, pl.ds(z, 1)] = hz[part][SUB - 1:]
    return after, sums


def inner_kernel(
    coeffs_ref, basis_ref, eps_ref, table_ref, sz_ref, raw_xf_ref, raw_yf_ref,
    image_ref, acc_ref, before_ref, hxf_ref, packed_ref, xf_ref, yt_ref, yf_ref, basis_hbm, sem,
):
    _, vectors, _, nz, nx, ny = basis_ref.shape
    keep = pltpu.make_async_copy(basis_ref, basis_hbm, sem)
    keep.start()
    turn_face(coeffs_ref, 1, raw_xf_ref, xf_ref)
    turn_column(coeffs_ref, raw_yf_ref, yt_ref, yf_ref)
    packed_ref[...] = jnp.zeros(packed_ref.shape, jnp.float32)
    count = nx // SUB

    for b in range(vectors):

        def step(z, carry, b=b):
            def up_of(comp, t):
                return tuple(basis_ref[part, b, comp, z + 1, SUB * t:SUB * (t + 1)] for part in range(2))

            return plane_step(
                b, z, *carry, up_of, basis_ref, eps_ref, table_ref, sz_ref, xf_ref, yf_ref,
                image_ref, hxf_ref, packed_ref,
            )

        none = (jnp.zeros((SUB, ny), jnp.float32),) * 2
        before, sums = lax.fori_loop(0, nz - 1, step, ([(none, none)] * count, [none] * vectors))
        for part in range(2):
            for a in range(vectors):
                acc_ref[b, part * vectors + a] = sums[a][part]
            for t in range(count):
                for slot in range(2):
                    before_ref[part, b, slot, SUB * t:SUB * (t + 1)] = before[t][slot][part]
    keep.wait()


def outer_kernel(
    pml_ref, coeffs_ref, basis_ref, eps_ref, table_ref, sz_ref, raw_zf_ref, xf_ref, yt_ref, yf_ref,
    image_in, acc_ref, before_ref, hxf_in, packed_in,
    image_ref, hxf_ref, packed_ref, gram_ref, hzf_ref, hyf_ref, zf_ref,
):
    del image_in, hxf_in, packed_in
    _, vectors, _, nz, nx, ny = basis_ref.shape
    count = nx // SUB
    turn_face(coeffs_ref, 0, raw_zf_ref, zf_ref)
    sz_next = axis_stretch(pml_ref, 0, nz, one_place(0, nz, nz, (1, ny)))
    sx_next = axis_stretch(pml_ref, 1, nx, one_place(1, nx, nx, (1, ny)))
    sy_next = axis_stretch(pml_ref, 2, ny, one_place(2, ny, ny, (1, nz * nx)))
    all_sums = []
    for b in range(vectors):

        def tile_of(ref, slot, t, b=b):
            return tuple(ref[part, b, slot, SUB * t:SUB * (t + 1)] for part in range(2))

        before = [tuple(tile_of(before_ref, slot, t) for slot in range(2)) for t in range(count)]
        sums = [(acc_ref[b, a], acc_ref[b, vectors + a]) for a in range(vectors)]
        after, sums = plane_step(
            b, nz - 1, before, sums, functools.partial(tile_of, zf_ref), basis_ref, eps_ref, table_ref, sz_ref,
            xf_ref, yf_ref, image_ref, hxf_ref, packed_ref,
        )
        h_y = tuple(hxf_ref[part, b, 0] for part in range(2))
        h_z = tuple(hxf_ref[part, b, 1] for part in range(2))
        for a in range(vectors):
            over = None
            for t, (hx, hy) in enumerate(after):
                ends = [tuple(zf_ref[part, a, slot, SUB * t:SUB * (t + 1)] for part in range(2)) for slot in range(2)]
                term = sub(cmul(ends[0], hy), cmul(ends[1], hx))
                over = term if over is None else add(over, term)
            total = add(sums[a], cmul(sz_next, over))
            over = cmul(tuple(xf_ref[part, a, 0] for part in range(2)), h_z)
            over = sub(over, cmul(tuple(xf_ref[part, a, 1] for part in range(2)), h_y))
            over = cmul(sx_next, over)
            for row in range(0, nz, SUB):
                total = add(total, tuple(part[row:row + SUB] for part in over))
            sums[a] = total
        all_sums.append(sums)
        for part in range(2):
            for t, pair in enumerate(after):
                for slot in range(2):
                    hzf_ref[part, b, slot, SUB * t:SUB * (t + 1)] = pair[slot][part]

    both = 2 * vectors
    hyf_ref[...] = packed_ref[...].reshape(nz * nx, ny).T[:2 * both]
    ends = [
        cmul(sy_next, (yt_ref[slot * both:slot * both + vectors], yt_ref[slot * both + vectors:(slot + 1) * both]))
        for slot in range(2)
    ]
    columns = lax.broadcasted_iota(jnp.int32, (both, ny), 1)
    gram = jnp.zeros((both, ny), jnp.float32)
    for b in range(vectors):
        flat = jnp.concatenate(
            [jnp.sum(all_sums[b][a][part], axis=0, keepdims=True) for part in range(2) for a in range(vectors)], axis=0
        )
        over = None
        for slot in range(2):
            h = tuple(hyf_ref[packed_row(slot, part, b, vectors)][None] for part in range(2))
            term = cmul(ends[slot], h)
            over = term if over is None else sub(term, over)
        side = jnp.concatenate(over, axis=0)
        total = jnp.sum(flat, axis=1, keepdims=True) + jnp.sum(side, axis=1, keepdims=True)
        gram = jnp.where(columns == b, total, gram)
    everywhere = 3.0 * nz * nx * ny
    for axis in AXES:
        everywhere = everywhere * lax.axis_size(axis)
    gram = gram * (1.0 / everywhere)
    for part in range(2):
        gram_ref[part] = gram[part * vectors:(part + 1) * vectors, :vectors]


def rim_kernel(
    pml_ref, ritz_ref, basis_ref, image_ref, hzf_ref, hxf_ref, hyf_ref, residual_hbm, residual_ref, packed_ref, sems
):
    _, vectors, _, nz, nx, ny = basis_ref.shape
    plane = (nx, ny)
    rows = lax.broadcasted_iota(jnp.int32, plane, 0)
    lanes = lax.broadcasted_iota(jnp.int32, plane, 1)
    sez = axis_stretch(pml_ref, 0, nz, one_place(0, nz, 0, plane))
    sex = axis_stretch(pml_ref, 1, nx, one_place(1, nx, 0, (1, ny)))
    sey = axis_stretch(pml_ref, 2, ny, one_place(2, ny, 0, plane))
    none = jnp.zeros(plane, jnp.float32)
    sez = tuple(part * has_neighbour(0, -1) for part in sez)
    sex = tuple(jnp.where(rows == 0, part * has_neighbour(1, -1), none) for part in sex)
    sey = tuple(jnp.where(lanes == 0, part * has_neighbour(2, -1), none) for part in sey)
    rest = jnp.zeros((ny - hyf_ref.shape[0], nz * nx), jnp.float32)
    packed_ref[...] = jnp.concatenate([hyf_ref[...], rest], axis=0).T.reshape(nz, nx, ny)

    def kept(z):
        return pltpu.make_async_copy(residual_ref.at[:, :, :, z], residual_hbm.at[:, :, :, z], sems.at[z])

    def step(z, first):
        packed = packed_ref[z]
        for b in range(vectors):

            def column(slot, b=b):
                return tuple(
                    pltpu.roll(packed, (ny - packed_row(slot, part, b, vectors)) % ny, 1) for part in range(2)
                )

            def row(slot, b=b):
                return tuple(hxf_ref[part, b, slot, pl.ds(z, 1)] for part in range(2))

            factor = (ritz_ref[0, b], ritz_ref[1, b])
            left = []
            for comp in range(3):
                u = (basis_ref[0, b, comp, z], basis_ref[1, b, comp, z])
                w = (image_ref[0, b, comp, z], image_ref[1, b, comp, z])
                left.append(sub(w, cmul(factor, u)))
            left[0] = sub(left[0], cmul(sey, column(0)))
            left[2] = add(left[2], cmul(sey, column(1)))
            left[1] = add(left[1], cmul(sex, row(1)))
            left[2] = sub(left[2], cmul(sex, row(0)))
            if first:
                left[0] = add(left[0], cmul(sez, (hzf_ref[0, b, 1], hzf_ref[1, b, 1])))
                left[1] = sub(left[1], cmul(sez, (hzf_ref[0, b, 0], hzf_ref[1, b, 0])))
            for comp in range(3):
                for part in range(2):
                    residual_ref[part, b, comp, z] = left[comp][part]
        kept(z).start()

    step(0, True)

    @pl.loop(1, nz)
    def _(z):
        step(z, False)

    @pl.loop(0, nz)
    def _(z):
        kept(z).wait()


def sum_phases():
    sizes = [lax.axis_size(axis) for axis in ("gx", "gy", "gz")]
    if any(size & (size - 1) for size in sizes):
        return None
    across = sizes[1] * sizes[2]
    masks = [1 << bit for bit in range((sizes[0] * across).bit_length() - 1)]
    along = [mask for mask in masks if mask >= across]
    rest = [mask for mask in masks if mask < across]
    phases = [along[place:place + 2] for place in range(1, len(along), 2)] + [along[:1]]
    phases += [rest[place:place + 2] for place in range(0, len(rest), 2)]
    return [phase for phase in phases if phase]


def from_partners(value, phase):
    axes = ("gx", "gy", "gz")
    count = 1
    for axis in axes:
        count *= lax.axis_size(axis)
    first, second = phase[0], phase[-1]
    distances = [first] if len(phase) == 1 else [first, second, first ^ second]
    return [
        lax.ppermute(value, axes, [(source, source ^ distance) for source in range(count)])
        for distance in distances
    ]


def joined(value, others):
    value = value + others[0]
    return value + (others[1] + others[2]) if others[1:] else value


def body(fields, material, pml_width, eps_real, eps_loss, coeffs, ritz):
    _, vectors, _, nz, nx, ny = fields.shape
    f32 = lambda *shape: jax.ShapeDtypeStruct(shape, jnp.float32)
    scratch = lambda *shape: pltpu.VMEM(shape, jnp.float32)
    params = pltpu.CompilerParams(vmem_limit_bytes=40 * 1024 * 1024)
    whole = f32(*fields.shape)
    zf_shape = (2, vectors, 2, nx, ny)
    xf_shape = (2, vectors, 2, nz, ny)
    yf_shape = (4 * vectors, nz * nx)
    faces = (f32(*zf_shape), f32(*xf_shape), f32(*yf_shape))
    near, zf, xf, yf = pl.pallas_call(
        face_kernel,
        out_shape=(whole,) + faces,
        in_specs=[HBM],
        out_specs=(VMEM,) * 4,
        scratch_shapes=[pltpu.SemaphoreType.DMA((2, 3))],
        compiler_params=params,
        name="take_faces",
    )(pltpu.with_memory_space_constraint(fields, pltpu.HBM))
    xf = passed_round(xf, "gx", -1)
    yf = passed_round(yf, "gy", -1)
    zf = passed_round(zf, "gz", -1)
    cells = fields.size // 6 // vectors

    def cost(flops, passes):
        return pl.CostEstimate(flops=flops * cells, bytes_accessed=passes * 4 * fields.size, transcendentals=0)

    planes = f32(nz, nx, ny)
    basis, eps, table, sz = pl.pallas_call(
        prepare_kernel,
        out_shape=(whole, f32(2, nz, nx, ny), f32(8, nx, ny), f32(4, nz, ny)),
        in_specs=[SMEM] * 4 + [VMEM] * 2,
        out_specs=(VMEM,) * 4,
        compiler_params=params,
        cost_estimate=cost(400, 2),
        name="prepare",
    )(pml_width, eps_real, eps_loss, coeffs, near, material)
    image, acc, before, hxf, packed, xf, yt, yf, basis_new = pl.pallas_call(
        inner_kernel,
        out_shape=(
            whole, f32(vectors, 2 * vectors, SUB, ny), f32(*zf_shape), f32(*xf_shape), planes,
            f32(*xf_shape), f32(*yf_shape), planes, whole,
        ),
        in_specs=[SMEM] + [VMEM] * 6,
        out_specs=(VMEM,) * 8 + (HBM,),
        scratch_shapes=[pltpu.SemaphoreType.DMA],
        compiler_params=params,
        cost_estimate=cost(1000, 2),
        name="apply_inner",
    )(coeffs, basis, eps, table, sz, xf, yf)
    image, hxf, packed, gram, hzf, hyf = pl.pallas_call(
        outer_kernel,
        out_shape=(
            whole, f32(*xf_shape), planes, f32(2, vectors, vectors), f32(*zf_shape), f32(*yf_shape),
        ),
        in_specs=[SMEM] * 2 + [VMEM] * 13,
        out_specs=(VMEM,) * 6,
        scratch_shapes=[scratch(*zf_shape)],
        input_output_aliases={10: 0, 13: 1, 14: 2},
        compiler_params=params,
        cost_estimate=cost(200, 1),
        name="apply_outer",
    )(pml_width, coeffs, basis, eps, table, sz, zf, xf, yt, yf, image, acc, before, hxf, packed)
    phases = sum_phases()
    others = from_partners(gram, phases[0])
    hzf = passed_round(hzf, "gz", 1)
    hxf = passed_round(hxf, "gx", 1)
    hyf = passed_round(hyf, "gy", 1)
    for phase in phases[1:]:
        gram = joined(gram, others)
        if phase is phases[-1]:
            gram, image = lax.optimization_barrier((gram, image))
        others = from_partners(gram, phase)
    residual = pl.pallas_call(
        rim_kernel,
        out_shape=whole,
        in_specs=[SMEM] * 2 + [VMEM] * 5,
        out_specs=HBM,
        scratch_shapes=[scratch(*fields.shape), scratch(nz, nx, ny), pltpu.SemaphoreType.DMA((nz,))],
        compiler_params=params,
        cost_estimate=cost(200, 3),
        name="add_rims",
    )(pml_width, ritz, basis, image, hzf, hxf, hyf)
    others, residual = lax.optimization_barrier((others, residual))
    return basis_new, residual, joined(gram, others)


def solution(mesh):
    in_specs = (P(None, None, None, "gz", "gx", "gy"), P("gz", "gx", "gy"), P(), P(), P(), P(), P())
    out_specs = (P(None, None, None, "gz", "gx", "gy"), P(None, None, None, "gz", "gx", "gy"), P())
    return jax.shard_map(body, mesh=mesh, in_specs=in_specs, out_specs=out_specs, check_vma=False)
```

time: 34.3 us -> 34.3 us (level)
  starting transfers between devices: 16.5 us -> 17.4 us
  Pallas kernels: 13.4 us -> 12.9 us
    ppermute x7, starting transfers between devices: 7.18 us -> 8.03 us  [from_partners(): lax.ppermute(value, axes, [(source, source ^ distance) for source in rang...]
    ppermute x7, waiting for transfers between devices: 2.22 us -> 1.7 us  [from_partners(): lax.ppermute(value, axes, [(source, source ^ distance) for source in rang...]
    pallas_call x1, Pallas kernels: 2.62 us -> 2.22 us  [body(): pl.pallas_call(rim_kernel, out_shape=whole, in_specs=[SMEM] * 2 + [VMEM]...]
    pallas_call x2 -> x3, Pallas kernels: 8.94 us -> 8.81 us  [the longest x1 5.97 us: body(): pl.pallas_call(inner_kernel, out_shape=(whole, f32(vectors, 2 * vectors,...]
  transfers between devices with their start and end apart: 13 -> 13, of which waited for: 4 -> 5; matrix products, arithmetic and copies ran while one was open for 0% -> 0% of each run, Pallas kernels for 12% -> 29%
where the time goes in v4:
time: 34.3 us; the launch traced here: 34.2 us
  starting transfers between devices  17.4 us (51%)
  Pallas kernels  12.9 us (38%)
  waiting for transfers between devices  2.51 us (7%)
  between operations  0.78 us (2%)
  other arithmetic  0.61 us (2%)
    ppermute x6, starting transfers between devices, passed_round(): lax.ppermute(value, axis, [(source, (source + steps) % count) for source...  9.34 us
    ppermute x7, starting transfers between devices, from_partners(): lax.ppermute(value, axes, [(source, source ^ distance) for source in rang...  8.03 us
    pallas_call x1, Pallas kernels, body(): pl.pallas_call(inner_kernel, out_shape=(whole, f32(vectors, 2 * vectors,...  5.97 us
    pallas_call x1, Pallas kernels, body(): pl.pallas_call(rim_kernel, out_shape=whole, in_specs=[SMEM] * 2 + [VMEM]...  2.22 us
    pallas_call x1, Pallas kernels, body(): pl.pallas_call(face_kernel, out_shape=(whole,) + faces, in_specs=[HBM], o...  1.83 us
    ppermute x7, waiting for transfers between devices, from_partners(): lax.ppermute(value, axes, [(source, source ^ distance) for source in rang...  1.7 us
    pallas_call x1, Pallas kernels, body(): pl.pallas_call(prepare_kernel, out_shape=(whole, f32(2, nz, nx, ny), f32(...  1.58 us
    pallas_call x1, Pallas kernels, body(): pl.pallas_call(outer_kernel, out_shape=(whole, f32(*xf_shape), planes, f3...  1.27 us
  transfers between devices with their start and end apart: 13, of which 5 were waited for; matrix products, arithmetic and copies ran while one was open for 0% of the time, Pallas kernels for 29%

profile of v4, /device:TPU:0, one launch (start us, length us, event | category | flops | bytes accessed | tf_op | source)
XLA Modules:
  0.0 34.2 jit_solution(12398551654347659226)
XLA Ops:
  0.7 1.8 %take_faces.1 = (f32[2,4,3,8,16,128]{5,4,3,2,1,0:T(8,128)S(1)}, f32[2,4,2,16,128]{4,3,2,1,0:T(8,128)S(1)}, f32[2,4,2,8,128]{4,3,2,1,0:T(8,128)S(1)}, f32[16,128]{1,0:T(8,128)S(1)}) custom-call(f32[2,4,3,8,16,128]{5,4,3,2,1,0:T(8,128)} %fields_hbm.1), custom_call_target="tpu_custom_call" | custom-call | tf_op jit(solution)/shard_map/take_faces/pallas_call | solution.py:483
  2.5 3.0 %collective-permute-start.2 = (f32[2,4,2,16,128]{4,3,2,1,0:T(8,128)S(1)}, f32[2,4,2,16,128]{4,3,2,1,0:T(8,128)S(1)}, u32[]{:S(2)}, u32[]{:S(2)}) collective-permute-start(f32[2,4,2,16,128]{4,3,2,1,0:T(8,128)S(1)} %get-tuple-element.39), channel_id=1, source_target_pairs={{0,1},{1,0},{2,3},{3,2},{4,5},{5,4},{6,7},{7,6},{8,9},{9,8},{10,11... | collective-permute-start | bytes 393224 | tf_op jit(solution)/shard_map/ppermute | solution.py:22
  5.5 2.8 %collective-permute-start = (f32[2,4,2,8,128]{4,3,2,1,0:T(8,128)S(1)}, f32[2,4,2,8,128]{4,3,2,1,0:T(8,128)S(1)}, u32[]{:S(2)}, u32[]{:S(2)}) collective-permute-start(f32[2,4,2,8,128]{4,3,2,1,0:T(8,128)S(1)} %get-tuple-element.36), channel_id=1, source_target_pairs={{0,28},{4,0},{8,4},{12,8},{16,12},{20,16},{24,20},{28,24},{1,29},{... | collective-permute-start | bytes 196616 | tf_op jit(solution)/shard_map/ppermute | solution.py:22
  8.3 1.5 %collective-permute-start.1 = (f32[16,128]{1,0:T(8,128)S(1)}, f32[16,128]{1,0:T(8,128)S(1)}, u32[]{:S(2)}, u32[]{:S(2)}) collective-permute-start(f32[16,128]{1,0:T(8,128)S(1)} %get-tuple-element.37), channel_id=1, source_target_pairs={{0,2},{2,0},{1,3},{3,1},{4,6},{6,4},{5,7},{7,5},{8,10},{10,8},{9,1... | collective-permute-start | bytes 24584 | tf_op jit(solution)/shard_map/ppermute | solution.py:22
  9.8 1.6 %prepare.1 = (f32[2,4,3,8,16,128]{5,4,3,2,1,0:T(8,128)S(1)}, f32[2,8,16,128]{3,2,1,0:T(8,128)S(1)}, f32[8,16,128]{2,1,0:T(8,128)S(1)}, f32[4,8,128]{2,1,0:T(8,128)S(1)}) custom-call(s32[6]{0:T(128)S(1)} %copy-done.2, f32[4]{0:T(128)S(1)} %copy-done.4, f32[4]{0:T(128)S(1)} %copy-done.5, f32[2,4,4]{2,1,0:T(4,128)S(1)} %copy-done.1, ...), custom_call_target="tpu_custom_call" | custom-call | flops 6553600 | bytes 3145728 | tf_op jit(solution)/shard_map/prepare/pallas_call | solution.py:501
  11.4 0.5 %collective-permute-done.1.raw_yf_ref = f32[16,128]{1,0:T(8,128)S(1)} collective-permute-done((f32[16,128]{1,0:T(8,128)S(1)}, f32[16,128]{1,0:T(8,128)S(1)}, u32[]{:S(2)}, u32[]{:S(2)}) %collective-permute-start.1) | collective-permute-done | bytes 8224 | tf_op jit(solution)/shard_map/ppermute | solution.py:22
  11.9 0.0 collective-permute-done.raw_xf_ref
  11.9 6.0 %apply_inner.1 = (f32[2,4,3,8,16,128]{5,4,3,2,1,0:T(8,128)S(1)}, f32[4,8,8,128]{3,2,1,0:T(8,128)S(1)}, f32[2,4,2,16,128]{4,3,2,1,0:T(8,128)S(1)}, f32[2,4,2,8,12...) custom-call(f32[2,4,4]{2,1,0:T(4,128)S(1)} %copy-done.1, ...), custom_call_target="tpu_custom_call" | custom-call | flops 16384000 | bytes 3145728 | tf_op jit(solution)/shard_map/apply_inner/pallas_call | solution.py:510
  17.9 0.0 copy-start.3
  17.9 1.3 %apply_outer.1 = (f32[2,4,3,8,16,128]{5,4,3,2,1,0:T(8,128)S(1)}, f32[2,4,2,8,128]{4,3,2,1,0:T(8,128)S(1)}, f32[8,16,128]{2,1,0:T(8,128)S(1)}, f32[2,4,4]{2,1,0:T...) custom-call(s32[6]{0:T(128)S(1)} %copy-done.2, ...), custom_call_target="tpu_custom_call", output_to_operand_aliasing={{0}: (10, {}), {1}: (13, {}), {2}: (14, {})} | custom-call | flops 3276800 | bytes 1572864 | tf_op jit(solution)/shard_map/apply_outer/pallas_call | solution.py:523
  19.2 0.9 %collective-permute-start.5 = (f32[2,4,4]{2,1,0:T(4,128)S(1)}, f32[2,4,4]{2,1,0:T(4,128)S(1)}, u32[]{:S(2)}, u32[]{:S(2)}) collective-permute-start(f32[2,4,4]{2,1,0:T(4,128)S(1)} %get-tuple-element.48), channel_id=1, source_target_pairs={{0,24},{1,25},{2,26},{3,27},{4,28},{5,29},{6,30},{7,31},{8,16},{9,... | collective-permute-start | bytes 392 | tf_op jit(solution)/shard_map/ppermute | solution.py:463
  20.1 3.5 %collective-permute-start.3 = (f32[2,4,4]{2,1,0:T(4,128)S(1)}, f32[2,4,4]{2,1,0:T(4,128)S(1)}, u32[]{:S(2)}, u32[]{:S(2)}) collective-permute-start(f32[2,4,4]{2,1,0:T(4,128)S(1)} %get-tuple-element.48), channel_id=1, source_target_pairs={{0,8},{1,9},{2,10},{3,11},{4,12},{5,13},{6,14},{7,15},{8,0},{9,1},... | collective-permute-start | bytes 392 | tf_op jit(solution)/shard_map/ppermute | solution.py:463
  23.7 1.5 %collective-permute-start.12 = (f32[16,128]{1,0:T(8,128)S(1)}, f32[16,128]{1,0:T(8,128)S(1)}, u32[]{:S(2)}, u32[]{:S(2)}) collective-permute-start(f32[16,128]{1,0:T(8,128)S(1)} %get-tuple-element.54), channel_id=1, source_target_pairs={{0,2},{2,0},{1,3},{3,1},{4,6},{6,4},{5,7},{7,5},{8,10},{10,8},{9,1... | collective-permute-start | bytes 24584 | tf_op jit(solution)/shard_map/ppermute | solution.py:22
  25.2 0.5 %collective-permute-start.10 = (f32[2,4,2,16,128]{4,3,2,1,0:T(8,128)S(1)}, f32[2,4,2,16,128]{4,3,2,1,0:T(8,128)S(1)}, u32[]{:S(2)}, u32[]{:S(2)}) collective-permute-start(f32[2,4,2,16,128]{4,3,2,1,0:T(8,128)S(1)} %get-tuple-element.52), channel_id=1, source_target_pairs={{0,1},{1,0},{2,3},{3,2},{4,5},{5,4},{6,7},{7,6},{8,9},{9,8},{10,11... | collective-permute-start | bytes 393224 | tf_op jit(solution)/shard_map/ppermute | solution.py:22
  25.8 0.1 collective-permute-start.6
  25.8 1.2 %collective-permute-done.6 = f32[2,4,4]{2,1,0:T(4,128)S(1)} collective-permute-done((f32[2,4,4]{2,1,0:T(4,128)S(1)}, f32[2,4,4]{2,1,0:T(4,128)S(1)}, u32[]{:S(2)}, u32[]{:S(2)}) %collective-permute-start.6) | collective-permute-done | bytes 160 | tf_op jit(solution)/shard_map/ppermute | solution.py:463
  27.0 1.9 %collective-permute-start.9 = (f32[2,4,4]{2,1,0:T(4,128)S(1)}, f32[2,4,4]{2,1,0:T(4,128)S(1)}, u32[]{:S(2)}, u32[]{:S(2)}) collective-permute-start(f32[2,4,4]{2,1,0:T(4,128)S(1)} %add.24), channel_id=1, source_target_pairs={{0,3},{1,2},{2,1},{3,0},{4,7},{5,6},{6,5},{7,4},{8,11},{9,10},{10,... | collective-permute-start | bytes 392 | tf_op jit(solution)/shard_map/ppermute | solution.py:463
  28.9 1.0 %collective-permute-start.8 = (f32[2,4,4]{2,1,0:T(4,128)S(1)}, f32[2,4,4]{2,1,0:T(4,128)S(1)}, u32[]{:S(2)}, u32[]{:S(2)}) collective-permute-start(f32[2,4,4]{2,1,0:T(4,128)S(1)} %add.24), channel_id=1, source_target_pairs={{0,2},{1,3},{2,0},{3,1},{4,6},{5,7},{6,4},{7,5},{8,10},{9,11},{10,... | collective-permute-start | bytes 392 | tf_op jit(solution)/shard_map/ppermute | solution.py:463
  30.0 0.5 %collective-permute-start.7 = (f32[2,4,4]{2,1,0:T(4,128)S(1)}, f32[2,4,4]{2,1,0:T(4,128)S(1)}, u32[]{:S(2)}, u32[]{:S(2)}) collective-permute-start(f32[2,4,4]{2,1,0:T(4,128)S(1)} %add.24), channel_id=1, source_target_pairs={{0,1},{1,0},{2,3},{3,2},{4,5},{5,4},{6,7},{7,6},{8,9},{9,8},{10,11... | collective-permute-start | bytes 392 | tf_op jit(solution)/shard_map/ppermute | solution.py:463
  30.5 0.2 collective-permute-done.11.hxf_ref
  30.7 0.1 collective-permute-done.10.hzf_ref
  30.8 2.2 %add_rims.1 = f32[2,4,3,8,16,128]{5,4,3,2,1,0:T(8,128)} custom-call(s32[6]{0:T(128)S(1)} %copy-done.2, f32[2,4]{1,0:T(2,128)S(1)} %copy-done.3, f32[2,4,3,8,16,128]{5,4,3,2,1,0:T(8,128)S(1)} %get-tuple-element.32.basis_ref, f32[2,4,3,8,16,128]{5,4,3,2,1,0:T(8,128)S(1)} %get-tuple-element.51.image_ref, ...), custom_call_target="tpu_custom_call" | custom-call | flops 3276800 | bytes 4718592 | tf_op jit(solution)/shard_map/add_rims/pallas_call | solution.py:546
  33.0 0.5 %collective-permute-done.7 = f32[2,4,4]{2,1,0:T(4,128)S(1)} collective-permute-done((f32[2,4,4]{2,1,0:T(4,128)S(1)}, f32[2,4,4]{2,1,0:T(4,128)S(1)}, u32[]{:S(2)}, u32[]{:S(2)}) %collective-permute-start.7) | collective-permute-done | bytes 160 | tf_op jit(solution)/shard_map/ppermute | solution.py:463
  33.6 0.6 %add_add_fusion = f32[1,8,4]{2,1,0:T(8,128)} fusion(f32[1,8,4]{2,1,0:T(8,128)S(1)} %bitcast.15, f32[1,8,4]{2,1,0:T(8,128)S(1)} %bitcast.14, f32[1,8,4]{2,1,0:T(8,128)S(1)} %bitcast.11, f32[1,8,4]{2,1,0:T(8,128)S(1)} %bitcast.18), kind=kLoop, calls=%fused_computation | loop fusion | flops 96 | bytes 640 | tf_op jit(solution)/shard_map/add | solution.py:470
  (22 shorter events, 0.1 us)
Async XLA Ops:
  0.6 9.2 %copy-start.1 = (f32[2,4,4]{2,1,0:T(4,128)S(1)}, f32[2,4,4]{2,1,0:T(4,128)}, u32[]{:S(2)}) copy-start(f32[2,4,4]{2,1,0:T(4,128)} %coeffs_ref.5) | copy-start | bytes 388
  0.6 9.2 %copy-start.2 = (s32[6]{0:T(128)S(1)}, s32[6]{0:T(128)}, u32[]{:S(2)}) copy-start(s32[6]{0:T(128)} %pml_ref.5) | copy-start | bytes 76
  0.7 9.2 %copy-start.5 = (f32[4]{0:T(128)S(1)}, f32[4]{0:T(128)}, u32[]{:S(2)}) copy-start(f32[4]{0:T(128)} %eps_loss_ref.1) | copy-start | bytes 52
  0.7 9.2 %copy-start.4 = (f32[4]{0:T(128)S(1)}, f32[4]{0:T(128)}, u32[]{:S(2)}) copy-start(f32[4]{0:T(128)} %eps_real_ref.1) | copy-start | bytes 52
  0.7 9.2 %copy-start = (s32[8,16,128]{2,1,0:T(8,128)S(1)}, s32[8,16,128]{2,1,0:T(8,128)}, u32[]{:S(2)}) copy-start(s32[8,16,128]{2,1,0:T(8,128)} %material_ref.1) | copy-start | bytes 196612
  2.5 15.4 %collective-permute-start.2 = (f32[2,4,2,16,128]{4,3,2,1,0:T(8,128)S(1)}, f32[2,4,2,16,128]{4,3,2,1,0:T(8,128)S(1)}, u32[]{:S(2)}, u32[]{:S(2)}) collective-permute-start(f32[2,4,2,16,128]{4,3,2,1,0:T(8,128)S(1)} %get-tuple-element.39), channel_id=1, source_target_pairs={{0,1},{1,0},{2,3},{3,2},{4,5},{5,4},{6,7},{7,6},{8,9},{9,8},{10,11... | collective-permute-start | bytes 393224 | tf_op jit(solution)/shard_map/ppermute | solution.py:22
  5.5 6.4 %collective-permute-start = (f32[2,4,2,8,128]{4,3,2,1,0:T(8,128)S(1)}, f32[2,4,2,8,128]{4,3,2,1,0:T(8,128)S(1)}, u32[]{:S(2)}, u32[]{:S(2)}) collective-permute-start(f32[2,4,2,8,128]{4,3,2,1,0:T(8,128)S(1)} %get-tuple-element.36), channel_id=1, source_target_pairs={{0,28},{4,0},{8,4},{12,8},{16,12},{20,16},{24,20},{28,24},{1,29},{... | collective-permute-start | bytes 196616 | tf_op jit(solution)/shard_map/ppermute | solution.py:22
  8.3 3.7 %collective-permute-start.1 = (f32[16,128]{1,0:T(8,128)S(1)}, f32[16,128]{1,0:T(8,128)S(1)}, u32[]{:S(2)}, u32[]{:S(2)}) collective-permute-start(f32[16,128]{1,0:T(8,128)S(1)} %get-tuple-element.37), channel_id=1, source_target_pairs={{0,2},{2,0},{1,3},{3,1},{4,6},{6,4},{5,7},{7,5},{8,10},{10,8},{9,1... | collective-permute-start | bytes 24584 | tf_op jit(solution)/shard_map/ppermute | solution.py:22
  17.9 12.8 %copy-start.3 = (f32[2,4]{1,0:T(2,128)S(1)}, f32[2,4]{1,0:T(2,128)}, u32[]{:S(2)}) copy-start(f32[2,4]{1,0:T(2,128)} %ritz_ref.1) | copy-start | bytes 100
  19.2 6.0 %collective-permute-start.5 = (f32[2,4,4]{2,1,0:T(4,128)S(1)}, f32[2,4,4]{2,1,0:T(4,128)S(1)}, u32[]{:S(2)}, u32[]{:S(2)}) collective-permute-start(f32[2,4,4]{2,1,0:T(4,128)S(1)} %get-tuple-element.48), channel_id=1, source_target_pairs={{0,24},{1,25},{2,26},{3,27},{4,28},{5,29},{6,30},{7,31},{8,16},{9,... | collective-permute-start | bytes 392 | tf_op jit(solution)/shard_map/ppermute | solution.py:463
  20.1 5.6 %collective-permute-start.4 = (f32[2,4,4]{2,1,0:T(4,128)S(1)}, f32[2,4,4]{2,1,0:T(4,128)S(1)}, u32[]{:S(2)}, u32[]{:S(2)}) collective-permute-start(f32[2,4,4]{2,1,0:T(4,128)S(1)} %get-tuple-element.48), channel_id=1, source_target_pairs={{0,16},{1,17},{2,18},{3,19},{4,20},{5,21},{6,22},{7,23},{8,24},{9,... | collective-permute-start | bytes 392 | tf_op jit(solution)/shard_map/ppermute | solution.py:463
  20.1 5.6 %collective-permute-start.3 = (f32[2,4,4]{2,1,0:T(4,128)S(1)}, f32[2,4,4]{2,1,0:T(4,128)S(1)}, u32[]{:S(2)}, u32[]{:S(2)}) collective-permute-start(f32[2,4,4]{2,1,0:T(4,128)S(1)} %get-tuple-element.48), channel_id=1, source_target_pairs={{0,8},{1,9},{2,10},{3,11},{4,12},{5,13},{6,14},{7,15},{8,0},{9,1},... | collective-permute-start | bytes 392 | tf_op jit(solution)/shard_map/ppermute | solution.py:463
  23.7 6.3 %collective-permute-start.12 = (f32[16,128]{1,0:T(8,128)S(1)}, f32[16,128]{1,0:T(8,128)S(1)}, u32[]{:S(2)}, u32[]{:S(2)}) collective-permute-start(f32[16,128]{1,0:T(8,128)S(1)} %get-tuple-element.54), channel_id=1, source_target_pairs={{0,2},{2,0},{1,3},{3,1},{4,6},{6,4},{5,7},{7,5},{8,10},{10,8},{9,1... | collective-permute-start | bytes 24584 | tf_op jit(solution)/shard_map/ppermute | solution.py:22
  25.2 5.5 %collective-permute-start.11 = (f32[2,4,2,8,128]{4,3,2,1,0:T(8,128)S(1)}, f32[2,4,2,8,128]{4,3,2,1,0:T(8,128)S(1)}, u32[]{:S(2)}, u32[]{:S(2)}) collective-permute-start(f32[2,4,2,8,128]{4,3,2,1,0:T(8,128)S(1)} %get-tuple-element.53), channel_id=1, source_target_pairs={{0,4},{4,8},{8,12},{12,16},{16,20},{20,24},{24,28},{28,0},{1,5},{5... | collective-permute-start | bytes 196616 | tf_op jit(solution)/shard_map/ppermute | solution.py:22
  25.2 5.6 %collective-permute-start.10 = (f32[2,4,2,16,128]{4,3,2,1,0:T(8,128)S(1)}, f32[2,4,2,16,128]{4,3,2,1,0:T(8,128)S(1)}, u32[]{:S(2)}, u32[]{:S(2)}) collective-permute-start(f32[2,4,2,16,128]{4,3,2,1,0:T(8,128)S(1)} %get-tuple-element.52), channel_id=1, source_target_pairs={{0,1},{1,0},{2,3},{3,2},{4,5},{5,4},{6,7},{7,6},{8,9},{9,8},{10,11... | collective-permute-start | bytes 393224 | tf_op jit(solution)/shard_map/ppermute | solution.py:22
  25.8 1.2 %collective-permute-start.6 = (f32[2,4,4]{2,1,0:T(4,128)S(1)}, f32[2,4,4]{2,1,0:T(4,128)S(1)}, u32[]{:S(2)}, u32[]{:S(2)}) collective-permute-start(f32[2,4,4]{2,1,0:T(4,128)S(1)} %bitcast.12), channel_id=1, source_target_pairs={{0,4},{1,5},{2,6},{3,7},{4,0},{5,1},{6,2},{7,3},{8,12},{9,13},{10,... | collective-permute-start | bytes 392 | tf_op jit(solution)/shard_map/ppermute | solution.py:463
  27.0 6.0 %collective-permute-start.9 = (f32[2,4,4]{2,1,0:T(4,128)S(1)}, f32[2,4,4]{2,1,0:T(4,128)S(1)}, u32[]{:S(2)}, u32[]{:S(2)}) collective-permute-start(f32[2,4,4]{2,1,0:T(4,128)S(1)} %add.24), channel_id=1, source_target_pairs={{0,3},{1,2},{2,1},{3,0},{4,7},{5,6},{6,5},{7,4},{8,11},{9,10},{10,... | collective-permute-start | bytes 392 | tf_op jit(solution)/shard_map/ppermute | solution.py:463
  28.9 4.1 %collective-permute-start.8 = (f32[2,4,4]{2,1,0:T(4,128)S(1)}, f32[2,4,4]{2,1,0:T(4,128)S(1)}, u32[]{:S(2)}, u32[]{:S(2)}) collective-permute-start(f32[2,4,4]{2,1,0:T(4,128)S(1)} %add.24), channel_id=1, source_target_pairs={{0,2},{1,3},{2,0},{3,1},{4,6},{5,7},{6,4},{7,5},{8,10},{9,11},{10,... | collective-permute-start | bytes 392 | tf_op jit(solution)/shard_map/ppermute | solution.py:463
  30.0 3.6 %collective-permute-start.7 = (f32[2,4,4]{2,1,0:T(4,128)S(1)}, f32[2,4,4]{2,1,0:T(4,128)S(1)}, u32[]{:S(2)}, u32[]{:S(2)}) collective-permute-start(f32[2,4,4]{2,1,0:T(4,128)S(1)} %add.24), channel_id=1, source_target_pairs={{0,1},{1,0},{2,3},{3,2},{4,5},{5,4},{6,7},{7,6},{8,9},{9,8},{10,11... | collective-permute-start | bytes 392 | tf_op jit(solution)/shard_map/ppermute | solution.py:463

commit v5 on v4

--- a/solution.py
+++ b/solution.py
@@ -71,7 +71,7 @@
     return jnp.where(inside, 1.0, 0.0).astype(jnp.float32)
 
 
-def face_kernel(fields_hbm, fields_ref, zf_ref, xf_ref, yf_ref, sems):
+def face_kernel(fields_hbm, fields_ref, xf_ref, yf_ref, sems):
     _, vectors, _, nz, nx, ny = fields_ref.shape
     lanes = lax.broadcasted_iota(jnp.int32, (nx, ny), 1)
     copies = [
@@ -96,7 +96,6 @@
     for part in range(2):
         for a in range(vectors):
             for slot in range(2):
-                zf_ref[part, a, slot] = fields_ref[part, a, slot, 0]
                 xf_ref[part, a, slot] = fields_ref[part, a, slot + 1, :, 0, :]
 
 
@@ -179,6 +178,42 @@
         rows_ref[slot * both:(slot + 1) * both] = turned[slot]
     rest = jnp.zeros((ny - 2 * both, nz * nx), jnp.float32)
     cells_ref[...] = jnp.concatenate(turned + [rest], axis=0).T.reshape(nz, nx, ny)
+
+
+def slab_kernel(
+    coeffs_ref, basis_ref, table_ref, sz_ref, raw_xf_ref, raw_yf_ref, xf_ref, yt_ref, yf_ref, zf_ref
+):
+    _, vectors, _, nz, nx, ny = basis_ref.shape
+    turn_face(coeffs_ref, 1, raw_xf_ref, xf_ref)
+    turn_column(coeffs_ref, raw_yf_ref, yt_ref, yf_ref)
+    tile = (SUB, ny)
+    rows = lax.broadcasted_iota(jnp.int32, tile, 0)
+    lanes = lax.broadcasted_iota(jnp.int32, tile, 1)
+    parts = range(2)
+    last = nz - 1
+    lower = jnp.full(tile, lax.axis_index(AXES[0]), jnp.int32) == 0
+    shz = tuple(sz_ref[2 + part, last:] for part in parts)
+    for b in range(vectors):
+        for t in range(nx // SUB):
+            cut = slice(SUB * t, SUB * (t + 1))
+            ex, ey, ez = (tuple(basis_ref[part, b, comp, last, cut] for part in parts) for comp in range(3))
+            ahead_x, ahead_y = [], []
+            for part in parts:
+                if SUB * (t + 1) < nx:
+                    edge = basis_ref[part, b, 2, last, SUB * (t + 1):SUB * (t + 1) + 1]
+                else:
+                    edge = xf_ref[part, b, 1, last:]
+                ahead_x.append(jnp.where(rows == SUB - 1, edge, pltpu.roll(ez[part], SUB - 1, 0)))
+                row = packed_row(1, part, b, vectors)
+                edge = pltpu.roll(yf_ref[last, cut], ny - 1 - row, 1)
+                ahead_y.append(jnp.where(lanes == ny - 1, edge, pltpu.roll(ez[part], ny - 1, 1)))
+            shx = tuple(table_ref[SHX + part, cut] for part in parts)
+            shy = tuple(table_ref[SHY + part, cut] for part in parts)
+            share_x = add(cmul(shy, sub(ahead_y, ez)), cmul(shz, ey))
+            share_y = add(cmul(shx, sub(ahead_x, ez)), cmul(shz, ex))
+            for part in parts:
+                zf_ref[part, b, 0, cut] = jnp.where(lower, share_x[part], basis_ref[part, b, 0, 0, cut])
+                zf_ref[part, b, 1, cut] = jnp.where(lower, -share_y[part], basis_ref[part, b, 1, 0, cut])
 
 
 def plane_step(
@@ -272,14 +307,12 @@
 
 
 def inner_kernel(
-    coeffs_ref, basis_ref, eps_ref, table_ref, sz_ref, raw_xf_ref, raw_yf_ref,
-    image_ref, acc_ref, before_ref, hxf_ref, packed_ref, xf_ref, yt_ref, yf_ref, basis_hbm, sem,
+    basis_ref, eps_ref, table_ref, sz_ref, xf_ref, yf_ref,
+    image_ref, acc_ref, before_ref, hxf_ref, packed_ref, basis_hbm, sem,
 ):
     _, vectors, _, nz, nx, ny = basis_ref.shape
     keep = pltpu.make_async_copy(basis_ref, basis_hbm, sem)
     keep.start()
-    turn_face(coeffs_ref, 1, raw_xf_ref, xf_ref)
-    turn_column(coeffs_ref, raw_yf_ref, yt_ref, yf_ref)
     packed_ref[...] = jnp.zeros(packed_ref.shape, jnp.float32)
     count = nx // SUB
 
@@ -306,52 +339,58 @@
 
 
 def outer_kernel(
-    pml_ref, coeffs_ref, basis_ref, eps_ref, table_ref, sz_ref, raw_zf_ref, xf_ref, yt_ref, yf_ref,
+    pml_ref, basis_ref, eps_ref, table_ref, sz_ref, zf_ref, xf_ref, yt_ref, yf_ref,
     image_in, acc_ref, before_ref, hxf_in, packed_in,
-    image_ref, hxf_ref, packed_ref, gram_ref, hzf_ref, hyf_ref, zf_ref,
+    image_ref, hxf_ref, packed_ref, hyf_ref,
 ):
     del image_in, hxf_in, packed_in
     _, vectors, _, nz, nx, ny = basis_ref.shape
+    parts = range(2)
     count = nx // SUB
-    turn_face(coeffs_ref, 0, raw_zf_ref, zf_ref)
-    sz_next = axis_stretch(pml_ref, 0, nz, one_place(0, nz, nz, (1, ny)))
+    above, below = has_neighbour(0, 1), has_neighbour(0, -1)
+    under = axis_stretch(pml_ref, 0, nz, one_place(0, nz, -1, (1, ny)) + 0.5)
+    sez = tuple(sz_ref[part, 0:1] * below for part in parts)
     sx_next = axis_stretch(pml_ref, 1, nx, one_place(1, nx, nx, (1, ny)))
     sy_next = axis_stretch(pml_ref, 2, ny, one_place(2, ny, ny, (1, nz * nx)))
     all_sums = []
     for b in range(vectors):
 
         def tile_of(ref, slot, t, b=b):
-            return tuple(ref[part, b, slot, SUB * t:SUB * (t + 1)] for part in range(2))
+            return tuple(ref[part, b, slot, SUB * t:SUB * (t + 1)] for part in parts)
+
+        def up_of(slot, t):
+            return tuple(value * above for value in tile_of(zf_ref, slot, t))
 
         before = [tuple(tile_of(before_ref, slot, t) for slot in range(2)) for t in range(count)]
         sums = [(acc_ref[b, a], acc_ref[b, vectors + a]) for a in range(vectors)]
-        after, sums = plane_step(
-            b, nz - 1, before, sums, functools.partial(tile_of, zf_ref), basis_ref, eps_ref, table_ref, sz_ref,
+        _, sums = plane_step(
+            b, nz - 1, before, sums, up_of, basis_ref, eps_ref, table_ref, sz_ref,
             xf_ref, yf_ref, image_ref, hxf_ref, packed_ref,
         )
-        h_y = tuple(hxf_ref[part, b, 0] for part in range(2))
-        h_z = tuple(hxf_ref[part, b, 1] for part in range(2))
+        for t in range(count):
+            cut = slice(SUB * t, SUB * (t + 1))
+            ex, ey = (tuple(basis_ref[part, b, comp, 0, cut] for part in parts) for comp in range(2))
+            hx = sub(tile_of(zf_ref, 0, t), cmul(under, ey))
+            hy = add(tile_of(zf_ref, 1, t), cmul(under, ex))
+            more = (cmul(sez, hy), cmul(sez, hx))
+            for part in parts:
+                image_ref[part, b, 0, 0, cut] = image_ref[part, b, 0, 0, cut] + more[0][part]
+                image_ref[part, b, 1, 0, cut] = image_ref[part, b, 1, 0, cut] - more[1][part]
+            for a in range(vectors):
+                ex, ey = (tuple(basis_ref[part, a, comp, 0, cut] for part in parts) for comp in range(2))
+                sums[a] = add(sums[a], sub(cmul(ex, more[0]), cmul(ey, more[1])))
+        h_y = tuple(hxf_ref[part, b, 0] for part in parts)
+        h_z = tuple(hxf_ref[part, b, 1] for part in parts)
         for a in range(vectors):
-            over = None
-            for t, (hx, hy) in enumerate(after):
-                ends = [tuple(zf_ref[part, a, slot, SUB * t:SUB * (t + 1)] for part in range(2)) for slot in range(2)]
-                term = sub(cmul(ends[0], hy), cmul(ends[1], hx))
-                over = term if over is None else add(over, term)
-            total = add(sums[a], cmul(sz_next, over))
-            over = cmul(tuple(xf_ref[part, a, 0] for part in range(2)), h_z)
-            over = sub(over, cmul(tuple(xf_ref[part, a, 1] for part in range(2)), h_y))
+            over = cmul(tuple(xf_ref[part, a, 0] for part in parts), h_z)
+            over = sub(over, cmul(tuple(xf_ref[part, a, 1] for part in parts), h_y))
             over = cmul(sx_next, over)
             for row in range(0, nz, SUB):
-                total = add(total, tuple(part[row:row + SUB] for part in over))
-            sums[a] = total
+                sums[a] = add(sums[a], tuple(part[row:row + SUB] for part in over))
         all_sums.append(sums)
-        for part in range(2):
-            for t, pair in enumerate(after):
-                for slot in range(2):
-                    hzf_ref[part, b, slot, SUB * t:SUB * (t + 1)] = pair[slot][part]
 
     both = 2 * vectors
-    hyf_ref[...] = packed_ref[...].reshape(nz * nx, ny).T[:2 * both]
+    hyf_ref[:2 * both] = packed_ref[...].reshape(nz * nx, ny).T[:2 * both]
     ends = [
         cmul(sy_next, (yt_ref[slot * both:slot * both + vectors], yt_ref[slot * both + vectors:(slot + 1) * both]))
         for slot in range(2)
@@ -373,32 +412,30 @@
     everywhere = 3.0 * nz * nx * ny
     for axis in AXES:
         everywhere = everywhere * lax.axis_size(axis)
-    gram = gram * (1.0 / everywhere)
-    for part in range(2):
-        gram_ref[part] = gram[part * vectors:(part + 1) * vectors, :vectors]
+    hyf_ref[2 * both:] = gram * (1.0 / everywhere)
 
 
 def rim_kernel(
-    pml_ref, ritz_ref, basis_ref, image_ref, hzf_ref, hxf_ref, hyf_ref, residual_hbm, residual_ref, packed_ref, sems
+    pml_ref, ritz_ref, basis_ref, image_ref, hxf_ref, hyf_ref, residual_hbm, residual_ref, packed_ref, sems
 ):
     _, vectors, _, nz, nx, ny = basis_ref.shape
     plane = (nx, ny)
     rows = lax.broadcasted_iota(jnp.int32, plane, 0)
     lanes = lax.broadcasted_iota(jnp.int32, plane, 1)
-    sez = axis_stretch(pml_ref, 0, nz, one_place(0, nz, 0, plane))
     sex = axis_stretch(pml_ref, 1, nx, one_place(1, nx, 0, (1, ny)))
     sey = axis_stretch(pml_ref, 2, ny, one_place(2, ny, 0, plane))
     none = jnp.zeros(plane, jnp.float32)
-    sez = tuple(part * has_neighbour(0, -1) for part in sez)
     sex = tuple(jnp.where(rows == 0, part * has_neighbour(1, -1), none) for part in sex)
     sey = tuple(jnp.where(lanes == 0, part * has_neighbour(2, -1), none) for part in sey)
-    rest = jnp.zeros((ny - hyf_ref.shape[0], nz * nx), jnp.float32)
-    packed_ref[...] = jnp.concatenate([hyf_ref[...], rest], axis=0).T.reshape(nz, nx, ny)
+    used = 4 * vectors
+    rest = jnp.zeros((ny - used, nz * nx), jnp.float32)
+    packed_ref[...] = jnp.concatenate([hyf_ref[:used], rest], axis=0).T.reshape(nz, nx, ny)
 
     def kept(z):
         return pltpu.make_async_copy(residual_ref.at[:, :, :, z], residual_hbm.at[:, :, :, z], sems.at[z])
 
-    def step(z, first):
+    @pl.loop(0, nz)
+    def _(z):
         packed = packed_ref[z]
         for b in range(vectors):
 
@@ -420,54 +457,22 @@
             left[2] = add(left[2], cmul(sey, column(1)))
             left[1] = add(left[1], cmul(sex, row(1)))
             left[2] = sub(left[2], cmul(sex, row(0)))
-            if first:
-                left[0] = add(left[0], cmul(sez, (hzf_ref[0, b, 1], hzf_ref[1, b, 1])))
-                left[1] = sub(left[1], cmul(sez, (hzf_ref[0, b, 0], hzf_ref[1, b, 0])))
             for comp in range(3):
                 for part in range(2):
                     residual_ref[part, b, comp, z] = left[comp][part]
         kept(z).start()
 
-    step(0, True)
-
-    @pl.loop(1, nz)
-    def _(z):
-        step(z, False)
-
     @pl.loop(0, nz)
     def _(z):
         kept(z).wait()
 
 
-def sum_phases():
-    sizes = [lax.axis_size(axis) for axis in ("gx", "gy", "gz")]
-    if any(size & (size - 1) for size in sizes):
-        return None
-    across = sizes[1] * sizes[2]
-    masks = [1 << bit for bit in range((sizes[0] * across).bit_length() - 1)]
-    along = [mask for mask in masks if mask >= across]
-    rest = [mask for mask in masks if mask < across]
-    phases = [along[place:place + 2] for place in range(1, len(along), 2)] + [along[:1]]
-    phases += [rest[place:place + 2] for place in range(0, len(rest), 2)]
-    return [phase for phase in phases if phase]
-
-
-def from_partners(value, phase):
+def from_partner(value, mask):
     axes = ("gx", "gy", "gz")
     count = 1
     for axis in axes:
         count *= lax.axis_size(axis)
-    first, second = phase[0], phase[-1]
-    distances = [first] if len(phase) == 1 else [first, second, first ^ second]
-    return [
-        lax.ppermute(value, axes, [(source, source ^ distance) for source in range(count)])
-        for distance in distances
-    ]
-
-
-def joined(value, others):
-    value = value + others[0]
-    return value + (others[1] + others[2]) if others[1:] else value
+    return lax.ppermute(value, axes, [(source, source ^ mask) for source in range(count)])
 
 
 def body(fields, material, pml_width, eps_real, eps_loss, coeffs, ritz):
@@ -479,19 +484,17 @@
     zf_shape = (2, vectors, 2, nx, ny)
     xf_shape = (2, vectors, 2, nz, ny)
     yf_shape = (4 * vectors, nz * nx)
-    faces = (f32(*zf_shape), f32(*xf_shape), f32(*yf_shape))
-    near, zf, xf, yf = pl.pallas_call(
+    near, xf, yf = pl.pallas_call(
         face_kernel,
-        out_shape=(whole,) + faces,
+        out_shape=(whole, f32(*xf_shape), f32(*yf_shape)),
         in_specs=[HBM],
-        out_specs=(VMEM,) * 4,
+        out_specs=(VMEM,) * 3,
         scratch_shapes=[pltpu.SemaphoreType.DMA((2, 3))],
         compiler_params=params,
         name="take_faces",
     )(pltpu.with_memory_space_constraint(fields, pltpu.HBM))
     xf = passed_round(xf, "gx", -1)
     yf = passed_round(yf, "gy", -1)
-    zf = passed_round(zf, "gz", -1)
     cells = fields.size // 6 // vectors
 
     def cost(flops, passes):
@@ -507,54 +510,63 @@
         cost_estimate=cost(400, 2),
         name="prepare",
     )(pml_width, eps_real, eps_loss, coeffs, near, material)
-    image, acc, before, hxf, packed, xf, yt, yf, basis_new = pl.pallas_call(
+    xf, yt, yf, zf = pl.pallas_call(
+        slab_kernel,
+        out_shape=(f32(*xf_shape), f32(*yf_shape), planes, f32(*zf_shape)),
+        in_specs=[SMEM] + [VMEM] * 5,
+        out_specs=(VMEM,) * 4,
+        compiler_params=params,
+        name="slab_face",
+    )(coeffs, basis, table, sz, xf, yf)
+    zf = passed_round(zf, "gz", 1)
+    image, acc, before, hxf, packed, basis_new = pl.pallas_call(
         inner_kernel,
         out_shape=(
-            whole, f32(vectors, 2 * vectors, SUB, ny), f32(*zf_shape), f32(*xf_shape), planes,
-            f32(*xf_shape), f32(*yf_shape), planes, whole,
+            whole, f32(vectors, 2 * vectors, SUB, ny), f32(*zf_shape), f32(*xf_shape), planes, whole,
         ),
-        in_specs=[SMEM] + [VMEM] * 6,
-        out_specs=(VMEM,) * 8 + (HBM,),
+        in_specs=[VMEM] * 6,
+        out_specs=(VMEM,) * 5 + (HBM,),
         scratch_shapes=[pltpu.SemaphoreType.DMA],
         compiler_params=params,
         cost_estimate=cost(1000, 2),
         name="apply_inner",
-    )(coeffs, basis, eps, table, sz, xf, yf)
-    image, hxf, packed, gram, hzf, hyf = pl.pallas_call(
+    )(basis, eps, table, sz, xf, yf)
+    image, hxf, packed, hyf = pl.pallas_call(
         outer_kernel,
-        out_shape=(
-            whole, f32(*xf_shape), planes, f32(2, vectors, vectors), f32(*zf_shape), f32(*yf_shape),
-        ),
-        in_specs=[SMEM] * 2 + [VMEM] * 13,
-        out_specs=(VMEM,) * 6,
-        scratch_shapes=[scratch(*zf_shape)],
-        input_output_aliases={10: 0, 13: 1, 14: 2},
+        out_shape=(whole, f32(*xf_shape), planes, f32(6 * vectors, nz * nx)),
+        in_specs=[SMEM] + [VMEM] * 13,
+        out_specs=(VMEM,) * 4,
+        input_output_aliases={9: 0, 12: 1, 13: 2},
         compiler_params=params,
         cost_estimate=cost(200, 1),
         name="apply_outer",
-    )(pml_width, coeffs, basis, eps, table, sz, zf, xf, yt, yf, image, acc, before, hxf, packed)
-    phases = sum_phases()
-    others = from_partners(gram, phases[0])
-    hzf = passed_round(hzf, "gz", 1)
+    )(pml_width, basis, eps, table, sz, zf, xf, yt, yf, image, acc, before, hxf, packed)
+    across = lax.axis_size("gy") * lax.axis_size("gz")
+    masks = [1 << bit for bit in range((across * lax.axis_size("gx") - 1).bit_length())]
+    order = [mask for mask in masks if mask > across] + [across] + [mask for mask in reversed(masks) if mask < across]
+    gram = hyf[4 * vectors:]
+    hyf = passed_round(hyf, "gy", 1)
+    if lax.axis_size("gy") == 2:
+        gram = gram + hyf[4 * vectors:]
+        order.remove(lax.axis_size("gz"))
     hxf = passed_round(hxf, "gx", 1)
-    hyf = passed_round(hyf, "gy", 1)
-    for phase in phases[1:]:
-        gram = joined(gram, others)
-        if phase is phases[-1]:
-            gram, image = lax.optimization_barrier((gram, image))
-        others = from_partners(gram, phase)
+    for mask in order[:-1]:
+        gram = gram + from_partner(gram, mask)
+    gram, image = lax.optimization_barrier((gram, image))
+    other = from_partner(gram, order[-1])
     residual = pl.pallas_call(
         rim_kernel,
         out_shape=whole,
-        in_specs=[SMEM] * 2 + [VMEM] * 5,
+        in_specs=[SMEM] * 2 + [VMEM] * 4,
         out_specs=HBM,
         scratch_shapes=[scratch(*fields.shape), scratch(nz, nx, ny), pltpu.SemaphoreType.DMA((nz,))],
         compiler_params=params,
         cost_estimate=cost(200, 3),
         name="add_rims",
-    )(pml_width, ritz, basis, image, hzf, hxf, hyf)
-    others, residual = lax.optimization_barrier((others, residual))
-    return basis_new, residual, joined(gram, others)
+    )(pml_width, ritz, basis, image, hxf, hyf)
+    other, residual = lax.optimization_barrier((other, residual))
+    gram = (gram + other)[:, :vectors].reshape(2, vectors, vectors)
+    return basis_new, residual, gram
 
 
 def solution(mesh):

time: 34.3 us -> 36.8 us (1.073)
  waiting for transfers between devices: 2.51 us -> 12.8 us
  starting transfers between devices: 17.4 us -> 9.74 us
    ppermute x7 -> x4, waiting for transfers between devices: 1.7 us -> 10.1 us  [from_partner(): lax.ppermute(value, axes, [(source, source ^ mask) for source in range(co...]
    ppermute x7 -> x4, starting transfers between devices: 8.03 us -> 0.54 us  [from_partner(): lax.ppermute(value, axes, [(source, source ^ mask) for source in range(co...]
    ppermute x6 -> x5, waiting for transfers between devices: 0.81 us -> 2.7 us  [passed_round(): lax.ppermute(value, axis, [(source, (source + steps) % count) for source...]
    pallas_call x1, Pallas kernels: 5.97 us -> 5.12 us  [body(): pl.pallas_call(inner_kernel, out_shape=(whole, f32(vectors, 2 * vectors,...]
    pallas_call x1 -> x2, Pallas kernels: 1.83 us -> 2.65 us  [the longest x1 1.81 us: body(): pl.pallas_call(face_kernel, out_shape=(whole, f32(*xf_shape), f32(*yf_sha...]
    ppermute x6 -> x5, starting transfers between devices: 9.34 us -> 9.19 us  [passed_round(): lax.ppermute(value, axis, [(source, (source + steps) % count) for source...]
  transfers between devices with their start and end apart: 13 -> 9, of which waited for: 5 -> 6; matrix products, arithmetic and copies ran while one was open for 0% -> 0% of each run, Pallas kernels for 29% -> 24%
where the time goes in v5:
time: 36.8 us; the launch traced here: 36.6 us
  waiting for transfers between devices  12.8 us (35%)
  Pallas kernels  12.7 us (35%)
  starting transfers between devices  9.74 us (26%)
  between operations  0.75 us (2%)
  other arithmetic  0.61 us (2%)
    ppermute x4, waiting for transfers between devices, from_partner(): lax.ppermute(value, axes, [(source, source ^ mask) for source in range(co...  10.1 us
    ppermute x5, starting transfers between devices, passed_round(): lax.ppermute(value, axis, [(source, (source + steps) % count) for source...  9.19 us
    pallas_call x1, Pallas kernels, body(): pl.pallas_call(inner_kernel, out_shape=(whole, f32(vectors, 2 * vectors,...  5.12 us
    ppermute x5, waiting for transfers between devices, passed_round(): lax.ppermute(value, axis, [(source, (source + steps) % count) for source...  2.7 us
    pallas_call x1, Pallas kernels, body(): pl.pallas_call(rim_kernel, out_shape=whole, in_specs=[SMEM] * 2 + [VMEM]...  2.24 us
    pallas_call x1, Pallas kernels, body(): pl.pallas_call(face_kernel, out_shape=(whole, f32(*xf_shape), f32(*yf_sha...  1.81 us
    pallas_call x1, Pallas kernels, body(): pl.pallas_call(prepare_kernel, out_shape=(whole, f32(2, nz, nx, ny), f32(...  1.58 us
    pallas_call x1, Pallas kernels, body(): pl.pallas_call(outer_kernel, out_shape=(whole, f32(*xf_shape), planes, f3...  1.14 us
  transfers between devices with their start and end apart: 9, of which 6 were waited for; matrix products, arithmetic and copies ran while one was open for 0% of the time, Pallas kernels for 24%

profile of v5, /device:TPU:0, one launch (start us, length us, event | category | flops | bytes accessed | tf_op | source)
XLA Modules:
  0.0 36.6 jit_solution(12556447780699295019)
XLA Ops:
  0.7 1.8 %take_faces.1 = (f32[2,4,3,8,16,128]{5,4,3,2,1,0:T(8,128)S(1)}, f32[2,4,2,8,128]{4,3,2,1,0:T(8,128)S(1)}, f32[16,128]{1,0:T(8,128)S(1)}) custom-call(f32[2,4,3,8,16,128]{5,4,3,2,1,0:T(8,128)} %fields_hbm.1), custom_call_target="tpu_custom_call" | custom-call | tf_op jit(solution)/shard_map/take_faces/pallas_call | solution.py:487
  2.5 4.5 %collective-permute-start = (f32[2,4,2,8,128]{4,3,2,1,0:T(8,128)S(1)}, f32[2,4,2,8,128]{4,3,2,1,0:T(8,128)S(1)}, u32[]{:S(2)}, u32[]{:S(2)}) collective-permute-start(f32[2,4,2,8,128]{4,3,2,1,0:T(8,128)S(1)} %get-tuple-element.32), channel_id=1, source_target_pairs={{0,28},{4,0},{8,4},{12,8},{16,12},{20,16},{24,20},{28,24},{1,29},{... | collective-permute-start | bytes 196616 | tf_op jit(solution)/shard_map/ppermute | solution.py:22
  7.0 1.5 %collective-permute-start.1 = (f32[16,128]{1,0:T(8,128)S(1)}, f32[16,128]{1,0:T(8,128)S(1)}, u32[]{:S(2)}, u32[]{:S(2)}) collective-permute-start(f32[16,128]{1,0:T(8,128)S(1)} %get-tuple-element.33), channel_id=1, source_target_pairs={{0,2},{2,0},{1,3},{3,1},{4,6},{6,4},{5,7},{7,5},{8,10},{10,8},{9,1... | collective-permute-start | bytes 24584 | tf_op jit(solution)/shard_map/ppermute | solution.py:22
  8.6 1.6 %prepare.1 = (f32[2,4,3,8,16,128]{5,4,3,2,1,0:T(8,128)S(1)}, f32[2,8,16,128]{3,2,1,0:T(8,128)S(1)}, f32[8,16,128]{2,1,0:T(8,128)S(1)}, f32[4,8,128]{2,1,0:T(8,128)S(1)}) custom-call(s32[6]{0:T(128)S(1)} %copy-done.2, f32[4]{0:T(128)S(1)} %copy-done.4, f32[4]{0:T(128)S(1)} %copy-done.5, f32[2,4,4]{2,1,0:T(4,128)S(1)} %copy-done.1, ...), custom_call_target="tpu_custom_call" | custom-call | flops 6553600 | bytes 3145728 | tf_op jit(solution)/shard_map/prepare/pallas_call | solution.py:504
  10.2 0.5 %collective-permute-done.1.raw_yf_ref = f32[16,128]{1,0:T(8,128)S(1)} collective-permute-done((f32[16,128]{1,0:T(8,128)S(1)}, f32[16,128]{1,0:T(8,128)S(1)}, u32[]{:S(2)}, u32[]{:S(2)}) %collective-permute-start.1) | collective-permute-done | bytes 8224 | tf_op jit(solution)/shard_map/ppermute | solution.py:22
  10.7 0.0 collective-permute-done.raw_xf_ref
  10.7 0.8 %slab_face.1 = (f32[2,4,2,8,128]{4,3,2,1,0:T(8,128)S(1)}, f32[16,128]{1,0:T(8,128)S(1)}, f32[8,16,128]{2,1,0:T(8,128)S(1)}, f32[2,4,2,16,128]{4,3,2,1,0:T(8,128)S(1)}) custom-call(f32[2,4,4]{2,1,0:T(4,128)S(1)} %copy-done.1, f32[2,4,3,8,16,128]{5,4,3,2,1,0:T(8,128)S(1)} %get-tuple-element.28.basis_ref, f32[8,16,128]{2,1,0:T(8,128)S(1)} %get-tuple-element.30.table_ref, ...), custom_call_target="tpu_custom_call" | custom-call | tf_op jit(solution)/shard_map/slab_face/pallas_call | solution.py:513
  11.5 1.6 %collective-permute-start.2 = (f32[2,4,2,16,128]{4,3,2,1,0:T(8,128)S(1)}, f32[2,4,2,16,128]{4,3,2,1,0:T(8,128)S(1)}, u32[]{:S(2)}, u32[]{:S(2)}) collective-permute-start(f32[2,4,2,16,128]{4,3,2,1,0:T(8,128)S(1)} %get-tuple-element.37), channel_id=1, source_target_pairs={{0,1},{1,0},{2,3},{3,2},{4,5},{5,4},{6,7},{7,6},{8,9},{9,8},{10,11... | collective-permute-start | bytes 393224 | tf_op jit(solution)/shard_map/ppermute | solution.py:22
  13.1 5.1 %apply_inner.1 = (f32[2,4,3,8,16,128]{5,4,3,2,1,0:T(8,128)S(1)}, f32[4,8,8,128]{3,2,1,0:T(8,128)S(1)}, f32[2,4,2,16,128]{4,3,2,1,0:T(8,128)S(1)}, f32[2,4,2,8,12...) custom-call(f32[2,4,3,8,16,128]{5,4,3,2,1,0:T(8,128)S(1)} %get-tuple-element.28.basis_ref, ...), custom_call_target="tpu_custom_call" | custom-call | flops 16384000 | bytes 3145728 | tf_op jit(solution)/shard_map/apply_inner/pallas_call | solution.py:522
  18.2 0.0 collective-permute-done.2.zf_ref
  18.2 0.0 copy-start.3
  18.3 1.1 %apply_outer.1 = (f32[2,4,3,8,16,128]{5,4,3,2,1,0:T(8,128)S(1)}, f32[2,4,2,8,128]{4,3,2,1,0:T(8,128)S(1)}, f32[8,16,128]{2,1,0:T(8,128)S(1)}, f32[24,128]{1,0:T(8,128)S(1)}) custom-call(s32[6]{0:T(128)S(1)} %copy-done.2, f32[2,4,3,8,16,128]{5,4,3,2,1,0:T(8,128)S(1)} %get-tuple-element.28.basis_ref, ...), custom_call_target="tpu_custom_call", output_to_operand_aliasing={{0}: (9, {}), {1}: (12, {}), {2}: (13, {})} | custom-call | flops 3276800 | bytes 1572864 | tf_op jit(solution)/shard_map/apply_outer/pallas_call | solution.py:534
  19.4 1.6 %collective-permute-start.3 = (f32[24,128]{1,0:T(8,128)S(1)}, f32[24,128]{1,0:T(8,128)S(1)}, u32[]{:S(2)}, u32[]{:S(2)}) collective-permute-start(f32[24,128]{1,0:T(8,128)S(1)} %get-tuple-element.44), channel_id=1, source_target_pairs={{0,2},{2,0},{1,3},{3,1},{4,6},{6,4},{5,7},{7,5},{8,10},{10,8},{9,1... | collective-permute-start | bytes 36872 | tf_op jit(solution)/shard_map/ppermute | solution.py:22
  21.0 0.0 collective-permute-start.8
  21.0 2.2 %collective-permute-done.3.hyf_ref = f32[24,128]{1,0:T(8,128)S(1)} collective-permute-done((f32[24,128]{1,0:T(8,128)S(1)}, f32[24,128]{1,0:T(8,128)S(1)}, u32[]{:S(2)}, u32[]{:S(2)}) %collective-permute-start.3) | collective-permute-done | bytes 12320 | tf_op jit(solution)/shard_map/ppermute | solution.py:22
  23.2 0.0 collective-permute-start.4
  23.2 3.6 %collective-permute-done.4 = f32[8,128]{1,0:T(8,128)S(1)} collective-permute-done((f32[8,128]{1,0:T(8,128)S(1)}, f32[8,128]{1,0:T(8,128)S(1)}, u32[]{:S(2)}, u32[]{:S(2)}) %collective-permute-start.4) | collective-permute-done | bytes 4128 | tf_op jit(solution)/shard_map/ppermute | solution.py:475
  26.8 4.5 %collective-permute-done.5 = f32[8,128]{1,0:T(8,128)S(1)} collective-permute-done((f32[8,128]{1,0:T(8,128)S(1)}, f32[8,128]{1,0:T(8,128)S(1)}, u32[]{:S(2)}, u32[]{:S(2)}) %collective-permute-start.5) | collective-permute-done | bytes 4128 | tf_op jit(solution)/shard_map/ppermute | solution.py:475
  31.3 0.0 collective-permute-start.6
  31.3 1.2 %collective-permute-done.6 = f32[8,128]{1,0:T(8,128)S(1)} collective-permute-done((f32[8,128]{1,0:T(8,128)S(1)}, f32[8,128]{1,0:T(8,128)S(1)}, u32[]{:S(2)}, u32[]{:S(2)}) %collective-permute-start.6) | collective-permute-done | bytes 4128 | tf_op jit(solution)/shard_map/ppermute | solution.py:475
  32.4 0.5 %collective-permute-start.7 = (f32[8,128]{1,0:T(8,128)S(1)}, f32[8,128]{1,0:T(8,128)S(1)}, u32[]{:S(2)}, u32[]{:S(2)}) collective-permute-start(f32[8,128]{1,0:T(8,128)S(1)} %add.18), channel_id=1, source_target_pairs={{0,1},{1,0},{2,3},{3,2},{4,5},{5,4},{6,7},{7,6},{8,9},{9,8},{10,11... | collective-permute-start | bytes 12296 | tf_op jit(solution)/shard_map/ppermute | solution.py:475
  33.0 2.2 %add_rims.1 = f32[2,4,3,8,16,128]{5,4,3,2,1,0:T(8,128)} custom-call(s32[6]{0:T(128)S(1)} %copy-done.2, f32[2,4]{1,0:T(2,128)S(1)} %copy-done.3, f32[2,4,3,8,16,128]{5,4,3,2,1,0:T(8,128)S(1)} %get-tuple-element.28.basis_ref, f32[2,4,3,8,16,128]{5,4,3,2,1,0:T(8,128)S(1)} %get-tuple-element.47.image_ref, ...), custom_call_target="tpu_custom_call" | custom-call | flops 3276800 | bytes 4718592 | tf_op jit(solution)/shard_map/add_rims/pallas_call | solution.py:557
  35.2 0.8 %collective-permute-done.7 = f32[8,128]{1,0:T(8,128)S(1)} collective-permute-done((f32[8,128]{1,0:T(8,128)S(1)}, f32[8,128]{1,0:T(8,128)S(1)}, u32[]{:S(2)}, u32[]{:S(2)}) %collective-permute-start.7) | collective-permute-done | bytes 4128 | tf_op jit(solution)/shard_map/ppermute | solution.py:475
  36.1 0.6 %add.19 = f32[8,128]{1,0:T(8,128)} add(f32[8,128]{1,0:T(8,128)S(1)} %add.18, f32[8,128]{1,0:T(8,128)S(1)} %collective-permute-done.7) | non-fusion elementwise | flops 1024 | bytes 12288 | tf_op jit(solution)/shard_map/add | solution.py:568
  (17 shorter events, 0.0 us)
Async XLA Ops:
  0.6 7.9 %copy-start.2 = (s32[6]{0:T(128)S(1)}, s32[6]{0:T(128)}, u32[]{:S(2)}) copy-start(s32[6]{0:T(128)} %pml_ref.5) | copy-start | bytes 76
  0.6 7.9 %copy-start.1 = (f32[2,4,4]{2,1,0:T(4,128)S(1)}, f32[2,4,4]{2,1,0:T(4,128)}, u32[]{:S(2)}) copy-start(f32[2,4,4]{2,1,0:T(4,128)} %coeffs_ref.3) | copy-start | bytes 388
  0.7 7.9 %copy-start.5 = (f32[4]{0:T(128)S(1)}, f32[4]{0:T(128)}, u32[]{:S(2)}) copy-start(f32[4]{0:T(128)} %eps_loss_ref.1) | copy-start | bytes 52
  0.7 7.9 %copy-start.4 = (f32[4]{0:T(128)S(1)}, f32[4]{0:T(128)}, u32[]{:S(2)}) copy-start(f32[4]{0:T(128)} %eps_real_ref.1) | copy-start | bytes 52
  0.7 7.9 %copy-start = (s32[8,16,128]{2,1,0:T(8,128)S(1)}, s32[8,16,128]{2,1,0:T(8,128)}, u32[]{:S(2)}) copy-start(s32[8,16,128]{2,1,0:T(8,128)} %material_ref.1) | copy-start | bytes 196612
  2.5 8.2 %collective-permute-start = (f32[2,4,2,8,128]{4,3,2,1,0:T(8,128)S(1)}, f32[2,4,2,8,128]{4,3,2,1,0:T(8,128)S(1)}, u32[]{:S(2)}, u32[]{:S(2)}) collective-permute-start(f32[2,4,2,8,128]{4,3,2,1,0:T(8,128)S(1)} %get-tuple-element.32), channel_id=1, source_target_pairs={{0,28},{4,0},{8,4},{12,8},{16,12},{20,16},{24,20},{28,24},{1,29},{... | collective-permute-start | bytes 196616 | tf_op jit(solution)/shard_map/ppermute | solution.py:22
  7.0 3.7 %collective-permute-start.1 = (f32[16,128]{1,0:T(8,128)S(1)}, f32[16,128]{1,0:T(8,128)S(1)}, u32[]{:S(2)}, u32[]{:S(2)}) collective-permute-start(f32[16,128]{1,0:T(8,128)S(1)} %get-tuple-element.33), channel_id=1, source_target_pairs={{0,2},{2,0},{1,3},{3,1},{4,6},{6,4},{5,7},{7,5},{8,10},{10,8},{9,1... | collective-permute-start | bytes 24584 | tf_op jit(solution)/shard_map/ppermute | solution.py:22
  11.5 6.7 %collective-permute-start.2 = (f32[2,4,2,16,128]{4,3,2,1,0:T(8,128)S(1)}, f32[2,4,2,16,128]{4,3,2,1,0:T(8,128)S(1)}, u32[]{:S(2)}, u32[]{:S(2)}) collective-permute-start(f32[2,4,2,16,128]{4,3,2,1,0:T(8,128)S(1)} %get-tuple-element.37), channel_id=1, source_target_pairs={{0,1},{1,0},{2,3},{3,2},{4,5},{5,4},{6,7},{7,6},{8,9},{9,8},{10,11... | collective-permute-start | bytes 393224 | tf_op jit(solution)/shard_map/ppermute | solution.py:22
  18.2 14.7 %copy-start.3 = (f32[2,4]{1,0:T(2,128)S(1)}, f32[2,4]{1,0:T(2,128)}, u32[]{:S(2)}) copy-start(f32[2,4]{1,0:T(2,128)} %ritz_ref.1) | copy-start | bytes 100
  19.4 3.8 %collective-permute-start.3 = (f32[24,128]{1,0:T(8,128)S(1)}, f32[24,128]{1,0:T(8,128)S(1)}, u32[]{:S(2)}, u32[]{:S(2)}) collective-permute-start(f32[24,128]{1,0:T(8,128)S(1)} %get-tuple-element.44), channel_id=1, source_target_pairs={{0,2},{2,0},{1,3},{3,1},{4,6},{6,4},{5,7},{7,5},{8,10},{10,8},{9,1... | collective-permute-start | bytes 36872 | tf_op jit(solution)/shard_map/ppermute | solution.py:22
  21.0 12.0 %collective-permute-start.8 = (f32[2,4,2,8,128]{4,3,2,1,0:T(8,128)S(1)}, f32[2,4,2,8,128]{4,3,2,1,0:T(8,128)S(1)}, u32[]{:S(2)}, u32[]{:S(2)}) collective-permute-start(f32[2,4,2,8,128]{4,3,2,1,0:T(8,128)S(1)} %get-tuple-element.48), channel_id=1, source_target_pairs={{0,4},{4,8},{8,12},{12,16},{16,20},{20,24},{24,28},{28,0},{1,5},{5... | collective-permute-start | bytes 196616 | tf_op jit(solution)/shard_map/ppermute | solution.py:22
  23.2 3.6 %collective-permute-start.4 = (f32[8,128]{1,0:T(8,128)S(1)}, f32[8,128]{1,0:T(8,128)S(1)}, u32[]{:S(2)}, u32[]{:S(2)}) collective-permute-start(f32[8,128]{1,0:T(8,128)S(1)} %slice_add_fusion), channel_id=1, source_target_pairs={{0,8},{1,9},{2,10},{3,11},{4,12},{5,13},{6,14},{7,15},{8,0},{9,1},... | collective-permute-start | bytes 12296 | tf_op jit(solution)/shard_map/ppermute | solution.py:475
  26.8 4.5 %collective-permute-start.5 = (f32[8,128]{1,0:T(8,128)S(1)}, f32[8,128]{1,0:T(8,128)S(1)}, u32[]{:S(2)}, u32[]{:S(2)}) collective-permute-start(f32[8,128]{1,0:T(8,128)S(1)} %add.16), channel_id=1, source_target_pairs={{0,16},{1,17},{2,18},{3,19},{4,20},{5,21},{6,22},{7,23},{8,24},{9,... | collective-permute-start | bytes 12296 | tf_op jit(solution)/shard_map/ppermute | solution.py:475
  31.3 1.2 %collective-permute-start.6 = (f32[8,128]{1,0:T(8,128)S(1)}, f32[8,128]{1,0:T(8,128)S(1)}, u32[]{:S(2)}, u32[]{:S(2)}) collective-permute-start(f32[8,128]{1,0:T(8,128)S(1)} %add.17), channel_id=1, source_target_pairs={{0,4},{1,5},{2,6},{3,7},{4,0},{5,1},{6,2},{7,3},{8,12},{9,13},{10,... | collective-permute-start | bytes 12296 | tf_op jit(solution)/shard_map/ppermute | solution.py:475
  32.4 3.6 %collective-permute-start.7 = (f32[8,128]{1,0:T(8,128)S(1)}, f32[8,128]{1,0:T(8,128)S(1)}, u32[]{:S(2)}, u32[]{:S(2)}) collective-permute-start(f32[8,128]{1,0:T(8,128)S(1)} %add.18), channel_id=1, source_target_pairs={{0,1},{1,0},{2,3},{3,2},{4,5},{5,4},{6,7},{7,6},{8,9},{9,8},{10,11... | collective-permute-start | bytes 12296 | tf_op jit(solution)/shard_map/ppermute | solution.py:475

commit v6 on v5

v6 whole, which is shorter than its diff:
```python
import functools

import jax
import jax.numpy as jnp
from jax import lax
from jax.experimental import pallas as pl
from jax.experimental.pallas import tpu as pltpu
from jax.sharding import PartitionSpec as P

OMEGA_SQ = 0.36
SIGMA_TOP = 3.0
BOUNDS = ((4, 5), (0, 1), (2, 3))
AXES = ("gz", "gx", "gy")

VMEM = pl.BlockSpec(memory_space=pltpu.VMEM)
SMEM = pl.BlockSpec(memory_space=pltpu.SMEM)
HBM = pl.BlockSpec(memory_space=pltpu.HBM)


def passed_round(value, axis, steps):
    count = lax.axis_size(axis)
    return lax.ppermute(value, axis, [(source, (source + steps) % count) for source in range(count)])


def inverse_stretch(places, length, low_width, high_width):
    inside_depth = jnp.clip((low_width - places) / low_width, 0.0, 1.0) + jnp.clip(
        (places + 1.0 - length + high_width) / high_width, 0.0, 1.0
    )
    absorb = SIGMA_TOP * inside_depth * inside_depth
    scaled = 1.0 / (1.0 + absorb * absorb)
    return scaled, -absorb * scaled


def cmul(left, right):
    return (left[0] * right[0] - left[1] * right[1], left[0] * right[1] + left[1] * right[0])


def add(left, right):
    return (left[0] + right[0], left[1] + right[1])


def sub(left, right):
    return (left[0] - right[0], left[1] - right[1])


def axis_stretch(pml_ref, direction, count, places):
    total = count * lax.axis_size(AXES[direction])
    low_slot, high_slot = BOUNDS[direction]
    low = jnp.full(places.shape, pml_ref[low_slot], jnp.int32).astype(jnp.float32)
    high = jnp.full(places.shape, pml_ref[high_slot], jnp.int32).astype(jnp.float32)
    return inverse_stretch(places, jnp.float32(total), low, high)


def local_places(direction, count, shape, dim):
    start = lax.axis_index(AXES[direction]) * count
    return (lax.broadcasted_iota(jnp.int32, shape, dim) + start).astype(jnp.float32)


def one_place(direction, count, offset, shape):
    start = lax.axis_index(AXES[direction]) * count + offset
    return jnp.full(shape, start, jnp.int32).astype(jnp.float32)


def packed_row(slot, part, vector, vectors):
    return (slot * 2 + part) * vectors + vector


def has_neighbour(direction, steps):
    place = lax.axis_index(AXES[direction]) + steps
    inside = (place >= 0) & (place < lax.axis_size(AXES[direction]))
    return jnp.where(inside, 1.0, 0.0).astype(jnp.float32)


def face_kernel(fields_hbm, fields_ref, xf_ref, yf_ref, sems):
    _, vectors, _, nz, nx, ny = fields_ref.shape
    lanes = lax.broadcasted_iota(jnp.int32, (nx, ny), 1)
    copies = [
        pltpu.make_async_copy(fields_hbm.at[part, :, comp], fields_ref.at[part, :, comp], sems.at[part, comp])
        for comp in (0, 2, 1) for part in range(2)
    ]
    for copy in copies:
        copy.start()
    for copy in copies:
        copy.wait()

    packed = [jnp.zeros((nx, ny), jnp.float32)] * nz
    for comp in (0, 2):
        for part in range(2):
            for a in range(vectors):
                row = packed_row(comp // 2, part, a, vectors)
                for z in range(nz):
                    value = fields_ref[part, a, comp, z]
                    packed[z] = jnp.where(lanes == row, pltpu.roll(value, row, 1) if row else value, packed[z])
    turned = jnp.concatenate(packed, axis=0).T
    yf_ref[...] = turned[:yf_ref.shape[0]]
    for part in range(2):
        for a in range(vectors):
            for slot in range(2):
                xf_ref[part, a, slot] = fields_ref[part, a, slot + 1, :, 0, :]


def rotated(coeffs_ref, old, b):
    new = None
    for a, value in enumerate(old):
        term = cmul((coeffs_ref[0, a, b], coeffs_ref[1, a, b]), value)
        new = term if new is None else add(new, term)
    return new


SUB = 8
SHX, SEX, SHY, SEY = range(0, 8, 2)


def field_of(ref, b, comp, z, cut):
    return tuple(ref[part, b, comp, z, cut] for part in range(2))


def tiles_of(nx):
    return [slice(SUB * t, SUB * (t + 1)) for t in range(nx // SUB)]


def prepare_kernel(
    pml_ref, eps_real_ref, eps_loss_ref, coeffs_ref, fields_ref, material_ref,
    basis_ref, loss_ref, h_ref, packed_ref, table_ref, sz_ref,
):
    _, vectors, _, nz, nx, ny = fields_ref.shape
    plane = (nx, ny)
    parts = range(2)
    for slot, direction, half, count, dim in (
        (SHX, 1, 0.5, nx, 0), (SEX, 1, 0.0, nx, 0), (SHY, 2, 0.5, ny, 1), (SEY, 2, 0.0, ny, 1),
    ):
        values = axis_stretch(pml_ref, direction, count, local_places(direction, count, plane, dim) + half)
        for part in parts:
            table_ref[slot + part] = values[part]
    for slot, half in ((0, 0.0), (2, 0.5)):
        values = axis_stretch(pml_ref, 0, nz, local_places(0, nz, (nz, ny), 0) + half)
        for part in parts:
            sz_ref[slot + part] = values[part]

    @pl.loop(0, nz)
    def _(z):
        material = material_ref[z]
        eps = []
        for source in (eps_real_ref, eps_loss_ref):
            value = jnp.zeros(plane, jnp.float32)
            for number in range(source.shape[0]):
                value = jnp.where(material == number, -OMEGA_SQ * source[number], value)
            eps.append(value)
        for comp in range(3):
            old = [(fields_ref[0, a, comp, z], fields_ref[1, a, comp, z]) for a in range(vectors)]
            for b in range(vectors):
                new = rotated(coeffs_ref, old, b)
                loss = cmul(eps, new)
                for part in parts:
                    basis_ref[part, b, comp, z] = new[part]
                    loss_ref[part, b, comp, z] = loss[part]
        packed_ref[z] = jnp.zeros(plane, jnp.float32)

    tile = (SUB, ny)
    rows = lax.broadcasted_iota(jnp.int32, tile, 0)
    lanes = lax.broadcasted_iota(jnp.int32, tile, 1)
    cuts = tiles_of(nx)

    def magnetic(b, z, last):
        shz = tuple(sz_ref[2 + part, pl.ds(z, 1)] for part in parts)
        for cut in cuts:
            u = [field_of(basis_ref, b, comp, z, cut) for comp in range(3)]

            def step_z(comp):
                if last:
                    return tuple(-value for value in u[comp])
                return sub(field_of(basis_ref, b, comp, z + 1, cut), u[comp])

            def step_x(comp):
                if cut.stop < nx:
                    ahead = field_of(basis_ref, b, comp, z, slice(cut.start + 1, cut.stop + 1))
                else:
                    ahead = tuple(jnp.where(rows == SUB - 1, 0.0, pltpu.roll(value, SUB - 1, 0)) for value in u[comp])
                return sub(ahead, u[comp])

            def step_y(comp):
                ahead = tuple(jnp.where(lanes == ny - 1, 0.0, pltpu.roll(value, ny - 1, 1)) for value in u[comp])
                return sub(ahead, u[comp])

            shx = tuple(table_ref[SHX + part, cut] for part in parts)
            shy = tuple(table_ref[SHY + part, cut] for part in parts)
            h = (
                sub(cmul(shy, step_y(2)), cmul(shz, step_z(1))),
                sub(cmul(shz, step_z(0)), cmul(shx, step_x(2))),
                sub(cmul(shx, step_x(1)), cmul(shy, step_y(0))),
            )
            for comp in range(3):
                for part in parts:
                    h_ref[part, b, comp, z, cut] = h[comp][part]
            packed = packed_ref[z, cut]
            for slot, value in enumerate((h[2], h[0])):
                for part in parts:
                    row = packed_row(slot, part, b, vectors)
                    packed = jnp.where(lanes == row, pltpu.roll(value[part], (row + 1) % ny, 1), packed)
            packed_ref[z, cut] = packed

    for b in range(vectors):

        @pl.loop(0, nz - 1)
        def _(z, b=b):
            magnetic(b, z, False)

        magnetic(b, nz - 1, True)


def turn_face(coeffs_ref, direction, raw_ref, face_ref):
    inside = has_neighbour(direction, 1)
    vectors = raw_ref.shape[1]
    for slot in range(2):
        old = [(raw_ref[0, a, slot] * inside, raw_ref[1, a, slot] * inside) for a in range(vectors)]
        for b in range(vectors):
            new = rotated(coeffs_ref, old, b)
            for part in range(2):
                face_ref[part, b, slot] = new[part]


def turn_column(coeffs_ref, raw_ref, rows_ref):
    vectors = coeffs_ref.shape[1]
    inside = has_neighbour(2, 1)
    both = 2 * vectors
    shape = (both, raw_ref.shape[1])
    which = lax.broadcasted_iota(jnp.int32, shape, 0)
    turned = [jnp.zeros(shape, jnp.float32)] * 2
    for part in range(2):
        for a in range(vectors):
            column = jnp.zeros(shape, jnp.float32)
            for b in range(vectors):
                first, second = coeffs_ref[0, a, b] * inside, coeffs_ref[1, a, b] * inside
                if part:
                    first, second = -second, first
                column = jnp.where(which == b, first, column)
                column = jnp.where(which == vectors + b, second, column)
            for slot in range(2):
                row = packed_row(slot, part, a, vectors)
                turned[slot] = turned[slot] + column * raw_ref[row:row + 1]
    for slot in range(2):
        rows_ref[slot * both:(slot + 1) * both] = turned[slot]


def lane_to_last(values, slot, part, b, vectors):
    ny = values.shape[-1]
    lanes = lax.broadcasted_iota(jnp.int32, values.shape, 1)
    row = packed_row(slot, part, b, vectors)
    return jnp.where(lanes == ny - 1, pltpu.roll(values, ny - 1 - row, 1), 0.0)


def with_halos(h, b, z, cut, nx, xadd_ref, yadd_ref):
    vectors = xadd_ref.shape[1]
    column = yadd_ref[z, cut]
    hx = tuple(h[0][part] + lane_to_last(column, 1, part, b, vectors) for part in range(2))
    hz = tuple(h[2][part] + lane_to_last(column, 0, part, b, vectors) for part in range(2))
    hy = h[1]
    if cut.stop == nx:
        rows = lax.broadcasted_iota(jnp.int32, column.shape, 0)

        def row_of(slot):
            return tuple(
                jnp.where(rows == SUB - 1, xadd_ref[part, b, slot, pl.ds(z, 1)], 0.0) for part in range(2)
            )

        hy, hz = add(hy, row_of(0)), add(hz, row_of(1))
    return hx, hy, hz


def slab_kernel(
    pml_ref, coeffs_ref, basis_ref, h_in, packed_in, raw_xf_ref, raw_yf_ref,
    h_ref, packed_ref, xf_ref, yt_ref, xadd_ref, yadd_ref, hxf_ref, zf_ref,
):
    del h_in, packed_in
    _, vectors, _, nz, nx, ny = basis_ref.shape
    parts = range(2)
    cells = nz * nx
    both = 2 * vectors
    turn_face(coeffs_ref, 1, raw_xf_ref, xf_ref)
    turn_column(coeffs_ref, raw_yf_ref, yt_ref)
    shx = axis_stretch(pml_ref, 1, nx, one_place(1, nx, nx - 1, (1, ny)) + 0.5)
    shy = axis_stretch(pml_ref, 2, ny, one_place(2, ny, ny - 1, (1, cells)) + 0.5)
    for b in range(vectors):
        for slot in range(2):
            value = cmul(shx, tuple(xf_ref[part, b, 1 - slot] for part in parts))
            for part in parts:
                xadd_ref[part, b, slot] = value[part] if slot else -value[part]
    added = []
    for slot in range(2):
        value = cmul(shy, (yt_ref[slot * both:slot * both + vectors], yt_ref[slot * both + vectors:(slot + 1) * both]))
        added += [part if slot else -part for part in value]
    rest = jnp.zeros((ny - 2 * both, cells), jnp.float32)
    yadd_ref[...] = jnp.concatenate(added + [rest], axis=0).T.reshape(nz, nx, ny)
    packed_ref[...] = packed_ref[...] + yadd_ref[...]
    last = nz - 1
    lower = jnp.full((SUB, ny), lax.axis_index(AXES[0]), jnp.int32) == 0
    lanes = lax.broadcasted_iota(jnp.int32, (nz, ny), 1)
    corner = packed_ref[:, nx - 1, :]
    for b in range(vectors):
        for part in parts:
            row = packed_row(0, part, b, vectors)
            edge = pltpu.roll(xadd_ref[part, b, 1], (row + 1) % ny, 1)
            corner = corner + jnp.where(lanes == row, edge, 0.0)
    packed_ref[:, nx - 1, :] = corner
    for b in range(vectors):
        for part in parts:
            hxf_ref[part, b, 0] = h_ref[part, b, 1, :, nx - 1, :] + xadd_ref[part, b, 0]
            hxf_ref[part, b, 1] = (
                h_ref[part, b, 2, :, nx - 1, :] + xadd_ref[part, b, 1]
                + lane_to_last(yadd_ref[:, nx - 1, :], 0, part, b, vectors)
            )
        for cut in tiles_of(nx):
            h = [field_of(h_ref, b, comp, last, cut) for comp in range(3)]
            h = with_halos(h, b, last, cut, nx, xadd_ref, yadd_ref)
            for part in parts:
                for comp in range(3):
                    h_ref[part, b, comp, last, cut] = h[comp][part]
                for comp in range(2):
                    zf_ref[part, b, comp, cut] = jnp.where(lower, h[comp][part], basis_ref[part, b, comp, 0, cut])


def plane_step(b, z, before, sums, basis_ref, loss_ref, table_ref, sz_ref, h_ref, image_ref, halos=None):
    _, vectors, _, _, nx, ny = basis_ref.shape
    rows = lax.broadcasted_iota(jnp.int32, (SUB, ny), 0)
    lanes = lax.broadcasted_iota(jnp.int32, (SUB, ny), 1)
    parts = range(2)
    cuts = tiles_of(nx)
    sez = tuple(sz_ref[part, pl.ds(z, 1)] for part in parts)
    fields = []
    for cut in cuts:
        h = [field_of(h_ref, b, comp, z, cut) for comp in range(3)]
        if halos is not None:
            h = with_halos(h, b, z, cut, nx, *halos)
            for comp in (1, 2):
                for part in parts:
                    h_ref[part, b, comp, z, cut] = h[comp][part]
        fields.append(h)
    sums = list(sums)
    for t, cut in enumerate(cuts):
        hx, hy, hz = fields[t]

        def back_x(comp):
            here = fields[t][comp]
            if t:
                past = field_of(h_ref, b, comp, z, slice(cut.start - 1, cut.stop - 1))
            else:
                past = tuple(jnp.where(rows == 0, 0.0, pltpu.roll(value, 1, 0)) for value in here)
            return sub(here, past)

        def back_y(value):
            return sub(value, tuple(jnp.where(lanes == 0, 0.0, pltpu.roll(part, 1, 1)) for part in value))

        sex = tuple(table_ref[SEX + part, cut] for part in parts)
        sey = tuple(table_ref[SEY + part, cut] for part in parts)
        bxy, bxz = (cmul(sex, back_x(comp)) for comp in (1, 2))
        byz, byx = (cmul(sey, back_y(value)) for value in (hz, hx))
        bzx, bzy = (cmul(sez, sub(value, past)) for value, past in zip((hx, hy), before[t]))
        curl = (sub(byz, bzy), sub(bzx, bxz), sub(bxy, byx))
        w = [add(curl[comp], field_of(loss_ref, b, comp, z, cut)) for comp in range(3)]
        for comp in range(3):
            for part in parts:
                image_ref[part, b, comp, z, cut] = w[comp][part]
        for a in range(vectors):
            total = sums[a]
            for comp in range(3):
                total = add(total, cmul(field_of(basis_ref, a, comp, z, cut), w[comp]))
            sums[a] = total
    return [(h[0], h[1]) for h in fields], sums


def inner_kernel(
    basis_ref, loss_ref, table_ref, sz_ref, h_in, xadd_ref, yadd_ref,
    h_ref, image_ref, acc_ref, before_ref, basis_hbm, sem,
):
    del h_in
    _, vectors, _, nz, nx, ny = basis_ref.shape
    keep = pltpu.make_async_copy(basis_ref, basis_hbm, sem)
    keep.start()
    count = nx // SUB
    for b in range(vectors):

        def step(z, carry, b=b):
            return plane_step(
                b, z, *carry, basis_ref, loss_ref, table_ref, sz_ref, h_ref, image_ref, (xadd_ref, yadd_ref)
            )

        none = (jnp.zeros((SUB, ny), jnp.float32),) * 2
        before, sums = lax.fori_loop(0, nz - 1, step, ([(none, none)] * count, [none] * vectors))
        for part in range(2):
            for a in range(vectors):
                acc_ref[b, part * vectors + a] = sums[a][part]
            for t, cut in enumerate(tiles_of(nx)):
                for slot in range(2):
                    before_ref[part, b, slot, cut] = before[t][slot][part]
    keep.wait()


def last_plane_kernel(sz_ref, zf_ref, h_in, packed_in, hxf_in, h_ref, packed_ref, hxf_ref):
    del h_in, packed_in, hxf_in
    _, vectors, _, nz, nx, ny = h_ref.shape
    parts = range(2)
    last = nz - 1
    lanes = lax.broadcasted_iota(jnp.int32, (SUB, ny), 1)
    shz = tuple(sz_ref[2 + part, last:] * has_neighbour(0, 1) for part in parts)
    packed = [packed_ref[last, cut] for cut in tiles_of(nx)]
    for b in range(vectors):
        for t, cut in enumerate(tiles_of(nx)):
            ex, ey = (tuple(zf_ref[part, b, slot, cut] for part in parts) for slot in range(2))
            more = (tuple(-value for value in cmul(shz, ey)), cmul(shz, ex))
            for part in parts:
                for comp in range(2):
                    h_ref[part, b, comp, last, cut] = h_ref[part, b, comp, last, cut] + more[comp][part]
                row = packed_row(1, part, b, vectors)
                edge = pltpu.roll(more[0][part], (row + 1) % ny, 1)
                packed[t] = packed[t] + jnp.where(lanes == row, edge, 0.0)
                if cut.stop == nx:
                    hxf_ref[part, b, 0, last:] = hxf_ref[part, b, 0, last:] + more[1][part][SUB - 1:]
    for t, cut in enumerate(tiles_of(nx)):
        packed_ref[last, cut] = packed[t]


def outer_kernel(
    pml_ref, basis_ref, loss_ref, table_ref, sz_ref, h_ref, zf_ref, xf_ref, yt_ref, hxf_ref, packed_ref,
    image_in, acc_ref, before_ref, image_ref, hyf_ref,
):
    del image_in
    _, vectors, _, nz, nx, ny = basis_ref.shape
    parts = range(2)
    cuts = tiles_of(nx)
    under = axis_stretch(pml_ref, 0, nz, one_place(0, nz, -1, (1, ny)) + 0.5)
    sez = tuple(sz_ref[part, 0:1] * has_neighbour(0, -1) for part in parts)
    sx_next = axis_stretch(pml_ref, 1, nx, one_place(1, nx, nx, (1, ny)))
    sy_next = axis_stretch(pml_ref, 2, ny, one_place(2, ny, ny, (1, nz * nx)))
    both = 2 * vectors
    hyf_ref[:2 * both] = packed_ref[...].reshape(nz * nx, ny).T[:2 * both]
    ends = [
        cmul(sy_next, (yt_ref[slot * both:slot * both + vectors], yt_ref[slot * both + vectors:(slot + 1) * both]))
        for slot in range(2)
    ]
    columns = lax.broadcasted_iota(jnp.int32, (both, ny), 1)
    gram = jnp.zeros((both, ny), jnp.float32)
    for b in range(vectors):

        def tile_of(ref, slot, cut, b=b):
            return tuple(ref[part, b, slot, cut] for part in parts)

        before = [tuple(tile_of(before_ref, slot, cut) for slot in range(2)) for cut in cuts]
        sums = [(acc_ref[b, a], acc_ref[b, vectors + a]) for a in range(vectors)]
        _, sums = plane_step(
            b, nz - 1, before, sums, basis_ref, loss_ref, table_ref, sz_ref, h_ref, image_ref
        )
        for cut in cuts:
            ex, ey = (field_of(basis_ref, b, comp, 0, cut) for comp in range(2))
            hx = sub(tile_of(zf_ref, 0, cut), cmul(under, ey))
            hy = add(tile_of(zf_ref, 1, cut), cmul(under, ex))
            more = (cmul(sez, hy), cmul(sez, hx))
            for part in parts:
                image_ref[part, b, 0, 0, cut] = image_ref[part, b, 0, 0, cut] + more[0][part]
                image_ref[part, b, 1, 0, cut] = image_ref[part, b, 1, 0, cut] - more[1][part]
            for a in range(vectors):
                ex, ey = (field_of(basis_ref, a, comp, 0, cut) for comp in range(2))
                sums[a] = add(sums[a], sub(cmul(ex, more[0]), cmul(ey, more[1])))
        h_y = tuple(hxf_ref[part, b, 0] for part in parts)
        h_z = tuple(hxf_ref[part, b, 1] for part in parts)
        for a in range(vectors):
            over = cmul(tuple(xf_ref[part, a, 0] for part in parts), h_z)
            over = sub(over, cmul(tuple(xf_ref[part, a, 1] for part in parts), h_y))
            over = cmul(sx_next, over)
            for row in range(0, nz, SUB):
                sums[a] = add(sums[a], tuple(part[row:row + SUB] for part in over))
        flat = jnp.concatenate(
            [jnp.sum(sums[a][part], axis=0, keepdims=True) for part in parts for a in range(vectors)], axis=0
        )
        over = None
        for slot in range(2):
            h = tuple(hyf_ref[packed_row(slot, part, b, vectors)][None] for part in parts)
            term = cmul(ends[slot], h)
            over = term if over is None else sub(term, over)
        side = jnp.concatenate(over, axis=0)
        total = jnp.sum(flat, axis=1, keepdims=True) + jnp.sum(side, axis=1, keepdims=True)
        gram = jnp.where(columns == b, total, gram)
    everywhere = 3.0 * nz * nx * ny
    for axis in AXES:
        everywhere = everywhere * lax.axis_size(axis)
    hyf_ref[2 * both:] = gram * (1.0 / everywhere)


def rim_kernel(
    pml_ref, ritz_ref, basis_ref, image_ref, hxf_ref, hyf_ref, residual_hbm, residual_ref, packed_ref, sems
):
    _, vectors, _, nz, nx, ny = basis_ref.shape
    plane = (nx, ny)
    rows = lax.broadcasted_iota(jnp.int32, plane, 0)
    lanes = lax.broadcasted_iota(jnp.int32, plane, 1)
    sex = axis_stretch(pml_ref, 1, nx, one_place(1, nx, 0, (1, ny)))
    sey = axis_stretch(pml_ref, 2, ny, one_place(2, ny, 0, plane))
    none = jnp.zeros(plane, jnp.float32)
    sex = tuple(jnp.where(rows == 0, part * has_neighbour(1, -1), none) for part in sex)
    sey = tuple(jnp.where(lanes == 0, part * has_neighbour(2, -1), none) for part in sey)
    used = 4 * vectors
    rest = jnp.zeros((ny - used, nz * nx), jnp.float32)
    packed_ref[...] = jnp.concatenate([hyf_ref[:used], rest], axis=0).T.reshape(nz, nx, ny)

    def kept(z):
        return pltpu.make_async_copy(residual_ref.at[:, :, :, z], residual_hbm.at[:, :, :, z], sems.at[z])

    @pl.loop(0, nz)
    def _(z):
        packed = packed_ref[z]
        for b in range(vectors):

            def column(slot, b=b):
                return tuple(
                    pltpu.roll(packed, (ny - packed_row(slot, part, b, vectors)) % ny, 1) for part in range(2)
                )

            def row(slot, b=b):
                return tuple(hxf_ref[part, b, slot, pl.ds(z, 1)] for part in range(2))

            factor = (ritz_ref[0, b], ritz_ref[1, b])
            left = []
            for comp in range(3):
                u = (basis_ref[0, b, comp, z], basis_ref[1, b, comp, z])
                w = (image_ref[0, b, comp, z], image_ref[1, b, comp, z])
                left.append(sub(w, cmul(factor, u)))
            left[0] = sub(left[0], cmul(sey, column(0)))
            left[2] = add(left[2], cmul(sey, column(1)))
            left[1] = add(left[1], cmul(sex, row(1)))
            left[2] = sub(left[2], cmul(sex, row(0)))
            for comp in range(3):
                for part in range(2):
                    residual_ref[part, b, comp, z] = left[comp][part]
        kept(z).start()

    @pl.loop(0, nz)
    def _(z):
        kept(z).wait()


def from_partner(value, mask):
    axes = ("gx", "gy", "gz")
    count = 1
    for axis in axes:
        count *= lax.axis_size(axis)
    return lax.ppermute(value, axes, [(source, source ^ mask) for source in range(count)])


def body(fields, material, pml_width, eps_real, eps_loss, coeffs, ritz):
    _, vectors, _, nz, nx, ny = fields.shape
    f32 = lambda *shape: jax.ShapeDtypeStruct(shape, jnp.float32)
    scratch = lambda *shape: pltpu.VMEM(shape, jnp.float32)
    params = pltpu.CompilerParams(vmem_limit_bytes=40 * 1024 * 1024)
    whole = f32(*fields.shape)
    zf_shape = (2, vectors, 2, nx, ny)
    xf_shape = (2, vectors, 2, nz, ny)
    yf_shape = (4 * vectors, nz * nx)
    near, xf, yf = pl.pallas_call(
        face_kernel,
        out_shape=(whole, f32(*xf_shape), f32(*yf_shape)),
        in_specs=[HBM],
        out_specs=(VMEM,) * 3,
        scratch_shapes=[pltpu.SemaphoreType.DMA((2, 3))],
        compiler_params=params,
        name="take_faces",
    )(pltpu.with_memory_space_constraint(fields, pltpu.HBM))
    xf = passed_round(xf, "gx", -1)
    yf = passed_round(yf, "gy", -1)
    cells = fields.size // 6 // vectors

    def cost(flops, passes):
        return pl.CostEstimate(flops=flops * cells, bytes_accessed=passes * 4 * fields.size, transcendentals=0)

    planes = f32(nz, nx, ny)
    face = f32(*xf_shape)
    basis, loss, h, packed, table, sz = pl.pallas_call(
        prepare_kernel,
        out_shape=(whole, whole, whole, planes, f32(8, nx, ny), f32(4, nz, ny)),
        in_specs=[SMEM] * 4 + [VMEM] * 2,
        out_specs=(VMEM,) * 6,
        compiler_params=params,
        cost_estimate=cost(800, 4),
        name="prepare",
    )(pml_width, eps_real, eps_loss, coeffs, near, material)
    h, packed, xf, yt, xadd, yadd, hxf, zf = pl.pallas_call(
        slab_kernel,
        out_shape=(whole, planes, face, f32(*yf_shape), face, planes, face, f32(*zf_shape)),
        in_specs=[SMEM] * 2 + [VMEM] * 5,
        out_specs=(VMEM,) * 8,
        input_output_aliases={3: 0, 4: 1},
        compiler_params=params,
        name="slab_face",
    )(pml_width, coeffs, basis, h, packed, xf, yf)
    zf = passed_round(zf, "gz", 1)
    h, image, acc, before, basis_new = pl.pallas_call(
        inner_kernel,
        out_shape=(whole, whole, f32(vectors, 2 * vectors, SUB, ny), f32(*zf_shape), whole),
        in_specs=[VMEM] * 7,
        out_specs=(VMEM,) * 4 + (HBM,),
        scratch_shapes=[pltpu.SemaphoreType.DMA],
        input_output_aliases={4: 0},
        compiler_params=params,
        cost_estimate=cost(800, 2),
        name="apply_inner",
    )(basis, loss, table, sz, h, xadd, yadd)
    h, packed, hxf = pl.pallas_call(
        last_plane_kernel,
        out_shape=(whole, planes, face),
        in_specs=[VMEM] * 5,
        out_specs=(VMEM,) * 3,
        input_output_aliases={2: 0, 3: 1, 4: 2},
        compiler_params=params,
        name="last_plane",
    )(sz, zf, h, packed, hxf)
    from_x = passed_round(hxf, "gx", 1)
    image, hyf = pl.pallas_call(
        outer_kernel,
        out_shape=(whole, f32(6 * vectors, nz * nx)),
        in_specs=[SMEM] + [VMEM] * 13,
        out_specs=(VMEM,) * 2,
        input_output_aliases={11: 0},
        compiler_params=params,
        cost_estimate=cost(300, 1),
        name="apply_outer",
    )(pml_width, basis, loss, table, sz, h, zf, xf, yt, hxf, packed, image, acc, before)
    across = lax.axis_size("gy") * lax.axis_size("gz")
    masks = [1 << bit for bit in range((across * lax.axis_size("gx") - 1).bit_length())]
    order = [mask for mask in masks if mask > across] + [across] + [mask for mask in reversed(masks) if mask < across]
    gram = hyf[4 * vectors:]
    hyf = passed_round(hyf, "gy", 1)
    hyf, from_x = lax.optimization_barrier((hyf, from_x))
    if lax.axis_size("gy") == 2:
        gram = gram + hyf[4 * vectors:]
        order.remove(lax.axis_size("gz"))
    for mask in order[:-1]:
        gram = gram + from_partner(gram, mask)
    gram, image = lax.optimization_barrier((gram, image))
    other = from_partner(gram, order[-1])
    residual = pl.pallas_call(
        rim_kernel,
        out_shape=whole,
        in_specs=[SMEM] * 2 + [VMEM] * 4,
        out_specs=HBM,
        scratch_shapes=[scratch(*fields.shape), scratch(nz, nx, ny), pltpu.SemaphoreType.DMA((nz,))],
        compiler_params=params,
        cost_estimate=cost(200, 3),
        name="add_rims",
    )(pml_width, ritz, basis, image, from_x, hyf)
    other, residual = lax.optimization_barrier((other, residual))
    gram = (gram + other)[:, :vectors].reshape(2, vectors, vectors)
    return basis_new, residual, gram


def solution(mesh):
    in_specs = (P(None, None, None, "gz", "gx", "gy"), P("gz", "gx", "gy"), P(), P(), P(), P(), P())
    out_specs = (P(None, None, None, "gz", "gx", "gy"), P(None, None, None, "gz", "gx", "gy"), P())
    return jax.shard_map(body, mesh=mesh, in_specs=in_specs, out_specs=out_specs, check_vma=False)
```

time: 36.8 us -> 41.7 us (1.13)
  Pallas kernels: 12.7 us -> 17.4 us
  waiting for transfers between devices: 12.8 us -> 14.1 us
  starting transfers between devices: 9.74 us -> 8.72 us
    pallas_call x4 -> x5, Pallas kernels: 8.68 us -> 13.3 us  [the longest x1 6.32 us: body(): pl.pallas_call(prepare_kernel, out_shape=(whole, whole, whole, planes, f3...]
    ppermute x5, waiting for transfers between devices: 2.7 us -> 3.98 us  [passed_round(): lax.ppermute(value, axis, [(source, (source + steps) % count) for source...]
    ppermute x5, starting transfers between devices: 9.19 us -> 8.18 us  [passed_round(): lax.ppermute(value, axis, [(source, (source + steps) % count) for source...]
  transfers between devices with their start and end apart: 9 -> 9, of which waited for: 6 -> 6; matrix products, arithmetic and copies ran while one was open for 0% -> 0% of each run, Pallas kernels for 24% -> 35%
where the time goes in v6:
time: 41.7 us; the launch traced here: 41.6 us
  Pallas kernels  17.4 us (42%)
  waiting for transfers between devices  14.1 us (34%)
  starting transfers between devices  8.72 us (21%)
  between operations  0.77 us (2%)
  other arithmetic  0.61 us (1%)
    ppermute x4, waiting for transfers between devices, from_partner(): lax.ppermute(value, axes, [(source, source ^ mask) for source in range(co...  10.1 us
    ppermute x5, starting transfers between devices, passed_round(): lax.ppermute(value, axis, [(source, (source + steps) % count) for source...  8.18 us
    pallas_call x1, Pallas kernels, body(): pl.pallas_call(prepare_kernel, out_shape=(whole, whole, whole, planes, f3...  6.32 us
    pallas_call x1, Pallas kernels, body(): pl.pallas_call(inner_kernel, out_shape=(whole, whole, f32(vectors, 2 * ve...  4.93 us
    ppermute x5, waiting for transfers between devices, passed_round(): lax.ppermute(value, axis, [(source, (source + steps) % count) for source...  3.98 us
    pallas_call x1, Pallas kernels, body(): pl.pallas_call(rim_kernel, out_shape=whole, in_specs=[SMEM] * 2 + [VMEM]...  2.23 us
    pallas_call x1, Pallas kernels, body(): pl.pallas_call(face_kernel, out_shape=(whole, f32(*xf_shape), f32(*yf_sha...  1.81 us
    pallas_call x1, Pallas kernels, body(): pl.pallas_call(outer_kernel, out_shape=(whole, f32(6 * vectors, nz * nx))...  1.03 us
  transfers between devices with their start and end apart: 9, of which 6 were waited for; matrix products, arithmetic and copies ran while one was open for 0% of the time, Pallas kernels for 35%

profile of v6, /device:TPU:0, one launch (start us, length us, event | category | flops | bytes accessed | tf_op | source)
XLA Modules:
  0.0 41.6 jit_solution(17791572572950439323)
XLA Ops:
  0.7 1.8 %take_faces.1 = (f32[2,4,3,8,16,128]{5,4,3,2,1,0:T(8,128)S(1)}, f32[2,4,2,8,128]{4,3,2,1,0:T(8,128)S(1)}, f32[16,128]{1,0:T(8,128)S(1)}) custom-call(f32[2,4,3,8,16,128]{5,4,3,2,1,0:T(8,128)} %fields_hbm.1), custom_call_target="tpu_custom_call" | custom-call | tf_op jit(solution)/shard_map/take_faces/pallas_call | solution.py:557
  2.5 4.5 %collective-permute-start = (f32[2,4,2,8,128]{4,3,2,1,0:T(8,128)S(1)}, f32[2,4,2,8,128]{4,3,2,1,0:T(8,128)S(1)}, u32[]{:S(2)}, u32[]{:S(2)}) collective-permute-start(f32[2,4,2,8,128]{4,3,2,1,0:T(8,128)S(1)} %get-tuple-element.43), channel_id=1, source_target_pairs={{0,28},{4,0},{8,4},{12,8},{16,12},{20,16},{24,20},{28,24},{1,29},{... | collective-permute-start | bytes 196616 | tf_op jit(solution)/shard_map/ppermute | solution.py:22
  7.0 1.5 %collective-permute-start.1 = (f32[16,128]{1,0:T(8,128)S(1)}, f32[16,128]{1,0:T(8,128)S(1)}, u32[]{:S(2)}, u32[]{:S(2)}) collective-permute-start(f32[16,128]{1,0:T(8,128)S(1)} %get-tuple-element.44), channel_id=1, source_target_pairs={{0,2},{2,0},{1,3},{3,1},{4,6},{6,4},{5,7},{7,5},{8,10},{10,8},{9,1... | collective-permute-start | bytes 24584 | tf_op jit(solution)/shard_map/ppermute | solution.py:22
  8.6 6.3 %prepare.1 = (f32[2,4,3,8,16,128]{5,4,3,2,1,0:T(8,128)S(1)}, f32[2,4,3,8,16,128]{5,4,3,2,1,0:T(8,128)S(1)}, f32[2,4,3,8,16,128]{5,4,3,2,1,0:T(8,128)S(1)}, f32[8...) custom-call(s32[6]{0:T(128)S(1)} %copy-done.2, f32[4]{0:T(128)S(1)} %copy-done.4, ...), custom_call_target="tpu_custom_call" | custom-call | flops 13107200 | bytes 6291456 | tf_op jit(solution)/shard_map/prepare/pallas_call | solution.py:575
  14.9 0.0 collective-permute-done.raw_xf_ref
  14.9 0.9 %slab_face.1 = (f32[2,4,3,8,16,128]{5,4,3,2,1,0:T(8,128)S(1)}, f32[8,16,128]{2,1,0:T(8,128)S(1)}, f32[2,4,2,8,128]{4,3,2,1,0:T(8,128)S(1)}, f32[16,128]{1,0:T(8,...) custom-call(s32[6]{0:T(128)S(1)} %copy-done.2, ...), custom_call_target="tpu_custom_call", output_to_operand_aliasing={{0}: (3, {}), {1}: (4, {})} | custom-call | tf_op jit(solution)/shard_map/slab_face/pallas_call | solution.py:584
  15.9 1.6 %collective-permute-start.2 = (f32[2,4,2,16,128]{4,3,2,1,0:T(8,128)S(1)}, f32[2,4,2,16,128]{4,3,2,1,0:T(8,128)S(1)}, u32[]{:S(2)}, u32[]{:S(2)}) collective-permute-start(f32[2,4,2,16,128]{4,3,2,1,0:T(8,128)S(1)} %get-tuple-element.49), channel_id=1, source_target_pairs={{0,1},{1,0},{2,3},{3,2},{4,5},{5,4},{6,7},{7,6},{8,9},{9,8},{10,11... | collective-permute-start | bytes 393224 | tf_op jit(solution)/shard_map/ppermute | solution.py:22
  17.4 4.9 %apply_inner.1 = (f32[2,4,3,8,16,128]{5,4,3,2,1,0:T(8,128)S(1)}, f32[2,4,3,8,16,128]{5,4,3,2,1,0:T(8,128)S(1)}, f32[4,8,8,128]{3,2,1,0:T(8,128)S(1)}, f32[2,4,2,...) custom-call(f32[2,4,3,8,16,128]{5,4,3,2,1,0:T(8,128)S(1)} %get-tuple-element.37.basis_ref, ...), custom_call_target="tpu_custom_call", output_to_operand_aliasing={{0}: (4, {})} | custom-call | flops 13107200 | bytes 3145728 | tf_op jit(solution)/shard_map/apply_inner/pallas_call | solution.py:594
  22.4 0.0 collective-permute-done.2.zf_ref
  22.4 0.1 last_plane.1
  22.5 0.1 collective-permute-start.4
  22.6 0.0 copy-start.3
  22.6 1.0 %apply_outer.1 = (f32[2,4,3,8,16,128]{5,4,3,2,1,0:T(8,128)S(1)}, f32[24,128]{1,0:T(8,128)S(1)}) custom-call(s32[6]{0:T(128)S(1)} %copy-done.2, f32[2,4,3,8,16,128]{5,4,3,2,1,0:T(8,128)S(1)} %get-tuple-element.37.basis_ref, f32[2,4,3,8,16,128]{5,4,3,2,1,0:T(8,128)S(1)} %get-tuple-element.38.loss_ref, ...), custom_call_target="tpu_custom_call", output_to_operand_aliasing={{0}: (11, {})} | custom-call | flops 4915200 | bytes 1572864 | tf_op jit(solution)/shard_map/apply_outer/pallas_call | solution.py:615
  23.6 0.5 %collective-permute-start.3 = (f32[24,128]{1,0:T(8,128)S(1)}, f32[24,128]{1,0:T(8,128)S(1)}, u32[]{:S(2)}, u32[]{:S(2)}) collective-permute-start(f32[24,128]{1,0:T(8,128)S(1)} %get-tuple-element.61), channel_id=1, source_target_pairs={{0,2},{2,0},{1,3},{3,1},{4,6},{6,4},{5,7},{7,5},{8,10},{10,8},{9,1... | collective-permute-start | bytes 36872 | tf_op jit(solution)/shard_map/ppermute | solution.py:22
  24.1 3.2 %collective-permute-done.3.hyf_ref = f32[24,128]{1,0:T(8,128)S(1)} collective-permute-done((f32[24,128]{1,0:T(8,128)S(1)}, f32[24,128]{1,0:T(8,128)S(1)}, u32[]{:S(2)}, u32[]{:S(2)}) %collective-permute-start.3) | collective-permute-done | bytes 12320 | tf_op jit(solution)/shard_map/ppermute | solution.py:22
  27.3 0.8 %collective-permute-done.4.hxf_ref = f32[2,4,2,8,128]{4,3,2,1,0:T(8,128)S(1)} collective-permute-done((f32[2,4,2,8,128]{4,3,2,1,0:T(8,128)S(1)}, f32[2,4,2,8,128]{4,3,2,1,0:T(8,128)S(1)}, u32[]{:S(2)}, u32[]{:S(2)}) %collective-permute-start.4) | collective-permute-done | bytes 65568 | tf_op jit(solution)/shard_map/ppermute | solution.py:22
  28.1 0.0 collective-permute-start.5
  28.1 3.6 %collective-permute-done.5 = f32[8,128]{1,0:T(8,128)S(1)} collective-permute-done((f32[8,128]{1,0:T(8,128)S(1)}, f32[8,128]{1,0:T(8,128)S(1)}, u32[]{:S(2)}, u32[]{:S(2)}) %collective-permute-start.5) | collective-permute-done | bytes 4128 | tf_op jit(solution)/shard_map/ppermute | solution.py:545
  31.7 4.5 %collective-permute-done.6 = f32[8,128]{1,0:T(8,128)S(1)} collective-permute-done((f32[8,128]{1,0:T(8,128)S(1)}, f32[8,128]{1,0:T(8,128)S(1)}, u32[]{:S(2)}, u32[]{:S(2)}) %collective-permute-start.6) | collective-permute-done | bytes 4128 | tf_op jit(solution)/shard_map/ppermute | solution.py:545
  36.2 1.2 %collective-permute-done.7 = f32[8,128]{1,0:T(8,128)S(1)} collective-permute-done((f32[8,128]{1,0:T(8,128)S(1)}, f32[8,128]{1,0:T(8,128)S(1)}, u32[]{:S(2)}, u32[]{:S(2)}) %collective-permute-start.7) | collective-permute-done | bytes 4128 | tf_op jit(solution)/shard_map/ppermute | solution.py:545
  37.4 0.5 %collective-permute-start.8 = (f32[8,128]{1,0:T(8,128)S(1)}, f32[8,128]{1,0:T(8,128)S(1)}, u32[]{:S(2)}, u32[]{:S(2)}) collective-permute-start(f32[8,128]{1,0:T(8,128)S(1)} %add.18), channel_id=1, source_target_pairs={{0,1},{1,0},{2,3},{3,2},{4,5},{5,4},{6,7},{7,6},{8,9},{9,8},{10,11... | collective-permute-start | bytes 12296 | tf_op jit(solution)/shard_map/ppermute | solution.py:545
  37.9 2.2 %add_rims.1 = f32[2,4,3,8,16,128]{5,4,3,2,1,0:T(8,128)} custom-call(s32[6]{0:T(128)S(1)} %copy-done.2, f32[2,4]{1,0:T(2,128)S(1)} %copy-done.3, f32[2,4,3,8,16,128]{5,4,3,2,1,0:T(8,128)S(1)} %get-tuple-element.37.basis_ref, f32[2,4,3,8,16,128]{5,4,3,2,1,0:T(8,128)S(1)} %get-tuple-element.65.image_ref, ...), custom_call_target="tpu_custom_call" | custom-call | flops 3276800 | bytes 4718592 | tf_op jit(solution)/shard_map/add_rims/pallas_call | solution.py:638
  40.2 0.8 %collective-permute-done.8 = f32[8,128]{1,0:T(8,128)S(1)} collective-permute-done((f32[8,128]{1,0:T(8,128)S(1)}, f32[8,128]{1,0:T(8,128)S(1)}, u32[]{:S(2)}, u32[]{:S(2)}) %collective-permute-start.8) | collective-permute-done | bytes 4128 | tf_op jit(solution)/shard_map/ppermute | solution.py:545
  41.0 0.6 %add.19 = f32[8,128]{1,0:T(8,128)} add(f32[8,128]{1,0:T(8,128)S(1)} %add.18, f32[8,128]{1,0:T(8,128)S(1)} %collective-permute-done.8) | non-fusion elementwise | flops 1024 | bytes 12288 | tf_op jit(solution)/shard_map/add | solution.py:649
  (18 shorter events, 0.0 us)
Async XLA Ops:
  0.6 7.9 %copy-start.2 = (s32[6]{0:T(128)S(1)}, s32[6]{0:T(128)}, u32[]{:S(2)}) copy-start(s32[6]{0:T(128)} %pml_ref.7) | copy-start | bytes 76
  0.6 7.9 %copy-start.1 = (f32[2,4,4]{2,1,0:T(4,128)S(1)}, f32[2,4,4]{2,1,0:T(4,128)}, u32[]{:S(2)}) copy-start(f32[2,4,4]{2,1,0:T(4,128)} %coeffs_ref.3) | copy-start | bytes 388
  0.7 7.9 %copy-start.5 = (f32[4]{0:T(128)S(1)}, f32[4]{0:T(128)}, u32[]{:S(2)}) copy-start(f32[4]{0:T(128)} %eps_loss_ref.1) | copy-start | bytes 52
  0.7 7.9 %copy-start.4 = (f32[4]{0:T(128)S(1)}, f32[4]{0:T(128)}, u32[]{:S(2)}) copy-start(f32[4]{0:T(128)} %eps_real_ref.1) | copy-start | bytes 52
  0.7 7.9 %copy-start = (s32[8,16,128]{2,1,0:T(8,128)S(1)}, s32[8,16,128]{2,1,0:T(8,128)}, u32[]{:S(2)}) copy-start(s32[8,16,128]{2,1,0:T(8,128)} %material_ref.1) | copy-start | bytes 196612
  2.5 12.4 %collective-permute-start = (f32[2,4,2,8,128]{4,3,2,1,0:T(8,128)S(1)}, f32[2,4,2,8,128]{4,3,2,1,0:T(8,128)S(1)}, u32[]{:S(2)}, u32[]{:S(2)}) collective-permute-start(f32[2,4,2,8,128]{4,3,2,1,0:T(8,128)S(1)} %get-tuple-element.43), channel_id=1, source_target_pairs={{0,28},{4,0},{8,4},{12,8},{16,12},{20,16},{24,20},{28,24},{1,29},{... | collective-permute-start | bytes 196616 | tf_op jit(solution)/shard_map/ppermute | solution.py:22
  7.0 7.9 %collective-permute-start.1 = (f32[16,128]{1,0:T(8,128)S(1)}, f32[16,128]{1,0:T(8,128)S(1)}, u32[]{:S(2)}, u32[]{:S(2)}) collective-permute-start(f32[16,128]{1,0:T(8,128)S(1)} %get-tuple-element.44), channel_id=1, source_target_pairs={{0,2},{2,0},{1,3},{3,1},{4,6},{6,4},{5,7},{7,5},{8,10},{10,8},{9,1... | collective-permute-start | bytes 24584 | tf_op jit(solution)/shard_map/ppermute | solution.py:22
  15.9 6.5 %collective-permute-start.2 = (f32[2,4,2,16,128]{4,3,2,1,0:T(8,128)S(1)}, f32[2,4,2,16,128]{4,3,2,1,0:T(8,128)S(1)}, u32[]{:S(2)}, u32[]{:S(2)}) collective-permute-start(f32[2,4,2,16,128]{4,3,2,1,0:T(8,128)S(1)} %get-tuple-element.49), channel_id=1, source_target_pairs={{0,1},{1,0},{2,3},{3,2},{4,5},{5,4},{6,7},{7,6},{8,9},{9,8},{10,11... | collective-permute-start | bytes 393224 | tf_op jit(solution)/shard_map/ppermute | solution.py:22
  22.5 5.6 %collective-permute-start.4 = (f32[2,4,2,8,128]{4,3,2,1,0:T(8,128)S(1)}, f32[2,4,2,8,128]{4,3,2,1,0:T(8,128)S(1)}, u32[]{:S(2)}, u32[]{:S(2)}) collective-permute-start(f32[2,4,2,8,128]{4,3,2,1,0:T(8,128)S(1)} %get-tuple-element.56.hxf_ref), channel_id=1, source_target_pairs={{0,4},{4,8},{8,12},{12,16},{16,20},{20,24},{24,28},{28,0},{1,5},{5... | collective-permute-start | bytes 196616 | tf_op jit(solution)/shard_map/ppermute | solution.py:22
  22.6 15.4 %copy-start.3 = (f32[2,4]{1,0:T(2,128)S(1)}, f32[2,4]{1,0:T(2,128)}, u32[]{:S(2)}) copy-start(f32[2,4]{1,0:T(2,128)} %ritz_ref.1) | copy-start | bytes 100
  23.6 3.7 %collective-permute-start.3 = (f32[24,128]{1,0:T(8,128)S(1)}, f32[24,128]{1,0:T(8,128)S(1)}, u32[]{:S(2)}, u32[]{:S(2)}) collective-permute-start(f32[24,128]{1,0:T(8,128)S(1)} %get-tuple-element.61), channel_id=1, source_target_pairs={{0,2},{2,0},{1,3},{3,1},{4,6},{6,4},{5,7},{7,5},{8,10},{10,8},{9,1... | collective-permute-start | bytes 36872 | tf_op jit(solution)/shard_map/ppermute | solution.py:22
  28.1 3.6 %collective-permute-start.5 = (f32[8,128]{1,0:T(8,128)S(1)}, f32[8,128]{1,0:T(8,128)S(1)}, u32[]{:S(2)}, u32[]{:S(2)}) collective-permute-start(f32[8,128]{1,0:T(8,128)S(1)} %slice_add_fusion), channel_id=1, source_target_pairs={{0,8},{1,9},{2,10},{3,11},{4,12},{5,13},{6,14},{7,15},{8,0},{9,1},... | collective-permute-start | bytes 12296 | tf_op jit(solution)/shard_map/ppermute | solution.py:545
  31.7 4.5 %collective-permute-start.6 = (f32[8,128]{1,0:T(8,128)S(1)}, f32[8,128]{1,0:T(8,128)S(1)}, u32[]{:S(2)}, u32[]{:S(2)}) collective-permute-start(f32[8,128]{1,0:T(8,128)S(1)} %add.16), channel_id=1, source_target_pairs={{0,16},{1,17},{2,18},{3,19},{4,20},{5,21},{6,22},{7,23},{8,24},{9,... | collective-permute-start | bytes 12296 | tf_op jit(solution)/shard_map/ppermute | solution.py:545
  36.2 1.2 %collective-permute-start.7 = (f32[8,128]{1,0:T(8,128)S(1)}, f32[8,128]{1,0:T(8,128)S(1)}, u32[]{:S(2)}, u32[]{:S(2)}) collective-permute-start(f32[8,128]{1,0:T(8,128)S(1)} %add.17), channel_id=1, source_target_pairs={{0,4},{1,5},{2,6},{3,7},{4,0},{5,1},{6,2},{7,3},{8,12},{9,13},{10,... | collective-permute-start | bytes 12296 | tf_op jit(solution)/shard_map/ppermute | solution.py:545
  37.4 3.6 %collective-permute-start.8 = (f32[8,128]{1,0:T(8,128)S(1)}, f32[8,128]{1,0:T(8,128)S(1)}, u32[]{:S(2)}, u32[]{:S(2)}) collective-permute-start(f32[8,128]{1,0:T(8,128)S(1)} %add.18), channel_id=1, source_target_pairs={{0,1},{1,0},{2,3},{3,2},{4,5},{5,4},{6,7},{7,6},{8,9},{9,8},{10,11... | collective-permute-start | bytes 12296 | tf_op jit(solution)/shard_map/ppermute | solution.py:545

commit v7 on v6

--- a/solution.py
+++ b/solution.py
@@ -199,12 +199,12 @@
                     packed = jnp.where(lanes == row, pltpu.roll(value[part], (row + 1) % ny, 1), packed)
             packed_ref[z, cut] = packed
 
+    @pl.loop(0, nz - 1)
+    def _(z):
+        for b in range(vectors):
+            magnetic(b, z, False)
+
     for b in range(vectors):
-
-        @pl.loop(0, nz - 1)
-        def _(z, b=b):
-            magnetic(b, z, False)
-
         magnetic(b, nz - 1, True)
 
 
@@ -376,22 +376,27 @@
     _, vectors, _, nz, nx, ny = basis_ref.shape
     keep = pltpu.make_async_copy(basis_ref, basis_hbm, sem)
     keep.start()
-    count = nx // SUB
-    for b in range(vectors):
-
-        def step(z, carry, b=b):
-            return plane_step(
-                b, z, *carry, basis_ref, loss_ref, table_ref, sz_ref, h_ref, image_ref, (xadd_ref, yadd_ref)
+    cuts = tiles_of(nx)
+    acc_ref[...] = jnp.zeros(acc_ref.shape, jnp.float32)
+    before_ref[...] = jnp.zeros(before_ref.shape, jnp.float32)
+
+    @pl.loop(0, nz - 1)
+    def _(z):
+        for b in range(vectors):
+            before = [
+                tuple(tuple(before_ref[part, b, slot, cut] for part in range(2)) for slot in range(2)) for cut in cuts
+            ]
+            sums = [(acc_ref[b, a], acc_ref[b, vectors + a]) for a in range(vectors)]
+            before, sums = plane_step(
+                b, z, before, sums, basis_ref, loss_ref, table_ref, sz_ref, h_ref, image_ref, (xadd_ref, yadd_ref)
             )
-
-        none = (jnp.zeros((SUB, ny), jnp.float32),) * 2
-        before, sums = lax.fori_loop(0, nz - 1, step, ([(none, none)] * count, [none] * vectors))
-        for part in range(2):
-            for a in range(vectors):
-                acc_ref[b, part * vectors + a] = sums[a][part]
-            for t, cut in enumerate(tiles_of(nx)):
-                for slot in range(2):
-                    before_ref[part, b, slot, cut] = before[t][slot][part]
+            for part in range(2):
+                for a in range(vectors):
+                    acc_ref[b, part * vectors + a] = sums[a][part]
+                for t, cut in enumerate(cuts):
+                    for slot in range(2):
+                        before_ref[part, b, slot, cut] = before[t][slot][part]
+
     keep.wait()
 
 

time: 41.7 us -> 37.2 us (0.89)
  Pallas kernels: 17.4 us -> 11.5 us
  starting transfers between devices: 8.72 us -> 9.68 us
    pallas_call x1, Pallas kernels: 6.32 us -> 3.17 us  [body(): pl.pallas_call(prepare_kernel, out_shape=(whole, whole, whole, planes, f3...]
    pallas_call x1, Pallas kernels: 4.93 us -> 2.25 us  [body(): pl.pallas_call(inner_kernel, out_shape=(whole, whole, f32(vectors, 2 * ve...]
    ppermute x5, waiting for transfers between devices: 3.98 us -> 5.15 us  [passed_round(): lax.ppermute(value, axis, [(source, (source + steps) % count) for source...]
    ppermute x4, starting transfers between devices: 0.54 us -> 1.5 us  [from_partner(): lax.ppermute(value, axes, [(source, source ^ mask) for source in range(co...]
    ppermute x4, waiting for transfers between devices: 10.1 us -> 9.27 us  [from_partner(): lax.ppermute(value, axes, [(source, source ^ mask) for source in range(co...]
  transfers between devices with their start and end apart: 9 -> 9, of which waited for: 6 -> 6; matrix products, arithmetic and copies ran while one was open for 0% -> 0% of each run, Pallas kernels for 35% -> 23%
where the time goes in v7:
time: 37.2 us; the launch traced here: 37 us
  waiting for transfers between devices  14.4 us (39%)
  Pallas kernels  11.5 us (31%)
  starting transfers between devices  9.68 us (26%)
  between operations  0.78 us (2%)
  other arithmetic  0.61 us (2%)
    ppermute x4, waiting for transfers between devices, from_partner(): lax.ppermute(value, axes, [(source, source ^ mask) for source in range(co...  9.27 us
    ppermute x5, starting transfers between devices, passed_round(): lax.ppermute(value, axis, [(source, (source + steps) % count) for source...  8.18 us
    ppermute x5, waiting for transfers between devices, passed_round(): lax.ppermute(value, axis, [(source, (source + steps) % count) for source...  5.15 us
    pallas_call x1, Pallas kernels, body(): pl.pallas_call(prepare_kernel, out_shape=(whole, whole, whole, planes, f3...  3.17 us
    pallas_call x1, Pallas kernels, body(): pl.pallas_call(inner_kernel, out_shape=(whole, whole, f32(vectors, 2 * ve...  2.25 us
    pallas_call x1, Pallas kernels, body(): pl.pallas_call(rim_kernel, out_shape=whole, in_specs=[SMEM] * 2 + [VMEM]...  2.23 us
    pallas_call x1, Pallas kernels, body(): pl.pallas_call(face_kernel, out_shape=(whole, f32(*xf_shape), f32(*yf_sha...  1.81 us
    ppermute x4, starting transfers between devices, from_partner(): lax.ppermute(value, axes, [(source, source ^ mask) for source in range(co...  1.5 us
  transfers between devices with their start and end apart: 9, of which 6 were waited for; matrix products, arithmetic and copies ran while one was open for 0% of the time, Pallas kernels for 23%

profile of v7, /device:TPU:0, one launch (start us, length us, event | category | flops | bytes accessed | tf_op | source)
XLA Modules:
  0.0 37.0 jit_solution(8716909443379130861)
XLA Ops:
  0.7 1.8 %take_faces.1 = (f32[2,4,3,8,16,128]{5,4,3,2,1,0:T(8,128)S(1)}, f32[2,4,2,8,128]{4,3,2,1,0:T(8,128)S(1)}, f32[16,128]{1,0:T(8,128)S(1)}) custom-call(f32[2,4,3,8,16,128]{5,4,3,2,1,0:T(8,128)} %fields_hbm.1), custom_call_target="tpu_custom_call" | custom-call | tf_op jit(solution)/shard_map/take_faces/pallas_call | solution.py:562
  2.5 4.5 %collective-permute-start = (f32[2,4,2,8,128]{4,3,2,1,0:T(8,128)S(1)}, f32[2,4,2,8,128]{4,3,2,1,0:T(8,128)S(1)}, u32[]{:S(2)}, u32[]{:S(2)}) collective-permute-start(f32[2,4,2,8,128]{4,3,2,1,0:T(8,128)S(1)} %get-tuple-element.43), channel_id=1, source_target_pairs={{0,28},{4,0},{8,4},{12,8},{16,12},{20,16},{24,20},{28,24},{1,29},{... | collective-permute-start | bytes 196616 | tf_op jit(solution)/shard_map/ppermute | solution.py:22
  7.0 1.5 %collective-permute-start.1 = (f32[16,128]{1,0:T(8,128)S(1)}, f32[16,128]{1,0:T(8,128)S(1)}, u32[]{:S(2)}, u32[]{:S(2)}) collective-permute-start(f32[16,128]{1,0:T(8,128)S(1)} %get-tuple-element.44), channel_id=1, source_target_pairs={{0,2},{2,0},{1,3},{3,1},{4,6},{6,4},{5,7},{7,5},{8,10},{10,8},{9,1... | collective-permute-start | bytes 24584 | tf_op jit(solution)/shard_map/ppermute | solution.py:22
  8.6 3.2 %prepare.1 = (f32[2,4,3,8,16,128]{5,4,3,2,1,0:T(8,128)S(1)}, f32[2,4,3,8,16,128]{5,4,3,2,1,0:T(8,128)S(1)}, f32[2,4,3,8,16,128]{5,4,3,2,1,0:T(8,128)S(1)}, f32[8...) custom-call(s32[6]{0:T(128)S(1)} %copy-done.2, f32[4]{0:T(128)S(1)} %copy-done.4, ...), custom_call_target="tpu_custom_call" | custom-call | flops 13107200 | bytes 6291456 | tf_op jit(solution)/shard_map/prepare/pallas_call | solution.py:580
  11.8 0.0 collective-permute-done.1.raw_yf_ref
  11.8 0.0 collective-permute-done.raw_xf_ref
  11.8 0.9 %slab_face.1 = (f32[2,4,3,8,16,128]{5,4,3,2,1,0:T(8,128)S(1)}, f32[8,16,128]{2,1,0:T(8,128)S(1)}, f32[2,4,2,8,128]{4,3,2,1,0:T(8,128)S(1)}, f32[16,128]{1,0:T(8,...) custom-call(s32[6]{0:T(128)S(1)} %copy-done.2, ...), custom_call_target="tpu_custom_call", output_to_operand_aliasing={{0}: (3, {}), {1}: (4, {})} | custom-call | tf_op jit(solution)/shard_map/slab_face/pallas_call | solution.py:589
  12.7 1.6 %collective-permute-start.2 = (f32[2,4,2,16,128]{4,3,2,1,0:T(8,128)S(1)}, f32[2,4,2,16,128]{4,3,2,1,0:T(8,128)S(1)}, u32[]{:S(2)}, u32[]{:S(2)}) collective-permute-start(f32[2,4,2,16,128]{4,3,2,1,0:T(8,128)S(1)} %get-tuple-element.49), channel_id=1, source_target_pairs={{0,1},{1,0},{2,3},{3,2},{4,5},{5,4},{6,7},{7,6},{8,9},{9,8},{10,11... | collective-permute-start | bytes 393224 | tf_op jit(solution)/shard_map/ppermute | solution.py:22
  14.3 2.3 %apply_inner.1 = (f32[2,4,3,8,16,128]{5,4,3,2,1,0:T(8,128)S(1)}, f32[2,4,3,8,16,128]{5,4,3,2,1,0:T(8,128)S(1)}, f32[4,8,8,128]{3,2,1,0:T(8,128)S(1)}, f32[2,4,2,...) custom-call(f32[2,4,3,8,16,128]{5,4,3,2,1,0:T(8,128)S(1)} %get-tuple-element.37.basis_ref, ...), custom_call_target="tpu_custom_call", output_to_operand_aliasing={{0}: (4, {})} | custom-call | flops 13107200 | bytes 3145728 | tf_op jit(solution)/shard_map/apply_inner/pallas_call | solution.py:599
  16.5 1.2 %collective-permute-done.2.zf_ref = f32[2,4,2,16,128]{4,3,2,1,0:T(8,128)S(1)} collective-permute-done((f32[2,4,2,16,128]{4,3,2,1,0:T(8,128)S(1)}, f32[2,4,2,16,128]{4,3,2,1,0:T(8,128)S(1)}, u32[]{:S(2)}, u32[]{:S(2)}) %collective-permute-start.2) | collective-permute-done | bytes 131104 | tf_op jit(solution)/shard_map/ppermute | solution.py:22
  17.8 0.1 last_plane.1
  17.9 0.1 collective-permute-start.4
  17.9 0.0 copy-start.3
  17.9 1.0 %apply_outer.1 = (f32[2,4,3,8,16,128]{5,4,3,2,1,0:T(8,128)S(1)}, f32[24,128]{1,0:T(8,128)S(1)}) custom-call(s32[6]{0:T(128)S(1)} %copy-done.2, f32[2,4,3,8,16,128]{5,4,3,2,1,0:T(8,128)S(1)} %get-tuple-element.37.basis_ref, f32[2,4,3,8,16,128]{5,4,3,2,1,0:T(8,128)S(1)} %get-tuple-element.38.loss_ref, ...), custom_call_target="tpu_custom_call", output_to_operand_aliasing={{0}: (11, {})} | custom-call | flops 4915200 | bytes 1572864 | tf_op jit(solution)/shard_map/apply_outer/pallas_call | solution.py:620
  19.0 0.5 %collective-permute-start.3 = (f32[24,128]{1,0:T(8,128)S(1)}, f32[24,128]{1,0:T(8,128)S(1)}, u32[]{:S(2)}, u32[]{:S(2)}) collective-permute-start(f32[24,128]{1,0:T(8,128)S(1)} %get-tuple-element.61), channel_id=1, source_target_pairs={{0,2},{2,0},{1,3},{3,1},{4,6},{6,4},{5,7},{7,5},{8,10},{10,8},{9,1... | collective-permute-start | bytes 36872 | tf_op jit(solution)/shard_map/ppermute | solution.py:22
  19.5 3.2 %collective-permute-done.3.hyf_ref = f32[24,128]{1,0:T(8,128)S(1)} collective-permute-done((f32[24,128]{1,0:T(8,128)S(1)}, f32[24,128]{1,0:T(8,128)S(1)}, u32[]{:S(2)}, u32[]{:S(2)}) %collective-permute-start.3) | collective-permute-done | bytes 12320 | tf_op jit(solution)/shard_map/ppermute | solution.py:22
  22.7 0.7 %collective-permute-done.4.hxf_ref = f32[2,4,2,8,128]{4,3,2,1,0:T(8,128)S(1)} collective-permute-done((f32[2,4,2,8,128]{4,3,2,1,0:T(8,128)S(1)}, f32[2,4,2,8,128]{4,3,2,1,0:T(8,128)S(1)}, u32[]{:S(2)}, u32[]{:S(2)}) %collective-permute-start.4) | collective-permute-done | bytes 65568 | tf_op jit(solution)/shard_map/ppermute | solution.py:22
  23.4 0.0 collective-permute-start.5
  23.4 3.6 %collective-permute-done.5 = f32[8,128]{1,0:T(8,128)S(1)} collective-permute-done((f32[8,128]{1,0:T(8,128)S(1)}, f32[8,128]{1,0:T(8,128)S(1)}, u32[]{:S(2)}, u32[]{:S(2)}) %collective-permute-start.5) | collective-permute-done | bytes 4128 | tf_op jit(solution)/shard_map/ppermute | solution.py:550
  27.0 4.5 %collective-permute-done.6 = f32[8,128]{1,0:T(8,128)S(1)} collective-permute-done((f32[8,128]{1,0:T(8,128)S(1)}, f32[8,128]{1,0:T(8,128)S(1)}, u32[]{:S(2)}, u32[]{:S(2)}) %collective-permute-start.6) | collective-permute-done | bytes 4128 | tf_op jit(solution)/shard_map/ppermute | solution.py:550
  31.5 1.2 %collective-permute-done.7 = f32[8,128]{1,0:T(8,128)S(1)} collective-permute-done((f32[8,128]{1,0:T(8,128)S(1)}, f32[8,128]{1,0:T(8,128)S(1)}, u32[]{:S(2)}, u32[]{:S(2)}) %collective-permute-start.7) | collective-permute-done | bytes 4128 | tf_op jit(solution)/shard_map/ppermute | solution.py:550
  32.7 1.5 %collective-permute-start.8 = (f32[8,128]{1,0:T(8,128)S(1)}, f32[8,128]{1,0:T(8,128)S(1)}, u32[]{:S(2)}, u32[]{:S(2)}) collective-permute-start(f32[8,128]{1,0:T(8,128)S(1)} %add.18), channel_id=1, source_target_pairs={{0,1},{1,0},{2,3},{3,2},{4,5},{5,4},{6,7},{7,6},{8,9},{9,8},{10,11... | collective-permute-start | bytes 12296 | tf_op jit(solution)/shard_map/ppermute | solution.py:550
  34.2 2.2 %add_rims.1 = f32[2,4,3,8,16,128]{5,4,3,2,1,0:T(8,128)} custom-call(s32[6]{0:T(128)S(1)} %copy-done.2, f32[2,4]{1,0:T(2,128)S(1)} %copy-done.3, f32[2,4,3,8,16,128]{5,4,3,2,1,0:T(8,128)S(1)} %get-tuple-element.37.basis_ref, f32[2,4,3,8,16,128]{5,4,3,2,1,0:T(8,128)S(1)} %get-tuple-element.65.image_ref, ...), custom_call_target="tpu_custom_call" | custom-call | flops 3276800 | bytes 4718592 | tf_op jit(solution)/shard_map/add_rims/pallas_call | solution.py:643
  36.4 0.6 %add.19 = f32[8,128]{1,0:T(8,128)} add(f32[8,128]{1,0:T(8,128)S(1)} %add.18, f32[8,128]{1,0:T(8,128)S(1)} %collective-permute-done.8) | non-fusion elementwise | flops 1024 | bytes 12288 | tf_op jit(solution)/shard_map/add | solution.py:654
  (18 shorter events, 0.0 us)
Async XLA Ops:
  0.6 7.9 %copy-start.2 = (s32[6]{0:T(128)S(1)}, s32[6]{0:T(128)}, u32[]{:S(2)}) copy-start(s32[6]{0:T(128)} %pml_ref.7) | copy-start | bytes 76
  0.6 7.9 %copy-start.1 = (f32[2,4,4]{2,1,0:T(4,128)S(1)}, f32[2,4,4]{2,1,0:T(4,128)}, u32[]{:S(2)}) copy-start(f32[2,4,4]{2,1,0:T(4,128)} %coeffs_ref.3) | copy-start | bytes 388
  0.7 7.9 %copy-start.5 = (f32[4]{0:T(128)S(1)}, f32[4]{0:T(128)}, u32[]{:S(2)}) copy-start(f32[4]{0:T(128)} %eps_loss_ref.1) | copy-start | bytes 52
  0.7 7.9 %copy-start.4 = (f32[4]{0:T(128)S(1)}, f32[4]{0:T(128)}, u32[]{:S(2)}) copy-start(f32[4]{0:T(128)} %eps_real_ref.1) | copy-start | bytes 52
  0.7 7.9 %copy-start = (s32[8,16,128]{2,1,0:T(8,128)S(1)}, s32[8,16,128]{2,1,0:T(8,128)}, u32[]{:S(2)}) copy-start(s32[8,16,128]{2,1,0:T(8,128)} %material_ref.1) | copy-start | bytes 196612
  2.5 9.3 %collective-permute-start = (f32[2,4,2,8,128]{4,3,2,1,0:T(8,128)S(1)}, f32[2,4,2,8,128]{4,3,2,1,0:T(8,128)S(1)}, u32[]{:S(2)}, u32[]{:S(2)}) collective-permute-start(f32[2,4,2,8,128]{4,3,2,1,0:T(8,128)S(1)} %get-tuple-element.43), channel_id=1, source_target_pairs={{0,28},{4,0},{8,4},{12,8},{16,12},{20,16},{24,20},{28,24},{1,29},{... | collective-permute-start | bytes 196616 | tf_op jit(solution)/shard_map/ppermute | solution.py:22
  7.0 4.7 %collective-permute-start.1 = (f32[16,128]{1,0:T(8,128)S(1)}, f32[16,128]{1,0:T(8,128)S(1)}, u32[]{:S(2)}, u32[]{:S(2)}) collective-permute-start(f32[16,128]{1,0:T(8,128)S(1)} %get-tuple-element.44), channel_id=1, source_target_pairs={{0,2},{2,0},{1,3},{3,1},{4,6},{6,4},{5,7},{7,5},{8,10},{10,8},{9,1... | collective-permute-start | bytes 24584 | tf_op jit(solution)/shard_map/ppermute | solution.py:22
  12.7 5.0 %collective-permute-start.2 = (f32[2,4,2,16,128]{4,3,2,1,0:T(8,128)S(1)}, f32[2,4,2,16,128]{4,3,2,1,0:T(8,128)S(1)}, u32[]{:S(2)}, u32[]{:S(2)}) collective-permute-start(f32[2,4,2,16,128]{4,3,2,1,0:T(8,128)S(1)} %get-tuple-element.49), channel_id=1, source_target_pairs={{0,1},{1,0},{2,3},{3,2},{4,5},{5,4},{6,7},{7,6},{8,9},{9,8},{10,11... | collective-permute-start | bytes 393224 | tf_op jit(solution)/shard_map/ppermute | solution.py:22
  17.9 5.5 %collective-permute-start.4 = (f32[2,4,2,8,128]{4,3,2,1,0:T(8,128)S(1)}, f32[2,4,2,8,128]{4,3,2,1,0:T(8,128)S(1)}, u32[]{:S(2)}, u32[]{:S(2)}) collective-permute-start(f32[2,4,2,8,128]{4,3,2,1,0:T(8,128)S(1)} %get-tuple-element.56.hxf_ref), channel_id=1, source_target_pairs={{0,4},{4,8},{8,12},{12,16},{16,20},{20,24},{24,28},{28,0},{1,5},{5... | collective-permute-start | bytes 196616 | tf_op jit(solution)/shard_map/ppermute | solution.py:22
  17.9 16.3 %copy-start.3 = (f32[2,4]{1,0:T(2,128)S(1)}, f32[2,4]{1,0:T(2,128)}, u32[]{:S(2)}) copy-start(f32[2,4]{1,0:T(2,128)} %ritz_ref.1) | copy-start | bytes 100
  19.0 3.7 %collective-permute-start.3 = (f32[24,128]{1,0:T(8,128)S(1)}, f32[24,128]{1,0:T(8,128)S(1)}, u32[]{:S(2)}, u32[]{:S(2)}) collective-permute-start(f32[24,128]{1,0:T(8,128)S(1)} %get-tuple-element.61), channel_id=1, source_target_pairs={{0,2},{2,0},{1,3},{3,1},{4,6},{6,4},{5,7},{7,5},{8,10},{10,8},{9,1... | collective-permute-start | bytes 36872 | tf_op jit(solution)/shard_map/ppermute | solution.py:22
  23.4 3.6 %collective-permute-start.5 = (f32[8,128]{1,0:T(8,128)S(1)}, f32[8,128]{1,0:T(8,128)S(1)}, u32[]{:S(2)}, u32[]{:S(2)}) collective-permute-start(f32[8,128]{1,0:T(8,128)S(1)} %slice_add_fusion), channel_id=1, source_target_pairs={{0,8},{1,9},{2,10},{3,11},{4,12},{5,13},{6,14},{7,15},{8,0},{9,1},... | collective-permute-start | bytes 12296 | tf_op jit(solution)/shard_map/ppermute | solution.py:550
  27.0 4.5 %collective-permute-start.6 = (f32[8,128]{1,0:T(8,128)S(1)}, f32[8,128]{1,0:T(8,128)S(1)}, u32[]{:S(2)}, u32[]{:S(2)}) collective-permute-start(f32[8,128]{1,0:T(8,128)S(1)} %add.16), channel_id=1, source_target_pairs={{0,16},{1,17},{2,18},{3,19},{4,20},{5,21},{6,22},{7,23},{8,24},{9,... | collective-permute-start | bytes 12296 | tf_op jit(solution)/shard_map/ppermute | solution.py:550
  31.5 1.2 %collective-permute-start.7 = (f32[8,128]{1,0:T(8,128)S(1)}, f32[8,128]{1,0:T(8,128)S(1)}, u32[]{:S(2)}, u32[]{:S(2)}) collective-permute-start(f32[8,128]{1,0:T(8,128)S(1)} %add.17), channel_id=1, source_target_pairs={{0,4},{1,5},{2,6},{3,7},{4,0},{5,1},{6,2},{7,3},{8,12},{9,13},{10,... | collective-permute-start | bytes 12296 | tf_op jit(solution)/shard_map/ppermute | solution.py:550
  32.7 3.7 %collective-permute-start.8 = (f32[8,128]{1,0:T(8,128)S(1)}, f32[8,128]{1,0:T(8,128)S(1)}, u32[]{:S(2)}, u32[]{:S(2)}) collective-permute-start(f32[8,128]{1,0:T(8,128)S(1)} %add.18), channel_id=1, source_target_pairs={{0,1},{1,0},{2,3},{3,2},{4,5},{5,4},{6,7},{7,6},{8,9},{9,8},{10,11... | collective-permute-start | bytes 12296 | tf_op jit(solution)/shard_map/ppermute | solution.py:550

commit v8 on v7

--- a/solution.py
+++ b/solution.py
@@ -400,14 +400,14 @@
     keep.wait()
 
 
-def last_plane_kernel(sz_ref, zf_ref, h_in, packed_in, hxf_in, h_ref, packed_ref, hxf_ref):
-    del h_in, packed_in, hxf_in
+def last_plane_kernel(sz_ref, zf_ref, h_in, packed_in, hxf_in, h_ref, hxf_ref, hyf_ref):
+    del h_in, hxf_in
     _, vectors, _, nz, nx, ny = h_ref.shape
     parts = range(2)
     last = nz - 1
     lanes = lax.broadcasted_iota(jnp.int32, (SUB, ny), 1)
     shz = tuple(sz_ref[2 + part, last:] * has_neighbour(0, 1) for part in parts)
-    packed = [packed_ref[last, cut] for cut in tiles_of(nx)]
+    packed = [packed_in[last, cut] for cut in tiles_of(nx)]
     for b in range(vectors):
         for t, cut in enumerate(tiles_of(nx)):
             ex, ey = (tuple(zf_ref[part, b, slot, cut] for part in parts) for slot in range(2))
@@ -420,13 +420,13 @@
                 packed[t] = packed[t] + jnp.where(lanes == row, edge, 0.0)
                 if cut.stop == nx:
                     hxf_ref[part, b, 0, last:] = hxf_ref[part, b, 0, last:] + more[1][part][SUB - 1:]
-    for t, cut in enumerate(tiles_of(nx)):
-        packed_ref[last, cut] = packed[t]
+    inner = packed_in[:last].reshape(last * nx, ny)
+    hyf_ref[...] = jnp.concatenate([inner] + packed, axis=0).T[:hyf_ref.shape[0]]
 
 
 def outer_kernel(
-    pml_ref, basis_ref, loss_ref, table_ref, sz_ref, h_ref, zf_ref, xf_ref, yt_ref, hxf_ref, packed_ref,
-    image_in, acc_ref, before_ref, image_ref, hyf_ref,
+    pml_ref, basis_ref, loss_ref, table_ref, sz_ref, h_ref, zf_ref, xf_ref, yt_ref, hxf_ref, hyf_ref,
+    image_in, acc_ref, before_ref, image_ref, gram_ref,
 ):
     del image_in
     _, vectors, _, nz, nx, ny = basis_ref.shape
@@ -437,7 +437,6 @@
     sx_next = axis_stretch(pml_ref, 1, nx, one_place(1, nx, nx, (1, ny)))
     sy_next = axis_stretch(pml_ref, 2, ny, one_place(2, ny, ny, (1, nz * nx)))
     both = 2 * vectors
-    hyf_ref[:2 * both] = packed_ref[...].reshape(nz * nx, ny).T[:2 * both]
     ends = [
         cmul(sy_next, (yt_ref[slot * both:slot * both + vectors], yt_ref[slot * both + vectors:(slot + 1) * both]))
         for slot in range(2)
@@ -487,7 +486,24 @@
     everywhere = 3.0 * nz * nx * ny
     for axis in AXES:
         everywhere = everywhere * lax.axis_size(axis)
-    hyf_ref[2 * both:] = gram * (1.0 / everywhere)
+    gram = gram * (1.0 / everywhere)
+    flat = gram[0:1]
+    for row in range(1, both):
+        flat = flat + pltpu.roll(gram[row:row + 1], row * vectors, 1)
+    for device in range(gram_ref.shape[0]):
+        gram_ref[device] = flat
+
+
+def gather_kernel(rows_ref, gram_ref):
+    vectors = gram_ref.shape[1]
+    total = rows_ref[0]
+    for device in range(1, rows_ref.shape[0]):
+        total = total + rows_ref[device]
+    for part in range(2):
+        for a in range(vectors):
+            row = (part * vectors + a) * vectors
+            turned = pltpu.roll(total, (total.shape[1] - row) % total.shape[1], 1)
+            gram_ref[part, a:a + 1] = turned[:, :vectors]
 
 
 def rim_kernel(
@@ -502,9 +518,8 @@
     none = jnp.zeros(plane, jnp.float32)
     sex = tuple(jnp.where(rows == 0, part * has_neighbour(1, -1), none) for part in sex)
     sey = tuple(jnp.where(lanes == 0, part * has_neighbour(2, -1), none) for part in sey)
-    used = 4 * vectors
-    rest = jnp.zeros((ny - used, nz * nx), jnp.float32)
-    packed_ref[...] = jnp.concatenate([hyf_ref[:used], rest], axis=0).T.reshape(nz, nx, ny)
+    rest = jnp.zeros((ny - hyf_ref.shape[0], nz * nx), jnp.float32)
+    packed_ref[...] = jnp.concatenate([hyf_ref[...], rest], axis=0).T.reshape(nz, nx, ny)
 
     def kept(z):
         return pltpu.make_async_copy(residual_ref.at[:, :, :, z], residual_hbm.at[:, :, :, z], sems.at[z])
@@ -540,14 +555,6 @@
     @pl.loop(0, nz)
     def _(z):
         kept(z).wait()
-
-
-def from_partner(value, mask):
-    axes = ("gx", "gy", "gz")
-    count = 1
-    for axis in axes:
-        count *= lax.axis_size(axis)
-    return lax.ppermute(value, axes, [(source, source ^ mask) for source in range(count)])
 
 
 def body(fields, material, pml_width, eps_real, eps_loss, coeffs, ritz):
@@ -607,39 +614,29 @@
         cost_estimate=cost(800, 2),
         name="apply_inner",
     )(basis, loss, table, sz, h, xadd, yadd)
-    h, packed, hxf = pl.pallas_call(
+    h, hxf, hyf = pl.pallas_call(
         last_plane_kernel,
-        out_shape=(whole, planes, face),
+        out_shape=(whole, face, f32(*yf_shape)),
         in_specs=[VMEM] * 5,
         out_specs=(VMEM,) * 3,
-        input_output_aliases={2: 0, 3: 1, 4: 2},
+        input_output_aliases={2: 0, 4: 1},
         compiler_params=params,
         name="last_plane",
     )(sz, zf, h, packed, hxf)
     from_x = passed_round(hxf, "gx", 1)
-    image, hyf = pl.pallas_call(
+    from_y = passed_round(hyf, "gy", 1)
+    devices = lax.axis_size("gx") * lax.axis_size("gy") * lax.axis_size("gz")
+    image, gram = pl.pallas_call(
         outer_kernel,
-        out_shape=(whole, f32(6 * vectors, nz * nx)),
+        out_shape=(whole, f32(devices, 1, ny)),
         in_specs=[SMEM] + [VMEM] * 13,
         out_specs=(VMEM,) * 2,
         input_output_aliases={11: 0},
         compiler_params=params,
         cost_estimate=cost(300, 1),
         name="apply_outer",
-    )(pml_width, basis, loss, table, sz, h, zf, xf, yt, hxf, packed, image, acc, before)
-    across = lax.axis_size("gy") * lax.axis_size("gz")
-    masks = [1 << bit for bit in range((across * lax.axis_size("gx") - 1).bit_length())]
-    order = [mask for mask in masks if mask > across] + [across] + [mask for mask in reversed(masks) if mask < across]
-    gram = hyf[4 * vectors:]
-    hyf = passed_round(hyf, "gy", 1)
-    hyf, from_x = lax.optimization_barrier((hyf, from_x))
-    if lax.axis_size("gy") == 2:
-        gram = gram + hyf[4 * vectors:]
-        order.remove(lax.axis_size("gz"))
-    for mask in order[:-1]:
-        gram = gram + from_partner(gram, mask)
-    gram, image = lax.optimization_barrier((gram, image))
-    other = from_partner(gram, order[-1])
+    )(pml_width, basis, loss, table, sz, h, zf, xf, yt, hxf, hyf, image, acc, before)
+    rows = lax.all_to_all(gram, ("gx", "gy", "gz"), 0, 0)
     residual = pl.pallas_call(
         rim_kernel,
         out_shape=whole,
@@ -649,9 +646,16 @@
         compiler_params=params,
         cost_estimate=cost(200, 3),
         name="add_rims",
-    )(pml_width, ritz, basis, image, from_x, hyf)
-    other, residual = lax.optimization_barrier((other, residual))
-    gram = (gram + other)[:, :vectors].reshape(2, vectors, vectors)
+    )(pml_width, ritz, basis, image, from_x, from_y)
+    rows, residual = lax.optimization_barrier((rows, residual))
+    gram = pl.pallas_call(
+        gather_kernel,
+        out_shape=f32(2, vectors, vectors),
+        in_specs=[VMEM],
+        out_specs=VMEM,
+        compiler_params=params,
+        name="sum_rows",
+    )(rows)
     return basis_new, residual, gram
 
 

time: 37.2 us -> 32.5 us (0.87)
  waiting for transfers between devices: 14.4 us -> 4.32 us
  starting transfers between devices: 9.68 us -> 14.3 us
  Pallas kernels: 11.5 us -> 12.9 us
  other arithmetic: 0.61 us -> 0 us
    ppermute x4 -> x0, waiting for transfers between devices: 9.27 us -> none  [from_partner(): lax.ppermute(value, axes, [(source, source ^ mask) for source in range(co...]
    all_to_all x0 -> x1, starting transfers between devices: none -> 4.81 us  [body(): rows = lax.all_to_all(gram, ('gx', 'gy', 'gz'), 0, 0)]
    ppermute x5, waiting for transfers between devices: 5.15 us -> 3.11 us  [passed_round(): lax.ppermute(value, axis, [(source, (source + steps) % count) for source...]
    ppermute x4 -> x0, starting transfers between devices: 1.5 us -> none  [from_partner(): lax.ppermute(value, axes, [(source, source ^ mask) for source in range(co...]
    pallas_call x2 -> x3, Pallas kernels: 1.13 us -> 2.55 us  [the longest x1 1.71 us: body(): pl.pallas_call(outer_kernel, out_shape=(whole, f32(devices, 1, ny)), in_s...]
    ppermute x5, starting transfers between devices: 8.18 us -> 9.48 us  [passed_round(): lax.ppermute(value, axis, [(source, (source + steps) % count) for source...]
    all_to_all x0 -> x1, waiting for transfers between devices: none -> 1.21 us  [body(): rows = lax.all_to_all(gram, ('gx', 'gy', 'gz'), 0, 0)]
    add x5 -> x0, other arithmetic: 0.61 us -> none  [the longest x1 0.6 us: body(): gram = (gram + other)[:, :vectors].reshape(2, vectors, vectors)]
  transfers between devices with their start and end apart: 9 -> 6, of which waited for: 6 -> 3; matrix products, arithmetic and copies ran while one was open for 0% -> 0% of each run, Pallas kernels for 23% -> 29%
where the time goes in v8:
time: 32.5 us; the launch traced here: 32.3 us
  starting transfers between devices  14.3 us (44%)
  Pallas kernels  12.9 us (40%)
  waiting for transfers between devices  4.32 us (13%)
  between operations  0.77 us (2%)
    ppermute x5, starting transfers between devices, passed_round(): lax.ppermute(value, axis, [(source, (source + steps) % count) for source...  9.48 us
    all_to_all x1, starting transfers between devices, body(): rows = lax.all_to_all(gram, ('gx', 'gy', 'gz'), 0, 0)  4.81 us
    pallas_call x1, Pallas kernels, body(): pl.pallas_call(prepare_kernel, out_shape=(whole, whole, whole, planes, f3...  3.16 us
    ppermute x5, waiting for transfers between devices, passed_round(): lax.ppermute(value, axis, [(source, (source + steps) % count) for source...  3.11 us
    pallas_call x1, Pallas kernels, body(): pl.pallas_call(inner_kernel, out_shape=(whole, whole, f32(vectors, 2 * ve...  2.25 us
    pallas_call x1, Pallas kernels, body(): pl.pallas_call(rim_kernel, out_shape=whole, in_specs=[SMEM] * 2 + [VMEM]...  2.23 us
    pallas_call x1, Pallas kernels, body(): pl.pallas_call(face_kernel, out_shape=(whole, f32(*xf_shape), f32(*yf_sha...  1.81 us
    pallas_call x1, Pallas kernels, body(): pl.pallas_call(outer_kernel, out_shape=(whole, f32(devices, 1, ny)), in_s...  1.71 us
  transfers between devices with their start and end apart: 6, of which 3 were waited for; matrix products, arithmetic and copies ran while one was open for 0% of the time, Pallas kernels for 29%

profile of v8, /device:TPU:0, one launch (start us, length us, event | category | flops | bytes accessed | tf_op | source)
XLA Modules:
  0.0 32.3 jit_solution(9311043504475493541)
XLA Ops:
  0.6 0.0 copy-start.2
  0.6 0.0 copy-start.1
  0.7 0.0 copy-start.5
  0.7 1.8 %take_faces.1 = (f32[2,4,3,8,16,128]{5,4,3,2,1,0:T(8,128)S(1)}, f32[2,4,2,8,128]{4,3,2,1,0:T(8,128)S(1)}, f32[16,128]{1,0:T(8,128)S(1)}) custom-call(f32[2,4,3,8,16,128]{5,4,3,2,1,0:T(8,128)} %fields_hbm.1), custom_call_target="tpu_custom_call" | custom-call | tf_op jit(solution)/shard_map/take_faces/pallas_call | solution.py:569
  2.5 4.5 %collective-permute-start = (f32[2,4,2,8,128]{4,3,2,1,0:T(8,128)S(1)}, f32[2,4,2,8,128]{4,3,2,1,0:T(8,128)S(1)}, u32[]{:S(2)}, u32[]{:S(2)}) collective-permute-start(f32[2,4,2,8,128]{4,3,2,1,0:T(8,128)S(1)} %get-tuple-element.39), channel_id=1, source_target_pairs={{0,28},{4,0},{8,4},{12,8},{16,12},{20,16},{24,20},{28,24},{1,29},{... | collective-permute-start | bytes 196616 | tf_op jit(solution)/shard_map/ppermute | solution.py:22
  7.0 1.5 %collective-permute-start.1 = (f32[16,128]{1,0:T(8,128)S(1)}, f32[16,128]{1,0:T(8,128)S(1)}, u32[]{:S(2)}, u32[]{:S(2)}) collective-permute-start(f32[16,128]{1,0:T(8,128)S(1)} %get-tuple-element.40), channel_id=1, source_target_pairs={{0,2},{2,0},{1,3},{3,1},{4,6},{6,4},{5,7},{7,5},{8,10},{10,8},{9,1... | collective-permute-start | bytes 24584 | tf_op jit(solution)/shard_map/ppermute | solution.py:22
  8.6 3.2 %prepare.1 = (f32[2,4,3,8,16,128]{5,4,3,2,1,0:T(8,128)S(1)}, f32[2,4,3,8,16,128]{5,4,3,2,1,0:T(8,128)S(1)}, f32[2,4,3,8,16,128]{5,4,3,2,1,0:T(8,128)S(1)}, f32[8...) custom-call(s32[6]{0:T(128)S(1)} %copy-done.2, f32[4]{0:T(128)S(1)} %copy-done.4, ...), custom_call_target="tpu_custom_call" | custom-call | flops 13107200 | bytes 6291456 | tf_op jit(solution)/shard_map/prepare/pallas_call | solution.py:587
  11.8 0.0 collective-permute-done.1.raw_yf_ref
  11.8 0.0 collective-permute-done.raw_xf_ref
  11.8 0.9 %slab_face.1 = (f32[2,4,3,8,16,128]{5,4,3,2,1,0:T(8,128)S(1)}, f32[8,16,128]{2,1,0:T(8,128)S(1)}, f32[2,4,2,8,128]{4,3,2,1,0:T(8,128)S(1)}, f32[16,128]{1,0:T(8,...) custom-call(s32[6]{0:T(128)S(1)} %copy-done.2, ...), custom_call_target="tpu_custom_call", output_to_operand_aliasing={{0}: (3, {}), {1}: (4, {})} | custom-call | tf_op jit(solution)/shard_map/slab_face/pallas_call | solution.py:596
  12.7 1.6 %collective-permute-start.2 = (f32[2,4,2,16,128]{4,3,2,1,0:T(8,128)S(1)}, f32[2,4,2,16,128]{4,3,2,1,0:T(8,128)S(1)}, u32[]{:S(2)}, u32[]{:S(2)}) collective-permute-start(f32[2,4,2,16,128]{4,3,2,1,0:T(8,128)S(1)} %get-tuple-element.45), channel_id=1, source_target_pairs={{0,1},{1,0},{2,3},{3,2},{4,5},{5,4},{6,7},{7,6},{8,9},{9,8},{10,11... | collective-permute-start | bytes 393224 | tf_op jit(solution)/shard_map/ppermute | solution.py:22
  14.3 2.2 %apply_inner.1 = (f32[2,4,3,8,16,128]{5,4,3,2,1,0:T(8,128)S(1)}, f32[2,4,3,8,16,128]{5,4,3,2,1,0:T(8,128)S(1)}, f32[4,8,8,128]{3,2,1,0:T(8,128)S(1)}, f32[2,4,2,...) custom-call(f32[2,4,3,8,16,128]{5,4,3,2,1,0:T(8,128)S(1)} %get-tuple-element.33.basis_ref, ...), custom_call_target="tpu_custom_call", output_to_operand_aliasing={{0}: (4, {})} | custom-call | flops 13107200 | bytes 3145728 | tf_op jit(solution)/shard_map/apply_inner/pallas_call | solution.py:606
  16.5 1.2 %collective-permute-done.2.zf_ref = f32[2,4,2,16,128]{4,3,2,1,0:T(8,128)S(1)} collective-permute-done((f32[2,4,2,16,128]{4,3,2,1,0:T(8,128)S(1)}, f32[2,4,2,16,128]{4,3,2,1,0:T(8,128)S(1)}, u32[]{:S(2)}, u32[]{:S(2)}) %collective-permute-start.2) | collective-permute-done | bytes 131104 | tf_op jit(solution)/shard_map/ppermute | solution.py:22
  17.7 0.1 last_plane.1
  17.9 0.0 collective-permute-start.3
  17.9 0.0 copy-start.3
  17.9 1.7 %apply_outer.1 = (f32[2,4,3,8,16,128]{5,4,3,2,1,0:T(8,128)S(1)}, f32[32,1,128]{2,1,0:T(1,128)}) custom-call(s32[6]{0:T(128)S(1)} %copy-done.2, f32[2,4,3,8,16,128]{5,4,3,2,1,0:T(8,128)S(1)} %get-tuple-element.33.basis_ref, f32[2,4,3,8,16,128]{5,4,3,2,1,0:T(8,128)S(1)} %get-tuple-element.34.loss_ref, ...), custom_call_target="tpu_custom_call", output_to_operand_aliasing={{0}: (11, {})} | custom-call | flops 4915200 | bytes 1572864 | tf_op jit(solution)/shard_map/apply_outer/pallas_call | solution.py:629
  19.6 4.8 %all-to-all-start = ((f32[32,1,128]{2,1,0:T(1,128)}), f32[32,1,128]{2,1,0:T(1,128)S(1)}, u32[]{:S(2)}, u32[]{:S(2)}) async-start(f32[32,1,128]{2,1,0:T(1,128)} %get-tuple-element.57), calls=%async_computation | async-start | bytes 32768 | tf_op jit(solution)/shard_map/all_to_all | solution.py:639
  24.5 1.8 %collective-permute-start.4 = (f32[16,128]{1,0:T(8,128)S(1)}, f32[16,128]{1,0:T(8,128)S(1)}, u32[]{:S(2)}, u32[]{:S(2)}) collective-permute-start(f32[16,128]{1,0:T(8,128)S(1)} %get-tuple-element.53.hyf_ref), channel_id=1, source_target_pairs={{0,2},{2,0},{1,3},{3,1},{4,6},{6,4},{5,7},{7,5},{8,10},{10,8},{9,1... | collective-permute-start | bytes 24584 | tf_op jit(solution)/shard_map/ppermute | solution.py:22
  26.3 1.9 %collective-permute-done.4.hyf_ref = f32[16,128]{1,0:T(8,128)S(1)} collective-permute-done((f32[16,128]{1,0:T(8,128)S(1)}, f32[16,128]{1,0:T(8,128)S(1)}, u32[]{:S(2)}, u32[]{:S(2)}) %collective-permute-start.4) | collective-permute-done | bytes 8224 | tf_op jit(solution)/shard_map/ppermute | solution.py:22
  28.2 0.0 collective-permute-done.3.hxf_ref
  28.2 2.2 %add_rims.1 = f32[2,4,3,8,16,128]{5,4,3,2,1,0:T(8,128)} custom-call(s32[6]{0:T(128)S(1)} %copy-done.2, f32[2,4]{1,0:T(2,128)S(1)} %copy-done.3, f32[2,4,3,8,16,128]{5,4,3,2,1,0:T(8,128)S(1)} %get-tuple-element.33.basis_ref, f32[2,4,3,8,16,128]{5,4,3,2,1,0:T(8,128)S(1)} %get-tuple-element.58.image_ref, ...), custom_call_target="tpu_custom_call" | custom-call | flops 3276800 | bytes 4718592 | tf_op jit(solution)/shard_map/add_rims/pallas_call | solution.py:640
  30.4 1.2 %all-to-all-done.rows_ref = f32[32,1,128]{2,1,0:T(1,128)S(1)} async-done(((f32[32,1,128]{2,1,0:T(1,128)}), f32[32,1,128]{2,1,0:T(1,128)S(1)}, u32[]{:S(2)}, u32[]{:S(2)}) %all-to-all-start) | async-done | bytes 16416 | tf_op jit(solution)/shard_map/all_to_all | solution.py:639
  31.6 0.7 %sum_rows.1 = f32[2,4,4]{2,1,0:T(4,128)} custom-call(f32[32,1,128]{2,1,0:T(1,128)S(1)} %all-to-all-done.rows_ref), custom_call_target="tpu_custom_call" | custom-call | tf_op jit(solution)/shard_map/sum_rows/pallas_call | solution.py:651
  (8 shorter events, 0.0 us)
Async XLA Ops:
  0.6 7.9 %copy-start.2 = (s32[6]{0:T(128)S(1)}, s32[6]{0:T(128)}, u32[]{:S(2)}) copy-start(s32[6]{0:T(128)} %pml_ref.7) | copy-start | bytes 76
  0.6 7.9 %copy-start.1 = (f32[2,4,4]{2,1,0:T(4,128)S(1)}, f32[2,4,4]{2,1,0:T(4,128)}, u32[]{:S(2)}) copy-start(f32[2,4,4]{2,1,0:T(4,128)} %coeffs_ref.3) | copy-start | bytes 388
  0.7 7.9 %copy-start.5 = (f32[4]{0:T(128)S(1)}, f32[4]{0:T(128)}, u32[]{:S(2)}) copy-start(f32[4]{0:T(128)} %eps_loss_ref.1) | copy-start | bytes 52
  0.7 7.9 %copy-start.4 = (f32[4]{0:T(128)S(1)}, f32[4]{0:T(128)}, u32[]{:S(2)}) copy-start(f32[4]{0:T(128)} %eps_real_ref.1) | copy-start | bytes 52
  0.7 7.9 %copy-start = (s32[8,16,128]{2,1,0:T(8,128)S(1)}, s32[8,16,128]{2,1,0:T(8,128)}, u32[]{:S(2)}) copy-start(s32[8,16,128]{2,1,0:T(8,128)} %material_ref.1) | copy-start | bytes 196612
  2.5 9.3 %collective-permute-start = (f32[2,4,2,8,128]{4,3,2,1,0:T(8,128)S(1)}, f32[2,4,2,8,128]{4,3,2,1,0:T(8,128)S(1)}, u32[]{:S(2)}, u32[]{:S(2)}) collective-permute-start(f32[2,4,2,8,128]{4,3,2,1,0:T(8,128)S(1)} %get-tuple-element.39), channel_id=1, source_target_pairs={{0,28},{4,0},{8,4},{12,8},{16,12},{20,16},{24,20},{28,24},{1,29},{... | collective-permute-start | bytes 196616 | tf_op jit(solution)/shard_map/ppermute | solution.py:22
  7.0 4.7 %collective-permute-start.1 = (f32[16,128]{1,0:T(8,128)S(1)}, f32[16,128]{1,0:T(8,128)S(1)}, u32[]{:S(2)}, u32[]{:S(2)}) collective-permute-start(f32[16,128]{1,0:T(8,128)S(1)} %get-tuple-element.40), channel_id=1, source_target_pairs={{0,2},{2,0},{1,3},{3,1},{4,6},{6,4},{5,7},{7,5},{8,10},{10,8},{9,1... | collective-permute-start | bytes 24584 | tf_op jit(solution)/shard_map/ppermute | solution.py:22
  12.7 5.0 %collective-permute-start.2 = (f32[2,4,2,16,128]{4,3,2,1,0:T(8,128)S(1)}, f32[2,4,2,16,128]{4,3,2,1,0:T(8,128)S(1)}, u32[]{:S(2)}, u32[]{:S(2)}) collective-permute-start(f32[2,4,2,16,128]{4,3,2,1,0:T(8,128)S(1)} %get-tuple-element.45), channel_id=1, source_target_pairs={{0,1},{1,0},{2,3},{3,2},{4,5},{5,4},{6,7},{7,6},{8,9},{9,8},{10,11... | collective-permute-start | bytes 393224 | tf_op jit(solution)/shard_map/ppermute | solution.py:22
  17.9 10.3 %collective-permute-start.3 = (f32[2,4,2,8,128]{4,3,2,1,0:T(8,128)S(1)}, f32[2,4,2,8,128]{4,3,2,1,0:T(8,128)S(1)}, u32[]{:S(2)}, u32[]{:S(2)}) collective-permute-start(f32[2,4,2,8,128]{4,3,2,1,0:T(8,128)S(1)} %get-tuple-element.52.hxf_ref), channel_id=1, source_target_pairs={{0,4},{4,8},{8,12},{12,16},{16,20},{20,24},{24,28},{28,0},{1,5},{5... | collective-permute-start | bytes 196616 | tf_op jit(solution)/shard_map/ppermute | solution.py:22
  17.9 10.3 %copy-start.3 = (f32[2,4]{1,0:T(2,128)S(1)}, f32[2,4]{1,0:T(2,128)}, u32[]{:S(2)}) copy-start(f32[2,4]{1,0:T(2,128)} %ritz_ref.1) | copy-start | bytes 100
  19.6 12.0 %all-to-all-start = ((f32[32,1,128]{2,1,0:T(1,128)}), f32[32,1,128]{2,1,0:T(1,128)S(1)}, u32[]{:S(2)}, u32[]{:S(2)}) async-start(f32[32,1,128]{2,1,0:T(1,128)} %get-tuple-element.57), calls=%async_computation | async-start | bytes 32768 | tf_op jit(solution)/shard_map/all_to_all | solution.py:639
  24.5 3.7 %collective-permute-start.4 = (f32[16,128]{1,0:T(8,128)S(1)}, f32[16,128]{1,0:T(8,128)S(1)}, u32[]{:S(2)}, u32[]{:S(2)}) collective-permute-start(f32[16,128]{1,0:T(8,128)S(1)} %get-tuple-element.53.hyf_ref), channel_id=1, source_target_pairs={{0,2},{2,0},{1,3},{3,1},{4,6},{6,4},{5,7},{7,5},{8,10},{10,8},{9,1... | collective-permute-start | bytes 24584 | tf_op jit(solution)/shard_map/ppermute | solution.py:22

commit v9 on v8

--- a/solution.py
+++ b/solution.py
@@ -80,12 +80,10 @@
     ]
     for copy in copies:
         copy.start()
-    for copy in copies:
-        copy.wait()
-
     packed = [jnp.zeros((nx, ny), jnp.float32)] * nz
-    for comp in (0, 2):
+    for place, comp in enumerate((0, 2)):
         for part in range(2):
+            copies[2 * place + part].wait()
             for a in range(vectors):
                 row = packed_row(comp // 2, part, a, vectors)
                 for z in range(nz):
@@ -95,8 +93,11 @@
     yf_ref[...] = turned[:yf_ref.shape[0]]
     for part in range(2):
         for a in range(vectors):
-            for slot in range(2):
-                xf_ref[part, a, slot] = fields_ref[part, a, slot + 1, :, 0, :]
+            xf_ref[part, a, 1] = fields_ref[part, a, 2, :, 0, :]
+    for part in range(2):
+        copies[4 + part].wait()
+        for a in range(vectors):
+            xf_ref[part, a, 0] = fields_ref[part, a, 1, :, 0, :]
 
 
 def rotated(coeffs_ref, old, b):
@@ -441,8 +442,7 @@
         cmul(sy_next, (yt_ref[slot * both:slot * both + vectors], yt_ref[slot * both + vectors:(slot + 1) * both]))
         for slot in range(2)
     ]
-    columns = lax.broadcasted_iota(jnp.int32, (both, ny), 1)
-    gram = jnp.zeros((both, ny), jnp.float32)
+    totals = {}
     for b in range(vectors):
 
         def tile_of(ref, slot, cut, b=b):
@@ -472,38 +472,54 @@
             over = cmul(sx_next, over)
             for row in range(0, nz, SUB):
                 sums[a] = add(sums[a], tuple(part[row:row + SUB] for part in over))
-        flat = jnp.concatenate(
-            [jnp.sum(sums[a][part], axis=0, keepdims=True) for part in parts for a in range(vectors)], axis=0
-        )
         over = None
         for slot in range(2):
             h = tuple(hyf_ref[packed_row(slot, part, b, vectors)][None] for part in parts)
             term = cmul(ends[slot], h)
             over = term if over is None else sub(term, over)
-        side = jnp.concatenate(over, axis=0)
-        total = jnp.sum(flat, axis=1, keepdims=True) + jnp.sum(side, axis=1, keepdims=True)
-        gram = jnp.where(columns == b, total, gram)
+        for a in range(vectors):
+            for part in parts:
+                side = jnp.concatenate([over[part][a:a + 1], jnp.zeros((SUB - 1, ny), jnp.float32)], axis=0)
+                totals[part, a, b] = sums[a][part] + side
     everywhere = 3.0 * nz * nx * ny
     for axis in AXES:
         everywhere = everywhere * lax.axis_size(axis)
-    gram = gram * (1.0 / everywhere)
-    flat = gram[0:1]
-    for row in range(1, both):
-        flat = flat + pltpu.roll(gram[row:row + 1], row * vectors, 1)
-    for device in range(gram_ref.shape[0]):
-        gram_ref[device] = flat
+    for part in parts:
+        stack = jnp.concatenate([totals[part, a, b] for a in range(vectors) for b in range(vectors)], axis=0)
+        row = jnp.sum(stack.T, axis=0, keepdims=True) * (1.0 / everywhere)
+        for device in range(gram_ref.shape[0]):
+            gram_ref[device, part:part + 1] = row
+
+
+def tree_sum(values):
+    while len(values) > 1:
+        pairs = [values[place] + values[place + 1] for place in range(0, len(values) - 1, 2)]
+        values = pairs + ([values[-1]] if len(values) % 2 else [])
+    return values[0]
+
+
+def share_kernel(rows_ref, next_ref):
+    total = tree_sum([rows_ref[device] for device in range(rows_ref.shape[0])])
+    for device in range(next_ref.shape[0]):
+        next_ref[device] = total
 
 
 def gather_kernel(rows_ref, gram_ref):
-    vectors = gram_ref.shape[1]
-    total = rows_ref[0]
-    for device in range(1, rows_ref.shape[0]):
-        total = total + rows_ref[device]
-    for part in range(2):
-        for a in range(vectors):
-            row = (part * vectors + a) * vectors
-            turned = pltpu.roll(total, (total.shape[1] - row) % total.shape[1], 1)
-            gram_ref[part, a:a + 1] = turned[:, :vectors]
+    _, vectors, _ = gram_ref.shape
+    total = tree_sum([rows_ref[device] for device in range(rows_ref.shape[0])])
+    count = total.shape[1]
+    reach = 1
+    while reach < SUB:
+        total = total + pltpu.roll(total, count - reach, 1)
+        reach *= 2
+    lanes = lax.broadcasted_iota(jnp.int32, total.shape, 1)
+    for a in range(vectors):
+        matrix_row = total
+        for b in range(vectors):
+            place = (a * vectors + b) * SUB
+            matrix_row = jnp.where(lanes == b, pltpu.roll(total, (count + b - place) % count, 1), matrix_row)
+        for part in range(2):
+            gram_ref[part, a:a + 1] = matrix_row[part:part + 1, :vectors]
 
 
 def rim_kernel(
@@ -623,12 +639,10 @@
         compiler_params=params,
         name="last_plane",
     )(sz, zf, h, packed, hxf)
-    from_x = passed_round(hxf, "gx", 1)
-    from_y = passed_round(hyf, "gy", 1)
-    devices = lax.axis_size("gx") * lax.axis_size("gy") * lax.axis_size("gz")
+    first, second = lax.axis_size("gx"), lax.axis_size("gy") * lax.axis_size("gz")
     image, gram = pl.pallas_call(
         outer_kernel,
-        out_shape=(whole, f32(devices, 1, ny)),
+        out_shape=(whole, f32(first, 2, ny)),
         in_specs=[SMEM] + [VMEM] * 13,
         out_specs=(VMEM,) * 2,
         input_output_aliases={11: 0},
@@ -636,7 +650,20 @@
         cost_estimate=cost(300, 1),
         name="apply_outer",
     )(pml_width, basis, loss, table, sz, h, zf, xf, yt, hxf, hyf, image, acc, before)
-    rows = lax.all_to_all(gram, ("gx", "gy", "gz"), 0, 0)
+    gram, hxf, hyf = lax.optimization_barrier((gram, hxf, hyf))
+    rows = lax.all_to_all(gram, "gx", 0, 0)
+    from_y = passed_round(hyf, "gy", 1)
+    from_x = passed_round(hxf, "gx", 1)
+    rows, from_y = lax.optimization_barrier((rows, from_y))
+    gram = pl.pallas_call(
+        share_kernel,
+        out_shape=f32(second, 2, ny),
+        in_specs=[VMEM],
+        out_specs=VMEM,
+        compiler_params=params,
+        name="share_rows",
+    )(rows)
+    rows = lax.all_to_all(gram, ("gy", "gz"), 0, 0)
     residual = pl.pallas_call(
         rim_kernel,
         out_shape=whole,

time: 32.5 us -> 39.4 us (1.21)
  waiting for transfers between devices: 4.32 us -> 8.69 us
  starting transfers between devices: 14.3 us -> 16.2 us
  Pallas kernels: 12.9 us -> 13.5 us
    all_to_all x1 -> x2, starting transfers between devices: 4.81 us -> 8.06 us  [the longest x1 4.82 us: body(): rows = lax.all_to_all(gram, 'gx', 0, 0)]
    all_to_all x1 -> x2, waiting for transfers between devices: 1.21 us -> 4.34 us  [the longest x1 2.38 us: body(): rows = lax.all_to_all(gram, ('gy', 'gz'), 0, 0)]
    ppermute x5, starting transfers between devices: 9.48 us -> 8.13 us  [passed_round(): lax.ppermute(value, axis, [(source, (source + steps) % count) for source...]
    ppermute x5, waiting for transfers between devices: 3.11 us -> 4.36 us  [passed_round(): lax.ppermute(value, axis, [(source, (source + steps) % count) for source...]
    pallas_call x1 -> x2, Pallas kernels: 1.71 us -> 2.21 us  [the longest x1 1.61 us: body(): pl.pallas_call(outer_kernel, out_shape=(whole, f32(first, 2, ny)), in_spe...]
  transfers between devices with their start and end apart: 6 -> 7, of which waited for: 3 -> 4; matrix products, arithmetic and copies ran while one was open for 0% -> 0% of each run, Pallas kernels for 29% -> 21%
where the time goes in v9:
time: 39.4 us; the launch traced here: 39.1 us
  starting transfers between devices  16.2 us (41%)
  Pallas kernels  13.5 us (34%)
  waiting for transfers between devices  8.69 us (22%)
  between operations  0.77 us (2%)
    ppermute x5, starting transfers between devices, passed_round(): lax.ppermute(value, axis, [(source, (source + steps) % count) for source...  8.13 us
    all_to_all x1, starting transfers between devices, body(): rows = lax.all_to_all(gram, 'gx', 0, 0)  4.82 us
    ppermute x5, waiting for transfers between devices, passed_round(): lax.ppermute(value, axis, [(source, (source + steps) % count) for source...  4.36 us
    all_to_all x1, starting transfers between devices, body(): rows = lax.all_to_all(gram, ('gy', 'gz'), 0, 0)  3.25 us
    pallas_call x1, Pallas kernels, body(): pl.pallas_call(prepare_kernel, out_shape=(whole, whole, whole, planes, f3...  3.16 us
    all_to_all x1, waiting for transfers between devices, body(): rows = lax.all_to_all(gram, ('gy', 'gz'), 0, 0)  2.38 us
    pallas_call x1, Pallas kernels, body(): pl.pallas_call(inner_kernel, out_shape=(whole, whole, f32(vectors, 2 * ve...  2.26 us
    pallas_call x1, Pallas kernels, body(): pl.pallas_call(rim_kernel, out_shape=whole, in_specs=[SMEM] * 2 + [VMEM]...  2.23 us
  transfers between devices with their start and end apart: 7, of which 4 were waited for; matrix products, arithmetic and copies ran while one was open for 0% of the time, Pallas kernels for 21%

profile of v9, /device:TPU:0, one launch (start us, length us, event | category | flops | bytes accessed | tf_op | source)
XLA Modules:
  0.0 39.1 jit_solution(12994601409912360155)
XLA Ops:
  0.7 1.6 %take_faces.1 = (f32[2,4,3,8,16,128]{5,4,3,2,1,0:T(8,128)S(1)}, f32[2,4,2,8,128]{4,3,2,1,0:T(8,128)S(1)}, f32[16,128]{1,0:T(8,128)S(1)}) custom-call(f32[2,4,3,8,16,128]{5,4,3,2,1,0:T(8,128)} %fields_hbm.1), custom_call_target="tpu_custom_call" | custom-call | tf_op jit(solution)/shard_map/take_faces/pallas_call | solution.py:585
  2.3 4.5 %collective-permute-start = (f32[2,4,2,8,128]{4,3,2,1,0:T(8,128)S(1)}, f32[2,4,2,8,128]{4,3,2,1,0:T(8,128)S(1)}, u32[]{:S(2)}, u32[]{:S(2)}) collective-permute-start(f32[2,4,2,8,128]{4,3,2,1,0:T(8,128)S(1)} %get-tuple-element.44), channel_id=1, source_target_pairs={{0,28},{4,0},{8,4},{12,8},{16,12},{20,16},{24,20},{28,24},{1,29},{... | collective-permute-start | bytes 196616 | tf_op jit(solution)/shard_map/ppermute | solution.py:22
  6.9 1.5 %collective-permute-start.1 = (f32[16,128]{1,0:T(8,128)S(1)}, f32[16,128]{1,0:T(8,128)S(1)}, u32[]{:S(2)}, u32[]{:S(2)}) collective-permute-start(f32[16,128]{1,0:T(8,128)S(1)} %get-tuple-element.45), channel_id=1, source_target_pairs={{0,2},{2,0},{1,3},{3,1},{4,6},{6,4},{5,7},{7,5},{8,10},{10,8},{9,1... | collective-permute-start | bytes 24584 | tf_op jit(solution)/shard_map/ppermute | solution.py:22
  8.4 0.0 copy-done.1
  8.4 3.2 %prepare.1 = (f32[2,4,3,8,16,128]{5,4,3,2,1,0:T(8,128)S(1)}, f32[2,4,3,8,16,128]{5,4,3,2,1,0:T(8,128)S(1)}, f32[2,4,3,8,16,128]{5,4,3,2,1,0:T(8,128)S(1)}, f32[8...) custom-call(s32[6]{0:T(128)S(1)} %copy-done.2, f32[4]{0:T(128)S(1)} %copy-done.4, ...), custom_call_target="tpu_custom_call" | custom-call | flops 13107200 | bytes 6291456 | tf_op jit(solution)/shard_map/prepare/pallas_call | solution.py:603
  11.6 0.0 collective-permute-done.1.raw_yf_ref
  11.6 0.0 collective-permute-done.raw_xf_ref
  11.6 0.9 %slab_face.1 = (f32[2,4,3,8,16,128]{5,4,3,2,1,0:T(8,128)S(1)}, f32[8,16,128]{2,1,0:T(8,128)S(1)}, f32[2,4,2,8,128]{4,3,2,1,0:T(8,128)S(1)}, f32[16,128]{1,0:T(8,...) custom-call(s32[6]{0:T(128)S(1)} %copy-done.2, ...), custom_call_target="tpu_custom_call", output_to_operand_aliasing={{0}: (3, {}), {1}: (4, {})} | custom-call | tf_op jit(solution)/shard_map/slab_face/pallas_call | solution.py:612
  12.5 1.6 %collective-permute-start.2 = (f32[2,4,2,16,128]{4,3,2,1,0:T(8,128)S(1)}, f32[2,4,2,16,128]{4,3,2,1,0:T(8,128)S(1)}, u32[]{:S(2)}, u32[]{:S(2)}) collective-permute-start(f32[2,4,2,16,128]{4,3,2,1,0:T(8,128)S(1)} %get-tuple-element.50), channel_id=1, source_target_pairs={{0,1},{1,0},{2,3},{3,2},{4,5},{5,4},{6,7},{7,6},{8,9},{9,8},{10,11... | collective-permute-start | bytes 393224 | tf_op jit(solution)/shard_map/ppermute | solution.py:22
  14.1 2.3 %apply_inner.1 = (f32[2,4,3,8,16,128]{5,4,3,2,1,0:T(8,128)S(1)}, f32[2,4,3,8,16,128]{5,4,3,2,1,0:T(8,128)S(1)}, f32[4,8,8,128]{3,2,1,0:T(8,128)S(1)}, f32[2,4,2,...) custom-call(f32[2,4,3,8,16,128]{5,4,3,2,1,0:T(8,128)S(1)} %get-tuple-element.38.basis_ref, ...), custom_call_target="tpu_custom_call", output_to_operand_aliasing={{0}: (4, {})} | custom-call | flops 13107200 | bytes 3145728 | tf_op jit(solution)/shard_map/apply_inner/pallas_call | solution.py:622
  16.4 1.2 %collective-permute-done.2.zf_ref = f32[2,4,2,16,128]{4,3,2,1,0:T(8,128)S(1)} collective-permute-done((f32[2,4,2,16,128]{4,3,2,1,0:T(8,128)S(1)}, f32[2,4,2,16,128]{4,3,2,1,0:T(8,128)S(1)}, u32[]{:S(2)}, u32[]{:S(2)}) %collective-permute-start.2) | collective-permute-done | bytes 131104 | tf_op jit(solution)/shard_map/ppermute | solution.py:22
  17.6 0.1 last_plane.1
  17.7 1.6 %apply_outer.1 = (f32[2,4,3,8,16,128]{5,4,3,2,1,0:T(8,128)S(1)}, f32[8,2,128]{2,1,0:T(2,128)}) custom-call(s32[6]{0:T(128)S(1)} %copy-done.2, f32[2,4,3,8,16,128]{5,4,3,2,1,0:T(8,128)S(1)} %get-tuple-element.38.basis_ref, f32[2,4,3,8,16,128]{5,4,3,2,1,0:T(8,128)S(1)} %get-tuple-element.39.loss_ref, ...), custom_call_target="tpu_custom_call", output_to_operand_aliasing={{0}: (11, {})} | custom-call | flops 4915200 | bytes 1572864 | tf_op jit(solution)/shard_map/apply_outer/pallas_call | solution.py:643
  19.3 0.0 collective-permute-start.4
  19.3 4.8 %all-to-all-start = ((f32[8,2,128]{2,1,0:T(2,128)}), f32[8,2,128]{2,1,0:T(2,128)S(1)}, u32[]{:S(2)}, u32[]{:S(2)}) async-start(f32[8,2,128]{2,1,0:T(2,128)} %get-tuple-element.63), calls=%async_computation | async-start | bytes 16384 | tf_op jit(solution)/shard_map/all_to_all | solution.py:654
  24.2 0.5 %collective-permute-start.3 = (f32[16,128]{1,0:T(8,128)S(1)}, f32[16,128]{1,0:T(8,128)S(1)}, u32[]{:S(2)}, u32[]{:S(2)}) collective-permute-start(f32[16,128]{1,0:T(8,128)S(1)} %get-tuple-element.64.hyf_ref), channel_id=1, source_target_pairs={{0,2},{2,0},{1,3},{3,1},{4,6},{6,4},{5,7},{7,5},{8,10},{10,8},{9,1... | collective-permute-start | bytes 24584 | tf_op jit(solution)/shard_map/ppermute | solution.py:22
  24.7 3.1 %collective-permute-done.3.hyf_ref = f32[16,128]{1,0:T(8,128)S(1)} collective-permute-done((f32[16,128]{1,0:T(8,128)S(1)}, f32[16,128]{1,0:T(8,128)S(1)}, u32[]{:S(2)}, u32[]{:S(2)}) %collective-permute-start.3) | collective-permute-done | bytes 8224 | tf_op jit(solution)/shard_map/ppermute | solution.py:22
  27.8 2.0 %all-to-all-done.rows_ref = f32[8,2,128]{2,1,0:T(2,128)S(1)} async-done(((f32[8,2,128]{2,1,0:T(2,128)}), f32[8,2,128]{2,1,0:T(2,128)S(1)}, u32[]{:S(2)}, u32[]{:S(2)}) %all-to-all-start) | async-done | bytes 8224 | tf_op jit(solution)/shard_map/all_to_all | solution.py:654
  29.8 0.6 %share_rows.1 = f32[4,2,128]{2,1,0:T(2,128)} custom-call(f32[8,2,128]{2,1,0:T(2,128)S(1)} %all-to-all-done.rows_ref), custom_call_target="tpu_custom_call" | custom-call | tf_op jit(solution)/shard_map/share_rows/pallas_call | solution.py:658
  30.4 3.2 %all-to-all-start.1 = ((f32[4,2,128]{2,1,0:T(2,128)}), f32[4,2,128]{2,1,0:T(2,128)S(1)}, u32[]{:S(2)}, u32[]{:S(2)}) async-start(f32[4,2,128]{2,1,0:T(2,128)} %share_rows.1), calls=%async_computation.1 | async-start | bytes 8192 | tf_op jit(solution)/shard_map/all_to_all | solution.py:666
  33.6 0.0 collective-permute-done.4.hxf_ref
  33.6 2.2 %add_rims.1 = f32[2,4,3,8,16,128]{5,4,3,2,1,0:T(8,128)} custom-call(s32[6]{0:T(128)S(1)} %copy-done.2, f32[2,4]{1,0:T(2,128)S(1)} %copy-done.3, f32[2,4,3,8,16,128]{5,4,3,2,1,0:T(8,128)S(1)} %get-tuple-element.38.basis_ref, f32[2,4,3,8,16,128]{5,4,3,2,1,0:T(8,128)S(1)} %get-tuple-element.66.image_ref, ...), custom_call_target="tpu_custom_call" | custom-call | flops 3276800 | bytes 4718592 | tf_op jit(solution)/shard_map/add_rims/pallas_call | solution.py:667
  35.9 2.4 %all-to-all-done.1.rows_ref = f32[4,2,128]{2,1,0:T(2,128)S(1)} async-done(((f32[4,2,128]{2,1,0:T(2,128)}), f32[4,2,128]{2,1,0:T(2,128)S(1)}, u32[]{:S(2)}, u32[]{:S(2)}) %all-to-all-start.1) | async-done | bytes 4128 | tf_op jit(solution)/shard_map/all_to_all | solution.py:666
  38.3 0.9 %sum_rows.1 = f32[2,4,4]{2,1,0:T(4,128)} custom-call(f32[4,2,128]{2,1,0:T(2,128)S(1)} %all-to-all-done.1.rows_ref), custom_call_target="tpu_custom_call" | custom-call | tf_op jit(solution)/shard_map/sum_rows/pallas_call | solution.py:678
  (11 shorter events, 0.0 us)
Async XLA Ops:
  0.6 7.8 %copy-start.2 = (s32[6]{0:T(128)S(1)}, s32[6]{0:T(128)}, u32[]{:S(2)}) copy-start(s32[6]{0:T(128)} %pml_ref.7) | copy-start | bytes 76
  0.6 7.8 %copy-start.1 = (f32[2,4,4]{2,1,0:T(4,128)S(1)}, f32[2,4,4]{2,1,0:T(4,128)}, u32[]{:S(2)}) copy-start(f32[2,4,4]{2,1,0:T(4,128)} %coeffs_ref.3) | copy-start | bytes 388
  0.7 7.8 %copy-start.5 = (f32[4]{0:T(128)S(1)}, f32[4]{0:T(128)}, u32[]{:S(2)}) copy-start(f32[4]{0:T(128)} %eps_loss_ref.1) | copy-start | bytes 52
  0.7 7.7 %copy-start.4 = (f32[4]{0:T(128)S(1)}, f32[4]{0:T(128)}, u32[]{:S(2)}) copy-start(f32[4]{0:T(128)} %eps_real_ref.1) | copy-start | bytes 52
  0.7 7.7 %copy-start = (s32[8,16,128]{2,1,0:T(8,128)S(1)}, s32[8,16,128]{2,1,0:T(8,128)}, u32[]{:S(2)}) copy-start(s32[8,16,128]{2,1,0:T(8,128)} %material_ref.1) | copy-start | bytes 196612
  2.3 9.3 %collective-permute-start = (f32[2,4,2,8,128]{4,3,2,1,0:T(8,128)S(1)}, f32[2,4,2,8,128]{4,3,2,1,0:T(8,128)S(1)}, u32[]{:S(2)}, u32[]{:S(2)}) collective-permute-start(f32[2,4,2,8,128]{4,3,2,1,0:T(8,128)S(1)} %get-tuple-element.44), channel_id=1, source_target_pairs={{0,28},{4,0},{8,4},{12,8},{16,12},{20,16},{24,20},{28,24},{1,29},{... | collective-permute-start | bytes 196616 | tf_op jit(solution)/shard_map/ppermute | solution.py:22
  6.9 4.7 %collective-permute-start.1 = (f32[16,128]{1,0:T(8,128)S(1)}, f32[16,128]{1,0:T(8,128)S(1)}, u32[]{:S(2)}, u32[]{:S(2)}) collective-permute-start(f32[16,128]{1,0:T(8,128)S(1)} %get-tuple-element.45), channel_id=1, source_target_pairs={{0,2},{2,0},{1,3},{3,1},{4,6},{6,4},{5,7},{7,5},{8,10},{10,8},{9,1... | collective-permute-start | bytes 24584 | tf_op jit(solution)/shard_map/ppermute | solution.py:22
  12.5 5.0 %collective-permute-start.2 = (f32[2,4,2,16,128]{4,3,2,1,0:T(8,128)S(1)}, f32[2,4,2,16,128]{4,3,2,1,0:T(8,128)S(1)}, u32[]{:S(2)}, u32[]{:S(2)}) collective-permute-start(f32[2,4,2,16,128]{4,3,2,1,0:T(8,128)S(1)} %get-tuple-element.50), channel_id=1, source_target_pairs={{0,1},{1,0},{2,3},{3,2},{4,5},{5,4},{6,7},{7,6},{8,9},{9,8},{10,11... | collective-permute-start | bytes 393224 | tf_op jit(solution)/shard_map/ppermute | solution.py:22
  17.7 15.9 %copy-start.3 = (f32[2,4]{1,0:T(2,128)S(1)}, f32[2,4]{1,0:T(2,128)}, u32[]{:S(2)}) copy-start(f32[2,4]{1,0:T(2,128)} %ritz_ref.1) | copy-start | bytes 100
  19.3 14.3 %collective-permute-start.4 = (f32[2,4,2,8,128]{4,3,2,1,0:T(8,128)S(1)}, f32[2,4,2,8,128]{4,3,2,1,0:T(8,128)S(1)}, u32[]{:S(2)}, u32[]{:S(2)}) collective-permute-start(f32[2,4,2,8,128]{4,3,2,1,0:T(8,128)S(1)} %get-tuple-element.67.hxf_ref), channel_id=1, source_target_pairs={{0,4},{4,8},{8,12},{12,16},{16,20},{20,24},{24,28},{28,0},{1,5},{5... | collective-permute-start | bytes 196616 | tf_op jit(solution)/shard_map/ppermute | solution.py:22
  19.3 10.4 %all-to-all-start = ((f32[8,2,128]{2,1,0:T(2,128)}), f32[8,2,128]{2,1,0:T(2,128)S(1)}, u32[]{:S(2)}, u32[]{:S(2)}) async-start(f32[8,2,128]{2,1,0:T(2,128)} %get-tuple-element.63), calls=%async_computation | async-start | bytes 16384 | tf_op jit(solution)/shard_map/all_to_all | solution.py:654
  24.2 3.7 %collective-permute-start.3 = (f32[16,128]{1,0:T(8,128)S(1)}, f32[16,128]{1,0:T(8,128)S(1)}, u32[]{:S(2)}, u32[]{:S(2)}) collective-permute-start(f32[16,128]{1,0:T(8,128)S(1)} %get-tuple-element.64.hyf_ref), channel_id=1, source_target_pairs={{0,2},{2,0},{1,3},{3,1},{4,6},{6,4},{5,7},{7,5},{8,10},{10,8},{9,1... | collective-permute-start | bytes 24584 | tf_op jit(solution)/shard_map/ppermute | solution.py:22
  30.4 7.9 %all-to-all-start.1 = ((f32[4,2,128]{2,1,0:T(2,128)}), f32[4,2,128]{2,1,0:T(2,128)S(1)}, u32[]{:S(2)}, u32[]{:S(2)}) async-start(f32[4,2,128]{2,1,0:T(2,128)} %share_rows.1), calls=%async_computation.1 | async-start | bytes 8192 | tf_op jit(solution)/shard_map/all_to_all | solution.py:666

commit v10 on v9

--- a/solution.py
+++ b/solution.py
@@ -20,6 +20,13 @@
 def passed_round(value, axis, steps):
     count = lax.axis_size(axis)
     return lax.ppermute(value, axis, [(source, (source + steps) % count) for source in range(count)])
+
+
+def swapped_with_neighbours(value, axis):
+    count = lax.axis_size(axis)
+    near = [(source, source ^ 1) for source in range(count)]
+    far = [(source, min(max(((source + 1) ^ 1) - 1, 0), count - 1)) for source in range(count)]
+    return lax.ppermute(value, axis, near), lax.ppermute(value, axis, far)
 
 
 def inverse_stretch(places, length, low_width, high_width):
@@ -209,11 +216,21 @@
         magnetic(b, nz - 1, True)
 
 
-def turn_face(coeffs_ref, direction, raw_ref, face_ref):
-    inside = has_neighbour(direction, 1)
-    vectors = raw_ref.shape[1]
+def pair_weights(steps):
+    place = lax.axis_index(AXES[1])
+    even = jnp.where(lax.rem(place, 2) == 0, 1.0, 0.0).astype(jnp.float32)
+    inside = has_neighbour(1, steps)
+    return (even * inside, (1.0 - even) * inside) if steps > 0 else ((1.0 - even) * inside, even * inside)
+
+
+def turn_face(coeffs_ref, near_ref, far_ref, face_ref):
+    near, far = pair_weights(1)
+    vectors = near_ref.shape[1]
     for slot in range(2):
-        old = [(raw_ref[0, a, slot] * inside, raw_ref[1, a, slot] * inside) for a in range(vectors)]
+        old = [
+            tuple(near_ref[part, a, slot] * near + far_ref[part, a, slot] * far for part in range(2))
+            for a in range(vectors)
+        ]
         for b in range(vectors):
             new = rotated(coeffs_ref, old, b)
             for part in range(2):
@@ -269,7 +286,7 @@
 
 
 def slab_kernel(
-    pml_ref, coeffs_ref, basis_ref, h_in, packed_in, raw_xf_ref, raw_yf_ref,
+    pml_ref, coeffs_ref, basis_ref, h_in, packed_in, near_xf_ref, far_xf_ref, raw_yf_ref,
     h_ref, packed_ref, xf_ref, yt_ref, xadd_ref, yadd_ref, hxf_ref, zf_ref,
 ):
     del h_in, packed_in
@@ -277,7 +294,7 @@
     parts = range(2)
     cells = nz * nx
     both = 2 * vectors
-    turn_face(coeffs_ref, 1, raw_xf_ref, xf_ref)
+    turn_face(coeffs_ref, near_xf_ref, far_xf_ref, xf_ref)
     turn_column(coeffs_ref, raw_yf_ref, yt_ref)
     shx = axis_stretch(pml_ref, 1, nx, one_place(1, nx, nx - 1, (1, ny)) + 0.5)
     shy = axis_stretch(pml_ref, 2, ny, one_place(2, ny, ny - 1, (1, cells)) + 0.5)
@@ -498,12 +515,6 @@
     return values[0]
 
 
-def share_kernel(rows_ref, next_ref):
-    total = tree_sum([rows_ref[device] for device in range(rows_ref.shape[0])])
-    for device in range(next_ref.shape[0]):
-        next_ref[device] = total
-
-
 def gather_kernel(rows_ref, gram_ref):
     _, vectors, _ = gram_ref.shape
     total = tree_sum([rows_ref[device] for device in range(rows_ref.shape[0])])
@@ -523,7 +534,7 @@
 
 
 def rim_kernel(
-    pml_ref, ritz_ref, basis_ref, image_ref, hxf_ref, hyf_ref, residual_hbm, residual_ref, packed_ref, sems
+    pml_ref, ritz_ref, basis_ref, image_ref, near_ref, far_ref, hyf_ref, residual_hbm, residual_ref, packed_ref, sems
 ):
     _, vectors, _, nz, nx, ny = basis_ref.shape
     plane = (nx, ny)
@@ -532,7 +543,8 @@
     sex = axis_stretch(pml_ref, 1, nx, one_place(1, nx, 0, (1, ny)))
     sey = axis_stretch(pml_ref, 2, ny, one_place(2, ny, 0, plane))
     none = jnp.zeros(plane, jnp.float32)
-    sex = tuple(jnp.where(rows == 0, part * has_neighbour(1, -1), none) for part in sex)
+    sex = tuple(jnp.where(rows == 0, part, none) for part in sex)
+    near, far = pair_weights(-1)
     sey = tuple(jnp.where(lanes == 0, part * has_neighbour(2, -1), none) for part in sey)
     rest = jnp.zeros((ny - hyf_ref.shape[0], nz * nx), jnp.float32)
     packed_ref[...] = jnp.concatenate([hyf_ref[...], rest], axis=0).T.reshape(nz, nx, ny)
@@ -551,7 +563,10 @@
                 )
 
             def row(slot, b=b):
-                return tuple(hxf_ref[part, b, slot, pl.ds(z, 1)] for part in range(2))
+                return tuple(
+                    near_ref[part, b, slot, pl.ds(z, 1)] * near + far_ref[part, b, slot, pl.ds(z, 1)] * far
+                    for part in range(2)
+                )
 
             factor = (ritz_ref[0, b], ritz_ref[1, b])
             left = []
@@ -591,7 +606,7 @@
         compiler_params=params,
         name="take_faces",
     )(pltpu.with_memory_space_constraint(fields, pltpu.HBM))
-    xf = passed_round(xf, "gx", -1)
+    near_xf, far_xf = swapped_with_neighbours(xf, "gx")
     yf = passed_round(yf, "gy", -1)
     cells = fields.size // 6 // vectors
 
@@ -612,12 +627,12 @@
     h, packed, xf, yt, xadd, yadd, hxf, zf = pl.pallas_call(
         slab_kernel,
         out_shape=(whole, planes, face, f32(*yf_shape), face, planes, face, f32(*zf_shape)),
-        in_specs=[SMEM] * 2 + [VMEM] * 5,
+        in_specs=[SMEM] * 2 + [VMEM] * 6,
         out_specs=(VMEM,) * 8,
         input_output_aliases={3: 0, 4: 1},
         compiler_params=params,
         name="slab_face",
-    )(pml_width, coeffs, basis, h, packed, xf, yf)
+    )(pml_width, coeffs, basis, h, packed, near_xf, far_xf, yf)
     zf = passed_round(zf, "gz", 1)
     h, image, acc, before, basis_new = pl.pallas_call(
         inner_kernel,
@@ -639,10 +654,12 @@
         compiler_params=params,
         name="last_plane",
     )(sz, zf, h, packed, hxf)
-    first, second = lax.axis_size("gx"), lax.axis_size("gy") * lax.axis_size("gz")
+    near_hxf, far_hxf = swapped_with_neighbours(hxf, "gx")
+    from_y = passed_round(hyf, "gy", 1)
+    devices = lax.axis_size("gx") * lax.axis_size("gy") * lax.axis_size("gz")
     image, gram = pl.pallas_call(
         outer_kernel,
-        out_shape=(whole, f32(first, 2, ny)),
+        out_shape=(whole, pltpu.VMEM((devices, 2, ny), jnp.float32)),
         in_specs=[SMEM] + [VMEM] * 13,
         out_specs=(VMEM,) * 2,
         input_output_aliases={11: 0},
@@ -650,30 +667,17 @@
         cost_estimate=cost(300, 1),
         name="apply_outer",
     )(pml_width, basis, loss, table, sz, h, zf, xf, yt, hxf, hyf, image, acc, before)
-    gram, hxf, hyf = lax.optimization_barrier((gram, hxf, hyf))
-    rows = lax.all_to_all(gram, "gx", 0, 0)
-    from_y = passed_round(hyf, "gy", 1)
-    from_x = passed_round(hxf, "gx", 1)
-    rows, from_y = lax.optimization_barrier((rows, from_y))
-    gram = pl.pallas_call(
-        share_kernel,
-        out_shape=f32(second, 2, ny),
-        in_specs=[VMEM],
-        out_specs=VMEM,
-        compiler_params=params,
-        name="share_rows",
-    )(rows)
-    rows = lax.all_to_all(gram, ("gy", "gz"), 0, 0)
+    rows = lax.all_to_all(gram, ("gx", "gy", "gz"), 0, 0)
     residual = pl.pallas_call(
         rim_kernel,
         out_shape=whole,
-        in_specs=[SMEM] * 2 + [VMEM] * 4,
+        in_specs=[SMEM] * 2 + [VMEM] * 5,
         out_specs=HBM,
         scratch_shapes=[scratch(*fields.shape), scratch(nz, nx, ny), pltpu.SemaphoreType.DMA((nz,))],
         compiler_params=params,
         cost_estimate=cost(200, 3),
         name="add_rims",
-    )(pml_width, ritz, basis, image, from_x, from_y)
+    )(pml_width, ritz, basis, image, near_hxf, far_hxf, from_y)
     rows, residual = lax.optimization_barrier((rows, residual))
     gram = pl.pallas_call(
         gather_kernel,

time: 39.4 us -> 35.1 us (0.89)
  waiting for transfers between devices: 8.69 us -> 4.66 us
  Pallas kernels: 13.5 us -> 12.9 us
  starting transfers between devices: 16.2 us -> 16.6 us
    ppermute x0 -> x4, starting transfers between devices: none -> 8.77 us  [swapped_with_neighbours(): return (lax.ppermute(value, axis, near), lax.ppermute(value, axis, far))]
    all_to_all x2 -> x1, starting transfers between devices: 8.06 us -> 2.87 us  [body(): rows = lax.all_to_all(gram, ('gx', 'gy', 'gz'), 0, 0)]
    ppermute x5 -> x3, starting transfers between devices: 8.13 us -> 4.91 us  [passed_round(): lax.ppermute(value, axis, [(source, (source + steps) % count) for source...]
    all_to_all x2 -> x1, waiting for transfers between devices: 4.34 us -> 1.31 us  [body(): rows = lax.all_to_all(gram, ('gx', 'gy', 'gz'), 0, 0)]
    ppermute x5 -> x3, waiting for transfers between devices: 4.36 us -> 3.34 us  [passed_round(): lax.ppermute(value, axis, [(source, (source + steps) % count) for source...]
    pallas_call x2 -> x1, Pallas kernels: 2.21 us -> 1.62 us  [body(): pl.pallas_call(outer_kernel, out_shape=(whole, pltpu.VMEM((devices, 2, ny...]
  transfers between devices with their start and end apart: 7 -> 8, of which waited for: 4 -> 3; matrix products, arithmetic and copies ran while one was open for 0% -> 0% of each run, Pallas kernels for 21% -> 27%
where the time goes in v10:
time: 35.1 us; the launch traced here: 34.9 us
  starting transfers between devices  16.6 us (47%)
  Pallas kernels  12.9 us (37%)
  waiting for transfers between devices  4.66 us (13%)
  between operations  0.78 us (2%)
    ppermute x4, starting transfers between devices, swapped_with_neighbours(): return (lax.ppermute(value, axis, near), lax.ppermute(value, axis, far))  8.77 us
    ppermute x3, starting transfers between devices, passed_round(): lax.ppermute(value, axis, [(source, (source + steps) % count) for source...  4.91 us
    ppermute x3, waiting for transfers between devices, passed_round(): lax.ppermute(value, axis, [(source, (source + steps) % count) for source...  3.34 us
    pallas_call x1, Pallas kernels, body(): pl.pallas_call(prepare_kernel, out_shape=(whole, whole, whole, planes, f3...  3.16 us
    all_to_all x1, starting transfers between devices, body(): rows = lax.all_to_all(gram, ('gx', 'gy', 'gz'), 0, 0)  2.87 us
    pallas_call x1, Pallas kernels, body(): pl.pallas_call(inner_kernel, out_shape=(whole, whole, f32(vectors, 2 * ve...  2.25 us
    pallas_call x1, Pallas kernels, body(): pl.pallas_call(rim_kernel, out_shape=whole, in_specs=[SMEM] * 2 + [VMEM]...  2.24 us
    pallas_call x1, Pallas kernels, body(): pl.pallas_call(face_kernel, out_shape=(whole, f32(*xf_shape), f32(*yf_sha...  1.64 us
  transfers between devices with their start and end apart: 8, of which 3 were waited for; matrix products, arithmetic and copies ran while one was open for 0% of the time, Pallas kernels for 27%

profile of v10, /device:TPU:0, one launch (start us, length us, event | category | flops | bytes accessed | tf_op | source)
XLA Modules:
  0.0 34.9 jit_solution(10997070277140605245)
XLA Ops:
  0.7 1.6 %take_faces.1 = (f32[2,4,3,8,16,128]{5,4,3,2,1,0:T(8,128)S(1)}, f32[2,4,2,8,128]{4,3,2,1,0:T(8,128)S(1)}, f32[16,128]{1,0:T(8,128)S(1)}) custom-call(f32[2,4,3,8,16,128]{5,4,3,2,1,0:T(8,128)} %fields_hbm.1), custom_call_target="tpu_custom_call" | custom-call | tf_op jit(solution)/shard_map/take_faces/pallas_call | solution.py:600
  2.3 0.7 %collective-permute-start.1 = (f32[2,4,2,8,128]{4,3,2,1,0:T(8,128)S(1)}, f32[2,4,2,8,128]{4,3,2,1,0:T(8,128)S(1)}, u32[]{:S(2)}, u32[]{:S(2)}) collective-permute-start(f32[2,4,2,8,128]{4,3,2,1,0:T(8,128)S(1)} %get-tuple-element.39), channel_id=1, source_target_pairs={{0,0},{4,8},{8,4},{12,16},{16,12},{20,24},{24,20},{28,28},{1,1},{5... | collective-permute-start | bytes 196616 | tf_op jit(solution)/shard_map/ppermute | solution.py:29
  3.0 4.4 %collective-permute-start = (f32[2,4,2,8,128]{4,3,2,1,0:T(8,128)S(1)}, f32[2,4,2,8,128]{4,3,2,1,0:T(8,128)S(1)}, u32[]{:S(2)}, u32[]{:S(2)}) collective-permute-start(f32[2,4,2,8,128]{4,3,2,1,0:T(8,128)S(1)} %get-tuple-element.39), channel_id=1, source_target_pairs={{0,4},{4,0},{8,12},{12,8},{16,20},{20,16},{24,28},{28,24},{1,5},{5... | collective-permute-start | bytes 196616 | tf_op jit(solution)/shard_map/ppermute | solution.py:29
  7.5 1.5 %collective-permute-start.2 = (f32[16,128]{1,0:T(8,128)S(1)}, f32[16,128]{1,0:T(8,128)S(1)}, u32[]{:S(2)}, u32[]{:S(2)}) collective-permute-start(f32[16,128]{1,0:T(8,128)S(1)} %get-tuple-element.40), channel_id=1, source_target_pairs={{0,2},{2,0},{1,3},{3,1},{4,6},{6,4},{5,7},{7,5},{8,10},{10,8},{9,1... | collective-permute-start | bytes 24584 | tf_op jit(solution)/shard_map/ppermute | solution.py:22
  9.0 3.2 %prepare.1 = (f32[2,4,3,8,16,128]{5,4,3,2,1,0:T(8,128)S(1)}, f32[2,4,3,8,16,128]{5,4,3,2,1,0:T(8,128)S(1)}, f32[2,4,3,8,16,128]{5,4,3,2,1,0:T(8,128)S(1)}, f32[8...) custom-call(s32[6]{0:T(128)S(1)} %copy-done.2, f32[4]{0:T(128)S(1)} %copy-done.4, ...), custom_call_target="tpu_custom_call" | custom-call | flops 13107200 | bytes 6291456 | tf_op jit(solution)/shard_map/prepare/pallas_call | solution.py:618
  12.2 0.0 collective-permute-done.2.raw_yf_ref
  12.2 0.0 collective-permute-done.1.far_xf_ref
  12.2 0.0 collective-permute-done.near_xf_ref
  12.2 0.9 %slab_face.1 = (f32[2,4,3,8,16,128]{5,4,3,2,1,0:T(8,128)S(1)}, f32[8,16,128]{2,1,0:T(8,128)S(1)}, f32[2,4,2,8,128]{4,3,2,1,0:T(8,128)S(1)}, f32[16,128]{1,0:T(8,...) custom-call(s32[6]{0:T(128)S(1)} %copy-done.2, ...), custom_call_target="tpu_custom_call", output_to_operand_aliasing={{0}: (3, {}), {1}: (4, {})} | custom-call | tf_op jit(solution)/shard_map/slab_face/pallas_call | solution.py:627
  13.1 1.6 %collective-permute-start.3 = (f32[2,4,2,16,128]{4,3,2,1,0:T(8,128)S(1)}, f32[2,4,2,16,128]{4,3,2,1,0:T(8,128)S(1)}, u32[]{:S(2)}, u32[]{:S(2)}) collective-permute-start(f32[2,4,2,16,128]{4,3,2,1,0:T(8,128)S(1)} %get-tuple-element.45), channel_id=1, source_target_pairs={{0,1},{1,0},{2,3},{3,2},{4,5},{5,4},{6,7},{7,6},{8,9},{9,8},{10,11... | collective-permute-start | bytes 393224 | tf_op jit(solution)/shard_map/ppermute | solution.py:22
  14.7 2.2 %apply_inner.1 = (f32[2,4,3,8,16,128]{5,4,3,2,1,0:T(8,128)S(1)}, f32[2,4,3,8,16,128]{5,4,3,2,1,0:T(8,128)S(1)}, f32[4,8,8,128]{3,2,1,0:T(8,128)S(1)}, f32[2,4,2,...) custom-call(f32[2,4,3,8,16,128]{5,4,3,2,1,0:T(8,128)S(1)} %get-tuple-element.33.basis_ref, ...), custom_call_target="tpu_custom_call", output_to_operand_aliasing={{0}: (4, {})} | custom-call | flops 13107200 | bytes 3145728 | tf_op jit(solution)/shard_map/apply_inner/pallas_call | solution.py:637
  17.0 1.5 %collective-permute-done.3.zf_ref = f32[2,4,2,16,128]{4,3,2,1,0:T(8,128)S(1)} collective-permute-done((f32[2,4,2,16,128]{4,3,2,1,0:T(8,128)S(1)}, f32[2,4,2,16,128]{4,3,2,1,0:T(8,128)S(1)}, u32[]{:S(2)}, u32[]{:S(2)}) %collective-permute-start.3) | collective-permute-done | bytes 131104 | tf_op jit(solution)/shard_map/ppermute | solution.py:22
  18.4 0.1 last_plane.1
  18.5 0.7 %collective-permute-start.5 = (f32[2,4,2,8,128]{4,3,2,1,0:T(8,128)S(1)}, f32[2,4,2,8,128]{4,3,2,1,0:T(8,128)S(1)}, u32[]{:S(2)}, u32[]{:S(2)}) collective-permute-start(f32[2,4,2,8,128]{4,3,2,1,0:T(8,128)S(1)} %get-tuple-element.52.hxf_ref), channel_id=1, source_target_pairs={{0,0},{4,8},{8,4},{12,16},{16,12},{20,24},{24,20},{28,28},{1,1},{5... | collective-permute-start | bytes 196616 | tf_op jit(solution)/shard_map/ppermute | solution.py:29
  19.2 3.0 %collective-permute-start.4 = (f32[2,4,2,8,128]{4,3,2,1,0:T(8,128)S(1)}, f32[2,4,2,8,128]{4,3,2,1,0:T(8,128)S(1)}, u32[]{:S(2)}, u32[]{:S(2)}) collective-permute-start(f32[2,4,2,8,128]{4,3,2,1,0:T(8,128)S(1)} %get-tuple-element.52.hxf_ref), channel_id=1, source_target_pairs={{0,4},{4,0},{8,12},{12,8},{16,20},{20,16},{24,28},{28,24},{1,5},{5... | collective-permute-start | bytes 196616 | tf_op jit(solution)/shard_map/ppermute | solution.py:29
  22.2 1.6 %apply_outer.1 = (f32[2,4,3,8,16,128]{5,4,3,2,1,0:T(8,128)S(1)}, f32[32,2,128]{2,1,0:T(2,128)}) custom-call(s32[6]{0:T(128)S(1)} %copy-done.2, f32[2,4,3,8,16,128]{5,4,3,2,1,0:T(8,128)S(1)} %get-tuple-element.33.basis_ref, f32[2,4,3,8,16,128]{5,4,3,2,1,0:T(8,128)S(1)} %get-tuple-element.34.loss_ref, ...), custom_call_target="tpu_custom_call", output_to_operand_aliasing={{0}: (11, {})} | custom-call | flops 4915200 | bytes 1572864 | tf_op jit(solution)/shard_map/apply_outer/pallas_call | solution.py:660
  23.8 2.9 %all-to-all-start = ((f32[32,2,128]{2,1,0:T(2,128)}), f32[32,2,128]{2,1,0:T(2,128)S(1)}, u32[]{:S(2)}, u32[]{:S(2)}) async-start(f32[32,2,128]{2,1,0:T(2,128)} %get-tuple-element.57), calls=%async_computation | async-start | bytes 65536 | tf_op jit(solution)/shard_map/all_to_all | solution.py:670
  26.7 1.8 %collective-permute-start.6 = (f32[16,128]{1,0:T(8,128)S(1)}, f32[16,128]{1,0:T(8,128)S(1)}, u32[]{:S(2)}, u32[]{:S(2)}) collective-permute-start(f32[16,128]{1,0:T(8,128)S(1)} %get-tuple-element.53.hyf_ref), channel_id=1, source_target_pairs={{0,2},{2,0},{1,3},{3,1},{4,6},{6,4},{5,7},{7,5},{8,10},{10,8},{9,1... | collective-permute-start | bytes 24584 | tf_op jit(solution)/shard_map/ppermute | solution.py:22
  28.6 1.9 %collective-permute-done.6.hyf_ref = f32[16,128]{1,0:T(8,128)S(1)} collective-permute-done((f32[16,128]{1,0:T(8,128)S(1)}, f32[16,128]{1,0:T(8,128)S(1)}, u32[]{:S(2)}, u32[]{:S(2)}) %collective-permute-start.6) | collective-permute-done | bytes 8224 | tf_op jit(solution)/shard_map/ppermute | solution.py:22
  30.4 0.0 collective-permute-done.5.far_ref
  30.4 0.0 collective-permute-done.4.near_ref
  30.4 2.2 %add_rims.1 = f32[2,4,3,8,16,128]{5,4,3,2,1,0:T(8,128)} custom-call(s32[6]{0:T(128)S(1)} %copy-done.2, f32[2,4]{1,0:T(2,128)S(1)} %copy-done.3, f32[2,4,3,8,16,128]{5,4,3,2,1,0:T(8,128)S(1)} %get-tuple-element.33.basis_ref, f32[2,4,3,8,16,128]{5,4,3,2,1,0:T(8,128)S(1)} %get-tuple-element.58.image_ref, ...), custom_call_target="tpu_custom_call" | custom-call | flops 3276800 | bytes 4718592 | tf_op jit(solution)/shard_map/add_rims/pallas_call | solution.py:671
  32.7 1.3 %all-to-all-done.rows_ref = f32[32,2,128]{2,1,0:T(2,128)S(1)} async-done(((f32[32,2,128]{2,1,0:T(2,128)}), f32[32,2,128]{2,1,0:T(2,128)S(1)}, u32[]{:S(2)}, u32[]{:S(2)}) %all-to-all-start) | async-done | bytes 32800 | tf_op jit(solution)/shard_map/all_to_all | solution.py:670
  34.0 0.9 %sum_rows.1 = f32[2,4,4]{2,1,0:T(4,128)} custom-call(f32[32,2,128]{2,1,0:T(2,128)S(1)} %all-to-all-done.rows_ref), custom_call_target="tpu_custom_call" | custom-call | tf_op jit(solution)/shard_map/sum_rows/pallas_call | solution.py:682
  (12 shorter events, 0.0 us)
Async XLA Ops:
  0.6 8.3 %copy-start.2 = (s32[6]{0:T(128)S(1)}, s32[6]{0:T(128)}, u32[]{:S(2)}) copy-start(s32[6]{0:T(128)} %pml_ref.7) | copy-start | bytes 76
  0.6 8.3 %copy-start.1 = (f32[2,4,4]{2,1,0:T(4,128)S(1)}, f32[2,4,4]{2,1,0:T(4,128)}, u32[]{:S(2)}) copy-start(f32[2,4,4]{2,1,0:T(4,128)} %coeffs_ref.3) | copy-start | bytes 388
  0.7 8.3 %copy-start.5 = (f32[4]{0:T(128)S(1)}, f32[4]{0:T(128)}, u32[]{:S(2)}) copy-start(f32[4]{0:T(128)} %eps_loss_ref.1) | copy-start | bytes 52
  0.7 8.3 %copy-start.4 = (f32[4]{0:T(128)S(1)}, f32[4]{0:T(128)}, u32[]{:S(2)}) copy-start(f32[4]{0:T(128)} %eps_real_ref.1) | copy-start | bytes 52
  0.7 8.3 %copy-start = (s32[8,16,128]{2,1,0:T(8,128)S(1)}, s32[8,16,128]{2,1,0:T(8,128)}, u32[]{:S(2)}) copy-start(s32[8,16,128]{2,1,0:T(8,128)} %material_ref.1) | copy-start | bytes 196612
  2.3 9.8 %collective-permute-start.1 = (f32[2,4,2,8,128]{4,3,2,1,0:T(8,128)S(1)}, f32[2,4,2,8,128]{4,3,2,1,0:T(8,128)S(1)}, u32[]{:S(2)}, u32[]{:S(2)}) collective-permute-start(f32[2,4,2,8,128]{4,3,2,1,0:T(8,128)S(1)} %get-tuple-element.39), channel_id=1, source_target_pairs={{0,0},{4,8},{8,4},{12,16},{16,12},{20,24},{24,20},{28,28},{1,1},{5... | collective-permute-start | bytes 196616 | tf_op jit(solution)/shard_map/ppermute | solution.py:29
  3.0 9.2 %collective-permute-start = (f32[2,4,2,8,128]{4,3,2,1,0:T(8,128)S(1)}, f32[2,4,2,8,128]{4,3,2,1,0:T(8,128)S(1)}, u32[]{:S(2)}, u32[]{:S(2)}) collective-permute-start(f32[2,4,2,8,128]{4,3,2,1,0:T(8,128)S(1)} %get-tuple-element.39), channel_id=1, source_target_pairs={{0,4},{4,0},{8,12},{12,8},{16,20},{20,16},{24,28},{28,24},{1,5},{5... | collective-permute-start | bytes 196616 | tf_op jit(solution)/shard_map/ppermute | solution.py:29
  7.5 4.7 %collective-permute-start.2 = (f32[16,128]{1,0:T(8,128)S(1)}, f32[16,128]{1,0:T(8,128)S(1)}, u32[]{:S(2)}, u32[]{:S(2)}) collective-permute-start(f32[16,128]{1,0:T(8,128)S(1)} %get-tuple-element.40), channel_id=1, source_target_pairs={{0,2},{2,0},{1,3},{3,1},{4,6},{6,4},{5,7},{7,5},{8,10},{10,8},{9,1... | collective-permute-start | bytes 24584 | tf_op jit(solution)/shard_map/ppermute | solution.py:22
  13.1 5.3 %collective-permute-start.3 = (f32[2,4,2,16,128]{4,3,2,1,0:T(8,128)S(1)}, f32[2,4,2,16,128]{4,3,2,1,0:T(8,128)S(1)}, u32[]{:S(2)}, u32[]{:S(2)}) collective-permute-start(f32[2,4,2,16,128]{4,3,2,1,0:T(8,128)S(1)} %get-tuple-element.45), channel_id=1, source_target_pairs={{0,1},{1,0},{2,3},{3,2},{4,5},{5,4},{6,7},{7,6},{8,9},{9,8},{10,11... | collective-permute-start | bytes 393224 | tf_op jit(solution)/shard_map/ppermute | solution.py:22
  18.5 11.9 %collective-permute-start.5 = (f32[2,4,2,8,128]{4,3,2,1,0:T(8,128)S(1)}, f32[2,4,2,8,128]{4,3,2,1,0:T(8,128)S(1)}, u32[]{:S(2)}, u32[]{:S(2)}) collective-permute-start(f32[2,4,2,8,128]{4,3,2,1,0:T(8,128)S(1)} %get-tuple-element.52.hxf_ref), channel_id=1, source_target_pairs={{0,0},{4,8},{8,4},{12,16},{16,12},{20,24},{24,20},{28,28},{1,1},{5... | collective-permute-start | bytes 196616 | tf_op jit(solution)/shard_map/ppermute | solution.py:29
  19.2 11.2 %collective-permute-start.4 = (f32[2,4,2,8,128]{4,3,2,1,0:T(8,128)S(1)}, f32[2,4,2,8,128]{4,3,2,1,0:T(8,128)S(1)}, u32[]{:S(2)}, u32[]{:S(2)}) collective-permute-start(f32[2,4,2,8,128]{4,3,2,1,0:T(8,128)S(1)} %get-tuple-element.52.hxf_ref), channel_id=1, source_target_pairs={{0,4},{4,0},{8,12},{12,8},{16,20},{20,16},{24,28},{28,24},{1,5},{5... | collective-permute-start | bytes 196616 | tf_op jit(solution)/shard_map/ppermute | solution.py:29
  22.2 8.2 %copy-start.3 = (f32[2,4]{1,0:T(2,128)S(1)}, f32[2,4]{1,0:T(2,128)}, u32[]{:S(2)}) copy-start(f32[2,4]{1,0:T(2,128)} %ritz_ref.1) | copy-start | bytes 100
  23.8 10.2 %all-to-all-start = ((f32[32,2,128]{2,1,0:T(2,128)}), f32[32,2,128]{2,1,0:T(2,128)S(1)}, u32[]{:S(2)}, u32[]{:S(2)}) async-start(f32[32,2,128]{2,1,0:T(2,128)} %get-tuple-element.57), calls=%async_computation | async-start | bytes 65536 | tf_op jit(solution)/shard_map/all_to_all | solution.py:670
  26.7 3.7 %collective-permute-start.6 = (f32[16,128]{1,0:T(8,128)S(1)}, f32[16,128]{1,0:T(8,128)S(1)}, u32[]{:S(2)}, u32[]{:S(2)}) collective-permute-start(f32[16,128]{1,0:T(8,128)S(1)} %get-tuple-element.53.hyf_ref), channel_id=1, source_target_pairs={{0,2},{2,0},{1,3},{3,1},{4,6},{6,4},{5,7},{7,5},{8,10},{10,8},{9,1... | collective-permute-start | bytes 24584 | tf_op jit(solution)/shard_map/ppermute | solution.py:22

commit v11 on v9

--- a/solution.py
+++ b/solution.py
@@ -320,7 +320,9 @@
                     zf_ref[part, b, comp, cut] = jnp.where(lower, h[comp][part], basis_ref[part, b, comp, 0, cut])
 
 
-def plane_step(b, z, before, sums, basis_ref, loss_ref, table_ref, sz_ref, h_ref, image_ref, halos=None):
+def plane_step(
+    b, z, before, sums, ritz_ref, basis_ref, loss_ref, table_ref, sz_ref, h_ref, left_ref, halos=None
+):
     _, vectors, _, _, nx, ny = basis_ref.shape
     rows = lax.broadcasted_iota(jnp.int32, (SUB, ny), 0)
     lanes = lax.broadcasted_iota(jnp.int32, (SUB, ny), 1)
@@ -359,8 +361,9 @@
         curl = (sub(byz, bzy), sub(bzx, bxz), sub(bxy, byx))
         w = [add(curl[comp], field_of(loss_ref, b, comp, z, cut)) for comp in range(3)]
         for comp in range(3):
+            left = sub(w[comp], cmul((ritz_ref[0, b], ritz_ref[1, b]), field_of(basis_ref, b, comp, z, cut)))
             for part in parts:
-                image_ref[part, b, comp, z, cut] = w[comp][part]
+                left_ref[part, b, comp, z, cut] = left[part]
         for a in range(vectors):
             total = sums[a]
             for comp in range(3):
@@ -370,8 +373,8 @@
 
 
 def inner_kernel(
-    basis_ref, loss_ref, table_ref, sz_ref, h_in, xadd_ref, yadd_ref,
-    h_ref, image_ref, acc_ref, before_ref, basis_hbm, sem,
+    ritz_ref, basis_ref, loss_ref, table_ref, sz_ref, h_in, xadd_ref, yadd_ref,
+    h_ref, left_ref, acc_ref, before_ref, basis_hbm, sem,
 ):
     del h_in
     _, vectors, _, nz, nx, ny = basis_ref.shape
@@ -389,7 +392,7 @@
             ]
             sums = [(acc_ref[b, a], acc_ref[b, vectors + a]) for a in range(vectors)]
             before, sums = plane_step(
-                b, z, before, sums, basis_ref, loss_ref, table_ref, sz_ref, h_ref, image_ref, (xadd_ref, yadd_ref)
+                b, z, before, sums, ritz_ref, basis_ref, loss_ref, table_ref, sz_ref, h_ref, left_ref, (xadd_ref, yadd_ref)
             )
             for part in range(2):
                 for a in range(vectors):
@@ -426,10 +429,10 @@
 
 
 def outer_kernel(
-    pml_ref, basis_ref, loss_ref, table_ref, sz_ref, h_ref, zf_ref, xf_ref, yt_ref, hxf_ref, hyf_ref,
-    image_in, acc_ref, before_ref, image_ref, gram_ref,
+    pml_ref, ritz_ref, basis_ref, loss_ref, table_ref, sz_ref, h_ref, zf_ref, xf_ref, yt_ref, hxf_ref, hyf_ref,
+    left_in, acc_ref, before_ref, left_ref, gram_ref,
 ):
-    del image_in
+    del left_in
     _, vectors, _, nz, nx, ny = basis_ref.shape
     parts = range(2)
     cuts = tiles_of(nx)
@@ -451,7 +454,7 @@
         before = [tuple(tile_of(before_ref, slot, cut) for slot in range(2)) for cut in cuts]
         sums = [(acc_ref[b, a], acc_ref[b, vectors + a]) for a in range(vectors)]
         _, sums = plane_step(
-            b, nz - 1, before, sums, basis_ref, loss_ref, table_ref, sz_ref, h_ref, image_ref
+            b, nz - 1, before, sums, ritz_ref, basis_ref, loss_ref, table_ref, sz_ref, h_ref, left_ref
         )
         for cut in cuts:
             ex, ey = (field_of(basis_ref, b, comp, 0, cut) for comp in range(2))
@@ -459,8 +462,8 @@
             hy = add(tile_of(zf_ref, 1, cut), cmul(under, ex))
             more = (cmul(sez, hy), cmul(sez, hx))
             for part in parts:
-                image_ref[part, b, 0, 0, cut] = image_ref[part, b, 0, 0, cut] + more[0][part]
-                image_ref[part, b, 1, 0, cut] = image_ref[part, b, 1, 0, cut] - more[1][part]
+                left_ref[part, b, 0, 0, cut] = left_ref[part, b, 0, 0, cut] + more[0][part]
+                left_ref[part, b, 1, 0, cut] = left_ref[part, b, 1, 0, cut] - more[1][part]
             for a in range(vectors):
                 ex, ey = (field_of(basis_ref, a, comp, 0, cut) for comp in range(2))
                 sums[a] = add(sums[a], sub(cmul(ex, more[0]), cmul(ey, more[1])))
@@ -498,12 +501,6 @@
     return values[0]
 
 
-def share_kernel(rows_ref, next_ref):
-    total = tree_sum([rows_ref[device] for device in range(rows_ref.shape[0])])
-    for device in range(next_ref.shape[0]):
-        next_ref[device] = total
-
-
 def gather_kernel(rows_ref, gram_ref):
     _, vectors, _ = gram_ref.shape
     total = tree_sum([rows_ref[device] for device in range(rows_ref.shape[0])])
@@ -522,50 +519,55 @@
             gram_ref[part, a:a + 1] = matrix_row[part:part + 1, :vectors]
 
 
-def rim_kernel(
-    pml_ref, ritz_ref, basis_ref, image_ref, hxf_ref, hyf_ref, residual_hbm, residual_ref, packed_ref, sems
-):
-    _, vectors, _, nz, nx, ny = basis_ref.shape
-    plane = (nx, ny)
-    rows = lax.broadcasted_iota(jnp.int32, plane, 0)
-    lanes = lax.broadcasted_iota(jnp.int32, plane, 1)
-    sex = axis_stretch(pml_ref, 1, nx, one_place(1, nx, 0, (1, ny)))
-    sey = axis_stretch(pml_ref, 2, ny, one_place(2, ny, 0, plane))
-    none = jnp.zeros(plane, jnp.float32)
-    sex = tuple(jnp.where(rows == 0, part * has_neighbour(1, -1), none) for part in sex)
-    sey = tuple(jnp.where(lanes == 0, part * has_neighbour(2, -1), none) for part in sey)
-    rest = jnp.zeros((ny - hyf_ref.shape[0], nz * nx), jnp.float32)
-    packed_ref[...] = jnp.concatenate([hyf_ref[...], rest], axis=0).T.reshape(nz, nx, ny)
+def rim_kernel(pml_ref, left_in, hxf_ref, hyf_ref, left_ref, residual_hbm, xadd_ref, yadd_ref, sems):
+    del left_in
+    _, vectors, _, nz, nx, ny = left_ref.shape
+    parts = range(2)
+    both = 2 * vectors
+    sex = axis_stretch(pml_ref, 1, nx, one_place(1, nx, 0, (nz, ny)))
+    sex = tuple(part * has_neighbour(1, -1) for part in sex)
+    sey = axis_stretch(pml_ref, 2, ny, one_place(2, ny, 0, (vectors, nz * nx)))
+    sey = tuple(part * has_neighbour(2, -1) for part in sey)
+    for b in range(vectors):
+        for slot in range(2):
+            value = cmul(sex, tuple(hxf_ref[part, b, slot] for part in parts))
+            for part in parts:
+                xadd_ref[part, b, slot] = value[part] if slot else -value[part]
+    added = []
+    for slot in range(2):
+        first = slot * both
+        value = cmul(sey, (hyf_ref[first:first + vectors], hyf_ref[first + vectors:first + both]))
+        added += [part if slot else -part for part in value]
+    rest = jnp.zeros((ny - 2 * both, nz * nx), jnp.float32)
+    yadd_ref[...] = jnp.concatenate(added + [rest], axis=0).T.reshape(nz, nx, ny)
+    rows = lax.broadcasted_iota(jnp.int32, (SUB, ny), 0)
+    lanes = lax.broadcasted_iota(jnp.int32, (SUB, ny), 1)
 
     def kept(z):
-        return pltpu.make_async_copy(residual_ref.at[:, :, :, z], residual_hbm.at[:, :, :, z], sems.at[z])
+        return pltpu.make_async_copy(left_ref.at[:, :, :, z], residual_hbm.at[:, :, :, z], sems.at[z])
 
     @pl.loop(0, nz)
     def _(z):
-        packed = packed_ref[z]
-        for b in range(vectors):
-
-            def column(slot, b=b):
-                return tuple(
-                    pltpu.roll(packed, (ny - packed_row(slot, part, b, vectors)) % ny, 1) for part in range(2)
-                )
-
-            def row(slot, b=b):
-                return tuple(hxf_ref[part, b, slot, pl.ds(z, 1)] for part in range(2))
-
-            factor = (ritz_ref[0, b], ritz_ref[1, b])
-            left = []
-            for comp in range(3):
-                u = (basis_ref[0, b, comp, z], basis_ref[1, b, comp, z])
-                w = (image_ref[0, b, comp, z], image_ref[1, b, comp, z])
-                left.append(sub(w, cmul(factor, u)))
-            left[0] = sub(left[0], cmul(sey, column(0)))
-            left[2] = add(left[2], cmul(sey, column(1)))
-            left[1] = add(left[1], cmul(sex, row(1)))
-            left[2] = sub(left[2], cmul(sex, row(0)))
-            for comp in range(3):
-                for part in range(2):
-                    residual_ref[part, b, comp, z] = left[comp][part]
+        for cut in tiles_of(nx):
+            column = yadd_ref[z, cut]
+            for b in range(vectors):
+                for part in parts:
+
+                    def turned(slot, b=b, part=part):
+                        row = packed_row(slot, part, b, vectors)
+                        value = pltpu.roll(column, ny - row, 1) if row else column
+                        return jnp.where(lanes == 0, value, 0.0)
+
+                    def row_of(slot, b=b, part=part):
+                        return jnp.where(rows == 0, xadd_ref[part, b, slot, pl.ds(z, 1)], 0.0)
+
+                    ex = left_ref[part, b, 0, z, cut] + turned(0)
+                    ez = left_ref[part, b, 2, z, cut] + turned(1)
+                    if cut.start == 0:
+                        left_ref[part, b, 1, z, cut] = left_ref[part, b, 1, z, cut] + row_of(1)
+                        ez = ez + row_of(0)
+                    left_ref[part, b, 0, z, cut] = ex
+                    left_ref[part, b, 2, z, cut] = ez
         kept(z).start()
 
     @pl.loop(0, nz)
@@ -619,17 +621,17 @@
         name="slab_face",
     )(pml_width, coeffs, basis, h, packed, xf, yf)
     zf = passed_round(zf, "gz", 1)
-    h, image, acc, before, basis_new = pl.pallas_call(
+    h, left, acc, before, basis_new = pl.pallas_call(
         inner_kernel,
         out_shape=(whole, whole, f32(vectors, 2 * vectors, SUB, ny), f32(*zf_shape), whole),
-        in_specs=[VMEM] * 7,
+        in_specs=[SMEM] + [VMEM] * 7,
         out_specs=(VMEM,) * 4 + (HBM,),
         scratch_shapes=[pltpu.SemaphoreType.DMA],
-        input_output_aliases={4: 0},
+        input_output_aliases={5: 0},
         compiler_params=params,
         cost_estimate=cost(800, 2),
         name="apply_inner",
-    )(basis, loss, table, sz, h, xadd, yadd)
+    )(ritz, basis, loss, table, sz, h, xadd, yadd)
     h, hxf, hyf = pl.pallas_call(
         last_plane_kernel,
         out_shape=(whole, face, f32(*yf_shape)),
@@ -639,41 +641,32 @@
         compiler_params=params,
         name="last_plane",
     )(sz, zf, h, packed, hxf)
-    first, second = lax.axis_size("gx"), lax.axis_size("gy") * lax.axis_size("gz")
-    image, gram = pl.pallas_call(
+    devices = lax.axis_size("gx") * lax.axis_size("gy") * lax.axis_size("gz")
+    left, gram = pl.pallas_call(
         outer_kernel,
-        out_shape=(whole, f32(first, 2, ny)),
-        in_specs=[SMEM] + [VMEM] * 13,
+        out_shape=(whole, pltpu.VMEM((devices, 2, ny), jnp.float32)),
+        in_specs=[SMEM] * 2 + [VMEM] * 13,
         out_specs=(VMEM,) * 2,
-        input_output_aliases={11: 0},
+        input_output_aliases={12: 0},
         compiler_params=params,
         cost_estimate=cost(300, 1),
         name="apply_outer",
-    )(pml_width, basis, loss, table, sz, h, zf, xf, yt, hxf, hyf, image, acc, before)
+    )(pml_width, ritz, basis, loss, table, sz, h, zf, xf, yt, hxf, hyf, left, acc, before)
     gram, hxf, hyf = lax.optimization_barrier((gram, hxf, hyf))
-    rows = lax.all_to_all(gram, "gx", 0, 0)
+    rows = lax.all_to_all(gram, ("gx", "gy", "gz"), 0, 0)
+    from_x = passed_round(hxf, "gx", 1)
     from_y = passed_round(hyf, "gy", 1)
-    from_x = passed_round(hxf, "gx", 1)
-    rows, from_y = lax.optimization_barrier((rows, from_y))
-    gram = pl.pallas_call(
-        share_kernel,
-        out_shape=f32(second, 2, ny),
-        in_specs=[VMEM],
-        out_specs=VMEM,
-        compiler_params=params,
-        name="share_rows",
-    )(rows)
-    rows = lax.all_to_all(gram, ("gy", "gz"), 0, 0)
-    residual = pl.pallas_call(
+    _, residual = pl.pallas_call(
         rim_kernel,
-        out_shape=whole,
-        in_specs=[SMEM] * 2 + [VMEM] * 4,
-        out_specs=HBM,
-        scratch_shapes=[scratch(*fields.shape), scratch(nz, nx, ny), pltpu.SemaphoreType.DMA((nz,))],
-        compiler_params=params,
-        cost_estimate=cost(200, 3),
+        out_shape=(whole, whole),
+        in_specs=[SMEM] + [VMEM] * 3,
+        out_specs=(VMEM, HBM),
+        scratch_shapes=[scratch(*xf_shape), scratch(nz, nx, ny), pltpu.SemaphoreType.DMA((nz,))],
+        input_output_aliases={1: 0},
+        compiler_params=params,
+        cost_estimate=pl.CostEstimate(flops=0, bytes_accessed=0, transcendentals=0),
         name="add_rims",
-    )(pml_width, ritz, basis, image, from_x, from_y)
+    )(pml_width, left, from_x, from_y)
     rows, residual = lax.optimization_barrier((rows, residual))
     gram = pl.pallas_call(
         gather_kernel,

time: 39.4 us -> 32.6 us (0.83)
  waiting for transfers between devices: 8.69 us -> 3.8 us
  starting transfers between devices: 16.2 us -> 14.3 us
    all_to_all x2 -> x1, starting transfers between devices: 8.06 us -> 4.83 us  [body(): rows = lax.all_to_all(gram, ('gx', 'gy', 'gz'), 0, 0)]
    all_to_all x2 -> x1, waiting for transfers between devices: 4.34 us -> 1.31 us  [body(): rows = lax.all_to_all(gram, ('gx', 'gy', 'gz'), 0, 0)]
    ppermute x5, waiting for transfers between devices: 4.36 us -> 2.48 us  [passed_round(): lax.ppermute(value, axis, [(source, (source + steps) % count) for source...]
    ppermute x5, starting transfers between devices: 8.13 us -> 9.45 us  [passed_round(): lax.ppermute(value, axis, [(source, (source + steps) % count) for source...]
    pallas_call x1, Pallas kernels: 2.26 us -> 2.87 us  [body(): pl.pallas_call(inner_kernel, out_shape=(whole, whole, f32(vectors, 2 * ve...]
    pallas_call x3 -> x2, Pallas kernels: 4.44 us -> 3.93 us  [the longest x1 2.25 us: body(): pl.pallas_call(rim_kernel, out_shape=(whole, whole), in_specs=[SMEM] + [V...]
  transfers between devices with their start and end apart: 7 -> 6, of which waited for: 4 -> 3; matrix products, arithmetic and copies ran while one was open for 0% -> 0% of each run, Pallas kernels for 21% -> 26%
where the time goes in v11:
time: 32.6 us; the launch traced here: 32.4 us
  starting transfers between devices  14.3 us (44%)
  Pallas kernels  13.6 us (42%)
  waiting for transfers between devices  3.8 us (12%)
  between operations  0.76 us (2%)
    ppermute x5, starting transfers between devices, passed_round(): lax.ppermute(value, axis, [(source, (source + steps) % count) for source...  9.45 us
    all_to_all x1, starting transfers between devices, body(): rows = lax.all_to_all(gram, ('gx', 'gy', 'gz'), 0, 0)  4.83 us
    pallas_call x1, Pallas kernels, body(): pl.pallas_call(prepare_kernel, out_shape=(whole, whole, whole, planes, f3...  3.16 us
    pallas_call x1, Pallas kernels, body(): pl.pallas_call(inner_kernel, out_shape=(whole, whole, f32(vectors, 2 * ve...  2.87 us
    ppermute x5, waiting for transfers between devices, passed_round(): lax.ppermute(value, axis, [(source, (source + steps) % count) for source...  2.48 us
    pallas_call x1, Pallas kernels, body(): pl.pallas_call(rim_kernel, out_shape=(whole, whole), in_specs=[SMEM] + [V...  2.25 us
    pallas_call x1, Pallas kernels, body(): pl.pallas_call(outer_kernel, out_shape=(whole, pltpu.VMEM((devices, 2, ny...  1.68 us
    pallas_call x1, Pallas kernels, body(): pl.pallas_call(face_kernel, out_shape=(whole, f32(*xf_shape), f32(*yf_sha...  1.64 us
  transfers between devices with their start and end apart: 6, of which 3 were waited for; matrix products, arithmetic and copies ran while one was open for 0% of the time, Pallas kernels for 26%

profile of v11, /device:TPU:0, one launch (start us, length us, event | category | flops | bytes accessed | tf_op | source)
XLA Modules:
  0.0 32.4 jit_solution(5641384920257497113)
XLA Ops:
  0.6 0.0 copy-start.2
  0.6 0.0 copy-start.1
  0.7 0.0 copy-start.5
  0.7 1.6 %take_faces.1 = (f32[2,4,3,8,16,128]{5,4,3,2,1,0:T(8,128)S(1)}, f32[2,4,2,8,128]{4,3,2,1,0:T(8,128)S(1)}, f32[16,128]{1,0:T(8,128)S(1)}) custom-call(f32[2,4,3,8,16,128]{5,4,3,2,1,0:T(8,128)} %fields_hbm.1), custom_call_target="tpu_custom_call" | custom-call | tf_op jit(solution)/shard_map/take_faces/pallas_call | solution.py:587
  2.3 4.5 %collective-permute-start = (f32[2,4,2,8,128]{4,3,2,1,0:T(8,128)S(1)}, f32[2,4,2,8,128]{4,3,2,1,0:T(8,128)S(1)}, u32[]{:S(2)}, u32[]{:S(2)}) collective-permute-start(f32[2,4,2,8,128]{4,3,2,1,0:T(8,128)S(1)} %get-tuple-element.43), channel_id=1, source_target_pairs={{0,28},{4,0},{8,4},{12,8},{16,12},{20,16},{24,20},{28,24},{1,29},{... | collective-permute-start | bytes 196616 | tf_op jit(solution)/shard_map/ppermute | solution.py:22
  6.9 1.5 %collective-permute-start.1 = (f32[16,128]{1,0:T(8,128)S(1)}, f32[16,128]{1,0:T(8,128)S(1)}, u32[]{:S(2)}, u32[]{:S(2)}) collective-permute-start(f32[16,128]{1,0:T(8,128)S(1)} %get-tuple-element.44), channel_id=1, source_target_pairs={{0,2},{2,0},{1,3},{3,1},{4,6},{6,4},{5,7},{7,5},{8,10},{10,8},{9,1... | collective-permute-start | bytes 24584 | tf_op jit(solution)/shard_map/ppermute | solution.py:22
  8.4 3.2 %prepare.1 = (f32[2,4,3,8,16,128]{5,4,3,2,1,0:T(8,128)S(1)}, f32[2,4,3,8,16,128]{5,4,3,2,1,0:T(8,128)S(1)}, f32[2,4,3,8,16,128]{5,4,3,2,1,0:T(8,128)S(1)}, f32[8...) custom-call(s32[6]{0:T(128)S(1)} %copy-done.2, f32[4]{0:T(128)S(1)} %copy-done.4, ...), custom_call_target="tpu_custom_call" | custom-call | flops 13107200 | bytes 6291456 | tf_op jit(solution)/shard_map/prepare/pallas_call | solution.py:605
  11.6 0.0 collective-permute-done.1.raw_yf_ref
  11.6 0.0 collective-permute-done.raw_xf_ref
  11.6 0.0 copy-start.3
  11.6 0.9 %slab_face.1 = (f32[2,4,3,8,16,128]{5,4,3,2,1,0:T(8,128)S(1)}, f32[8,16,128]{2,1,0:T(8,128)S(1)}, f32[2,4,2,8,128]{4,3,2,1,0:T(8,128)S(1)}, f32[16,128]{1,0:T(8,...) custom-call(s32[6]{0:T(128)S(1)} %copy-done.2, ...), custom_call_target="tpu_custom_call", output_to_operand_aliasing={{0}: (3, {}), {1}: (4, {})} | custom-call | tf_op jit(solution)/shard_map/slab_face/pallas_call | solution.py:614
  12.6 1.6 %collective-permute-start.2 = (f32[2,4,2,16,128]{4,3,2,1,0:T(8,128)S(1)}, f32[2,4,2,16,128]{4,3,2,1,0:T(8,128)S(1)}, u32[]{:S(2)}, u32[]{:S(2)}) collective-permute-start(f32[2,4,2,16,128]{4,3,2,1,0:T(8,128)S(1)} %get-tuple-element.49), channel_id=1, source_target_pairs={{0,1},{1,0},{2,3},{3,2},{4,5},{5,4},{6,7},{7,6},{8,9},{9,8},{10,11... | collective-permute-start | bytes 393224 | tf_op jit(solution)/shard_map/ppermute | solution.py:22
  14.1 2.9 %apply_inner.1 = (f32[2,4,3,8,16,128]{5,4,3,2,1,0:T(8,128)S(1)}, f32[2,4,3,8,16,128]{5,4,3,2,1,0:T(8,128)S(1)}, f32[4,8,8,128]{3,2,1,0:T(8,128)S(1)}, f32[2,4,2,...) custom-call(f32[2,4]{1,0:T(2,128)S(1)} %copy-done.3, ...), custom_call_target="tpu_custom_call", output_to_operand_aliasing={{0}: (5, {})} | custom-call | flops 13107200 | bytes 3145728 | tf_op jit(solution)/shard_map/apply_inner/pallas_call | solution.py:624
  17.0 0.6 %collective-permute-done.2.zf_ref = f32[2,4,2,16,128]{4,3,2,1,0:T(8,128)S(1)} collective-permute-done((f32[2,4,2,16,128]{4,3,2,1,0:T(8,128)S(1)}, f32[2,4,2,16,128]{4,3,2,1,0:T(8,128)S(1)}, u32[]{:S(2)}, u32[]{:S(2)}) %collective-permute-start.2) | collective-permute-done | bytes 131104 | tf_op jit(solution)/shard_map/ppermute | solution.py:22
  17.6 0.1 last_plane.1
  17.7 1.7 %apply_outer.1 = (f32[2,4,3,8,16,128]{5,4,3,2,1,0:T(8,128)S(1)}, f32[32,2,128]{2,1,0:T(2,128)}) custom-call(s32[6]{0:T(128)S(1)} %copy-done.2, f32[2,4]{1,0:T(2,128)S(1)} %copy-done.3, f32[2,4,3,8,16,128]{5,4,3,2,1,0:T(8,128)S(1)} %get-tuple-element.37.basis_ref, ...), custom_call_target="tpu_custom_call", output_to_operand_aliasing={{0}: (12, {})} | custom-call | flops 4915200 | bytes 1572864 | tf_op jit(solution)/shard_map/apply_outer/pallas_call | solution.py:645
  19.4 0.0 collective-permute-start.3
  19.4 4.8 %all-to-all-start = ((f32[32,2,128]{2,1,0:T(2,128)}), f32[32,2,128]{2,1,0:T(2,128)S(1)}, u32[]{:S(2)}, u32[]{:S(2)}) async-start(f32[32,2,128]{2,1,0:T(2,128)} %get-tuple-element.62), calls=%async_computation | async-start | bytes 65536 | tf_op jit(solution)/shard_map/all_to_all | solution.py:656
  24.3 1.8 %collective-permute-start.4 = (f32[16,128]{1,0:T(8,128)S(1)}, f32[16,128]{1,0:T(8,128)S(1)}, u32[]{:S(2)}, u32[]{:S(2)}) collective-permute-start(f32[16,128]{1,0:T(8,128)S(1)} %get-tuple-element.65.hyf_ref), channel_id=1, source_target_pairs={{0,2},{2,0},{1,3},{3,1},{4,6},{6,4},{5,7},{7,5},{8,10},{10,8},{9,1... | collective-permute-start | bytes 24584 | tf_op jit(solution)/shard_map/ppermute | solution.py:22
  26.1 1.9 %collective-permute-done.4.hyf_ref = f32[16,128]{1,0:T(8,128)S(1)} collective-permute-done((f32[16,128]{1,0:T(8,128)S(1)}, f32[16,128]{1,0:T(8,128)S(1)}, u32[]{:S(2)}, u32[]{:S(2)}) %collective-permute-start.4) | collective-permute-done | bytes 8224 | tf_op jit(solution)/shard_map/ppermute | solution.py:22
  28.0 0.0 collective-permute-done.3.hxf_ref
  28.0 2.3 %add_rims.1 = (f32[2,4,3,8,16,128]{5,4,3,2,1,0:T(8,128)S(1)}, f32[2,4,3,8,16,128]{5,4,3,2,1,0:T(8,128)}) custom-call(s32[6]{0:T(128)S(1)} %copy-done.2, f32[2,4,3,8,16,128]{5,4,3,2,1,0:T(8,128)S(1)} %get-tuple-element.63.left_in, f32[2,4,2,8,128]{4,3,2,1,0:T(8,128)S(1)} %collective-permute-done.3.hxf_ref, ...), custom_call_target="tpu_custom_call", output_to_operand_aliasing={{0}: (1, {})} | custom-call | tf_op jit(solution)/shard_map/add_rims/pallas_call | solution.py:659
  30.2 1.3 %all-to-all-done.rows_ref = f32[32,2,128]{2,1,0:T(2,128)S(1)} async-done(((f32[32,2,128]{2,1,0:T(2,128)}), f32[32,2,128]{2,1,0:T(2,128)S(1)}, u32[]{:S(2)}, u32[]{:S(2)}) %all-to-all-start) | async-done | bytes 32800 | tf_op jit(solution)/shard_map/all_to_all | solution.py:656
  31.5 0.9 %sum_rows.1 = f32[2,4,4]{2,1,0:T(4,128)} custom-call(f32[32,2,128]{2,1,0:T(2,128)S(1)} %all-to-all-done.rows_ref), custom_call_target="tpu_custom_call" | custom-call | tf_op jit(solution)/shard_map/sum_rows/pallas_call | solution.py:671
  (8 shorter events, 0.0 us)
Async XLA Ops:
  0.6 7.8 %copy-start.2 = (s32[6]{0:T(128)S(1)}, s32[6]{0:T(128)}, u32[]{:S(2)}) copy-start(s32[6]{0:T(128)} %pml_ref.7) | copy-start | bytes 76
  0.6 7.8 %copy-start.1 = (f32[2,4,4]{2,1,0:T(4,128)S(1)}, f32[2,4,4]{2,1,0:T(4,128)}, u32[]{:S(2)}) copy-start(f32[2,4,4]{2,1,0:T(4,128)} %coeffs_ref.3) | copy-start | bytes 388
  0.7 7.8 %copy-start.5 = (f32[4]{0:T(128)S(1)}, f32[4]{0:T(128)}, u32[]{:S(2)}) copy-start(f32[4]{0:T(128)} %eps_loss_ref.1) | copy-start | bytes 52
  0.7 7.7 %copy-start.4 = (f32[4]{0:T(128)S(1)}, f32[4]{0:T(128)}, u32[]{:S(2)}) copy-start(f32[4]{0:T(128)} %eps_real_ref.1) | copy-start | bytes 52
  0.7 7.7 %copy-start = (s32[8,16,128]{2,1,0:T(8,128)S(1)}, s32[8,16,128]{2,1,0:T(8,128)}, u32[]{:S(2)}) copy-start(s32[8,16,128]{2,1,0:T(8,128)} %material_ref.1) | copy-start | bytes 196612
  2.3 9.3 %collective-permute-start = (f32[2,4,2,8,128]{4,3,2,1,0:T(8,128)S(1)}, f32[2,4,2,8,128]{4,3,2,1,0:T(8,128)S(1)}, u32[]{:S(2)}, u32[]{:S(2)}) collective-permute-start(f32[2,4,2,8,128]{4,3,2,1,0:T(8,128)S(1)} %get-tuple-element.43), channel_id=1, source_target_pairs={{0,28},{4,0},{8,4},{12,8},{16,12},{20,16},{24,20},{28,24},{1,29},{... | collective-permute-start | bytes 196616 | tf_op jit(solution)/shard_map/ppermute | solution.py:22
  6.9 4.7 %collective-permute-start.1 = (f32[16,128]{1,0:T(8,128)S(1)}, f32[16,128]{1,0:T(8,128)S(1)}, u32[]{:S(2)}, u32[]{:S(2)}) collective-permute-start(f32[16,128]{1,0:T(8,128)S(1)} %get-tuple-element.44), channel_id=1, source_target_pairs={{0,2},{2,0},{1,3},{3,1},{4,6},{6,4},{5,7},{7,5},{8,10},{10,8},{9,1... | collective-permute-start | bytes 24584 | tf_op jit(solution)/shard_map/ppermute | solution.py:22
  11.6 2.5 %copy-start.3 = (f32[2,4]{1,0:T(2,128)S(1)}, f32[2,4]{1,0:T(2,128)}, u32[]{:S(2)}) copy-start(f32[2,4]{1,0:T(2,128)} %ritz_ref.3) | copy-start | bytes 100
  12.6 5.0 %collective-permute-start.2 = (f32[2,4,2,16,128]{4,3,2,1,0:T(8,128)S(1)}, f32[2,4,2,16,128]{4,3,2,1,0:T(8,128)S(1)}, u32[]{:S(2)}, u32[]{:S(2)}) collective-permute-start(f32[2,4,2,16,128]{4,3,2,1,0:T(8,128)S(1)} %get-tuple-element.49), channel_id=1, source_target_pairs={{0,1},{1,0},{2,3},{3,2},{4,5},{5,4},{6,7},{7,6},{8,9},{9,8},{10,11... | collective-permute-start | bytes 393224 | tf_op jit(solution)/shard_map/ppermute | solution.py:22
  19.4 8.6 %collective-permute-start.3 = (f32[2,4,2,8,128]{4,3,2,1,0:T(8,128)S(1)}, f32[2,4,2,8,128]{4,3,2,1,0:T(8,128)S(1)}, u32[]{:S(2)}, u32[]{:S(2)}) collective-permute-start(f32[2,4,2,8,128]{4,3,2,1,0:T(8,128)S(1)} %get-tuple-element.64.hxf_ref), channel_id=1, source_target_pairs={{0,4},{4,8},{8,12},{12,16},{16,20},{20,24},{24,28},{28,0},{1,5},{5... | collective-permute-start | bytes 196616 | tf_op jit(solution)/shard_map/ppermute | solution.py:22
  19.4 12.1 %all-to-all-start = ((f32[32,2,128]{2,1,0:T(2,128)}), f32[32,2,128]{2,1,0:T(2,128)S(1)}, u32[]{:S(2)}, u32[]{:S(2)}) async-start(f32[32,2,128]{2,1,0:T(2,128)} %get-tuple-element.62), calls=%async_computation | async-start | bytes 65536 | tf_op jit(solution)/shard_map/all_to_all | solution.py:656
  24.3 3.7 %collective-permute-start.4 = (f32[16,128]{1,0:T(8,128)S(1)}, f32[16,128]{1,0:T(8,128)S(1)}, u32[]{:S(2)}, u32[]{:S(2)}) collective-permute-start(f32[16,128]{1,0:T(8,128)S(1)} %get-tuple-element.65.hyf_ref), channel_id=1, source_target_pairs={{0,2},{2,0},{1,3},{3,1},{4,6},{6,4},{5,7},{7,5},{8,10},{10,8},{9,1... | collective-permute-start | bytes 24584 | tf_op jit(solution)/shard_map/ppermute | solution.py:22

commit v12 on v11

--- a/solution.py
+++ b/solution.py
@@ -269,10 +269,10 @@
 
 
 def slab_kernel(
-    pml_ref, coeffs_ref, basis_ref, h_in, packed_in, raw_xf_ref, raw_yf_ref,
-    h_ref, packed_ref, xf_ref, yt_ref, xadd_ref, yadd_ref, hxf_ref, zf_ref,
+    pml_ref, coeffs_ref, basis_ref, h_in, raw_xf_ref, raw_yf_ref,
+    h_ref, xf_ref, yt_ref, xadd_ref, yadd_ref, zf_ref,
 ):
-    del h_in, packed_in
+    del h_in
     _, vectors, _, nz, nx, ny = basis_ref.shape
     parts = range(2)
     cells = nz * nx
@@ -292,24 +292,9 @@
         added += [part if slot else -part for part in value]
     rest = jnp.zeros((ny - 2 * both, cells), jnp.float32)
     yadd_ref[...] = jnp.concatenate(added + [rest], axis=0).T.reshape(nz, nx, ny)
-    packed_ref[...] = packed_ref[...] + yadd_ref[...]
     last = nz - 1
     lower = jnp.full((SUB, ny), lax.axis_index(AXES[0]), jnp.int32) == 0
-    lanes = lax.broadcasted_iota(jnp.int32, (nz, ny), 1)
-    corner = packed_ref[:, nx - 1, :]
     for b in range(vectors):
-        for part in parts:
-            row = packed_row(0, part, b, vectors)
-            edge = pltpu.roll(xadd_ref[part, b, 1], (row + 1) % ny, 1)
-            corner = corner + jnp.where(lanes == row, edge, 0.0)
-    packed_ref[:, nx - 1, :] = corner
-    for b in range(vectors):
-        for part in parts:
-            hxf_ref[part, b, 0] = h_ref[part, b, 1, :, nx - 1, :] + xadd_ref[part, b, 0]
-            hxf_ref[part, b, 1] = (
-                h_ref[part, b, 2, :, nx - 1, :] + xadd_ref[part, b, 1]
-                + lane_to_last(yadd_ref[:, nx - 1, :], 0, part, b, vectors)
-            )
         for cut in tiles_of(nx):
             h = [field_of(h_ref, b, comp, last, cut) for comp in range(3)]
             h = with_halos(h, b, last, cut, nx, xadd_ref, yadd_ref)
@@ -373,14 +358,27 @@
 
 
 def inner_kernel(
-    ritz_ref, basis_ref, loss_ref, table_ref, sz_ref, h_in, xadd_ref, yadd_ref,
-    h_ref, left_ref, acc_ref, before_ref, basis_hbm, sem,
+    ritz_ref, basis_ref, loss_ref, table_ref, sz_ref, h_in, packed_in, xadd_ref, yadd_ref,
+    h_ref, packed_ref, left_ref, acc_ref, before_ref, hxf_ref, basis_hbm, sem,
 ):
-    del h_in
+    del h_in, packed_in
     _, vectors, _, nz, nx, ny = basis_ref.shape
     keep = pltpu.make_async_copy(basis_ref, basis_hbm, sem)
     keep.start()
     cuts = tiles_of(nx)
+    lanes = lax.broadcasted_iota(jnp.int32, (nz, ny), 1)
+    open_plane = lax.broadcasted_iota(jnp.int32, (nz, ny), 0) < nz - 1
+    packed_ref[...] = packed_ref[...] + yadd_ref[...]
+    corner = packed_ref[:, nx - 1, :]
+    for b in range(vectors):
+        for part in range(2):
+            row = packed_row(0, part, b, vectors)
+            more = xadd_ref[part, b, 1]
+            corner = corner + jnp.where(lanes == row, pltpu.roll(more, (row + 1) % ny, 1), 0.0)
+            more = more + lane_to_last(yadd_ref[:, nx - 1, :], 0, part, b, vectors)
+            hxf_ref[part, b, 0] = h_ref[part, b, 1, :, nx - 1, :] + jnp.where(open_plane, xadd_ref[part, b, 0], 0.0)
+            hxf_ref[part, b, 1] = h_ref[part, b, 2, :, nx - 1, :] + jnp.where(open_plane, more, 0.0)
+    packed_ref[:, nx - 1, :] = corner
     acc_ref[...] = jnp.zeros(acc_ref.shape, jnp.float32)
     before_ref[...] = jnp.zeros(before_ref.shape, jnp.float32)
 
@@ -445,7 +443,8 @@
         cmul(sy_next, (yt_ref[slot * both:slot * both + vectors], yt_ref[slot * both + vectors:(slot + 1) * both]))
         for slot in range(2)
     ]
-    totals = {}
+    columns = lax.broadcasted_iota(jnp.int32, (both, ny), 1)
+    gram = jnp.zeros((both, ny), jnp.float32)
     for b in range(vectors):
 
         def tile_of(ref, slot, cut, b=b):
@@ -475,23 +474,24 @@
             over = cmul(sx_next, over)
             for row in range(0, nz, SUB):
                 sums[a] = add(sums[a], tuple(part[row:row + SUB] for part in over))
+        flat = jnp.concatenate(
+            [jnp.sum(sums[a][part], axis=0, keepdims=True) for part in parts for a in range(vectors)], axis=0
+        )
         over = None
         for slot in range(2):
             h = tuple(hyf_ref[packed_row(slot, part, b, vectors)][None] for part in parts)
             term = cmul(ends[slot], h)
             over = term if over is None else sub(term, over)
-        for a in range(vectors):
-            for part in parts:
-                side = jnp.concatenate([over[part][a:a + 1], jnp.zeros((SUB - 1, ny), jnp.float32)], axis=0)
-                totals[part, a, b] = sums[a][part] + side
+        side = jnp.concatenate(over, axis=0)
+        total = jnp.sum(flat, axis=1, keepdims=True) + jnp.sum(side, axis=1, keepdims=True)
+        gram = jnp.where(columns == b, total, gram)
     everywhere = 3.0 * nz * nx * ny
     for axis in AXES:
         everywhere = everywhere * lax.axis_size(axis)
-    for part in parts:
-        stack = jnp.concatenate([totals[part, a, b] for a in range(vectors) for b in range(vectors)], axis=0)
-        row = jnp.sum(stack.T, axis=0, keepdims=True) * (1.0 / everywhere)
-        for device in range(gram_ref.shape[0]):
-            gram_ref[device, part:part + 1] = row
+    gram = gram * (1.0 / everywhere)
+    row = tree_sum([gram[0:1]] + [pltpu.roll(gram[row:row + 1], row * vectors, 1) for row in range(1, both)])
+    for device in range(gram_ref.shape[0]):
+        gram_ref[device] = row
 
 
 def tree_sum(values):
@@ -502,21 +502,14 @@
 
 
 def gather_kernel(rows_ref, gram_ref):
-    _, vectors, _ = gram_ref.shape
+    vectors = gram_ref.shape[1]
     total = tree_sum([rows_ref[device] for device in range(rows_ref.shape[0])])
     count = total.shape[1]
-    reach = 1
-    while reach < SUB:
-        total = total + pltpu.roll(total, count - reach, 1)
-        reach *= 2
-    lanes = lax.broadcasted_iota(jnp.int32, total.shape, 1)
-    for a in range(vectors):
-        matrix_row = total
-        for b in range(vectors):
-            place = (a * vectors + b) * SUB
-            matrix_row = jnp.where(lanes == b, pltpu.roll(total, (count + b - place) % count, 1), matrix_row)
-        for part in range(2):
-            gram_ref[part, a:a + 1] = matrix_row[part:part + 1, :vectors]
+    for part in range(2):
+        for a in range(vectors):
+            row = (part * vectors + a) * vectors
+            turned = pltpu.roll(total, count - row, 1) if row else total
+            gram_ref[part, a:a + 1] = turned[:, :vectors]
 
 
 def rim_kernel(pml_ref, left_in, hxf_ref, hyf_ref, left_ref, residual_hbm, xadd_ref, yadd_ref, sems):
@@ -611,27 +604,27 @@
         cost_estimate=cost(800, 4),
         name="prepare",
     )(pml_width, eps_real, eps_loss, coeffs, near, material)
-    h, packed, xf, yt, xadd, yadd, hxf, zf = pl.pallas_call(
+    h, xf, yt, xadd, yadd, zf = pl.pallas_call(
         slab_kernel,
-        out_shape=(whole, planes, face, f32(*yf_shape), face, planes, face, f32(*zf_shape)),
-        in_specs=[SMEM] * 2 + [VMEM] * 5,
-        out_specs=(VMEM,) * 8,
-        input_output_aliases={3: 0, 4: 1},
+        out_shape=(whole, face, f32(*yf_shape), face, planes, f32(*zf_shape)),
+        in_specs=[SMEM] * 2 + [VMEM] * 4,
+        out_specs=(VMEM,) * 6,
+        input_output_aliases={3: 0},
         compiler_params=params,
         name="slab_face",
-    )(pml_width, coeffs, basis, h, packed, xf, yf)
+    )(pml_width, coeffs, basis, h, xf, yf)
     zf = passed_round(zf, "gz", 1)
-    h, left, acc, before, basis_new = pl.pallas_call(
+    h, packed, left, acc, before, hxf, basis_new = pl.pallas_call(
         inner_kernel,
-        out_shape=(whole, whole, f32(vectors, 2 * vectors, SUB, ny), f32(*zf_shape), whole),
-        in_specs=[SMEM] + [VMEM] * 7,
-        out_specs=(VMEM,) * 4 + (HBM,),
+        out_shape=(whole, planes, whole, f32(vectors, 2 * vectors, SUB, ny), f32(*zf_shape), face, whole),
+        in_specs=[SMEM] + [VMEM] * 8,
+        out_specs=(VMEM,) * 6 + (HBM,),
         scratch_shapes=[pltpu.SemaphoreType.DMA],
-        input_output_aliases={5: 0},
+        input_output_aliases={5: 0, 6: 1},
         compiler_params=params,
         cost_estimate=cost(800, 2),
         name="apply_inner",
-    )(ritz, basis, loss, table, sz, h, xadd, yadd)
+    )(ritz, basis, loss, table, sz, h, packed, xadd, yadd)
     h, hxf, hyf = pl.pallas_call(
         last_plane_kernel,
         out_shape=(whole, face, f32(*yf_shape)),
@@ -644,7 +637,7 @@
     devices = lax.axis_size("gx") * lax.axis_size("gy") * lax.axis_size("gz")
     left, gram = pl.pallas_call(
         outer_kernel,
-        out_shape=(whole, pltpu.VMEM((devices, 2, ny), jnp.float32)),
+        out_shape=(whole, pltpu.VMEM((devices, 1, ny), jnp.float32)),
         in_specs=[SMEM] * 2 + [VMEM] * 13,
         out_specs=(VMEM,) * 2,
         input_output_aliases={12: 0},

time: 32.6 us -> 32.3 us (level)
  no operation moved by 1% of the time
where the time goes in v12:
time: 32.3 us; the launch traced here: 32.1 us
  starting transfers between devices  14.3 us (44%)
  Pallas kernels  13.5 us (42%)
  waiting for transfers between devices  3.58 us (11%)
  between operations  0.75 us (2%)
    ppermute x5, starting transfers between devices, passed_round(): lax.ppermute(value, axis, [(source, (source + steps) % count) for source...  9.45 us
    all_to_all x1, starting transfers between devices, body(): rows = lax.all_to_all(gram, ('gx', 'gy', 'gz'), 0, 0)  4.83 us
    pallas_call x1, Pallas kernels, body(): pl.pallas_call(prepare_kernel, out_shape=(whole, whole, whole, planes, f3...  3.16 us
    pallas_call x1, Pallas kernels, body(): pl.pallas_call(inner_kernel, out_shape=(whole, planes, whole, f32(vectors...  2.96 us
    ppermute x5, waiting for transfers between devices, passed_round(): lax.ppermute(value, axis, [(source, (source + steps) % count) for source...  2.4 us
    pallas_call x1, Pallas kernels, body(): pl.pallas_call(rim_kernel, out_shape=(whole, whole), in_specs=[SMEM] + [V...  2.25 us
    pallas_call x1, Pallas kernels, body(): pl.pallas_call(outer_kernel, out_shape=(whole, pltpu.VMEM((devices, 1, ny...  1.76 us
    pallas_call x1, Pallas kernels, body(): pl.pallas_call(face_kernel, out_shape=(whole, f32(*xf_shape), f32(*yf_sha...  1.64 us
  transfers between devices with their start and end apart: 6, of which 3 were waited for; matrix products, arithmetic and copies ran while one was open for 0% of the time, Pallas kernels for 26%

profile of v12, /device:TPU:0, one launch (start us, length us, event | category | flops | bytes accessed | tf_op | source)
XLA Modules:
  0.0 32.1 jit_solution(6710985048361161300)
XLA Ops:
  0.6 0.0 copy-start.2
  0.6 0.0 copy-start.1
  0.7 0.0 copy-start.5
  0.7 1.6 %take_faces.1 = (f32[2,4,3,8,16,128]{5,4,3,2,1,0:T(8,128)S(1)}, f32[2,4,2,8,128]{4,3,2,1,0:T(8,128)S(1)}, f32[16,128]{1,0:T(8,128)S(1)}) custom-call(f32[2,4,3,8,16,128]{5,4,3,2,1,0:T(8,128)} %fields_hbm.1), custom_call_target="tpu_custom_call" | custom-call | tf_op jit(solution)/shard_map/take_faces/pallas_call | solution.py:580
  2.3 4.5 %collective-permute-start = (f32[2,4,2,8,128]{4,3,2,1,0:T(8,128)S(1)}, f32[2,4,2,8,128]{4,3,2,1,0:T(8,128)S(1)}, u32[]{:S(2)}, u32[]{:S(2)}) collective-permute-start(f32[2,4,2,8,128]{4,3,2,1,0:T(8,128)S(1)} %get-tuple-element.42), channel_id=1, source_target_pairs={{0,28},{4,0},{8,4},{12,8},{16,12},{20,16},{24,20},{28,24},{1,29},{... | collective-permute-start | bytes 196616 | tf_op jit(solution)/shard_map/ppermute | solution.py:22
  6.9 1.5 %collective-permute-start.1 = (f32[16,128]{1,0:T(8,128)S(1)}, f32[16,128]{1,0:T(8,128)S(1)}, u32[]{:S(2)}, u32[]{:S(2)}) collective-permute-start(f32[16,128]{1,0:T(8,128)S(1)} %get-tuple-element.43), channel_id=1, source_target_pairs={{0,2},{2,0},{1,3},{3,1},{4,6},{6,4},{5,7},{7,5},{8,10},{10,8},{9,1... | collective-permute-start | bytes 24584 | tf_op jit(solution)/shard_map/ppermute | solution.py:22
  8.4 3.2 %prepare.1 = (f32[2,4,3,8,16,128]{5,4,3,2,1,0:T(8,128)S(1)}, f32[2,4,3,8,16,128]{5,4,3,2,1,0:T(8,128)S(1)}, f32[2,4,3,8,16,128]{5,4,3,2,1,0:T(8,128)S(1)}, f32[8...) custom-call(s32[6]{0:T(128)S(1)} %copy-done.2, f32[4]{0:T(128)S(1)} %copy-done.4, ...), custom_call_target="tpu_custom_call" | custom-call | flops 13107200 | bytes 6291456 | tf_op jit(solution)/shard_map/prepare/pallas_call | solution.py:598
  11.6 0.0 collective-permute-done.1.raw_yf_ref
  11.6 0.0 collective-permute-done.raw_xf_ref
  11.6 0.0 copy-start.3
  11.6 0.9 %slab_face.1 = (f32[2,4,3,8,16,128]{5,4,3,2,1,0:T(8,128)S(1)}, f32[2,4,2,8,128]{4,3,2,1,0:T(8,128)S(1)}, f32[16,128]{1,0:T(8,128)S(1)}, f32[2,4,2,8,128]{4,3,2,1...) custom-call(s32[6]{0:T(128)S(1)} %copy-done.2, ...), custom_call_target="tpu_custom_call", output_to_operand_aliasing={{0}: (3, {})} | custom-call | tf_op jit(solution)/shard_map/slab_face/pallas_call | solution.py:607
  12.5 1.6 %collective-permute-start.2 = (f32[2,4,2,16,128]{4,3,2,1,0:T(8,128)S(1)}, f32[2,4,2,16,128]{4,3,2,1,0:T(8,128)S(1)}, u32[]{:S(2)}, u32[]{:S(2)}) collective-permute-start(f32[2,4,2,16,128]{4,3,2,1,0:T(8,128)S(1)} %get-tuple-element.49), channel_id=1, source_target_pairs={{0,1},{1,0},{2,3},{3,2},{4,5},{5,4},{6,7},{7,6},{8,9},{9,8},{10,11... | collective-permute-start | bytes 393224 | tf_op jit(solution)/shard_map/ppermute | solution.py:22
  14.1 3.0 %apply_inner.1 = (f32[2,4,3,8,16,128]{5,4,3,2,1,0:T(8,128)S(1)}, f32[8,16,128]{2,1,0:T(8,128)S(1)}, f32[2,4,3,8,16,128]{5,4,3,2,1,0:T(8,128)S(1)}, f32[4,8,8,128...) custom-call(f32[2,4]{1,0:T(2,128)S(1)} %copy-done.3, ...), custom_call_target="tpu_custom_call", output_to_operand_aliasing={{0}: (5, {}), {1}: (6, {})} | custom-call | flops 13107200 | bytes 3145728 | tf_op jit(solution)/shard_map/apply_inner/pallas_call | solution.py:617
  17.0 0.5 %collective-permute-done.2.zf_ref = f32[2,4,2,16,128]{4,3,2,1,0:T(8,128)S(1)} collective-permute-done((f32[2,4,2,16,128]{4,3,2,1,0:T(8,128)S(1)}, f32[2,4,2,16,128]{4,3,2,1,0:T(8,128)S(1)}, u32[]{:S(2)}, u32[]{:S(2)}) %collective-permute-start.2) | collective-permute-done | bytes 131104 | tf_op jit(solution)/shard_map/ppermute | solution.py:22
  17.6 0.1 last_plane.1
  17.7 1.8 %apply_outer.1 = (f32[2,4,3,8,16,128]{5,4,3,2,1,0:T(8,128)S(1)}, f32[32,1,128]{2,1,0:T(1,128)}) custom-call(s32[6]{0:T(128)S(1)} %copy-done.2, f32[2,4]{1,0:T(2,128)S(1)} %copy-done.3, f32[2,4,3,8,16,128]{5,4,3,2,1,0:T(8,128)S(1)} %get-tuple-element.37.basis_ref, ...), custom_call_target="tpu_custom_call", output_to_operand_aliasing={{0}: (12, {})} | custom-call | flops 4915200 | bytes 1572864 | tf_op jit(solution)/shard_map/apply_outer/pallas_call | solution.py:638
  19.4 0.0 collective-permute-start.3
  19.5 4.8 %all-to-all-start = ((f32[32,1,128]{2,1,0:T(1,128)}), f32[32,1,128]{2,1,0:T(1,128)S(1)}, u32[]{:S(2)}, u32[]{:S(2)}) async-start(f32[32,1,128]{2,1,0:T(1,128)} %get-tuple-element.62), calls=%async_computation | async-start | bytes 32768 | tf_op jit(solution)/shard_map/all_to_all | solution.py:649
  24.3 1.8 %collective-permute-start.4 = (f32[16,128]{1,0:T(8,128)S(1)}, f32[16,128]{1,0:T(8,128)S(1)}, u32[]{:S(2)}, u32[]{:S(2)}) collective-permute-start(f32[16,128]{1,0:T(8,128)S(1)} %get-tuple-element.65.hyf_ref), channel_id=1, source_target_pairs={{0,2},{2,0},{1,3},{3,1},{4,6},{6,4},{5,7},{7,5},{8,10},{10,8},{9,1... | collective-permute-start | bytes 24584 | tf_op jit(solution)/shard_map/ppermute | solution.py:22
  26.1 1.9 %collective-permute-done.4.hyf_ref = f32[16,128]{1,0:T(8,128)S(1)} collective-permute-done((f32[16,128]{1,0:T(8,128)S(1)}, f32[16,128]{1,0:T(8,128)S(1)}, u32[]{:S(2)}, u32[]{:S(2)}) %collective-permute-start.4) | collective-permute-done | bytes 8224 | tf_op jit(solution)/shard_map/ppermute | solution.py:22
  28.0 0.0 collective-permute-done.3.hxf_ref
  28.0 2.3 %add_rims.1 = (f32[2,4,3,8,16,128]{5,4,3,2,1,0:T(8,128)S(1)}, f32[2,4,3,8,16,128]{5,4,3,2,1,0:T(8,128)}) custom-call(s32[6]{0:T(128)S(1)} %copy-done.2, f32[2,4,3,8,16,128]{5,4,3,2,1,0:T(8,128)S(1)} %get-tuple-element.63.left_in, f32[2,4,2,8,128]{4,3,2,1,0:T(8,128)S(1)} %collective-permute-done.3.hxf_ref, ...), custom_call_target="tpu_custom_call", output_to_operand_aliasing={{0}: (1, {})} | custom-call | tf_op jit(solution)/shard_map/add_rims/pallas_call | solution.py:652
  30.3 1.2 %all-to-all-done.rows_ref = f32[32,1,128]{2,1,0:T(1,128)S(1)} async-done(((f32[32,1,128]{2,1,0:T(1,128)}), f32[32,1,128]{2,1,0:T(1,128)S(1)}, u32[]{:S(2)}, u32[]{:S(2)}) %all-to-all-start) | async-done | bytes 16416 | tf_op jit(solution)/shard_map/all_to_all | solution.py:649
  31.5 0.7 %sum_rows.1 = f32[2,4,4]{2,1,0:T(4,128)} custom-call(f32[32,1,128]{2,1,0:T(1,128)S(1)} %all-to-all-done.rows_ref), custom_call_target="tpu_custom_call" | custom-call | tf_op jit(solution)/shard_map/sum_rows/pallas_call | solution.py:664
  (8 shorter events, 0.0 us)
Async XLA Ops:
  0.6 7.8 %copy-start.2 = (s32[6]{0:T(128)S(1)}, s32[6]{0:T(128)}, u32[]{:S(2)}) copy-start(s32[6]{0:T(128)} %pml_ref.7) | copy-start | bytes 76
  0.6 7.8 %copy-start.1 = (f32[2,4,4]{2,1,0:T(4,128)S(1)}, f32[2,4,4]{2,1,0:T(4,128)}, u32[]{:S(2)}) copy-start(f32[2,4,4]{2,1,0:T(4,128)} %coeffs_ref.3) | copy-start | bytes 388
  0.7 7.8 %copy-start.5 = (f32[4]{0:T(128)S(1)}, f32[4]{0:T(128)}, u32[]{:S(2)}) copy-start(f32[4]{0:T(128)} %eps_loss_ref.1) | copy-start | bytes 52
  0.7 7.7 %copy-start.4 = (f32[4]{0:T(128)S(1)}, f32[4]{0:T(128)}, u32[]{:S(2)}) copy-start(f32[4]{0:T(128)} %eps_real_ref.1) | copy-start | bytes 52
  0.7 7.7 %copy-start = (s32[8,16,128]{2,1,0:T(8,128)S(1)}, s32[8,16,128]{2,1,0:T(8,128)}, u32[]{:S(2)}) copy-start(s32[8,16,128]{2,1,0:T(8,128)} %material_ref.1) | copy-start | bytes 196612
  2.3 9.3 %collective-permute-start = (f32[2,4,2,8,128]{4,3,2,1,0:T(8,128)S(1)}, f32[2,4,2,8,128]{4,3,2,1,0:T(8,128)S(1)}, u32[]{:S(2)}, u32[]{:S(2)}) collective-permute-start(f32[2,4,2,8,128]{4,3,2,1,0:T(8,128)S(1)} %get-tuple-element.42), channel_id=1, source_target_pairs={{0,28},{4,0},{8,4},{12,8},{16,12},{20,16},{24,20},{28,24},{1,29},{... | collective-permute-start | bytes 196616 | tf_op jit(solution)/shard_map/ppermute | solution.py:22
  6.9 4.7 %collective-permute-start.1 = (f32[16,128]{1,0:T(8,128)S(1)}, f32[16,128]{1,0:T(8,128)S(1)}, u32[]{:S(2)}, u32[]{:S(2)}) collective-permute-start(f32[16,128]{1,0:T(8,128)S(1)} %get-tuple-element.43), channel_id=1, source_target_pairs={{0,2},{2,0},{1,3},{3,1},{4,6},{6,4},{5,7},{7,5},{8,10},{10,8},{9,1... | collective-permute-start | bytes 24584 | tf_op jit(solution)/shard_map/ppermute | solution.py:22
  11.6 2.5 %copy-start.3 = (f32[2,4]{1,0:T(2,128)S(1)}, f32[2,4]{1,0:T(2,128)}, u32[]{:S(2)}) copy-start(f32[2,4]{1,0:T(2,128)} %ritz_ref.3) | copy-start | bytes 100
  12.5 5.0 %collective-permute-start.2 = (f32[2,4,2,16,128]{4,3,2,1,0:T(8,128)S(1)}, f32[2,4,2,16,128]{4,3,2,1,0:T(8,128)S(1)}, u32[]{:S(2)}, u32[]{:S(2)}) collective-permute-start(f32[2,4,2,16,128]{4,3,2,1,0:T(8,128)S(1)} %get-tuple-element.49), channel_id=1, source_target_pairs={{0,1},{1,0},{2,3},{3,2},{4,5},{5,4},{6,7},{7,6},{8,9},{9,8},{10,11... | collective-permute-start | bytes 393224 | tf_op jit(solution)/shard_map/ppermute | solution.py:22
  19.4 8.6 %collective-permute-start.3 = (f32[2,4,2,8,128]{4,3,2,1,0:T(8,128)S(1)}, f32[2,4,2,8,128]{4,3,2,1,0:T(8,128)S(1)}, u32[]{:S(2)}, u32[]{:S(2)}) collective-permute-start(f32[2,4,2,8,128]{4,3,2,1,0:T(8,128)S(1)} %get-tuple-element.64.hxf_ref), channel_id=1, source_target_pairs={{0,4},{4,8},{8,12},{12,16},{16,20},{20,24},{24,28},{28,0},{1,5},{5... | collective-permute-start | bytes 196616 | tf_op jit(solution)/shard_map/ppermute | solution.py:22
  19.5 12.0 %all-to-all-start = ((f32[32,1,128]{2,1,0:T(1,128)}), f32[32,1,128]{2,1,0:T(1,128)S(1)}, u32[]{:S(2)}, u32[]{:S(2)}) async-start(f32[32,1,128]{2,1,0:T(1,128)} %get-tuple-element.62), calls=%async_computation | async-start | bytes 32768 | tf_op jit(solution)/shard_map/all_to_all | solution.py:649
  24.3 3.7 %collective-permute-start.4 = (f32[16,128]{1,0:T(8,128)S(1)}, f32[16,128]{1,0:T(8,128)S(1)}, u32[]{:S(2)}, u32[]{:S(2)}) collective-permute-start(f32[16,128]{1,0:T(8,128)S(1)} %get-tuple-element.65.hyf_ref), channel_id=1, source_target_pairs={{0,2},{2,0},{1,3},{3,1},{4,6},{6,4},{5,7},{7,5},{8,10},{10,8},{9,1... | collective-permute-start | bytes 24584 | tf_op jit(solution)/shard_map/ppermute | solution.py:22

commit v13 on v12

--- a/solution.py
+++ b/solution.py
@@ -490,8 +490,9 @@
         everywhere = everywhere * lax.axis_size(axis)
     gram = gram * (1.0 / everywhere)
     row = tree_sum([gram[0:1]] + [pltpu.roll(gram[row:row + 1], row * vectors, 1) for row in range(1, both)])
+    block = jnp.concatenate([row, jnp.zeros((gram_ref.shape[1] - 1, ny), jnp.float32)], axis=0)
     for device in range(gram_ref.shape[0]):
-        gram_ref[device] = row
+        gram_ref[device] = block
 
 
 def tree_sum(values):
@@ -503,7 +504,7 @@
 
 def gather_kernel(rows_ref, gram_ref):
     vectors = gram_ref.shape[1]
-    total = tree_sum([rows_ref[device] for device in range(rows_ref.shape[0])])
+    total = tree_sum([rows_ref[device] for device in range(rows_ref.shape[0])])[0:1]
     count = total.shape[1]
     for part in range(2):
         for a in range(vectors):
@@ -637,7 +638,7 @@
     devices = lax.axis_size("gx") * lax.axis_size("gy") * lax.axis_size("gz")
     left, gram = pl.pallas_call(
         outer_kernel,
-        out_shape=(whole, pltpu.VMEM((devices, 1, ny), jnp.float32)),
+        out_shape=(whole, f32(devices, 4, ny)),
         in_specs=[SMEM] * 2 + [VMEM] * 13,
         out_specs=(VMEM,) * 2,
         input_output_aliases={12: 0},

time: 32.3 us -> 31.9 us (0.988)
  starting transfers between devices: 14.3 us -> 12.4 us
  waiting for transfers between devices: 3.58 us -> 5.01 us
    ppermute x5, waiting for transfers between devices: 2.4 us -> 5.01 us  [passed_round(): lax.ppermute(value, axis, [(source, (source + steps) % count) for source...]
    all_to_all x1, starting transfers between devices: 4.83 us -> 2.86 us  [body(): rows = lax.all_to_all(gram, ('gx', 'gy', 'gz'), 0, 0)]
    all_to_all x1, waiting for transfers between devices: 1.19 us -> 0.01 us  [body(): rows = lax.all_to_all(gram, ('gx', 'gy', 'gz'), 0, 0)]
where the time goes in v13:
time: 31.9 us; the launch traced here: 31.8 us
  Pallas kernels  13.5 us (42%)
  starting transfers between devices  12.4 us (39%)
  waiting for transfers between devices  5.01 us (16%)
  between operations  0.76 us (2%)
    ppermute x5, starting transfers between devices, passed_round(): lax.ppermute(value, axis, [(source, (source + steps) % count) for source...  9.59 us
    ppermute x5, waiting for transfers between devices, passed_round(): lax.ppermute(value, axis, [(source, (source + steps) % count) for source...  5.01 us
    pallas_call x1, Pallas kernels, body(): pl.pallas_call(prepare_kernel, out_shape=(whole, whole, whole, planes, f3...  3.16 us
    pallas_call x1, Pallas kernels, body(): pl.pallas_call(inner_kernel, out_shape=(whole, planes, whole, f32(vectors...  2.96 us
    all_to_all x1, starting transfers between devices, body(): rows = lax.all_to_all(gram, ('gx', 'gy', 'gz'), 0, 0)  2.86 us
    pallas_call x1, Pallas kernels, body(): pl.pallas_call(rim_kernel, out_shape=(whole, whole), in_specs=[SMEM] + [V...  2.25 us
    pallas_call x1, Pallas kernels, body(): pl.pallas_call(outer_kernel, out_shape=(whole, f32(devices, 4, ny)), in_s...  1.79 us
    pallas_call x1, Pallas kernels, body(): pl.pallas_call(face_kernel, out_shape=(whole, f32(*xf_shape), f32(*yf_sha...  1.64 us
  transfers between devices with their start and end apart: 6, of which 3 were waited for; matrix products, arithmetic and copies ran while one was open for 0% of the time, Pallas kernels for 26%

profile of v13, /device:TPU:0, one launch (start us, length us, event | category | flops | bytes accessed | tf_op | source)
XLA Modules:
  0.0 31.8 jit_solution(10021353084181834492)
XLA Ops:
  0.6 0.0 copy-start.2
  0.7 1.6 %take_faces.1 = (f32[2,4,3,8,16,128]{5,4,3,2,1,0:T(8,128)S(1)}, f32[2,4,2,8,128]{4,3,2,1,0:T(8,128)S(1)}, f32[16,128]{1,0:T(8,128)S(1)}) custom-call(f32[2,4,3,8,16,128]{5,4,3,2,1,0:T(8,128)} %fields_hbm.1), custom_call_target="tpu_custom_call" | custom-call | tf_op jit(solution)/shard_map/take_faces/pallas_call | solution.py:581
  2.3 4.5 %collective-permute-start = (f32[2,4,2,8,128]{4,3,2,1,0:T(8,128)S(1)}, f32[2,4,2,8,128]{4,3,2,1,0:T(8,128)S(1)}, u32[]{:S(2)}, u32[]{:S(2)}) collective-permute-start(f32[2,4,2,8,128]{4,3,2,1,0:T(8,128)S(1)} %get-tuple-element.42), channel_id=1, source_target_pairs={{0,28},{4,0},{8,4},{12,8},{16,12},{20,16},{24,20},{28,24},{1,29},{... | collective-permute-start | bytes 196616 | tf_op jit(solution)/shard_map/ppermute | solution.py:22
  6.9 1.5 %collective-permute-start.1 = (f32[16,128]{1,0:T(8,128)S(1)}, f32[16,128]{1,0:T(8,128)S(1)}, u32[]{:S(2)}, u32[]{:S(2)}) collective-permute-start(f32[16,128]{1,0:T(8,128)S(1)} %get-tuple-element.43), channel_id=1, source_target_pairs={{0,2},{2,0},{1,3},{3,1},{4,6},{6,4},{5,7},{7,5},{8,10},{10,8},{9,1... | collective-permute-start | bytes 24584 | tf_op jit(solution)/shard_map/ppermute | solution.py:22
  8.4 0.0 copy-done.2
  8.4 0.0 copy-done
  8.4 3.2 %prepare.1 = (f32[2,4,3,8,16,128]{5,4,3,2,1,0:T(8,128)S(1)}, f32[2,4,3,8,16,128]{5,4,3,2,1,0:T(8,128)S(1)}, f32[2,4,3,8,16,128]{5,4,3,2,1,0:T(8,128)S(1)}, f32[8...) custom-call(s32[6]{0:T(128)S(1)} %copy-done.2, f32[4]{0:T(128)S(1)} %copy-done.4, ...), custom_call_target="tpu_custom_call" | custom-call | flops 13107200 | bytes 6291456 | tf_op jit(solution)/shard_map/prepare/pallas_call | solution.py:599
  11.6 0.0 collective-permute-done.1.raw_yf_ref
  11.6 0.0 collective-permute-done.raw_xf_ref
  11.6 0.0 copy-start.3
  11.6 0.9 %slab_face.1 = (f32[2,4,3,8,16,128]{5,4,3,2,1,0:T(8,128)S(1)}, f32[2,4,2,8,128]{4,3,2,1,0:T(8,128)S(1)}, f32[16,128]{1,0:T(8,128)S(1)}, f32[2,4,2,8,128]{4,3,2,1...) custom-call(s32[6]{0:T(128)S(1)} %copy-done.2, ...), custom_call_target="tpu_custom_call", output_to_operand_aliasing={{0}: (3, {})} | custom-call | tf_op jit(solution)/shard_map/slab_face/pallas_call | solution.py:608
  12.5 1.6 %collective-permute-start.2 = (f32[2,4,2,16,128]{4,3,2,1,0:T(8,128)S(1)}, f32[2,4,2,16,128]{4,3,2,1,0:T(8,128)S(1)}, u32[]{:S(2)}, u32[]{:S(2)}) collective-permute-start(f32[2,4,2,16,128]{4,3,2,1,0:T(8,128)S(1)} %get-tuple-element.49), channel_id=1, source_target_pairs={{0,1},{1,0},{2,3},{3,2},{4,5},{5,4},{6,7},{7,6},{8,9},{9,8},{10,11... | collective-permute-start | bytes 393224 | tf_op jit(solution)/shard_map/ppermute | solution.py:22
  14.1 3.0 %apply_inner.1 = (f32[2,4,3,8,16,128]{5,4,3,2,1,0:T(8,128)S(1)}, f32[8,16,128]{2,1,0:T(8,128)S(1)}, f32[2,4,3,8,16,128]{5,4,3,2,1,0:T(8,128)S(1)}, f32[4,8,8,128...) custom-call(f32[2,4]{1,0:T(2,128)S(1)} %copy-done.3, ...), custom_call_target="tpu_custom_call", output_to_operand_aliasing={{0}: (5, {}), {1}: (6, {})} | custom-call | flops 13107200 | bytes 3145728 | tf_op jit(solution)/shard_map/apply_inner/pallas_call | solution.py:618
  17.0 0.5 %collective-permute-done.2.zf_ref = f32[2,4,2,16,128]{4,3,2,1,0:T(8,128)S(1)} collective-permute-done((f32[2,4,2,16,128]{4,3,2,1,0:T(8,128)S(1)}, f32[2,4,2,16,128]{4,3,2,1,0:T(8,128)S(1)}, u32[]{:S(2)}, u32[]{:S(2)}) %collective-permute-start.2) | collective-permute-done | bytes 131104 | tf_op jit(solution)/shard_map/ppermute | solution.py:22
  17.6 0.1 last_plane.1
  17.7 1.8 %apply_outer.1 = (f32[2,4,3,8,16,128]{5,4,3,2,1,0:T(8,128)S(1)}, f32[32,4,128]{2,1,0:T(4,128)}) custom-call(s32[6]{0:T(128)S(1)} %copy-done.2, f32[2,4]{1,0:T(2,128)S(1)} %copy-done.3, f32[2,4,3,8,16,128]{5,4,3,2,1,0:T(8,128)S(1)} %get-tuple-element.37.basis_ref, ...), custom_call_target="tpu_custom_call", output_to_operand_aliasing={{0}: (12, {})} | custom-call | flops 4915200 | bytes 1572864 | tf_op jit(solution)/shard_map/apply_outer/pallas_call | solution.py:639
  19.5 2.9 %all-to-all-start = ((f32[32,4,128]{2,1,0:T(4,128)}), f32[32,4,128]{2,1,0:T(4,128)S(1)}, u32[]{:S(2)}, u32[]{:S(2)}) async-start(f32[32,4,128]{2,1,0:T(4,128)} %get-tuple-element.62), calls=%async_computation | async-start | bytes 131072 | tf_op jit(solution)/shard_map/all_to_all | solution.py:650
  22.3 0.3 collective-permute-start.3
  22.7 1.7 %collective-permute-start.4 = (f32[16,128]{1,0:T(8,128)S(1)}, f32[16,128]{1,0:T(8,128)S(1)}, u32[]{:S(2)}, u32[]{:S(2)}) collective-permute-start(f32[16,128]{1,0:T(8,128)S(1)} %get-tuple-element.65.hyf_ref), channel_id=1, source_target_pairs={{0,2},{2,0},{1,3},{3,1},{4,6},{6,4},{5,7},{7,5},{8,10},{10,8},{9,1... | collective-permute-start | bytes 24584 | tf_op jit(solution)/shard_map/ppermute | solution.py:22
  24.3 2.0 %collective-permute-done.4.hyf_ref = f32[16,128]{1,0:T(8,128)S(1)} collective-permute-done((f32[16,128]{1,0:T(8,128)S(1)}, f32[16,128]{1,0:T(8,128)S(1)}, u32[]{:S(2)}, u32[]{:S(2)}) %collective-permute-start.4) | collective-permute-done | bytes 8224 | tf_op jit(solution)/shard_map/ppermute | solution.py:22
  26.3 2.5 %collective-permute-done.3.hxf_ref = f32[2,4,2,8,128]{4,3,2,1,0:T(8,128)S(1)} collective-permute-done((f32[2,4,2,8,128]{4,3,2,1,0:T(8,128)S(1)}, f32[2,4,2,8,128]{4,3,2,1,0:T(8,128)S(1)}, u32[]{:S(2)}, u32[]{:S(2)}) %collective-permute-start.3) | collective-permute-done | bytes 65568 | tf_op jit(solution)/shard_map/ppermute | solution.py:22
  28.8 2.3 %add_rims.1 = (f32[2,4,3,8,16,128]{5,4,3,2,1,0:T(8,128)S(1)}, f32[2,4,3,8,16,128]{5,4,3,2,1,0:T(8,128)}) custom-call(s32[6]{0:T(128)S(1)} %copy-done.2, f32[2,4,3,8,16,128]{5,4,3,2,1,0:T(8,128)S(1)} %get-tuple-element.63.left_in, f32[2,4,2,8,128]{4,3,2,1,0:T(8,128)S(1)} %collective-permute-done.3.hxf_ref, ...), custom_call_target="tpu_custom_call", output_to_operand_aliasing={{0}: (1, {})} | custom-call | tf_op jit(solution)/shard_map/add_rims/pallas_call | solution.py:653
  31.1 0.0 all-to-all-done.rows_ref
  31.1 0.7 %sum_rows.1 = f32[2,4,4]{2,1,0:T(4,128)} custom-call(f32[32,4,128]{2,1,0:T(4,128)S(1)} %all-to-all-done.rows_ref), custom_call_target="tpu_custom_call" | custom-call | tf_op jit(solution)/shard_map/sum_rows/pallas_call | solution.py:665
  (8 shorter events, 0.0 us)
Async XLA Ops:
  0.6 7.8 %copy-start.2 = (s32[6]{0:T(128)S(1)}, s32[6]{0:T(128)}, u32[]{:S(2)}) copy-start(s32[6]{0:T(128)} %pml_ref.7) | copy-start | bytes 76
  0.6 7.8 %copy-start.1 = (f32[2,4,4]{2,1,0:T(4,128)S(1)}, f32[2,4,4]{2,1,0:T(4,128)}, u32[]{:S(2)}) copy-start(f32[2,4,4]{2,1,0:T(4,128)} %coeffs_ref.3) | copy-start | bytes 388
  0.7 7.8 %copy-start.5 = (f32[4]{0:T(128)S(1)}, f32[4]{0:T(128)}, u32[]{:S(2)}) copy-start(f32[4]{0:T(128)} %eps_loss_ref.1) | copy-start | bytes 52
  0.7 7.7 %copy-start.4 = (f32[4]{0:T(128)S(1)}, f32[4]{0:T(128)}, u32[]{:S(2)}) copy-start(f32[4]{0:T(128)} %eps_real_ref.1) | copy-start | bytes 52
  0.7 7.7 %copy-start = (s32[8,16,128]{2,1,0:T(8,128)S(1)}, s32[8,16,128]{2,1,0:T(8,128)}, u32[]{:S(2)}) copy-start(s32[8,16,128]{2,1,0:T(8,128)} %material_ref.1) | copy-start | bytes 196612
  2.3 9.3 %collective-permute-start = (f32[2,4,2,8,128]{4,3,2,1,0:T(8,128)S(1)}, f32[2,4,2,8,128]{4,3,2,1,0:T(8,128)S(1)}, u32[]{:S(2)}, u32[]{:S(2)}) collective-permute-start(f32[2,4,2,8,128]{4,3,2,1,0:T(8,128)S(1)} %get-tuple-element.42), channel_id=1, source_target_pairs={{0,28},{4,0},{8,4},{12,8},{16,12},{20,16},{24,20},{28,24},{1,29},{... | collective-permute-start | bytes 196616 | tf_op jit(solution)/shard_map/ppermute | solution.py:22
  6.9 4.7 %collective-permute-start.1 = (f32[16,128]{1,0:T(8,128)S(1)}, f32[16,128]{1,0:T(8,128)S(1)}, u32[]{:S(2)}, u32[]{:S(2)}) collective-permute-start(f32[16,128]{1,0:T(8,128)S(1)} %get-tuple-element.43), channel_id=1, source_target_pairs={{0,2},{2,0},{1,3},{3,1},{4,6},{6,4},{5,7},{7,5},{8,10},{10,8},{9,1... | collective-permute-start | bytes 24584 | tf_op jit(solution)/shard_map/ppermute | solution.py:22
  11.6 2.5 %copy-start.3 = (f32[2,4]{1,0:T(2,128)S(1)}, f32[2,4]{1,0:T(2,128)}, u32[]{:S(2)}) copy-start(f32[2,4]{1,0:T(2,128)} %ritz_ref.3) | copy-start | bytes 100
  12.5 5.0 %collective-permute-start.2 = (f32[2,4,2,16,128]{4,3,2,1,0:T(8,128)S(1)}, f32[2,4,2,16,128]{4,3,2,1,0:T(8,128)S(1)}, u32[]{:S(2)}, u32[]{:S(2)}) collective-permute-start(f32[2,4,2,16,128]{4,3,2,1,0:T(8,128)S(1)} %get-tuple-element.49), channel_id=1, source_target_pairs={{0,1},{1,0},{2,3},{3,2},{4,5},{5,4},{6,7},{7,6},{8,9},{9,8},{10,11... | collective-permute-start | bytes 393224 | tf_op jit(solution)/shard_map/ppermute | solution.py:22
  19.5 11.6 %all-to-all-start = ((f32[32,4,128]{2,1,0:T(4,128)}), f32[32,4,128]{2,1,0:T(4,128)S(1)}, u32[]{:S(2)}, u32[]{:S(2)}) async-start(f32[32,4,128]{2,1,0:T(4,128)} %get-tuple-element.62), calls=%async_computation | async-start | bytes 131072 | tf_op jit(solution)/shard_map/all_to_all | solution.py:650
  22.3 6.5 %collective-permute-start.3 = (f32[2,4,2,8,128]{4,3,2,1,0:T(8,128)S(1)}, f32[2,4,2,8,128]{4,3,2,1,0:T(8,128)S(1)}, u32[]{:S(2)}, u32[]{:S(2)}) collective-permute-start(f32[2,4,2,8,128]{4,3,2,1,0:T(8,128)S(1)} %get-tuple-element.64.hxf_ref), channel_id=1, source_target_pairs={{0,4},{4,8},{8,12},{12,16},{16,20},{20,24},{24,28},{28,0},{1,5},{5... | collective-permute-start | bytes 196616 | tf_op jit(solution)/shard_map/ppermute | solution.py:22
  22.7 3.7 %collective-permute-start.4 = (f32[16,128]{1,0:T(8,128)S(1)}, f32[16,128]{1,0:T(8,128)S(1)}, u32[]{:S(2)}, u32[]{:S(2)}) collective-permute-start(f32[16,128]{1,0:T(8,128)S(1)} %get-tuple-element.65.hyf_ref), channel_id=1, source_target_pairs={{0,2},{2,0},{1,3},{3,1},{4,6},{6,4},{5,7},{7,5},{8,10},{10,8},{9,1... | collective-permute-start | bytes 24584 | tf_op jit(solution)/shard_map/ppermute | solution.py:22

commit v14 on v13

--- a/solution.py
+++ b/solution.py
@@ -20,6 +20,12 @@
 def passed_round(value, axis, steps):
     count = lax.axis_size(axis)
     return lax.ppermute(value, axis, [(source, (source + steps) % count) for source in range(count)])
+
+
+def passed_along(value, axis, steps):
+    count = lax.axis_size(axis)
+    leading, last = (max(0, -steps), min(count, count - steps))
+    return lax.ppermute(value, axis, [(source, source + steps) for source in range(leading, last)])
 
 
 def inverse_stretch(places, length, low_width, high_width):
@@ -513,20 +519,13 @@
             gram_ref[part, a:a + 1] = turned[:, :vectors]
 
 
-def rim_kernel(pml_ref, left_in, hxf_ref, hyf_ref, left_ref, residual_hbm, xadd_ref, yadd_ref, sems):
+def rim_y_kernel(pml_ref, left_in, hyf_ref, left_ref, residual_hbm, yadd_ref, sems):
     del left_in
     _, vectors, _, nz, nx, ny = left_ref.shape
     parts = range(2)
     both = 2 * vectors
-    sex = axis_stretch(pml_ref, 1, nx, one_place(1, nx, 0, (nz, ny)))
-    sex = tuple(part * has_neighbour(1, -1) for part in sex)
     sey = axis_stretch(pml_ref, 2, ny, one_place(2, ny, 0, (vectors, nz * nx)))
     sey = tuple(part * has_neighbour(2, -1) for part in sey)
-    for b in range(vectors):
-        for slot in range(2):
-            value = cmul(sex, tuple(hxf_ref[part, b, slot] for part in parts))
-            for part in parts:
-                xadd_ref[part, b, slot] = value[part] if slot else -value[part]
     added = []
     for slot in range(2):
         first = slot * both
@@ -534,11 +533,15 @@
         added += [part if slot else -part for part in value]
     rest = jnp.zeros((ny - 2 * both, nz * nx), jnp.float32)
     yadd_ref[...] = jnp.concatenate(added + [rest], axis=0).T.reshape(nz, nx, ny)
-    rows = lax.broadcasted_iota(jnp.int32, (SUB, ny), 0)
     lanes = lax.broadcasted_iota(jnp.int32, (SUB, ny), 1)
 
     def kept(z):
-        return pltpu.make_async_copy(left_ref.at[:, :, :, z], residual_hbm.at[:, :, :, z], sems.at[z])
+        blocks = [(slice(None), slice(None), 0, z)]
+        blocks += [(slice(None), slice(None), comp, z, slice(SUB, nx)) for comp in (1, 2)]
+        return [
+            pltpu.make_async_copy(left_ref.at[block], residual_hbm.at[block], sems.at[place, z])
+            for place, block in enumerate(blocks)
+        ]
 
     @pl.loop(0, nz)
     def _(z):
@@ -546,27 +549,43 @@
             column = yadd_ref[z, cut]
             for b in range(vectors):
                 for part in parts:
-
-                    def turned(slot, b=b, part=part):
+                    for slot, comp in enumerate((0, 2)):
                         row = packed_row(slot, part, b, vectors)
                         value = pltpu.roll(column, ny - row, 1) if row else column
-                        return jnp.where(lanes == 0, value, 0.0)
-
-                    def row_of(slot, b=b, part=part):
-                        return jnp.where(rows == 0, xadd_ref[part, b, slot, pl.ds(z, 1)], 0.0)
-
-                    ex = left_ref[part, b, 0, z, cut] + turned(0)
-                    ez = left_ref[part, b, 2, z, cut] + turned(1)
-                    if cut.start == 0:
-                        left_ref[part, b, 1, z, cut] = left_ref[part, b, 1, z, cut] + row_of(1)
-                        ez = ez + row_of(0)
-                    left_ref[part, b, 0, z, cut] = ex
-                    left_ref[part, b, 2, z, cut] = ez
-        kept(z).start()
+                        value = jnp.where(lanes == 0, value, 0.0)
+                        left_ref[part, b, comp, z, cut] = left_ref[part, b, comp, z, cut] + value
+        for copy in kept(z):
+            copy.start()
 
     @pl.loop(0, nz)
     def _(z):
-        kept(z).wait()
+        for copy in kept(z):
+            copy.wait()
+
+
+def rim_x_kernel(pml_ref, left_in, residual_in, hxf_ref, left_ref, residual_hbm, xadd_ref, sem):
+    del left_in, residual_in
+    _, vectors, _, nz, nx, ny = left_ref.shape
+    parts = range(2)
+    sex = axis_stretch(pml_ref, 1, nx, one_place(1, nx, 0, (nz, ny)))
+    sex = tuple(part * has_neighbour(1, -1) for part in sex)
+    for b in range(vectors):
+        for slot in range(2):
+            value = cmul(sex, tuple(hxf_ref[part, b, slot] for part in parts))
+            for part in parts:
+                xadd_ref[part, b, slot] = value[part] if slot else -value[part]
+    rows = lax.broadcasted_iota(jnp.int32, (SUB, ny), 0)
+    first = slice(0, SUB)
+    for z in range(nz):
+        for b in range(vectors):
+            for part in parts:
+                for slot, comp in ((1, 1), (0, 2)):
+                    value = jnp.where(rows == 0, xadd_ref[part, b, slot, z:z + 1], 0.0)
+                    left_ref[part, b, comp, z, first] = left_ref[part, b, comp, z, first] + value
+    block = (slice(None), slice(None), slice(1, 3), slice(None), first)
+    copy = pltpu.make_async_copy(left_ref.at[block], residual_hbm.at[block], sem)
+    copy.start()
+    copy.wait()
 
 
 def body(fields, material, pml_width, eps_real, eps_loss, coeffs, ritz):
@@ -648,19 +667,31 @@
     )(pml_width, ritz, basis, loss, table, sz, h, zf, xf, yt, hxf, hyf, left, acc, before)
     gram, hxf, hyf = lax.optimization_barrier((gram, hxf, hyf))
     rows = lax.all_to_all(gram, ("gx", "gy", "gz"), 0, 0)
-    from_x = passed_round(hxf, "gx", 1)
+    from_x = passed_along(hxf, "gx", 1)
     from_y = passed_round(hyf, "gy", 1)
+    free = pl.CostEstimate(flops=0, bytes_accessed=0, transcendentals=0)
+    left, residual = pl.pallas_call(
+        rim_y_kernel,
+        out_shape=(whole, whole),
+        in_specs=[SMEM] + [VMEM] * 2,
+        out_specs=(VMEM, HBM),
+        scratch_shapes=[scratch(nz, nx, ny), pltpu.SemaphoreType.DMA((3, nz))],
+        input_output_aliases={1: 0},
+        compiler_params=params,
+        cost_estimate=free,
+        name="add_y_rims",
+    )(pml_width, left, from_y)
     _, residual = pl.pallas_call(
-        rim_kernel,
+        rim_x_kernel,
         out_shape=(whole, whole),
-        in_specs=[SMEM] + [VMEM] * 3,
+        in_specs=[SMEM, VMEM, HBM, VMEM],
         out_specs=(VMEM, HBM),
-        scratch_shapes=[scratch(*xf_shape), scratch(nz, nx, ny), pltpu.SemaphoreType.DMA((nz,))],
-        input_output_aliases={1: 0},
-        compiler_params=params,
-        cost_estimate=pl.CostEstimate(flops=0, bytes_accessed=0, transcendentals=0),
-        name="add_rims",
-    )(pml_width, left, from_x, from_y)
+        scratch_shapes=[scratch(*xf_shape), pltpu.SemaphoreType.DMA],
+        input_output_aliases={1: 0, 2: 1},
+        compiler_params=params,
+        cost_estimate=free,
+        name="add_x_rims",
+    )(pml_width, left, residual, from_x)
     rows, residual = lax.optimization_barrier((rows, residual))
     gram = pl.pallas_call(
         gather_kernel,

time: 31.9 us -> 33.3 us (1.044); the launches traced: 31.8 us -> 32.8 us
  waiting for transfers between devices: 5.01 us -> 2.5 us
  starting transfers between devices: 12.4 us -> 14.4 us
  Pallas kernels: 13.5 us -> 15.1 us
    ppermute x5 -> x4, waiting for transfers between devices: 5.01 us -> 2.5 us  [passed_round(): lax.ppermute(value, axis, [(source, (source + steps) % count) for source...]
    ppermute x0 -> x1, starting transfers between devices: none -> 2.16 us  [passed_along(): lax.ppermute(value, axis, [(source, source + steps) for source in range(l...]
    pallas_call x1 -> x2, Pallas kernels: 2.25 us -> 3.82 us  [the longest x1 2.36 us: body(): pl.pallas_call(rim_y_kernel, out_shape=(whole, whole), in_specs=[SMEM] +...]
    ppermute x5 -> x4, starting transfers between devices: 9.59 us -> 9.35 us  [passed_round(): lax.ppermute(value, axis, [(source, (source + steps) % count) for source...]
  transfers between devices with their start and end apart: 6 -> 6, of which waited for: 3 -> 2; matrix products, arithmetic and copies ran while one was open for 0% -> 0% of each run, Pallas kernels for 26% -> 30%
where the time goes in v14:
time: 33.3 us; the launch traced here: 32.8 us
  Pallas kernels  15.1 us (45%)
  starting transfers between devices  14.4 us (43%)
  waiting for transfers between devices  2.5 us (8%)
  between operations  0.78 us (2%)
    ppermute x4, starting transfers between devices, passed_round(): lax.ppermute(value, axis, [(source, (source + steps) % count) for source...  9.35 us
    pallas_call x1, Pallas kernels, body(): pl.pallas_call(prepare_kernel, out_shape=(whole, whole, whole, planes, f3...  3.16 us
    pallas_call x1, Pallas kernels, body(): pl.pallas_call(inner_kernel, out_shape=(whole, planes, whole, f32(vectors...  2.96 us
    all_to_all x1, starting transfers between devices, body(): rows = lax.all_to_all(gram, ('gx', 'gy', 'gz'), 0, 0)  2.86 us
    ppermute x4, waiting for transfers between devices, passed_round(): lax.ppermute(value, axis, [(source, (source + steps) % count) for source...  2.5 us
    pallas_call x1, Pallas kernels, body(): pl.pallas_call(rim_y_kernel, out_shape=(whole, whole), in_specs=[SMEM] +...  2.36 us
    ppermute x1, starting transfers between devices, passed_along(): lax.ppermute(value, axis, [(source, source + steps) for source in range(l...  2.16 us
    pallas_call x1, Pallas kernels, body(): pl.pallas_call(outer_kernel, out_shape=(whole, f32(devices, 4, ny)), in_s...  1.77 us
  transfers between devices with their start and end apart: 6, of which 2 were waited for; matrix products, arithmetic and copies ran while one was open for 0% of the time, Pallas kernels for 30%

profile of v14, /device:TPU:0, one launch (start us, length us, event | category | flops | bytes accessed | tf_op | source)
XLA Modules:
  0.0 32.8 jit_solution(6800889153538480301)
XLA Ops:
  0.6 0.0 copy-start.2
  0.7 1.6 %take_faces.1 = (f32[2,4,3,8,16,128]{5,4,3,2,1,0:T(8,128)S(1)}, f32[2,4,2,8,128]{4,3,2,1,0:T(8,128)S(1)}, f32[16,128]{1,0:T(8,128)S(1)}) custom-call(f32[2,4,3,8,16,128]{5,4,3,2,1,0:T(8,128)} %fields_hbm.1), custom_call_target="tpu_custom_call" | custom-call | tf_op jit(solution)/shard_map/take_faces/pallas_call | solution.py:600
  2.3 4.5 %collective-permute-start = (f32[2,4,2,8,128]{4,3,2,1,0:T(8,128)S(1)}, f32[2,4,2,8,128]{4,3,2,1,0:T(8,128)S(1)}, u32[]{:S(2)}, u32[]{:S(2)}) collective-permute-start(f32[2,4,2,8,128]{4,3,2,1,0:T(8,128)S(1)} %get-tuple-element.44), channel_id=1, source_target_pairs={{0,28},{4,0},{8,4},{12,8},{16,12},{20,16},{24,20},{28,24},{1,29},{... | collective-permute-start | bytes 196616 | tf_op jit(solution)/shard_map/ppermute | solution.py:22
  6.9 1.5 %collective-permute-start.1 = (f32[16,128]{1,0:T(8,128)S(1)}, f32[16,128]{1,0:T(8,128)S(1)}, u32[]{:S(2)}, u32[]{:S(2)}) collective-permute-start(f32[16,128]{1,0:T(8,128)S(1)} %get-tuple-element.45), channel_id=1, source_target_pairs={{0,2},{2,0},{1,3},{3,1},{4,6},{6,4},{5,7},{7,5},{8,10},{10,8},{9,1... | collective-permute-start | bytes 24584 | tf_op jit(solution)/shard_map/ppermute | solution.py:22
  8.4 0.0 copy-done.5
  8.4 3.2 %prepare.1 = (f32[2,4,3,8,16,128]{5,4,3,2,1,0:T(8,128)S(1)}, f32[2,4,3,8,16,128]{5,4,3,2,1,0:T(8,128)S(1)}, f32[2,4,3,8,16,128]{5,4,3,2,1,0:T(8,128)S(1)}, f32[8...) custom-call(s32[6]{0:T(128)S(1)} %copy-done.2, f32[4]{0:T(128)S(1)} %copy-done.4, ...), custom_call_target="tpu_custom_call" | custom-call | flops 13107200 | bytes 6291456 | tf_op jit(solution)/shard_map/prepare/pallas_call | solution.py:618
  11.6 0.0 collective-permute-done.1.raw_yf_ref
  11.6 0.0 collective-permute-done.raw_xf_ref
  11.6 0.0 copy-start.3
  11.6 0.9 %slab_face.1 = (f32[2,4,3,8,16,128]{5,4,3,2,1,0:T(8,128)S(1)}, f32[2,4,2,8,128]{4,3,2,1,0:T(8,128)S(1)}, f32[16,128]{1,0:T(8,128)S(1)}, f32[2,4,2,8,128]{4,3,2,1...) custom-call(s32[6]{0:T(128)S(1)} %copy-done.2, ...), custom_call_target="tpu_custom_call", output_to_operand_aliasing={{0}: (3, {})} | custom-call | tf_op jit(solution)/shard_map/slab_face/pallas_call | solution.py:627
  12.5 1.6 %collective-permute-start.2 = (f32[2,4,2,16,128]{4,3,2,1,0:T(8,128)S(1)}, f32[2,4,2,16,128]{4,3,2,1,0:T(8,128)S(1)}, u32[]{:S(2)}, u32[]{:S(2)}) collective-permute-start(f32[2,4,2,16,128]{4,3,2,1,0:T(8,128)S(1)} %get-tuple-element.51), channel_id=1, source_target_pairs={{0,1},{1,0},{2,3},{3,2},{4,5},{5,4},{6,7},{7,6},{8,9},{9,8},{10,11... | collective-permute-start | bytes 393224 | tf_op jit(solution)/shard_map/ppermute | solution.py:22
  14.1 3.0 %apply_inner.1 = (f32[2,4,3,8,16,128]{5,4,3,2,1,0:T(8,128)S(1)}, f32[8,16,128]{2,1,0:T(8,128)S(1)}, f32[2,4,3,8,16,128]{5,4,3,2,1,0:T(8,128)S(1)}, f32[4,8,8,128...) custom-call(f32[2,4]{1,0:T(2,128)S(1)} %copy-done.3, ...), custom_call_target="tpu_custom_call", output_to_operand_aliasing={{0}: (5, {}), {1}: (6, {})} | custom-call | flops 13107200 | bytes 3145728 | tf_op jit(solution)/shard_map/apply_inner/pallas_call | solution.py:637
  17.0 0.5 %collective-permute-done.2.zf_ref = f32[2,4,2,16,128]{4,3,2,1,0:T(8,128)S(1)} collective-permute-done((f32[2,4,2,16,128]{4,3,2,1,0:T(8,128)S(1)}, f32[2,4,2,16,128]{4,3,2,1,0:T(8,128)S(1)}, u32[]{:S(2)}, u32[]{:S(2)}) %collective-permute-start.2) | collective-permute-done | bytes 131104 | tf_op jit(solution)/shard_map/ppermute | solution.py:22
  17.6 0.1 last_plane.1
  17.7 1.8 %apply_outer.1 = (f32[2,4,3,8,16,128]{5,4,3,2,1,0:T(8,128)S(1)}, f32[32,4,128]{2,1,0:T(4,128)}) custom-call(s32[6]{0:T(128)S(1)} %copy-done.2, f32[2,4]{1,0:T(2,128)S(1)} %copy-done.3, f32[2,4,3,8,16,128]{5,4,3,2,1,0:T(8,128)S(1)} %get-tuple-element.39.basis_ref, ...), custom_call_target="tpu_custom_call", output_to_operand_aliasing={{0}: (12, {})} | custom-call | flops 4915200 | bytes 1572864 | tf_op jit(solution)/shard_map/apply_outer/pallas_call | solution.py:658
  19.5 2.9 %all-to-all-start = ((f32[32,4,128]{2,1,0:T(4,128)}), f32[32,4,128]{2,1,0:T(4,128)S(1)}, u32[]{:S(2)}, u32[]{:S(2)}) async-start(f32[32,4,128]{2,1,0:T(4,128)} %get-tuple-element.64), calls=%async_computation | async-start | bytes 131072 | tf_op jit(solution)/shard_map/all_to_all | solution.py:669
  22.3 2.2 %collective-permute-start.4 = (f32[2,4,2,8,128]{4,3,2,1,0:T(8,128)S(1)}, f32[2,4,2,8,128]{4,3,2,1,0:T(8,128)S(1)}, u32[]{:S(2)}, u32[]{:S(2)}) collective-permute-start(f32[2,4,2,8,128]{4,3,2,1,0:T(8,128)S(1)} %get-tuple-element.69.hxf_ref), channel_id=1, source_target_pairs={{0,4},{4,8},{8,12},{12,16},{16,20},{20,24},{24,28},{1,5},{5,9},{9,... | collective-permute-start | bytes 196616 | tf_op jit(solution)/shard_map/ppermute | solution.py:28
  24.5 1.7 %collective-permute-start.3 = (f32[16,128]{1,0:T(8,128)S(1)}, f32[16,128]{1,0:T(8,128)S(1)}, u32[]{:S(2)}, u32[]{:S(2)}) collective-permute-start(f32[16,128]{1,0:T(8,128)S(1)} %get-tuple-element.66.hyf_ref), channel_id=1, source_target_pairs={{0,2},{2,0},{1,3},{3,1},{4,6},{6,4},{5,7},{7,5},{8,10},{10,8},{9,1... | collective-permute-start | bytes 24584 | tf_op jit(solution)/shard_map/ppermute | solution.py:22
  26.2 2.0 %collective-permute-done.3.hyf_ref = f32[16,128]{1,0:T(8,128)S(1)} collective-permute-done((f32[16,128]{1,0:T(8,128)S(1)}, f32[16,128]{1,0:T(8,128)S(1)}, u32[]{:S(2)}, u32[]{:S(2)}) %collective-permute-start.3) | collective-permute-done | bytes 8224 | tf_op jit(solution)/shard_map/ppermute | solution.py:22
  28.2 2.4 %add_y_rims.1 = (f32[2,4,3,8,16,128]{5,4,3,2,1,0:T(8,128)S(1)}, f32[2,4,3,8,16,128]{5,4,3,2,1,0:T(8,128)}) custom-call(s32[6]{0:T(128)S(1)} %copy-done.2, f32[2,4,3,8,16,128]{5,4,3,2,1,0:T(8,128)S(1)} %get-tuple-element.65.left_in, f32[16,128]{1,0:T(8,128)S(1)} %collective-permute-done.3.hyf_ref), custom_call_target="tpu_custom_call", output_to_operand_aliasing={{0}: (1, {})} | custom-call | tf_op jit(solution)/shard_map/add_y_rims/pallas_call | solution.py:673
  30.6 0.0 collective-permute-done.4.hxf_ref
  30.6 1.5 %add_x_rims.1 = (f32[2,4,3,8,16,128]{5,4,3,2,1,0:T(8,128)S(1)}, f32[2,4,3,8,16,128]{5,4,3,2,1,0:T(8,128)}) custom-call(s32[6]{0:T(128)S(1)} %copy-done.2, f32[2,4,3,8,16,128]{5,4,3,2,1,0:T(8,128)S(1)} %get-tuple-element.67.left_in, f32[2,4,3,8,16,128]{5,4,3,2,1,0:T(8,128)} %get-tuple-element.68.residual_in, ...), custom_call_target="tpu_custom_call", output_to_operand_aliasing={{0}: (1, {}), {1}: (2, {})} | custom-call | tf_op jit(solution)/shard_map/add_x_rims/pallas_call | solution.py:684
  32.1 0.0 all-to-all-done.rows_ref
  32.1 0.7 %sum_rows.1 = f32[2,4,4]{2,1,0:T(4,128)} custom-call(f32[32,4,128]{2,1,0:T(4,128)S(1)} %all-to-all-done.rows_ref), custom_call_target="tpu_custom_call" | custom-call | tf_op jit(solution)/shard_map/sum_rows/pallas_call | solution.py:696
  (9 shorter events, 0.0 us)
Async XLA Ops:
  0.6 7.8 %copy-start.2 = (s32[6]{0:T(128)S(1)}, s32[6]{0:T(128)}, u32[]{:S(2)}) copy-start(s32[6]{0:T(128)} %pml_ref.9) | copy-start | bytes 76
  0.6 7.8 %copy-start.1 = (f32[2,4,4]{2,1,0:T(4,128)S(1)}, f32[2,4,4]{2,1,0:T(4,128)}, u32[]{:S(2)}) copy-start(f32[2,4,4]{2,1,0:T(4,128)} %coeffs_ref.3) | copy-start | bytes 388
  0.7 7.8 %copy-start.5 = (f32[4]{0:T(128)S(1)}, f32[4]{0:T(128)}, u32[]{:S(2)}) copy-start(f32[4]{0:T(128)} %eps_loss_ref.1) | copy-start | bytes 52
  0.7 7.7 %copy-start.4 = (f32[4]{0:T(128)S(1)}, f32[4]{0:T(128)}, u32[]{:S(2)}) copy-start(f32[4]{0:T(128)} %eps_real_ref.1) | copy-start | bytes 52
  0.7 7.7 %copy-start = (s32[8,16,128]{2,1,0:T(8,128)S(1)}, s32[8,16,128]{2,1,0:T(8,128)}, u32[]{:S(2)}) copy-start(s32[8,16,128]{2,1,0:T(8,128)} %material_ref.1) | copy-start | bytes 196612
  2.3 9.3 %collective-permute-start = (f32[2,4,2,8,128]{4,3,2,1,0:T(8,128)S(1)}, f32[2,4,2,8,128]{4,3,2,1,0:T(8,128)S(1)}, u32[]{:S(2)}, u32[]{:S(2)}) collective-permute-start(f32[2,4,2,8,128]{4,3,2,1,0:T(8,128)S(1)} %get-tuple-element.44), channel_id=1, source_target_pairs={{0,28},{4,0},{8,4},{12,8},{16,12},{20,16},{24,20},{28,24},{1,29},{... | collective-permute-start | bytes 196616 | tf_op jit(solution)/shard_map/ppermute | solution.py:22
  6.9 4.7 %collective-permute-start.1 = (f32[16,128]{1,0:T(8,128)S(1)}, f32[16,128]{1,0:T(8,128)S(1)}, u32[]{:S(2)}, u32[]{:S(2)}) collective-permute-start(f32[16,128]{1,0:T(8,128)S(1)} %get-tuple-element.45), channel_id=1, source_target_pairs={{0,2},{2,0},{1,3},{3,1},{4,6},{6,4},{5,7},{7,5},{8,10},{10,8},{9,1... | collective-permute-start | bytes 24584 | tf_op jit(solution)/shard_map/ppermute | solution.py:22
  11.6 2.5 %copy-start.3 = (f32[2,4]{1,0:T(2,128)S(1)}, f32[2,4]{1,0:T(2,128)}, u32[]{:S(2)}) copy-start(f32[2,4]{1,0:T(2,128)} %ritz_ref.3) | copy-start | bytes 100
  12.5 5.0 %collective-permute-start.2 = (f32[2,4,2,16,128]{4,3,2,1,0:T(8,128)S(1)}, f32[2,4,2,16,128]{4,3,2,1,0:T(8,128)S(1)}, u32[]{:S(2)}, u32[]{:S(2)}) collective-permute-start(f32[2,4,2,16,128]{4,3,2,1,0:T(8,128)S(1)} %get-tuple-element.51), channel_id=1, source_target_pairs={{0,1},{1,0},{2,3},{3,2},{4,5},{5,4},{6,7},{7,6},{8,9},{9,8},{10,11... | collective-permute-start | bytes 393224 | tf_op jit(solution)/shard_map/ppermute | solution.py:22
  19.5 12.6 %all-to-all-start = ((f32[32,4,128]{2,1,0:T(4,128)}), f32[32,4,128]{2,1,0:T(4,128)S(1)}, u32[]{:S(2)}, u32[]{:S(2)}) async-start(f32[32,4,128]{2,1,0:T(4,128)} %get-tuple-element.64), calls=%async_computation | async-start | bytes 131072 | tf_op jit(solution)/shard_map/all_to_all | solution.py:669
  22.3 8.3 %collective-permute-start.4 = (f32[2,4,2,8,128]{4,3,2,1,0:T(8,128)S(1)}, f32[2,4,2,8,128]{4,3,2,1,0:T(8,128)S(1)}, u32[]{:S(2)}, u32[]{:S(2)}) collective-permute-start(f32[2,4,2,8,128]{4,3,2,1,0:T(8,128)S(1)} %get-tuple-element.69.hxf_ref), channel_id=1, source_target_pairs={{0,4},{4,8},{8,12},{12,16},{16,20},{20,24},{24,28},{1,5},{5,9},{9,... | collective-permute-start | bytes 196616 | tf_op jit(solution)/shard_map/ppermute | solution.py:28
  24.5 3.7 %collective-permute-start.3 = (f32[16,128]{1,0:T(8,128)S(1)}, f32[16,128]{1,0:T(8,128)S(1)}, u32[]{:S(2)}, u32[]{:S(2)}) collective-permute-start(f32[16,128]{1,0:T(8,128)S(1)} %get-tuple-element.66.hyf_ref), channel_id=1, source_target_pairs={{0,2},{2,0},{1,3},{3,1},{4,6},{6,4},{5,7},{7,5},{8,10},{10,8},{9,1... | collective-permute-start | bytes 24584 | tf_op jit(solution)/shard_map/ppermute | solution.py:22

commit v15 on v13

--- a/solution.py
+++ b/solution.py
@@ -587,8 +587,8 @@
         compiler_params=params,
         name="take_faces",
     )(pltpu.with_memory_space_constraint(fields, pltpu.HBM))
+    yf = passed_round(yf, "gy", -1)
     xf = passed_round(xf, "gx", -1)
-    yf = passed_round(yf, "gy", -1)
     cells = fields.size // 6 // vectors
 
     def cost(flops, passes):
@@ -602,7 +602,7 @@
         in_specs=[SMEM] * 4 + [VMEM] * 2,
         out_specs=(VMEM,) * 6,
         compiler_params=params,
-        cost_estimate=cost(800, 4),
+        cost_estimate=cost(80000, 400),
         name="prepare",
     )(pml_width, eps_real, eps_loss, coeffs, near, material)
     h, xf, yt, xadd, yadd, zf = pl.pallas_call(

time: 31.9 us -> 31.8 us (level)
  no operation moved by 1% of the time
where the time goes in v15:
time: 31.8 us; the launch traced here: 31.6 us
  Pallas kernels  13.5 us (42%)
  starting transfers between devices  12.3 us (39%)
  waiting for transfers between devices  5.01 us (16%)
  between operations  0.76 us (2%)
    ppermute x5, starting transfers between devices, passed_round(): lax.ppermute(value, axis, [(source, (source + steps) % count) for source...  9.32 us
    ppermute x5, waiting for transfers between devices, passed_round(): lax.ppermute(value, axis, [(source, (source + steps) % count) for source...  5.01 us
    pallas_call x1, Pallas kernels, body(): pl.pallas_call(prepare_kernel, out_shape=(whole, whole, whole, planes, f3...  3.16 us
    all_to_all x1, starting transfers between devices, body(): rows = lax.all_to_all(gram, ('gx', 'gy', 'gz'), 0, 0)  2.98 us
    pallas_call x1, Pallas kernels, body(): pl.pallas_call(inner_kernel, out_shape=(whole, planes, whole, f32(vectors...  2.96 us
    pallas_call x1, Pallas kernels, body(): pl.pallas_call(rim_kernel, out_shape=(whole, whole), in_specs=[SMEM] + [V...  2.25 us
    pallas_call x1, Pallas kernels, body(): pl.pallas_call(outer_kernel, out_shape=(whole, f32(devices, 4, ny)), in_s...  1.79 us
    pallas_call x1, Pallas kernels, body(): pl.pallas_call(face_kernel, out_shape=(whole, f32(*xf_shape), f32(*yf_sha...  1.64 us
  transfers between devices with their start and end apart: 6, of which 3 were waited for; matrix products, arithmetic and copies ran while one was open for 0% of the time, Pallas kernels for 26%

profile of v15, /device:TPU:0, one launch (start us, length us, event | category | flops | bytes accessed | tf_op | source)
XLA Modules:
  0.0 31.6 jit_solution(8937887886389685788)
XLA Ops:
  0.6 0.0 copy-start
  0.6 0.0 copy-start.1
  0.7 0.0 copy-start.5
  0.7 1.6 %take_faces.1 = (f32[2,4,3,8,16,128]{5,4,3,2,1,0:T(8,128)S(1)}, f32[2,4,2,8,128]{4,3,2,1,0:T(8,128)S(1)}, f32[16,128]{1,0:T(8,128)S(1)}) custom-call(f32[2,4,3,8,16,128]{5,4,3,2,1,0:T(8,128)} %fields_hbm.1), custom_call_target="tpu_custom_call" | custom-call | tf_op jit(solution)/shard_map/take_faces/pallas_call | solution.py:581
  2.3 3.0 %collective-permute-start.1 = (f32[16,128]{1,0:T(8,128)S(1)}, f32[16,128]{1,0:T(8,128)S(1)}, u32[]{:S(2)}, u32[]{:S(2)}) collective-permute-start(f32[16,128]{1,0:T(8,128)S(1)} %get-tuple-element.43), channel_id=1, source_target_pairs={{0,2},{2,0},{1,3},{3,1},{4,6},{6,4},{5,7},{7,5},{8,10},{10,8},{9,1... | collective-permute-start | bytes 24584 | tf_op jit(solution)/shard_map/ppermute | solution.py:22
  5.4 2.8 %collective-permute-start = (f32[2,4,2,8,128]{4,3,2,1,0:T(8,128)S(1)}, f32[2,4,2,8,128]{4,3,2,1,0:T(8,128)S(1)}, u32[]{:S(2)}, u32[]{:S(2)}) collective-permute-start(f32[2,4,2,8,128]{4,3,2,1,0:T(8,128)S(1)} %get-tuple-element.42), channel_id=1, source_target_pairs={{0,28},{4,0},{8,4},{12,8},{16,12},{20,16},{24,20},{28,24},{1,29},{... | collective-permute-start | bytes 196616 | tf_op jit(solution)/shard_map/ppermute | solution.py:22
  8.2 3.2 %prepare.1 = (f32[2,4,3,8,16,128]{5,4,3,2,1,0:T(8,128)S(1)}, f32[2,4,3,8,16,128]{5,4,3,2,1,0:T(8,128)S(1)}, f32[2,4,3,8,16,128]{5,4,3,2,1,0:T(8,128)S(1)}, f32[8...) custom-call(s32[6]{0:T(128)S(1)} %copy-done, f32[4]{0:T(128)S(1)} %copy-done.4, ...), custom_call_target="tpu_custom_call" | custom-call | flops 1310720000 | bytes 629145600 | tf_op jit(solution)/shard_map/prepare/pallas_call | solution.py:599
  11.3 0.0 collective-permute-done.1.raw_yf_ref
  11.3 0.0 collective-permute-done.raw_xf_ref
  11.3 0.0 copy-start.2
  11.4 0.9 %slab_face.1 = (f32[2,4,3,8,16,128]{5,4,3,2,1,0:T(8,128)S(1)}, f32[2,4,2,8,128]{4,3,2,1,0:T(8,128)S(1)}, f32[16,128]{1,0:T(8,128)S(1)}, f32[2,4,2,8,128]{4,3,2,1...) custom-call(s32[6]{0:T(128)S(1)} %copy-done, ...), custom_call_target="tpu_custom_call", output_to_operand_aliasing={{0}: (3, {})} | custom-call | tf_op jit(solution)/shard_map/slab_face/pallas_call | solution.py:608
  12.2 1.6 %collective-permute-start.2 = (f32[2,4,2,16,128]{4,3,2,1,0:T(8,128)S(1)}, f32[2,4,2,16,128]{4,3,2,1,0:T(8,128)S(1)}, u32[]{:S(2)}, u32[]{:S(2)}) collective-permute-start(f32[2,4,2,16,128]{4,3,2,1,0:T(8,128)S(1)} %get-tuple-element.49), channel_id=1, source_target_pairs={{0,1},{1,0},{2,3},{3,2},{4,5},{5,4},{6,7},{7,6},{8,9},{9,8},{10,11... | collective-permute-start | bytes 393224 | tf_op jit(solution)/shard_map/ppermute | solution.py:22
  13.8 3.0 %apply_inner.1 = (f32[2,4,3,8,16,128]{5,4,3,2,1,0:T(8,128)S(1)}, f32[8,16,128]{2,1,0:T(8,128)S(1)}, f32[2,4,3,8,16,128]{5,4,3,2,1,0:T(8,128)S(1)}, f32[4,8,8,128...) custom-call(f32[2,4]{1,0:T(2,128)S(1)} %copy-done.2, ...), custom_call_target="tpu_custom_call", output_to_operand_aliasing={{0}: (5, {}), {1}: (6, {})} | custom-call | flops 13107200 | bytes 3145728 | tf_op jit(solution)/shard_map/apply_inner/pallas_call | solution.py:618
  16.8 0.5 %collective-permute-done.2.zf_ref = f32[2,4,2,16,128]{4,3,2,1,0:T(8,128)S(1)} collective-permute-done((f32[2,4,2,16,128]{4,3,2,1,0:T(8,128)S(1)}, f32[2,4,2,16,128]{4,3,2,1,0:T(8,128)S(1)}, u32[]{:S(2)}, u32[]{:S(2)}) %collective-permute-start.2) | collective-permute-done | bytes 131104 | tf_op jit(solution)/shard_map/ppermute | solution.py:22
  17.3 0.1 last_plane.1
  17.4 1.8 %apply_outer.1 = (f32[2,4,3,8,16,128]{5,4,3,2,1,0:T(8,128)S(1)}, f32[32,4,128]{2,1,0:T(4,128)}) custom-call(s32[6]{0:T(128)S(1)} %copy-done, f32[2,4]{1,0:T(2,128)S(1)} %copy-done.2, f32[2,4,3,8,16,128]{5,4,3,2,1,0:T(8,128)S(1)} %get-tuple-element.37.basis_ref, ...), custom_call_target="tpu_custom_call", output_to_operand_aliasing={{0}: (12, {})} | custom-call | flops 4915200 | bytes 1572864 | tf_op jit(solution)/shard_map/apply_outer/pallas_call | solution.py:639
  19.2 3.0 %all-to-all-start = ((f32[32,4,128]{2,1,0:T(4,128)}), f32[32,4,128]{2,1,0:T(4,128)S(1)}, u32[]{:S(2)}, u32[]{:S(2)}) async-start(f32[32,4,128]{2,1,0:T(4,128)} %get-tuple-element.62), calls=%async_computation | async-start | bytes 131072 | tf_op jit(solution)/shard_map/all_to_all | solution.py:650
  22.2 0.3 collective-permute-start.3
  22.5 1.7 %collective-permute-start.4 = (f32[16,128]{1,0:T(8,128)S(1)}, f32[16,128]{1,0:T(8,128)S(1)}, u32[]{:S(2)}, u32[]{:S(2)}) collective-permute-start(f32[16,128]{1,0:T(8,128)S(1)} %get-tuple-element.65.hyf_ref), channel_id=1, source_target_pairs={{0,2},{2,0},{1,3},{3,1},{4,6},{6,4},{5,7},{7,5},{8,10},{10,8},{9,1... | collective-permute-start | bytes 24584 | tf_op jit(solution)/shard_map/ppermute | solution.py:22
  24.2 2.0 %collective-permute-done.4.hyf_ref = f32[16,128]{1,0:T(8,128)S(1)} collective-permute-done((f32[16,128]{1,0:T(8,128)S(1)}, f32[16,128]{1,0:T(8,128)S(1)}, u32[]{:S(2)}, u32[]{:S(2)}) %collective-permute-start.4) | collective-permute-done | bytes 8224 | tf_op jit(solution)/shard_map/ppermute | solution.py:22
  26.2 2.5 %collective-permute-done.3.hxf_ref = f32[2,4,2,8,128]{4,3,2,1,0:T(8,128)S(1)} collective-permute-done((f32[2,4,2,8,128]{4,3,2,1,0:T(8,128)S(1)}, f32[2,4,2,8,128]{4,3,2,1,0:T(8,128)S(1)}, u32[]{:S(2)}, u32[]{:S(2)}) %collective-permute-start.3) | collective-permute-done | bytes 65568 | tf_op jit(solution)/shard_map/ppermute | solution.py:22
  28.7 2.3 %add_rims.1 = (f32[2,4,3,8,16,128]{5,4,3,2,1,0:T(8,128)S(1)}, f32[2,4,3,8,16,128]{5,4,3,2,1,0:T(8,128)}) custom-call(s32[6]{0:T(128)S(1)} %copy-done, f32[2,4,3,8,16,128]{5,4,3,2,1,0:T(8,128)S(1)} %get-tuple-element.63.left_in, f32[2,4,2,8,128]{4,3,2,1,0:T(8,128)S(1)} %collective-permute-done.3.hxf_ref, ...), custom_call_target="tpu_custom_call", output_to_operand_aliasing={{0}: (1, {})} | custom-call | tf_op jit(solution)/shard_map/add_rims/pallas_call | solution.py:653
  30.9 0.0 all-to-all-done.rows_ref
  30.9 0.7 %sum_rows.1 = f32[2,4,4]{2,1,0:T(4,128)} custom-call(f32[32,4,128]{2,1,0:T(4,128)S(1)} %all-to-all-done.rows_ref), custom_call_target="tpu_custom_call" | custom-call | tf_op jit(solution)/shard_map/sum_rows/pallas_call | solution.py:665
  (8 shorter events, 0.0 us)
Async XLA Ops:
  0.6 7.5 %copy-start = (s32[6]{0:T(128)S(1)}, s32[6]{0:T(128)}, u32[]{:S(2)}) copy-start(s32[6]{0:T(128)} %pml_ref.7) | copy-start | bytes 76
  0.6 7.5 %copy-start.1 = (f32[2,4,4]{2,1,0:T(4,128)S(1)}, f32[2,4,4]{2,1,0:T(4,128)}, u32[]{:S(2)}) copy-start(f32[2,4,4]{2,1,0:T(4,128)} %coeffs_ref.3) | copy-start | bytes 388
  0.7 7.5 %copy-start.5 = (f32[4]{0:T(128)S(1)}, f32[4]{0:T(128)}, u32[]{:S(2)}) copy-start(f32[4]{0:T(128)} %eps_loss_ref.1) | copy-start | bytes 52
  0.7 7.5 %copy-start.4 = (f32[4]{0:T(128)S(1)}, f32[4]{0:T(128)}, u32[]{:S(2)}) copy-start(f32[4]{0:T(128)} %eps_real_ref.1) | copy-start | bytes 52
  0.7 7.5 %copy-start.3 = (s32[8,16,128]{2,1,0:T(8,128)S(1)}, s32[8,16,128]{2,1,0:T(8,128)}, u32[]{:S(2)}) copy-start(s32[8,16,128]{2,1,0:T(8,128)} %material_ref.1) | copy-start | bytes 196612
  2.3 9.0 %collective-permute-start.1 = (f32[16,128]{1,0:T(8,128)S(1)}, f32[16,128]{1,0:T(8,128)S(1)}, u32[]{:S(2)}, u32[]{:S(2)}) collective-permute-start(f32[16,128]{1,0:T(8,128)S(1)} %get-tuple-element.43), channel_id=1, source_target_pairs={{0,2},{2,0},{1,3},{3,1},{4,6},{6,4},{5,7},{7,5},{8,10},{10,8},{9,1... | collective-permute-start | bytes 24584 | tf_op jit(solution)/shard_map/ppermute | solution.py:22
  5.4 6.0 %collective-permute-start = (f32[2,4,2,8,128]{4,3,2,1,0:T(8,128)S(1)}, f32[2,4,2,8,128]{4,3,2,1,0:T(8,128)S(1)}, u32[]{:S(2)}, u32[]{:S(2)}) collective-permute-start(f32[2,4,2,8,128]{4,3,2,1,0:T(8,128)S(1)} %get-tuple-element.42), channel_id=1, source_target_pairs={{0,28},{4,0},{8,4},{12,8},{16,12},{20,16},{24,20},{28,24},{1,29},{... | collective-permute-start | bytes 196616 | tf_op jit(solution)/shard_map/ppermute | solution.py:22
  11.3 2.5 %copy-start.2 = (f32[2,4]{1,0:T(2,128)S(1)}, f32[2,4]{1,0:T(2,128)}, u32[]{:S(2)}) copy-start(f32[2,4]{1,0:T(2,128)} %ritz_ref.3) | copy-start | bytes 100
  12.2 5.0 %collective-permute-start.2 = (f32[2,4,2,16,128]{4,3,2,1,0:T(8,128)S(1)}, f32[2,4,2,16,128]{4,3,2,1,0:T(8,128)S(1)}, u32[]{:S(2)}, u32[]{:S(2)}) collective-permute-start(f32[2,4,2,16,128]{4,3,2,1,0:T(8,128)S(1)} %get-tuple-element.49), channel_id=1, source_target_pairs={{0,1},{1,0},{2,3},{3,2},{4,5},{5,4},{6,7},{7,6},{8,9},{9,8},{10,11... | collective-permute-start | bytes 393224 | tf_op jit(solution)/shard_map/ppermute | solution.py:22
  19.2 11.7 %all-to-all-start = ((f32[32,4,128]{2,1,0:T(4,128)}), f32[32,4,128]{2,1,0:T(4,128)S(1)}, u32[]{:S(2)}, u32[]{:S(2)}) async-start(f32[32,4,128]{2,1,0:T(4,128)} %get-tuple-element.62), calls=%async_computation | async-start | bytes 131072 | tf_op jit(solution)/shard_map/all_to_all | solution.py:650
  22.2 6.5 %collective-permute-start.3 = (f32[2,4,2,8,128]{4,3,2,1,0:T(8,128)S(1)}, f32[2,4,2,8,128]{4,3,2,1,0:T(8,128)S(1)}, u32[]{:S(2)}, u32[]{:S(2)}) collective-permute-start(f32[2,4,2,8,128]{4,3,2,1,0:T(8,128)S(1)} %get-tuple-element.64.hxf_ref), channel_id=1, source_target_pairs={{0,4},{4,8},{8,12},{12,16},{16,20},{20,24},{24,28},{28,0},{1,5},{5... | collective-permute-start | bytes 196616 | tf_op jit(solution)/shard_map/ppermute | solution.py:22
  22.5 3.7 %collective-permute-start.4 = (f32[16,128]{1,0:T(8,128)S(1)}, f32[16,128]{1,0:T(8,128)S(1)}, u32[]{:S(2)}, u32[]{:S(2)}) collective-permute-start(f32[16,128]{1,0:T(8,128)S(1)} %get-tuple-element.65.hyf_ref), channel_id=1, source_target_pairs={{0,2},{2,0},{1,3},{3,1},{4,6},{6,4},{5,7},{7,5},{8,10},{10,8},{9,1... | collective-permute-start | bytes 24584 | tf_op jit(solution)/shard_map/ppermute | solution.py:22

commit v16 on v12

--- a/solution.py
+++ b/solution.py
@@ -20,6 +20,12 @@
 def passed_round(value, axis, steps):
     count = lax.axis_size(axis)
     return lax.ppermute(value, axis, [(source, (source + steps) % count) for source in range(count)])
+
+
+def passed_along(value, axis, steps):
+    count = lax.axis_size(axis)
+    leading, last = (max(0, -steps), min(count, count - steps))
+    return lax.ppermute(value, axis, [(source, source + steps) for source in range(leading, last)])
 
 
 def inverse_stretch(places, length, low_width, high_width):
@@ -586,8 +592,8 @@
         compiler_params=params,
         name="take_faces",
     )(pltpu.with_memory_space_constraint(fields, pltpu.HBM))
+    yf = passed_round(yf, "gy", -1)
     xf = passed_round(xf, "gx", -1)
-    yf = passed_round(yf, "gy", -1)
     cells = fields.size // 6 // vectors
 
     def cost(flops, passes):
@@ -601,7 +607,7 @@
         in_specs=[SMEM] * 4 + [VMEM] * 2,
         out_specs=(VMEM,) * 6,
         compiler_params=params,
-        cost_estimate=cost(800, 4),
+        cost_estimate=cost(80000, 400),
         name="prepare",
     )(pml_width, eps_real, eps_loss, coeffs, near, material)
     h, xf, yt, xadd, yadd, zf = pl.pallas_call(
@@ -637,7 +643,7 @@
     devices = lax.axis_size("gx") * lax.axis_size("gy") * lax.axis_size("gz")
     left, gram = pl.pallas_call(
         outer_kernel,
-        out_shape=(whole, pltpu.VMEM((devices, 1, ny), jnp.float32)),
+        out_shape=(whole, f32(devices, 1, ny)),
         in_specs=[SMEM] * 2 + [VMEM] * 13,
         out_specs=(VMEM,) * 2,
         input_output_aliases={12: 0},
@@ -647,8 +653,8 @@
     )(pml_width, ritz, basis, loss, table, sz, h, zf, xf, yt, hxf, hyf, left, acc, before)
     gram, hxf, hyf = lax.optimization_barrier((gram, hxf, hyf))
     rows = lax.all_to_all(gram, ("gx", "gy", "gz"), 0, 0)
-    from_x = passed_round(hxf, "gx", 1)
     from_y = passed_round(hyf, "gy", 1)
+    from_x = passed_along(hxf, "gx", 1)
     _, residual = pl.pallas_call(
         rim_kernel,
         out_shape=(whole, whole),
@@ -657,7 +663,7 @@
         scratch_shapes=[scratch(*xf_shape), scratch(nz, nx, ny), pltpu.SemaphoreType.DMA((nz,))],
         input_output_aliases={1: 0},
         compiler_params=params,
-        cost_estimate=pl.CostEstimate(flops=0, bytes_accessed=0, transcendentals=0),
+        cost_estimate=cost(80000, 400),
         name="add_rims",
     )(pml_width, left, from_x, from_y)
     rows, residual = lax.optimization_barrier((rows, residual))

time: 32.3 us -> 34 us (1.053)
  waiting for transfers between devices: 3.58 us -> 5.4 us
    all_to_all x1, waiting for transfers between devices: 1.19 us -> 4.89 us  [body(): rows = lax.all_to_all(gram, ('gx', 'gy', 'gz'), 0, 0)]
    ppermute x5 -> x4, waiting for transfers between devices: 2.4 us -> 0.51 us  [passed_round(): lax.ppermute(value, axis, [(source, (source + steps) % count) for source...]
    ppermute x5 -> x4, starting transfers between devices: 9.45 us -> 7.92 us  [passed_round(): lax.ppermute(value, axis, [(source, (source + steps) % count) for source...]
    ppermute x0 -> x1, starting transfers between devices: none -> 1.28 us  [passed_along(): lax.ppermute(value, axis, [(source, source + steps) for source in range(l...]
  transfers between devices with their start and end apart: 6 -> 6, of which waited for: 3 -> 2; matrix products, arithmetic and copies ran while one was open for 0% -> 0% of each run, Pallas kernels for 26% -> 25%
where the time goes in v16:
time: 34 us; the launch traced here: 33.8 us
  starting transfers between devices  14.1 us (41%)
  Pallas kernels  13.5 us (40%)
  waiting for transfers between devices  5.4 us (16%)
  between operations  0.78 us (2%)
    ppermute x4, starting transfers between devices, passed_round(): lax.ppermute(value, axis, [(source, (source + steps) % count) for source...  7.92 us
    all_to_all x1, starting transfers between devices, body(): rows = lax.all_to_all(gram, ('gx', 'gy', 'gz'), 0, 0)  4.95 us
    all_to_all x1, waiting for transfers between devices, body(): rows = lax.all_to_all(gram, ('gx', 'gy', 'gz'), 0, 0)  4.89 us
    pallas_call x1, Pallas kernels, body(): pl.pallas_call(prepare_kernel, out_shape=(whole, whole, whole, planes, f3...  3.16 us
    pallas_call x1, Pallas kernels, body(): pl.pallas_call(inner_kernel, out_shape=(whole, planes, whole, f32(vectors...  2.96 us
    pallas_call x1, Pallas kernels, body(): pl.pallas_call(rim_kernel, out_shape=(whole, whole), in_specs=[SMEM] + [V...  2.25 us
    pallas_call x1, Pallas kernels, body(): pl.pallas_call(outer_kernel, out_shape=(whole, f32(devices, 1, ny)), in_s...  1.76 us
    pallas_call x1, Pallas kernels, body(): pl.pallas_call(face_kernel, out_shape=(whole, f32(*xf_shape), f32(*yf_sha...  1.64 us
  transfers between devices with their start and end apart: 6, of which 2 were waited for; matrix products, arithmetic and copies ran while one was open for 0% of the time, Pallas kernels for 25%

profile of v16, /device:TPU:0, one launch (start us, length us, event | category | flops | bytes accessed | tf_op | source)
XLA Modules:
  0.0 33.8 jit_solution(508305494401345138)
XLA Ops:
  0.6 0.0 copy-start.2
  0.7 1.6 %take_faces.1 = (f32[2,4,3,8,16,128]{5,4,3,2,1,0:T(8,128)S(1)}, f32[2,4,2,8,128]{4,3,2,1,0:T(8,128)S(1)}, f32[16,128]{1,0:T(8,128)S(1)}) custom-call(f32[2,4,3,8,16,128]{5,4,3,2,1,0:T(8,128)} %fields_hbm.1), custom_call_target="tpu_custom_call" | custom-call | tf_op jit(solution)/shard_map/take_faces/pallas_call | solution.py:586
  2.3 3.0 %collective-permute-start.1 = (f32[16,128]{1,0:T(8,128)S(1)}, f32[16,128]{1,0:T(8,128)S(1)}, u32[]{:S(2)}, u32[]{:S(2)}) collective-permute-start(f32[16,128]{1,0:T(8,128)S(1)} %get-tuple-element.43), channel_id=1, source_target_pairs={{0,2},{2,0},{1,3},{3,1},{4,6},{6,4},{5,7},{7,5},{8,10},{10,8},{9,1... | collective-permute-start | bytes 24584 | tf_op jit(solution)/shard_map/ppermute | solution.py:22
  5.4 2.8 %collective-permute-start = (f32[2,4,2,8,128]{4,3,2,1,0:T(8,128)S(1)}, f32[2,4,2,8,128]{4,3,2,1,0:T(8,128)S(1)}, u32[]{:S(2)}, u32[]{:S(2)}) collective-permute-start(f32[2,4,2,8,128]{4,3,2,1,0:T(8,128)S(1)} %get-tuple-element.42), channel_id=1, source_target_pairs={{0,28},{4,0},{8,4},{12,8},{16,12},{20,16},{24,20},{28,24},{1,29},{... | collective-permute-start | bytes 196616 | tf_op jit(solution)/shard_map/ppermute | solution.py:22
  8.1 0.0 copy-done.2
  8.1 0.0 copy-done.5
  8.2 3.2 %prepare.1 = (f32[2,4,3,8,16,128]{5,4,3,2,1,0:T(8,128)S(1)}, f32[2,4,3,8,16,128]{5,4,3,2,1,0:T(8,128)S(1)}, f32[2,4,3,8,16,128]{5,4,3,2,1,0:T(8,128)S(1)}, f32[8...) custom-call(s32[6]{0:T(128)S(1)} %copy-done.2, f32[4]{0:T(128)S(1)} %copy-done.4, ...), custom_call_target="tpu_custom_call" | custom-call | flops 1310720000 | bytes 629145600 | tf_op jit(solution)/shard_map/prepare/pallas_call | solution.py:604
  11.3 0.0 collective-permute-done.1.raw_yf_ref
  11.3 0.0 collective-permute-done.raw_xf_ref
  11.3 0.0 copy-start.1
  11.4 0.9 %slab_face.1 = (f32[2,4,3,8,16,128]{5,4,3,2,1,0:T(8,128)S(1)}, f32[2,4,2,8,128]{4,3,2,1,0:T(8,128)S(1)}, f32[16,128]{1,0:T(8,128)S(1)}, f32[2,4,2,8,128]{4,3,2,1...) custom-call(s32[6]{0:T(128)S(1)} %copy-done.2, ...), custom_call_target="tpu_custom_call", output_to_operand_aliasing={{0}: (3, {})} | custom-call | tf_op jit(solution)/shard_map/slab_face/pallas_call | solution.py:613
  12.2 1.6 %collective-permute-start.2 = (f32[2,4,2,16,128]{4,3,2,1,0:T(8,128)S(1)}, f32[2,4,2,16,128]{4,3,2,1,0:T(8,128)S(1)}, u32[]{:S(2)}, u32[]{:S(2)}) collective-permute-start(f32[2,4,2,16,128]{4,3,2,1,0:T(8,128)S(1)} %get-tuple-element.49), channel_id=1, source_target_pairs={{0,1},{1,0},{2,3},{3,2},{4,5},{5,4},{6,7},{7,6},{8,9},{9,8},{10,11... | collective-permute-start | bytes 393224 | tf_op jit(solution)/shard_map/ppermute | solution.py:22
  13.8 3.0 %apply_inner.1 = (f32[2,4,3,8,16,128]{5,4,3,2,1,0:T(8,128)S(1)}, f32[8,16,128]{2,1,0:T(8,128)S(1)}, f32[2,4,3,8,16,128]{5,4,3,2,1,0:T(8,128)S(1)}, f32[4,8,8,128...) custom-call(f32[2,4]{1,0:T(2,128)S(1)} %copy-done.1, ...), custom_call_target="tpu_custom_call", output_to_operand_aliasing={{0}: (5, {}), {1}: (6, {})} | custom-call | flops 13107200 | bytes 3145728 | tf_op jit(solution)/shard_map/apply_inner/pallas_call | solution.py:623
  16.8 0.5 %collective-permute-done.2.zf_ref = f32[2,4,2,16,128]{4,3,2,1,0:T(8,128)S(1)} collective-permute-done((f32[2,4,2,16,128]{4,3,2,1,0:T(8,128)S(1)}, f32[2,4,2,16,128]{4,3,2,1,0:T(8,128)S(1)}, u32[]{:S(2)}, u32[]{:S(2)}) %collective-permute-start.2) | collective-permute-done | bytes 131104 | tf_op jit(solution)/shard_map/ppermute | solution.py:22
  17.3 0.1 last_plane.1
  17.4 1.8 %apply_outer.1 = (f32[2,4,3,8,16,128]{5,4,3,2,1,0:T(8,128)S(1)}, f32[32,1,128]{2,1,0:T(1,128)}) custom-call(s32[6]{0:T(128)S(1)} %copy-done.2, f32[2,4]{1,0:T(2,128)S(1)} %copy-done.1, f32[2,4,3,8,16,128]{5,4,3,2,1,0:T(8,128)S(1)} %get-tuple-element.37.basis_ref, ...), custom_call_target="tpu_custom_call", output_to_operand_aliasing={{0}: (12, {})} | custom-call | flops 4915200 | bytes 1572864 | tf_op jit(solution)/shard_map/apply_outer/pallas_call | solution.py:644
  19.2 1.3 %collective-permute-start.3 = (f32[2,4,2,8,128]{4,3,2,1,0:T(8,128)S(1)}, f32[2,4,2,8,128]{4,3,2,1,0:T(8,128)S(1)}, u32[]{:S(2)}, u32[]{:S(2)}) collective-permute-start(f32[2,4,2,8,128]{4,3,2,1,0:T(8,128)S(1)} %get-tuple-element.64.hxf_ref), channel_id=1, source_target_pairs={{0,4},{4,8},{8,12},{12,16},{16,20},{20,24},{24,28},{1,5},{5,9},{9,... | collective-permute-start | bytes 196616 | tf_op jit(solution)/shard_map/ppermute | solution.py:28
  20.5 0.6 %collective-permute-start.4 = (f32[16,128]{1,0:T(8,128)S(1)}, f32[16,128]{1,0:T(8,128)S(1)}, u32[]{:S(2)}, u32[]{:S(2)}) collective-permute-start(f32[16,128]{1,0:T(8,128)S(1)} %get-tuple-element.65.hyf_ref), channel_id=1, source_target_pairs={{0,2},{2,0},{1,3},{3,1},{4,6},{6,4},{5,7},{7,5},{8,10},{10,8},{9,1... | collective-permute-start | bytes 24584 | tf_op jit(solution)/shard_map/ppermute | solution.py:22
  21.0 4.9 %all-to-all-start = ((f32[32,1,128]{2,1,0:T(1,128)}), f32[32,1,128]{2,1,0:T(1,128)S(1)}, u32[]{:S(2)}, u32[]{:S(2)}) async-start(f32[32,1,128]{2,1,0:T(1,128)} %get-tuple-element.62), calls=%async_computation | async-start | bytes 32768 | tf_op jit(solution)/shard_map/all_to_all | solution.py:655
  26.0 0.0 collective-permute-done.4.hyf_ref
  26.0 0.0 collective-permute-done.3.hxf_ref
  26.0 2.3 %add_rims.1 = (f32[2,4,3,8,16,128]{5,4,3,2,1,0:T(8,128)S(1)}, f32[2,4,3,8,16,128]{5,4,3,2,1,0:T(8,128)}) custom-call(s32[6]{0:T(128)S(1)} %copy-done.2, f32[2,4,3,8,16,128]{5,4,3,2,1,0:T(8,128)S(1)} %get-tuple-element.63.left_in, f32[2,4,2,8,128]{4,3,2,1,0:T(8,128)S(1)} %collective-permute-done.3.hxf_ref, ...), custom_call_target="tpu_custom_call", output_to_operand_aliasing={{0}: (1, {})} | custom-call | flops 1310720000 | bytes 629145600 | tf_op jit(solution)/shard_map/add_rims/pallas_call | solution.py:658
  28.3 4.9 %all-to-all-done.rows_ref = f32[32,1,128]{2,1,0:T(1,128)S(1)} async-done(((f32[32,1,128]{2,1,0:T(1,128)}), f32[32,1,128]{2,1,0:T(1,128)S(1)}, u32[]{:S(2)}, u32[]{:S(2)}) %all-to-all-start) | async-done | bytes 16416 | tf_op jit(solution)/shard_map/all_to_all | solution.py:655
  33.2 0.7 %sum_rows.1 = f32[2,4,4]{2,1,0:T(4,128)} custom-call(f32[32,1,128]{2,1,0:T(1,128)S(1)} %all-to-all-done.rows_ref), custom_call_target="tpu_custom_call" | custom-call | tf_op jit(solution)/shard_map/sum_rows/pallas_call | solution.py:670
  (8 shorter events, 0.0 us)
Async XLA Ops:
  0.6 7.5 %copy-start.2 = (s32[6]{0:T(128)S(1)}, s32[6]{0:T(128)}, u32[]{:S(2)}) copy-start(s32[6]{0:T(128)} %pml_ref.7) | copy-start | bytes 76
  0.6 7.5 %copy-start = (f32[2,4,4]{2,1,0:T(4,128)S(1)}, f32[2,4,4]{2,1,0:T(4,128)}, u32[]{:S(2)}) copy-start(f32[2,4,4]{2,1,0:T(4,128)} %coeffs_ref.3) | copy-start | bytes 388
  0.7 7.5 %copy-start.5 = (f32[4]{0:T(128)S(1)}, f32[4]{0:T(128)}, u32[]{:S(2)}) copy-start(f32[4]{0:T(128)} %eps_loss_ref.1) | copy-start | bytes 52
  0.7 7.5 %copy-start.4 = (f32[4]{0:T(128)S(1)}, f32[4]{0:T(128)}, u32[]{:S(2)}) copy-start(f32[4]{0:T(128)} %eps_real_ref.1) | copy-start | bytes 52
  0.7 7.5 %copy-start.3 = (s32[8,16,128]{2,1,0:T(8,128)S(1)}, s32[8,16,128]{2,1,0:T(8,128)}, u32[]{:S(2)}) copy-start(s32[8,16,128]{2,1,0:T(8,128)} %material_ref.1) | copy-start | bytes 196612
  2.3 9.0 %collective-permute-start.1 = (f32[16,128]{1,0:T(8,128)S(1)}, f32[16,128]{1,0:T(8,128)S(1)}, u32[]{:S(2)}, u32[]{:S(2)}) collective-permute-start(f32[16,128]{1,0:T(8,128)S(1)} %get-tuple-element.43), channel_id=1, source_target_pairs={{0,2},{2,0},{1,3},{3,1},{4,6},{6,4},{5,7},{7,5},{8,10},{10,8},{9,1... | collective-permute-start | bytes 24584 | tf_op jit(solution)/shard_map/ppermute | solution.py:22
  5.4 6.0 %collective-permute-start = (f32[2,4,2,8,128]{4,3,2,1,0:T(8,128)S(1)}, f32[2,4,2,8,128]{4,3,2,1,0:T(8,128)S(1)}, u32[]{:S(2)}, u32[]{:S(2)}) collective-permute-start(f32[2,4,2,8,128]{4,3,2,1,0:T(8,128)S(1)} %get-tuple-element.42), channel_id=1, source_target_pairs={{0,28},{4,0},{8,4},{12,8},{16,12},{20,16},{24,20},{28,24},{1,29},{... | collective-permute-start | bytes 196616 | tf_op jit(solution)/shard_map/ppermute | solution.py:22
  11.3 2.5 %copy-start.1 = (f32[2,4]{1,0:T(2,128)S(1)}, f32[2,4]{1,0:T(2,128)}, u32[]{:S(2)}) copy-start(f32[2,4]{1,0:T(2,128)} %ritz_ref.3) | copy-start | bytes 100
  12.2 5.0 %collective-permute-start.2 = (f32[2,4,2,16,128]{4,3,2,1,0:T(8,128)S(1)}, f32[2,4,2,16,128]{4,3,2,1,0:T(8,128)S(1)}, u32[]{:S(2)}, u32[]{:S(2)}) collective-permute-start(f32[2,4,2,16,128]{4,3,2,1,0:T(8,128)S(1)} %get-tuple-element.49), channel_id=1, source_target_pairs={{0,1},{1,0},{2,3},{3,2},{4,5},{5,4},{6,7},{7,6},{8,9},{9,8},{10,11... | collective-permute-start | bytes 393224 | tf_op jit(solution)/shard_map/ppermute | solution.py:22
  19.2 6.8 %collective-permute-start.3 = (f32[2,4,2,8,128]{4,3,2,1,0:T(8,128)S(1)}, f32[2,4,2,8,128]{4,3,2,1,0:T(8,128)S(1)}, u32[]{:S(2)}, u32[]{:S(2)}) collective-permute-start(f32[2,4,2,8,128]{4,3,2,1,0:T(8,128)S(1)} %get-tuple-element.64.hxf_ref), channel_id=1, source_target_pairs={{0,4},{4,8},{8,12},{12,16},{16,20},{20,24},{24,28},{1,5},{5,9},{9,... | collective-permute-start | bytes 196616 | tf_op jit(solution)/shard_map/ppermute | solution.py:28
  20.5 5.5 %collective-permute-start.4 = (f32[16,128]{1,0:T(8,128)S(1)}, f32[16,128]{1,0:T(8,128)S(1)}, u32[]{:S(2)}, u32[]{:S(2)}) collective-permute-start(f32[16,128]{1,0:T(8,128)S(1)} %get-tuple-element.65.hyf_ref), channel_id=1, source_target_pairs={{0,2},{2,0},{1,3},{3,1},{4,6},{6,4},{5,7},{7,5},{8,10},{10,8},{9,1... | collective-permute-start | bytes 24584 | tf_op jit(solution)/shard_map/ppermute | solution.py:22
  21.0 12.1 %all-to-all-start = ((f32[32,1,128]{2,1,0:T(1,128)}), f32[32,1,128]{2,1,0:T(1,128)S(1)}, u32[]{:S(2)}, u32[]{:S(2)}) async-start(f32[32,1,128]{2,1,0:T(1,128)} %get-tuple-element.62), calls=%async_computation | async-start | bytes 32768 | tf_op jit(solution)/shard_map/all_to_all | solution.py:655

commit v17 on v15

--- a/solution.py
+++ b/solution.py
@@ -20,6 +20,12 @@
 def passed_round(value, axis, steps):
     count = lax.axis_size(axis)
     return lax.ppermute(value, axis, [(source, (source + steps) % count) for source in range(count)])
+
+
+def passed_along(value, axis, steps):
+    count = lax.axis_size(axis)
+    leading, last = (max(0, -steps), min(count, count - steps))
+    return lax.ppermute(value, axis, [(source, source + steps) for source in range(leading, last)])
 
 
 def inverse_stretch(places, length, low_width, high_width):
@@ -502,7 +508,7 @@
     return values[0]
 
 
-def gather_kernel(rows_ref, gram_ref):
+def put_gram(rows_ref, gram_ref):
     vectors = gram_ref.shape[1]
     total = tree_sum([rows_ref[device] for device in range(rows_ref.shape[0])])[0:1]
     count = total.shape[1]
@@ -513,8 +519,14 @@
             gram_ref[part, a:a + 1] = turned[:, :vectors]
 
 
-def rim_kernel(pml_ref, left_in, hxf_ref, hyf_ref, left_ref, residual_hbm, xadd_ref, yadd_ref, sems):
+def rim_kernel(
+    pml_ref, left_in, hxf_ref, hyf_ref, rows_ref,
+    left_ref, residual_hbm, gram_hbm, xadd_ref, yadd_ref, gram_ref, sems, gram_sem,
+):
     del left_in
+    put_gram(rows_ref, gram_ref)
+    gram_copy = pltpu.make_async_copy(gram_ref, gram_hbm, gram_sem)
+    gram_copy.start()
     _, vectors, _, nz, nx, ny = left_ref.shape
     parts = range(2)
     both = 2 * vectors
@@ -567,6 +579,8 @@
     @pl.loop(0, nz)
     def _(z):
         kept(z).wait()
+
+    gram_copy.wait()
 
 
 def body(fields, material, pml_width, eps_real, eps_loss, coeffs, ritz):
@@ -647,29 +661,23 @@
         name="apply_outer",
     )(pml_width, ritz, basis, loss, table, sz, h, zf, xf, yt, hxf, hyf, left, acc, before)
     gram, hxf, hyf = lax.optimization_barrier((gram, hxf, hyf))
-    rows = lax.all_to_all(gram, ("gx", "gy", "gz"), 0, 0)
-    from_x = passed_round(hxf, "gx", 1)
+    rows = lax.all_to_all(gram, ("gx", "gy", "gz"), 0, 0, axis_index_groups=[list(range(devices))[::-1]])
+    from_x = passed_along(hxf, "gx", 1)
     from_y = passed_round(hyf, "gy", 1)
-    _, residual = pl.pallas_call(
+    _, residual, gram = pl.pallas_call(
         rim_kernel,
-        out_shape=(whole, whole),
-        in_specs=[SMEM] + [VMEM] * 3,
-        out_specs=(VMEM, HBM),
-        scratch_shapes=[scratch(*xf_shape), scratch(nz, nx, ny), pltpu.SemaphoreType.DMA((nz,))],
+        out_shape=(whole, whole, f32(2, vectors, vectors)),
+        in_specs=[SMEM] + [VMEM] * 4,
+        out_specs=(VMEM, HBM, HBM),
+        scratch_shapes=[
+            scratch(*xf_shape), scratch(nz, nx, ny), scratch(2, vectors, vectors),
+            pltpu.SemaphoreType.DMA((nz,)), pltpu.SemaphoreType.DMA,
+        ],
         input_output_aliases={1: 0},
         compiler_params=params,
         cost_estimate=pl.CostEstimate(flops=0, bytes_accessed=0, transcendentals=0),
         name="add_rims",
-    )(pml_width, left, from_x, from_y)
-    rows, residual = lax.optimization_barrier((rows, residual))
-    gram = pl.pallas_call(
-        gather_kernel,
-        out_shape=f32(2, vectors, vectors),
-        in_specs=[VMEM],
-        out_specs=VMEM,
-        compiler_params=params,
-        name="sum_rows",
-    )(rows)
+    )(pml_width, left, from_x, from_y, rows)
     return basis_new, residual, gram
 
 

time: 31.8 us -> 31.9 us (level)
  starting transfers between devices: 12.3 us -> 14.2 us
  waiting for transfers between devices: 5.01 us -> 3.85 us
  Pallas kernels: 13.5 us -> 12.9 us
    ppermute x5 -> x4, waiting for transfers between devices: 5.01 us -> 2.51 us  [passed_round(): lax.ppermute(value, axis, [(source, (source + steps) % count) for source...]
    ppermute x0 -> x1, starting transfers between devices: none -> 2.16 us  [passed_along(): lax.ppermute(value, axis, [(source, source + steps) for source in range(l...]
    all_to_all x1, waiting for transfers between devices: 0.01 us -> 1.34 us  [body(): lax.all_to_all(gram, ('gx', 'gy', 'gz'), 0, 0, axis_index_groups=[list(ra...]
    pallas_call x2 -> x1, Pallas kernels: 2.93 us -> 2.27 us  [body(): pl.pallas_call(rim_kernel, out_shape=(whole, whole, f32(2, vectors, vecto...]
    ppermute x5 -> x4, starting transfers between devices: 9.32 us -> 9.08 us  [passed_round(): lax.ppermute(value, axis, [(source, (source + steps) % count) for source...]
  transfers between devices with their start and end apart: 6 -> 6, of which waited for: 3 -> 3; matrix products, arithmetic and copies ran while one was open for 0% -> 0% of each run, Pallas kernels for 26% -> 19%
where the time goes in v17:
time: 31.9 us; the launch traced here: 31.7 us
  starting transfers between devices  14.2 us (45%)
  Pallas kernels  12.9 us (40%)
  waiting for transfers between devices  3.85 us (12%)
  between operations  0.75 us (2%)
    ppermute x4, starting transfers between devices, passed_round(): lax.ppermute(value, axis, [(source, (source + steps) % count) for source...  9.08 us
    pallas_call x1, Pallas kernels, body(): pl.pallas_call(prepare_kernel, out_shape=(whole, whole, whole, planes, f3...  3.16 us
    all_to_all x1, starting transfers between devices, body(): lax.all_to_all(gram, ('gx', 'gy', 'gz'), 0, 0, axis_index_groups=[list(ra...  2.98 us
    pallas_call x1, Pallas kernels, body(): pl.pallas_call(inner_kernel, out_shape=(whole, planes, whole, f32(vectors...  2.96 us
    ppermute x4, waiting for transfers between devices, passed_round(): lax.ppermute(value, axis, [(source, (source + steps) % count) for source...  2.51 us
    pallas_call x1, Pallas kernels, body(): pl.pallas_call(rim_kernel, out_shape=(whole, whole, f32(2, vectors, vecto...  2.27 us
    ppermute x1, starting transfers between devices, passed_along(): lax.ppermute(value, axis, [(source, source + steps) for source in range(l...  2.16 us
    pallas_call x1, Pallas kernels, body(): pl.pallas_call(outer_kernel, out_shape=(whole, f32(devices, 4, ny)), in_s...  1.79 us
  transfers between devices with their start and end apart: 6, of which 3 were waited for; matrix products, arithmetic and copies ran while one was open for 0% of the time, Pallas kernels for 19%

profile of v17, /device:TPU:0, one launch (start us, length us, event | category | flops | bytes accessed | tf_op | source)
XLA Modules:
  0.0 31.7 jit_solution(12421427302968741136)
XLA Ops:
  0.6 0.0 copy-start
  0.6 0.0 copy-start.1
  0.7 0.0 copy-start.5
  0.7 1.6 %take_faces.1 = (f32[2,4,3,8,16,128]{5,4,3,2,1,0:T(8,128)S(1)}, f32[2,4,2,8,128]{4,3,2,1,0:T(8,128)S(1)}, f32[16,128]{1,0:T(8,128)S(1)}) custom-call(f32[2,4,3,8,16,128]{5,4,3,2,1,0:T(8,128)} %fields_hbm.1), custom_call_target="tpu_custom_call" | custom-call | tf_op jit(solution)/shard_map/take_faces/pallas_call | solution.py:595
  2.3 3.0 %collective-permute-start.1 = (f32[16,128]{1,0:T(8,128)S(1)}, f32[16,128]{1,0:T(8,128)S(1)}, u32[]{:S(2)}, u32[]{:S(2)}) collective-permute-start(f32[16,128]{1,0:T(8,128)S(1)} %get-tuple-element.42), channel_id=1, source_target_pairs={{0,2},{2,0},{1,3},{3,1},{4,6},{6,4},{5,7},{7,5},{8,10},{10,8},{9,1... | collective-permute-start | bytes 24584 | tf_op jit(solution)/shard_map/ppermute | solution.py:22
  5.4 2.8 %collective-permute-start = (f32[2,4,2,8,128]{4,3,2,1,0:T(8,128)S(1)}, f32[2,4,2,8,128]{4,3,2,1,0:T(8,128)S(1)}, u32[]{:S(2)}, u32[]{:S(2)}) collective-permute-start(f32[2,4,2,8,128]{4,3,2,1,0:T(8,128)S(1)} %get-tuple-element.41), channel_id=1, source_target_pairs={{0,28},{4,0},{8,4},{12,8},{16,12},{20,16},{24,20},{28,24},{1,29},{... | collective-permute-start | bytes 196616 | tf_op jit(solution)/shard_map/ppermute | solution.py:22
  8.1 0.0 copy-done.1
  8.2 3.2 %prepare.1 = (f32[2,4,3,8,16,128]{5,4,3,2,1,0:T(8,128)S(1)}, f32[2,4,3,8,16,128]{5,4,3,2,1,0:T(8,128)S(1)}, f32[2,4,3,8,16,128]{5,4,3,2,1,0:T(8,128)S(1)}, f32[8...) custom-call(s32[6]{0:T(128)S(1)} %copy-done, f32[4]{0:T(128)S(1)} %copy-done.4, ...), custom_call_target="tpu_custom_call" | custom-call | flops 1310720000 | bytes 629145600 | tf_op jit(solution)/shard_map/prepare/pallas_call | solution.py:613
  11.3 0.0 collective-permute-done.1.raw_yf_ref
  11.3 0.0 collective-permute-done.raw_xf_ref
  11.3 0.0 copy-start.2
  11.4 0.9 %slab_face.1 = (f32[2,4,3,8,16,128]{5,4,3,2,1,0:T(8,128)S(1)}, f32[2,4,2,8,128]{4,3,2,1,0:T(8,128)S(1)}, f32[16,128]{1,0:T(8,128)S(1)}, f32[2,4,2,8,128]{4,3,2,1...) custom-call(s32[6]{0:T(128)S(1)} %copy-done, ...), custom_call_target="tpu_custom_call", output_to_operand_aliasing={{0}: (3, {})} | custom-call | tf_op jit(solution)/shard_map/slab_face/pallas_call | solution.py:622
  12.2 1.6 %collective-permute-start.2 = (f32[2,4,2,16,128]{4,3,2,1,0:T(8,128)S(1)}, f32[2,4,2,16,128]{4,3,2,1,0:T(8,128)S(1)}, u32[]{:S(2)}, u32[]{:S(2)}) collective-permute-start(f32[2,4,2,16,128]{4,3,2,1,0:T(8,128)S(1)} %get-tuple-element.48), channel_id=1, source_target_pairs={{0,1},{1,0},{2,3},{3,2},{4,5},{5,4},{6,7},{7,6},{8,9},{9,8},{10,11... | collective-permute-start | bytes 393224 | tf_op jit(solution)/shard_map/ppermute | solution.py:22
  13.8 3.0 %apply_inner.1 = (f32[2,4,3,8,16,128]{5,4,3,2,1,0:T(8,128)S(1)}, f32[8,16,128]{2,1,0:T(8,128)S(1)}, f32[2,4,3,8,16,128]{5,4,3,2,1,0:T(8,128)S(1)}, f32[4,8,8,128...) custom-call(f32[2,4]{1,0:T(2,128)S(1)} %copy-done.2, ...), custom_call_target="tpu_custom_call", output_to_operand_aliasing={{0}: (5, {}), {1}: (6, {})} | custom-call | flops 13107200 | bytes 3145728 | tf_op jit(solution)/shard_map/apply_inner/pallas_call | solution.py:632
  16.8 0.5 %collective-permute-done.2.zf_ref = f32[2,4,2,16,128]{4,3,2,1,0:T(8,128)S(1)} collective-permute-done((f32[2,4,2,16,128]{4,3,2,1,0:T(8,128)S(1)}, f32[2,4,2,16,128]{4,3,2,1,0:T(8,128)S(1)}, u32[]{:S(2)}, u32[]{:S(2)}) %collective-permute-start.2) | collective-permute-done | bytes 131104 | tf_op jit(solution)/shard_map/ppermute | solution.py:22
  17.3 0.1 last_plane.1
  17.4 1.8 %apply_outer.1 = (f32[2,4,3,8,16,128]{5,4,3,2,1,0:T(8,128)S(1)}, f32[32,4,128]{2,1,0:T(4,128)}) custom-call(s32[6]{0:T(128)S(1)} %copy-done, f32[2,4]{1,0:T(2,128)S(1)} %copy-done.2, f32[2,4,3,8,16,128]{5,4,3,2,1,0:T(8,128)S(1)} %get-tuple-element.36.basis_ref, ...), custom_call_target="tpu_custom_call", output_to_operand_aliasing={{0}: (12, {})} | custom-call | flops 4915200 | bytes 1572864 | tf_op jit(solution)/shard_map/apply_outer/pallas_call | solution.py:653
  19.2 3.0 %all-to-all-start = ((f32[32,4,128]{2,1,0:T(4,128)}), f32[32,4,128]{2,1,0:T(4,128)S(1)}, u32[]{:S(2)}, u32[]{:S(2)}) async-start(f32[32,4,128]{2,1,0:T(4,128)} %get-tuple-element.64), calls=%async_computation | async-start | bytes 131072 | tf_op jit(solution)/shard_map/all_to_all | solution.py:664
  22.2 2.2 %collective-permute-start.3 = (f32[2,4,2,8,128]{4,3,2,1,0:T(8,128)S(1)}, f32[2,4,2,8,128]{4,3,2,1,0:T(8,128)S(1)}, u32[]{:S(2)}, u32[]{:S(2)}) collective-permute-start(f32[2,4,2,8,128]{4,3,2,1,0:T(8,128)S(1)} %get-tuple-element.62.hxf_ref), channel_id=1, source_target_pairs={{0,4},{4,8},{8,12},{12,16},{16,20},{20,24},{24,28},{1,5},{5,9},{9,... | collective-permute-start | bytes 196616 | tf_op jit(solution)/shard_map/ppermute | solution.py:28
  24.4 1.7 %collective-permute-start.4 = (f32[16,128]{1,0:T(8,128)S(1)}, f32[16,128]{1,0:T(8,128)S(1)}, u32[]{:S(2)}, u32[]{:S(2)}) collective-permute-start(f32[16,128]{1,0:T(8,128)S(1)} %get-tuple-element.63.hyf_ref), channel_id=1, source_target_pairs={{0,2},{2,0},{1,3},{3,1},{4,6},{6,4},{5,7},{7,5},{8,10},{10,8},{9,1... | collective-permute-start | bytes 24584 | tf_op jit(solution)/shard_map/ppermute | solution.py:22
  26.1 2.0 %collective-permute-done.4.hyf_ref = f32[16,128]{1,0:T(8,128)S(1)} collective-permute-done((f32[16,128]{1,0:T(8,128)S(1)}, f32[16,128]{1,0:T(8,128)S(1)}, u32[]{:S(2)}, u32[]{:S(2)}) %collective-permute-start.4) | collective-permute-done | bytes 8224 | tf_op jit(solution)/shard_map/ppermute | solution.py:22
  28.1 0.0 collective-permute-done.3.hxf_ref
  28.1 1.3 %all-to-all-done.rows_ref = f32[32,4,128]{2,1,0:T(4,128)S(1)} async-done(((f32[32,4,128]{2,1,0:T(4,128)}), f32[32,4,128]{2,1,0:T(4,128)S(1)}, u32[]{:S(2)}, u32[]{:S(2)}) %all-to-all-start) | async-done | bytes 65568 | tf_op jit(solution)/shard_map/all_to_all | solution.py:664
  29.4 2.3 %add_rims.1 = (f32[2,4,3,8,16,128]{5,4,3,2,1,0:T(8,128)S(1)}, f32[2,4,3,8,16,128]{5,4,3,2,1,0:T(8,128)}, f32[2,4,4]{2,1,0:T(4,128)}) custom-call(s32[6]{0:T(128)S(1)} %copy-done, f32[2,4,3,8,16,128]{5,4,3,2,1,0:T(8,128)S(1)} %get-tuple-element.60.left_in, f32[2,4,2,8,128]{4,3,2,1,0:T(8,128)S(1)} %collective-permute-done.3.hxf_ref, ...), custom_call_target="tpu_custom_call", output_to_operand_aliasing={{0}: (1, {})} | custom-call | tf_op jit(solution)/shard_map/add_rims/pallas_call | solution.py:667
  (7 shorter events, 0.0 us)
Async XLA Ops:
  0.6 7.5 %copy-start = (s32[6]{0:T(128)S(1)}, s32[6]{0:T(128)}, u32[]{:S(2)}) copy-start(s32[6]{0:T(128)} %pml_ref.7) | copy-start | bytes 76
  0.6 7.5 %copy-start.1 = (f32[2,4,4]{2,1,0:T(4,128)S(1)}, f32[2,4,4]{2,1,0:T(4,128)}, u32[]{:S(2)}) copy-start(f32[2,4,4]{2,1,0:T(4,128)} %coeffs_ref.3) | copy-start | bytes 388
  0.7 7.5 %copy-start.5 = (f32[4]{0:T(128)S(1)}, f32[4]{0:T(128)}, u32[]{:S(2)}) copy-start(f32[4]{0:T(128)} %eps_loss_ref.1) | copy-start | bytes 52
  0.7 7.5 %copy-start.4 = (f32[4]{0:T(128)S(1)}, f32[4]{0:T(128)}, u32[]{:S(2)}) copy-start(f32[4]{0:T(128)} %eps_real_ref.1) | copy-start | bytes 52
  0.7 7.5 %copy-start.3 = (s32[8,16,128]{2,1,0:T(8,128)S(1)}, s32[8,16,128]{2,1,0:T(8,128)}, u32[]{:S(2)}) copy-start(s32[8,16,128]{2,1,0:T(8,128)} %material_ref.1) | copy-start | bytes 196612
  2.3 9.0 %collective-permute-start.1 = (f32[16,128]{1,0:T(8,128)S(1)}, f32[16,128]{1,0:T(8,128)S(1)}, u32[]{:S(2)}, u32[]{:S(2)}) collective-permute-start(f32[16,128]{1,0:T(8,128)S(1)} %get-tuple-element.42), channel_id=1, source_target_pairs={{0,2},{2,0},{1,3},{3,1},{4,6},{6,4},{5,7},{7,5},{8,10},{10,8},{9,1... | collective-permute-start | bytes 24584 | tf_op jit(solution)/shard_map/ppermute | solution.py:22
  5.4 6.0 %collective-permute-start = (f32[2,4,2,8,128]{4,3,2,1,0:T(8,128)S(1)}, f32[2,4,2,8,128]{4,3,2,1,0:T(8,128)S(1)}, u32[]{:S(2)}, u32[]{:S(2)}) collective-permute-start(f32[2,4,2,8,128]{4,3,2,1,0:T(8,128)S(1)} %get-tuple-element.41), channel_id=1, source_target_pairs={{0,28},{4,0},{8,4},{12,8},{16,12},{20,16},{24,20},{28,24},{1,29},{... | collective-permute-start | bytes 196616 | tf_op jit(solution)/shard_map/ppermute | solution.py:22
  11.3 2.5 %copy-start.2 = (f32[2,4]{1,0:T(2,128)S(1)}, f32[2,4]{1,0:T(2,128)}, u32[]{:S(2)}) copy-start(f32[2,4]{1,0:T(2,128)} %ritz_ref.3) | copy-start | bytes 100
  12.2 5.0 %collective-permute-start.2 = (f32[2,4,2,16,128]{4,3,2,1,0:T(8,128)S(1)}, f32[2,4,2,16,128]{4,3,2,1,0:T(8,128)S(1)}, u32[]{:S(2)}, u32[]{:S(2)}) collective-permute-start(f32[2,4,2,16,128]{4,3,2,1,0:T(8,128)S(1)} %get-tuple-element.48), channel_id=1, source_target_pairs={{0,1},{1,0},{2,3},{3,2},{4,5},{5,4},{6,7},{7,6},{8,9},{9,8},{10,11... | collective-permute-start | bytes 393224 | tf_op jit(solution)/shard_map/ppermute | solution.py:22
  19.2 10.2 %all-to-all-start = ((f32[32,4,128]{2,1,0:T(4,128)}), f32[32,4,128]{2,1,0:T(4,128)S(1)}, u32[]{:S(2)}, u32[]{:S(2)}) async-start(f32[32,4,128]{2,1,0:T(4,128)} %get-tuple-element.64), calls=%async_computation | async-start | bytes 131072 | tf_op jit(solution)/shard_map/all_to_all | solution.py:664
  22.2 5.9 %collective-permute-start.3 = (f32[2,4,2,8,128]{4,3,2,1,0:T(8,128)S(1)}, f32[2,4,2,8,128]{4,3,2,1,0:T(8,128)S(1)}, u32[]{:S(2)}, u32[]{:S(2)}) collective-permute-start(f32[2,4,2,8,128]{4,3,2,1,0:T(8,128)S(1)} %get-tuple-element.62.hxf_ref), channel_id=1, source_target_pairs={{0,4},{4,8},{8,12},{12,16},{16,20},{20,24},{24,28},{1,5},{5,9},{9,... | collective-permute-start | bytes 196616 | tf_op jit(solution)/shard_map/ppermute | solution.py:28
  24.4 3.7 %collective-permute-start.4 = (f32[16,128]{1,0:T(8,128)S(1)}, f32[16,128]{1,0:T(8,128)S(1)}, u32[]{:S(2)}, u32[]{:S(2)}) collective-permute-start(f32[16,128]{1,0:T(8,128)S(1)} %get-tuple-element.63.hyf_ref), channel_id=1, source_target_pairs={{0,2},{2,0},{1,3},{3,1},{4,6},{6,4},{5,7},{7,5},{8,10},{10,8},{9,1... | collective-permute-start | bytes 24584 | tf_op jit(solution)/shard_map/ppermute | solution.py:22

commit v18 on v15

--- a/solution.py
+++ b/solution.py
@@ -20,6 +20,12 @@
 def passed_round(value, axis, steps):
     count = lax.axis_size(axis)
     return lax.ppermute(value, axis, [(source, (source + steps) % count) for source in range(count)])
+
+
+def passed_along(value, axis, steps):
+    count = lax.axis_size(axis)
+    leading, last = (max(0, -steps), min(count, count - steps))
+    return lax.ppermute(value, axis, [(source, source + steps) for source in range(leading, last)])
 
 
 def inverse_stretch(places, length, low_width, high_width):
@@ -423,7 +429,7 @@
                 if cut.stop == nx:
                     hxf_ref[part, b, 0, last:] = hxf_ref[part, b, 0, last:] + more[1][part][SUB - 1:]
     inner = packed_in[:last].reshape(last * nx, ny)
-    hyf_ref[...] = jnp.concatenate([inner] + packed, axis=0).T[:hyf_ref.shape[0]]
+    hyf_ref[...] = jnp.concatenate([inner] + packed, axis=0).T
 
 
 def outer_kernel(
@@ -628,7 +634,7 @@
     )(ritz, basis, loss, table, sz, h, packed, xadd, yadd)
     h, hxf, hyf = pl.pallas_call(
         last_plane_kernel,
-        out_shape=(whole, face, f32(*yf_shape)),
+        out_shape=(whole, face, f32(ny, nz * nx)),
         in_specs=[VMEM] * 5,
         out_specs=(VMEM,) * 3,
         input_output_aliases={2: 0, 4: 1},
@@ -648,8 +654,8 @@
     )(pml_width, ritz, basis, loss, table, sz, h, zf, xf, yt, hxf, hyf, left, acc, before)
     gram, hxf, hyf = lax.optimization_barrier((gram, hxf, hyf))
     rows = lax.all_to_all(gram, ("gx", "gy", "gz"), 0, 0)
-    from_x = passed_round(hxf, "gx", 1)
     from_y = passed_round(hyf, "gy", 1)
+    from_x = passed_along(hxf, "gx", 1)
     _, residual = pl.pallas_call(
         rim_kernel,
         out_shape=(whole, whole),

time: 31.8 us -> 32.4 us (1.019)
  starting transfers between devices: 12.3 us -> 14.2 us
  waiting for transfers between devices: 5.01 us -> 3.47 us
    ppermute x0 -> x1, starting transfers between devices: none -> 2.16 us  [passed_along(): lax.ppermute(value, axis, [(source, source + steps) for source in range(l...]
    ppermute x5 -> x4, waiting for transfers between devices: 5.01 us -> 3.47 us  [passed_round(): lax.ppermute(value, axis, [(source, (source + steps) % count) for source...]
    ppermute x5 -> x4, starting transfers between devices: 9.32 us -> 9.08 us  [passed_round(): lax.ppermute(value, axis, [(source, (source + steps) % count) for source...]
  transfers between devices with their start and end apart: 6 -> 6, of which waited for: 3 -> 2; matrix products, arithmetic and copies ran while one was open for 0% -> 0% of each run, Pallas kernels for 26% -> 26%
where the time goes in v18:
time: 32.4 us; the launch traced here: 32 us
  starting transfers between devices  14.2 us (44%)
  Pallas kernels  13.5 us (42%)
  waiting for transfers between devices  3.47 us (11%)
  between operations  0.77 us (2%)
    ppermute x4, starting transfers between devices, passed_round(): lax.ppermute(value, axis, [(source, (source + steps) % count) for source...  9.08 us
    ppermute x4, waiting for transfers between devices, passed_round(): lax.ppermute(value, axis, [(source, (source + steps) % count) for source...  3.47 us
    pallas_call x1, Pallas kernels, body(): pl.pallas_call(prepare_kernel, out_shape=(whole, whole, whole, planes, f3...  3.16 us
    all_to_all x1, starting transfers between devices, body(): rows = lax.all_to_all(gram, ('gx', 'gy', 'gz'), 0, 0)  2.98 us
    pallas_call x1, Pallas kernels, body(): pl.pallas_call(inner_kernel, out_shape=(whole, planes, whole, f32(vectors...  2.95 us
    pallas_call x1, Pallas kernels, body(): pl.pallas_call(rim_kernel, out_shape=(whole, whole), in_specs=[SMEM] + [V...  2.25 us
    ppermute x1, starting transfers between devices, passed_along(): lax.ppermute(value, axis, [(source, source + steps) for source in range(l...  2.16 us
    pallas_call x1, Pallas kernels, body(): pl.pallas_call(outer_kernel, out_shape=(whole, f32(devices, 4, ny)), in_s...  1.77 us
  transfers between devices with their start and end apart: 6, of which 2 were waited for; matrix products, arithmetic and copies ran while one was open for 0% of the time, Pallas kernels for 26%

profile of v18, /device:TPU:0, one launch (start us, length us, event | category | flops | bytes accessed | tf_op | source)
XLA Modules:
  0.0 32.0 jit_solution(7997575133766624879)
XLA Ops:
  0.6 0.0 copy-start
  0.6 0.0 copy-start.1
  0.7 0.0 copy-start.5
  0.7 1.6 %take_faces.1 = (f32[2,4,3,8,16,128]{5,4,3,2,1,0:T(8,128)S(1)}, f32[2,4,2,8,128]{4,3,2,1,0:T(8,128)S(1)}, f32[16,128]{1,0:T(8,128)S(1)}) custom-call(f32[2,4,3,8,16,128]{5,4,3,2,1,0:T(8,128)} %fields_hbm.1), custom_call_target="tpu_custom_call" | custom-call | tf_op jit(solution)/shard_map/take_faces/pallas_call | solution.py:587
  2.3 3.0 %collective-permute-start.1 = (f32[16,128]{1,0:T(8,128)S(1)}, f32[16,128]{1,0:T(8,128)S(1)}, u32[]{:S(2)}, u32[]{:S(2)}) collective-permute-start(f32[16,128]{1,0:T(8,128)S(1)} %get-tuple-element.43), channel_id=1, source_target_pairs={{0,2},{2,0},{1,3},{3,1},{4,6},{6,4},{5,7},{7,5},{8,10},{10,8},{9,1... | collective-permute-start | bytes 24584 | tf_op jit(solution)/shard_map/ppermute | solution.py:22
  5.4 2.8 %collective-permute-start = (f32[2,4,2,8,128]{4,3,2,1,0:T(8,128)S(1)}, f32[2,4,2,8,128]{4,3,2,1,0:T(8,128)S(1)}, u32[]{:S(2)}, u32[]{:S(2)}) collective-permute-start(f32[2,4,2,8,128]{4,3,2,1,0:T(8,128)S(1)} %get-tuple-element.42), channel_id=1, source_target_pairs={{0,28},{4,0},{8,4},{12,8},{16,12},{20,16},{24,20},{28,24},{1,29},{... | collective-permute-start | bytes 196616 | tf_op jit(solution)/shard_map/ppermute | solution.py:22
  8.2 3.2 %prepare.1 = (f32[2,4,3,8,16,128]{5,4,3,2,1,0:T(8,128)S(1)}, f32[2,4,3,8,16,128]{5,4,3,2,1,0:T(8,128)S(1)}, f32[2,4,3,8,16,128]{5,4,3,2,1,0:T(8,128)S(1)}, f32[8...) custom-call(s32[6]{0:T(128)S(1)} %copy-done, f32[4]{0:T(128)S(1)} %copy-done.4, ...), custom_call_target="tpu_custom_call" | custom-call | flops 1310720000 | bytes 629145600 | tf_op jit(solution)/shard_map/prepare/pallas_call | solution.py:605
  11.3 0.0 collective-permute-done.1.raw_yf_ref
  11.3 0.0 collective-permute-done.raw_xf_ref
  11.3 0.0 copy-start.2
  11.4 0.9 %slab_face.1 = (f32[2,4,3,8,16,128]{5,4,3,2,1,0:T(8,128)S(1)}, f32[2,4,2,8,128]{4,3,2,1,0:T(8,128)S(1)}, f32[16,128]{1,0:T(8,128)S(1)}, f32[2,4,2,8,128]{4,3,2,1...) custom-call(s32[6]{0:T(128)S(1)} %copy-done, ...), custom_call_target="tpu_custom_call", output_to_operand_aliasing={{0}: (3, {})} | custom-call | tf_op jit(solution)/shard_map/slab_face/pallas_call | solution.py:614
  12.2 1.6 %collective-permute-start.2 = (f32[2,4,2,16,128]{4,3,2,1,0:T(8,128)S(1)}, f32[2,4,2,16,128]{4,3,2,1,0:T(8,128)S(1)}, u32[]{:S(2)}, u32[]{:S(2)}) collective-permute-start(f32[2,4,2,16,128]{4,3,2,1,0:T(8,128)S(1)} %get-tuple-element.49), channel_id=1, source_target_pairs={{0,1},{1,0},{2,3},{3,2},{4,5},{5,4},{6,7},{7,6},{8,9},{9,8},{10,11... | collective-permute-start | bytes 393224 | tf_op jit(solution)/shard_map/ppermute | solution.py:22
  13.8 2.9 %apply_inner.1 = (f32[2,4,3,8,16,128]{5,4,3,2,1,0:T(8,128)S(1)}, f32[8,16,128]{2,1,0:T(8,128)S(1)}, f32[2,4,3,8,16,128]{5,4,3,2,1,0:T(8,128)S(1)}, f32[4,8,8,128...) custom-call(f32[2,4]{1,0:T(2,128)S(1)} %copy-done.2, ...), custom_call_target="tpu_custom_call", output_to_operand_aliasing={{0}: (5, {}), {1}: (6, {})} | custom-call | flops 13107200 | bytes 3145728 | tf_op jit(solution)/shard_map/apply_inner/pallas_call | solution.py:624
  16.8 0.5 %collective-permute-done.2.zf_ref = f32[2,4,2,16,128]{4,3,2,1,0:T(8,128)S(1)} collective-permute-done((f32[2,4,2,16,128]{4,3,2,1,0:T(8,128)S(1)}, f32[2,4,2,16,128]{4,3,2,1,0:T(8,128)S(1)}, u32[]{:S(2)}, u32[]{:S(2)}) %collective-permute-start.2) | collective-permute-done | bytes 131104 | tf_op jit(solution)/shard_map/ppermute | solution.py:22
  17.3 0.2 last_plane.1
  17.5 1.8 %apply_outer.1 = (f32[2,4,3,8,16,128]{5,4,3,2,1,0:T(8,128)S(1)}, f32[32,4,128]{2,1,0:T(4,128)}) custom-call(s32[6]{0:T(128)S(1)} %copy-done, f32[2,4]{1,0:T(2,128)S(1)} %copy-done.2, f32[2,4,3,8,16,128]{5,4,3,2,1,0:T(8,128)S(1)} %get-tuple-element.37.basis_ref, ...), custom_call_target="tpu_custom_call", output_to_operand_aliasing={{0}: (12, {})} | custom-call | flops 4915200 | bytes 1572864 | tf_op jit(solution)/shard_map/apply_outer/pallas_call | solution.py:645
  19.2 3.0 %all-to-all-start = ((f32[32,4,128]{2,1,0:T(4,128)}), f32[32,4,128]{2,1,0:T(4,128)S(1)}, u32[]{:S(2)}, u32[]{:S(2)}) async-start(f32[32,4,128]{2,1,0:T(4,128)} %get-tuple-element.62), calls=%async_computation | async-start | bytes 131072 | tf_op jit(solution)/shard_map/all_to_all | solution.py:656
  22.2 2.2 %collective-permute-start.3 = (f32[2,4,2,8,128]{4,3,2,1,0:T(8,128)S(1)}, f32[2,4,2,8,128]{4,3,2,1,0:T(8,128)S(1)}, u32[]{:S(2)}, u32[]{:S(2)}) collective-permute-start(f32[2,4,2,8,128]{4,3,2,1,0:T(8,128)S(1)} %get-tuple-element.64.hxf_ref), channel_id=1, source_target_pairs={{0,4},{4,8},{8,12},{12,16},{16,20},{20,24},{24,28},{1,5},{5,9},{9,... | collective-permute-start | bytes 196616 | tf_op jit(solution)/shard_map/ppermute | solution.py:28
  24.4 1.7 %collective-permute-start.4 = (f32[128,128]{1,0:T(8,128)S(1)}, f32[128,128]{1,0:T(8,128)S(1)}, u32[]{:S(2)}, u32[]{:S(2)}) collective-permute-start(f32[128,128]{1,0:T(8,128)S(1)} %get-tuple-element.65.hyf_ref), channel_id=1, source_target_pairs={{0,2},{2,0},{1,3},{3,1},{4,6},{6,4},{5,7},{7,5},{8,10},{10,8},{9,1... | collective-permute-start | bytes 196616 | tf_op jit(solution)/shard_map/ppermute | solution.py:22
  26.1 0.0 collective-permute-done.3.hxf_ref
  26.1 2.9 %collective-permute-done.4.hyf_ref = f32[128,128]{1,0:T(8,128)S(1)} collective-permute-done((f32[128,128]{1,0:T(8,128)S(1)}, f32[128,128]{1,0:T(8,128)S(1)}, u32[]{:S(2)}, u32[]{:S(2)}) %collective-permute-start.4) | collective-permute-done | bytes 65568 | tf_op jit(solution)/shard_map/ppermute | solution.py:22
  29.1 2.3 %add_rims.1 = (f32[2,4,3,8,16,128]{5,4,3,2,1,0:T(8,128)S(1)}, f32[2,4,3,8,16,128]{5,4,3,2,1,0:T(8,128)}) custom-call(s32[6]{0:T(128)S(1)} %copy-done, f32[2,4,3,8,16,128]{5,4,3,2,1,0:T(8,128)S(1)} %get-tuple-element.63.left_in, f32[2,4,2,8,128]{4,3,2,1,0:T(8,128)S(1)} %collective-permute-done.3.hxf_ref, ...), custom_call_target="tpu_custom_call", output_to_operand_aliasing={{0}: (1, {})} | custom-call | tf_op jit(solution)/shard_map/add_rims/pallas_call | solution.py:659
  31.3 0.0 all-to-all-done.rows_ref
  31.3 0.7 %sum_rows.1 = f32[2,4,4]{2,1,0:T(4,128)} custom-call(f32[32,4,128]{2,1,0:T(4,128)S(1)} %all-to-all-done.rows_ref), custom_call_target="tpu_custom_call" | custom-call | tf_op jit(solution)/shard_map/sum_rows/pallas_call | solution.py:671
  (8 shorter events, 0.0 us)
Async XLA Ops:
  0.6 7.5 %copy-start = (s32[6]{0:T(128)S(1)}, s32[6]{0:T(128)}, u32[]{:S(2)}) copy-start(s32[6]{0:T(128)} %pml_ref.7) | copy-start | bytes 76
  0.6 7.5 %copy-start.1 = (f32[2,4,4]{2,1,0:T(4,128)S(1)}, f32[2,4,4]{2,1,0:T(4,128)}, u32[]{:S(2)}) copy-start(f32[2,4,4]{2,1,0:T(4,128)} %coeffs_ref.3) | copy-start | bytes 388
  0.7 7.5 %copy-start.5 = (f32[4]{0:T(128)S(1)}, f32[4]{0:T(128)}, u32[]{:S(2)}) copy-start(f32[4]{0:T(128)} %eps_loss_ref.1) | copy-start | bytes 52
  0.7 7.5 %copy-start.4 = (f32[4]{0:T(128)S(1)}, f32[4]{0:T(128)}, u32[]{:S(2)}) copy-start(f32[4]{0:T(128)} %eps_real_ref.1) | copy-start | bytes 52
  0.7 7.5 %copy-start.3 = (s32[8,16,128]{2,1,0:T(8,128)S(1)}, s32[8,16,128]{2,1,0:T(8,128)}, u32[]{:S(2)}) copy-start(s32[8,16,128]{2,1,0:T(8,128)} %material_ref.1) | copy-start | bytes 196612
  2.3 9.0 %collective-permute-start.1 = (f32[16,128]{1,0:T(8,128)S(1)}, f32[16,128]{1,0:T(8,128)S(1)}, u32[]{:S(2)}, u32[]{:S(2)}) collective-permute-start(f32[16,128]{1,0:T(8,128)S(1)} %get-tuple-element.43), channel_id=1, source_target_pairs={{0,2},{2,0},{1,3},{3,1},{4,6},{6,4},{5,7},{7,5},{8,10},{10,8},{9,1... | collective-permute-start | bytes 24584 | tf_op jit(solution)/shard_map/ppermute | solution.py:22
  5.4 6.0 %collective-permute-start = (f32[2,4,2,8,128]{4,3,2,1,0:T(8,128)S(1)}, f32[2,4,2,8,128]{4,3,2,1,0:T(8,128)S(1)}, u32[]{:S(2)}, u32[]{:S(2)}) collective-permute-start(f32[2,4,2,8,128]{4,3,2,1,0:T(8,128)S(1)} %get-tuple-element.42), channel_id=1, source_target_pairs={{0,28},{4,0},{8,4},{12,8},{16,12},{20,16},{24,20},{28,24},{1,29},{... | collective-permute-start | bytes 196616 | tf_op jit(solution)/shard_map/ppermute | solution.py:22
  11.3 2.5 %copy-start.2 = (f32[2,4]{1,0:T(2,128)S(1)}, f32[2,4]{1,0:T(2,128)}, u32[]{:S(2)}) copy-start(f32[2,4]{1,0:T(2,128)} %ritz_ref.3) | copy-start | bytes 100
  12.2 5.0 %collective-permute-start.2 = (f32[2,4,2,16,128]{4,3,2,1,0:T(8,128)S(1)}, f32[2,4,2,16,128]{4,3,2,1,0:T(8,128)S(1)}, u32[]{:S(2)}, u32[]{:S(2)}) collective-permute-start(f32[2,4,2,16,128]{4,3,2,1,0:T(8,128)S(1)} %get-tuple-element.49), channel_id=1, source_target_pairs={{0,1},{1,0},{2,3},{3,2},{4,5},{5,4},{6,7},{7,6},{8,9},{9,8},{10,11... | collective-permute-start | bytes 393224 | tf_op jit(solution)/shard_map/ppermute | solution.py:22
  19.2 12.1 %all-to-all-start = ((f32[32,4,128]{2,1,0:T(4,128)}), f32[32,4,128]{2,1,0:T(4,128)S(1)}, u32[]{:S(2)}, u32[]{:S(2)}) async-start(f32[32,4,128]{2,1,0:T(4,128)} %get-tuple-element.62), calls=%async_computation | async-start | bytes 131072 | tf_op jit(solution)/shard_map/all_to_all | solution.py:656
  22.2 3.9 %collective-permute-start.3 = (f32[2,4,2,8,128]{4,3,2,1,0:T(8,128)S(1)}, f32[2,4,2,8,128]{4,3,2,1,0:T(8,128)S(1)}, u32[]{:S(2)}, u32[]{:S(2)}) collective-permute-start(f32[2,4,2,8,128]{4,3,2,1,0:T(8,128)S(1)} %get-tuple-element.64.hxf_ref), channel_id=1, source_target_pairs={{0,4},{4,8},{8,12},{12,16},{16,20},{20,24},{24,28},{1,5},{5,9},{9,... | collective-permute-start | bytes 196616 | tf_op jit(solution)/shard_map/ppermute | solution.py:28
  24.4 4.7 %collective-permute-start.4 = (f32[128,128]{1,0:T(8,128)S(1)}, f32[128,128]{1,0:T(8,128)S(1)}, u32[]{:S(2)}, u32[]{:S(2)}) collective-permute-start(f32[128,128]{1,0:T(8,128)S(1)} %get-tuple-element.65.hyf_ref), channel_id=1, source_target_pairs={{0,2},{2,0},{1,3},{3,1},{4,6},{6,4},{5,7},{7,5},{8,10},{10,8},{9,1... | collective-permute-start | bytes 196616 | tf_op jit(solution)/shard_map/ppermute | solution.py:22

commit v19 on v18

--- a/solution.py
+++ b/solution.py
@@ -429,7 +429,8 @@
                 if cut.stop == nx:
                     hxf_ref[part, b, 0, last:] = hxf_ref[part, b, 0, last:] + more[1][part][SUB - 1:]
     inner = packed_in[:last].reshape(last * nx, ny)
-    hyf_ref[...] = jnp.concatenate([inner] + packed, axis=0).T
+    hyf_ref[:ny] = jnp.concatenate([inner] + packed, axis=0).T
+    hyf_ref[ny:] = jnp.zeros((hyf_ref.shape[0] - ny, nz * nx), jnp.float32)
 
 
 def outer_kernel(
@@ -634,7 +635,7 @@
     )(ritz, basis, loss, table, sz, h, packed, xadd, yadd)
     h, hxf, hyf = pl.pallas_call(
         last_plane_kernel,
-        out_shape=(whole, face, f32(ny, nz * nx)),
+        out_shape=(whole, face, f32(ny + SUB, nz * nx)),
         in_specs=[VMEM] * 5,
         out_specs=(VMEM,) * 3,
         input_output_aliases={2: 0, 4: 1},
@@ -644,7 +645,7 @@
     devices = lax.axis_size("gx") * lax.axis_size("gy") * lax.axis_size("gz")
     left, gram = pl.pallas_call(
         outer_kernel,
-        out_shape=(whole, f32(devices, 4, ny)),
+        out_shape=(whole, f32(devices, 5, ny)),
         in_specs=[SMEM] * 2 + [VMEM] * 13,
         out_specs=(VMEM,) * 2,
         input_output_aliases={12: 0},

time: 32.4 us -> 31.6 us (0.975)
  waiting for transfers between devices: 3.47 us -> 3.02 us
    ppermute x4, waiting for transfers between devices: 3.47 us -> 1.04 us  [passed_round(): lax.ppermute(value, axis, [(source, (source + steps) % count) for source...]
    all_to_all x1, waiting for transfers between devices: 0.01 us -> 1.1 us  [body(): rows = lax.all_to_all(gram, ('gx', 'gy', 'gz'), 0, 0)]
    ppermute x1, waiting for transfers between devices: 0.01 us -> 0.88 us  [passed_along(): lax.ppermute(value, axis, [(source, source + steps) for source in range(l...]
    ppermute x1, starting transfers between devices: 2.16 us -> 1.76 us  [passed_along(): lax.ppermute(value, axis, [(source, source + steps) for source in range(l...]
  transfers between devices with their start and end apart: 6 -> 6, of which waited for: 2 -> 4; matrix products, arithmetic and copies ran while one was open for 0% -> 0% of each run, Pallas kernels for 26% -> 27%
where the time goes in v19:
time: 31.6 us; the launch traced here: 31.3 us
  starting transfers between devices  13.9 us (44%)
  Pallas kernels  13.6 us (43%)
  waiting for transfers between devices  3.02 us (10%)
  between operations  0.76 us (2%)
    ppermute x4, starting transfers between devices, passed_round(): lax.ppermute(value, axis, [(source, (source + steps) % count) for source...  9.18 us
    pallas_call x1, Pallas kernels, body(): pl.pallas_call(prepare_kernel, out_shape=(whole, whole, whole, planes, f3...  3.16 us
    pallas_call x1, Pallas kernels, body(): pl.pallas_call(inner_kernel, out_shape=(whole, planes, whole, f32(vectors...  2.99 us
    all_to_all x1, starting transfers between devices, body(): rows = lax.all_to_all(gram, ('gx', 'gy', 'gz'), 0, 0)  2.98 us
    pallas_call x1, Pallas kernels, body(): pl.pallas_call(rim_kernel, out_shape=(whole, whole), in_specs=[SMEM] + [V...  2.25 us
    pallas_call x1, Pallas kernels, body(): pl.pallas_call(outer_kernel, out_shape=(whole, f32(devices, 5, ny)), in_s...  1.8 us
    ppermute x1, starting transfers between devices, passed_along(): lax.ppermute(value, axis, [(source, source + steps) for source in range(l...  1.76 us
    pallas_call x1, Pallas kernels, body(): pl.pallas_call(face_kernel, out_shape=(whole, f32(*xf_shape), f32(*yf_sha...  1.64 us
  transfers between devices with their start and end apart: 6, of which 4 were waited for; matrix products, arithmetic and copies ran while one was open for 0% of the time, Pallas kernels for 27%

profile of v19, /device:TPU:0, one launch (start us, length us, event | category | flops | bytes accessed | tf_op | source)
XLA Modules:
  0.0 31.3 jit_solution(4860045704196515251)
XLA Ops:
  0.7 1.6 %take_faces.1 = (f32[2,4,3,8,16,128]{5,4,3,2,1,0:T(8,128)S(1)}, f32[2,4,2,8,128]{4,3,2,1,0:T(8,128)S(1)}, f32[16,128]{1,0:T(8,128)S(1)}) custom-call(f32[2,4,3,8,16,128]{5,4,3,2,1,0:T(8,128)} %fields_hbm.1), custom_call_target="tpu_custom_call" | custom-call | tf_op jit(solution)/shard_map/take_faces/pallas_call | solution.py:588
  2.3 3.0 %collective-permute-start.1 = (f32[16,128]{1,0:T(8,128)S(1)}, f32[16,128]{1,0:T(8,128)S(1)}, u32[]{:S(2)}, u32[]{:S(2)}) collective-permute-start(f32[16,128]{1,0:T(8,128)S(1)} %get-tuple-element.43), channel_id=1, source_target_pairs={{0,2},{2,0},{1,3},{3,1},{4,6},{6,4},{5,7},{7,5},{8,10},{10,8},{9,1... | collective-permute-start | bytes 24584 | tf_op jit(solution)/shard_map/ppermute | solution.py:22
  5.4 2.8 %collective-permute-start = (f32[2,4,2,8,128]{4,3,2,1,0:T(8,128)S(1)}, f32[2,4,2,8,128]{4,3,2,1,0:T(8,128)S(1)}, u32[]{:S(2)}, u32[]{:S(2)}) collective-permute-start(f32[2,4,2,8,128]{4,3,2,1,0:T(8,128)S(1)} %get-tuple-element.42), channel_id=1, source_target_pairs={{0,28},{4,0},{8,4},{12,8},{16,12},{20,16},{24,20},{28,24},{1,29},{... | collective-permute-start | bytes 196616 | tf_op jit(solution)/shard_map/ppermute | solution.py:22
  8.1 0.0 copy-done.1
  8.1 0.0 copy-done.4
  8.2 3.2 %prepare.1 = (f32[2,4,3,8,16,128]{5,4,3,2,1,0:T(8,128)S(1)}, f32[2,4,3,8,16,128]{5,4,3,2,1,0:T(8,128)S(1)}, f32[2,4,3,8,16,128]{5,4,3,2,1,0:T(8,128)S(1)}, f32[8...) custom-call(s32[6]{0:T(128)S(1)} %copy-done, f32[4]{0:T(128)S(1)} %copy-done.4, ...), custom_call_target="tpu_custom_call" | custom-call | flops 1310720000 | bytes 629145600 | tf_op jit(solution)/shard_map/prepare/pallas_call | solution.py:606
  11.3 0.0 collective-permute-done.1.raw_yf_ref
  11.3 0.0 collective-permute-done.raw_xf_ref
  11.3 0.0 copy-start.2
  11.4 0.9 %slab_face.1 = (f32[2,4,3,8,16,128]{5,4,3,2,1,0:T(8,128)S(1)}, f32[2,4,2,8,128]{4,3,2,1,0:T(8,128)S(1)}, f32[16,128]{1,0:T(8,128)S(1)}, f32[2,4,2,8,128]{4,3,2,1...) custom-call(s32[6]{0:T(128)S(1)} %copy-done, ...), custom_call_target="tpu_custom_call", output_to_operand_aliasing={{0}: (3, {})} | custom-call | tf_op jit(solution)/shard_map/slab_face/pallas_call | solution.py:615
  12.3 1.6 %collective-permute-start.2 = (f32[2,4,2,16,128]{4,3,2,1,0:T(8,128)S(1)}, f32[2,4,2,16,128]{4,3,2,1,0:T(8,128)S(1)}, u32[]{:S(2)}, u32[]{:S(2)}) collective-permute-start(f32[2,4,2,16,128]{4,3,2,1,0:T(8,128)S(1)} %get-tuple-element.49), channel_id=1, source_target_pairs={{0,1},{1,0},{2,3},{3,2},{4,5},{5,4},{6,7},{7,6},{8,9},{9,8},{10,11... | collective-permute-start | bytes 393224 | tf_op jit(solution)/shard_map/ppermute | solution.py:22
  13.8 0.0 copy-done.2
  13.8 3.0 %apply_inner.1 = (f32[2,4,3,8,16,128]{5,4,3,2,1,0:T(8,128)S(1)}, f32[8,16,128]{2,1,0:T(8,128)S(1)}, f32[2,4,3,8,16,128]{5,4,3,2,1,0:T(8,128)S(1)}, f32[4,8,8,128...) custom-call(f32[2,4]{1,0:T(2,128)S(1)} %copy-done.2, ...), custom_call_target="tpu_custom_call", output_to_operand_aliasing={{0}: (5, {}), {1}: (6, {})} | custom-call | flops 13107200 | bytes 3145728 | tf_op jit(solution)/shard_map/apply_inner/pallas_call | solution.py:625
  16.8 0.5 %collective-permute-done.2.zf_ref = f32[2,4,2,16,128]{4,3,2,1,0:T(8,128)S(1)} collective-permute-done((f32[2,4,2,16,128]{4,3,2,1,0:T(8,128)S(1)}, f32[2,4,2,16,128]{4,3,2,1,0:T(8,128)S(1)}, u32[]{:S(2)}, u32[]{:S(2)}) %collective-permute-start.2) | collective-permute-done | bytes 131104 | tf_op jit(solution)/shard_map/ppermute | solution.py:22
  17.3 0.2 last_plane.1
  17.5 1.8 %apply_outer.1 = (f32[2,4,3,8,16,128]{5,4,3,2,1,0:T(8,128)S(1)}, f32[32,5,128]{2,1,0:T(8,128)}) custom-call(s32[6]{0:T(128)S(1)} %copy-done, f32[2,4]{1,0:T(2,128)S(1)} %copy-done.2, f32[2,4,3,8,16,128]{5,4,3,2,1,0:T(8,128)S(1)} %get-tuple-element.37.basis_ref, ...), custom_call_target="tpu_custom_call", output_to_operand_aliasing={{0}: (12, {})} | custom-call | flops 4915200 | bytes 1572864 | tf_op jit(solution)/shard_map/apply_outer/pallas_call | solution.py:646
  19.3 3.0 %all-to-all-start = ((f32[32,5,128]{2,1,0:T(8,128)}), f32[32,5,128]{2,1,0:T(8,128)S(1)}, u32[]{:S(2)}, u32[]{:S(2)}) async-start(f32[32,5,128]{2,1,0:T(8,128)} %get-tuple-element.62), calls=%async_computation | async-start | bytes 262144 | tf_op jit(solution)/shard_map/all_to_all | solution.py:657
  22.2 1.8 %collective-permute-start.4 = (f32[136,128]{1,0:T(8,128)S(1)}, f32[136,128]{1,0:T(8,128)S(1)}, u32[]{:S(2)}, u32[]{:S(2)}) collective-permute-start(f32[136,128]{1,0:T(8,128)S(1)} %get-tuple-element.65.hyf_ref), channel_id=1, source_target_pairs={{0,2},{2,0},{1,3},{3,1},{4,6},{6,4},{5,7},{7,5},{8,10},{10,8},{9,1... | collective-permute-start | bytes 208904 | tf_op jit(solution)/shard_map/ppermute | solution.py:22
  24.1 1.8 %collective-permute-start.3 = (f32[2,4,2,8,128]{4,3,2,1,0:T(8,128)S(1)}, f32[2,4,2,8,128]{4,3,2,1,0:T(8,128)S(1)}, u32[]{:S(2)}, u32[]{:S(2)}) collective-permute-start(f32[2,4,2,8,128]{4,3,2,1,0:T(8,128)S(1)} %get-tuple-element.64.hxf_ref), channel_id=1, source_target_pairs={{0,4},{4,8},{8,12},{12,16},{16,20},{20,24},{24,28},{1,5},{5,9},{9,... | collective-permute-start | bytes 196616 | tf_op jit(solution)/shard_map/ppermute | solution.py:28
  25.9 0.9 %collective-permute-done.3.hxf_ref = f32[2,4,2,8,128]{4,3,2,1,0:T(8,128)S(1)} collective-permute-done((f32[2,4,2,8,128]{4,3,2,1,0:T(8,128)S(1)}, f32[2,4,2,8,128]{4,3,2,1,0:T(8,128)S(1)}, u32[]{:S(2)}, u32[]{:S(2)}) %collective-permute-start.3) | collective-permute-done | bytes 65568 | tf_op jit(solution)/shard_map/ppermute | solution.py:28
  26.7 0.6 %collective-permute-done.4.hyf_ref = f32[136,128]{1,0:T(8,128)S(1)} collective-permute-done((f32[136,128]{1,0:T(8,128)S(1)}, f32[136,128]{1,0:T(8,128)S(1)}, u32[]{:S(2)}, u32[]{:S(2)}) %collective-permute-start.4) | collective-permute-done | bytes 69664 | tf_op jit(solution)/shard_map/ppermute | solution.py:22
  27.3 2.3 %add_rims.1 = (f32[2,4,3,8,16,128]{5,4,3,2,1,0:T(8,128)S(1)}, f32[2,4,3,8,16,128]{5,4,3,2,1,0:T(8,128)}) custom-call(s32[6]{0:T(128)S(1)} %copy-done, f32[2,4,3,8,16,128]{5,4,3,2,1,0:T(8,128)S(1)} %get-tuple-element.63.left_in, f32[2,4,2,8,128]{4,3,2,1,0:T(8,128)S(1)} %collective-permute-done.3.hxf_ref, ...), custom_call_target="tpu_custom_call", output_to_operand_aliasing={{0}: (1, {})} | custom-call | tf_op jit(solution)/shard_map/add_rims/pallas_call | solution.py:660
  29.5 1.1 %all-to-all-done.rows_ref = f32[32,5,128]{2,1,0:T(8,128)S(1)} async-done(((f32[32,5,128]{2,1,0:T(8,128)}), f32[32,5,128]{2,1,0:T(8,128)S(1)}, u32[]{:S(2)}, u32[]{:S(2)}) %all-to-all-start) | async-done | bytes 81952 | tf_op jit(solution)/shard_map/all_to_all | solution.py:657
  30.7 0.7 %sum_rows.1 = f32[2,4,4]{2,1,0:T(4,128)} custom-call(f32[32,5,128]{2,1,0:T(8,128)S(1)} %all-to-all-done.rows_ref), custom_call_target="tpu_custom_call" | custom-call | tf_op jit(solution)/shard_map/sum_rows/pallas_call | solution.py:672
  (8 shorter events, 0.0 us)
Async XLA Ops:
  0.6 7.5 %copy-start = (s32[6]{0:T(128)S(1)}, s32[6]{0:T(128)}, u32[]{:S(2)}) copy-start(s32[6]{0:T(128)} %pml_ref.7) | copy-start | bytes 76
  0.6 7.5 %copy-start.1 = (f32[2,4,4]{2,1,0:T(4,128)S(1)}, f32[2,4,4]{2,1,0:T(4,128)}, u32[]{:S(2)}) copy-start(f32[2,4,4]{2,1,0:T(4,128)} %coeffs_ref.3) | copy-start | bytes 388
  0.7 7.5 %copy-start.5 = (f32[4]{0:T(128)S(1)}, f32[4]{0:T(128)}, u32[]{:S(2)}) copy-start(f32[4]{0:T(128)} %eps_loss_ref.1) | copy-start | bytes 52
  0.7 7.5 %copy-start.4 = (f32[4]{0:T(128)S(1)}, f32[4]{0:T(128)}, u32[]{:S(2)}) copy-start(f32[4]{0:T(128)} %eps_real_ref.1) | copy-start | bytes 52
  0.7 7.5 %copy-start.3 = (s32[8,16,128]{2,1,0:T(8,128)S(1)}, s32[8,16,128]{2,1,0:T(8,128)}, u32[]{:S(2)}) copy-start(s32[8,16,128]{2,1,0:T(8,128)} %material_ref.1) | copy-start | bytes 196612
  2.3 9.0 %collective-permute-start.1 = (f32[16,128]{1,0:T(8,128)S(1)}, f32[16,128]{1,0:T(8,128)S(1)}, u32[]{:S(2)}, u32[]{:S(2)}) collective-permute-start(f32[16,128]{1,0:T(8,128)S(1)} %get-tuple-element.43), channel_id=1, source_target_pairs={{0,2},{2,0},{1,3},{3,1},{4,6},{6,4},{5,7},{7,5},{8,10},{10,8},{9,1... | collective-permute-start | bytes 24584 | tf_op jit(solution)/shard_map/ppermute | solution.py:22
  5.4 6.0 %collective-permute-start = (f32[2,4,2,8,128]{4,3,2,1,0:T(8,128)S(1)}, f32[2,4,2,8,128]{4,3,2,1,0:T(8,128)S(1)}, u32[]{:S(2)}, u32[]{:S(2)}) collective-permute-start(f32[2,4,2,8,128]{4,3,2,1,0:T(8,128)S(1)} %get-tuple-element.42), channel_id=1, source_target_pairs={{0,28},{4,0},{8,4},{12,8},{16,12},{20,16},{24,20},{28,24},{1,29},{... | collective-permute-start | bytes 196616 | tf_op jit(solution)/shard_map/ppermute | solution.py:22
  11.3 2.5 %copy-start.2 = (f32[2,4]{1,0:T(2,128)S(1)}, f32[2,4]{1,0:T(2,128)}, u32[]{:S(2)}) copy-start(f32[2,4]{1,0:T(2,128)} %ritz_ref.3) | copy-start | bytes 100
  12.3 5.0 %collective-permute-start.2 = (f32[2,4,2,16,128]{4,3,2,1,0:T(8,128)S(1)}, f32[2,4,2,16,128]{4,3,2,1,0:T(8,128)S(1)}, u32[]{:S(2)}, u32[]{:S(2)}) collective-permute-start(f32[2,4,2,16,128]{4,3,2,1,0:T(8,128)S(1)} %get-tuple-element.49), channel_id=1, source_target_pairs={{0,1},{1,0},{2,3},{3,2},{4,5},{5,4},{6,7},{7,6},{8,9},{9,8},{10,11... | collective-permute-start | bytes 393224 | tf_op jit(solution)/shard_map/ppermute | solution.py:22
  19.3 11.4 %all-to-all-start = ((f32[32,5,128]{2,1,0:T(8,128)}), f32[32,5,128]{2,1,0:T(8,128)S(1)}, u32[]{:S(2)}, u32[]{:S(2)}) async-start(f32[32,5,128]{2,1,0:T(8,128)} %get-tuple-element.62), calls=%async_computation | async-start | bytes 262144 | tf_op jit(solution)/shard_map/all_to_all | solution.py:657
  22.2 5.0 %collective-permute-start.4 = (f32[136,128]{1,0:T(8,128)S(1)}, f32[136,128]{1,0:T(8,128)S(1)}, u32[]{:S(2)}, u32[]{:S(2)}) collective-permute-start(f32[136,128]{1,0:T(8,128)S(1)} %get-tuple-element.65.hyf_ref), channel_id=1, source_target_pairs={{0,2},{2,0},{1,3},{3,1},{4,6},{6,4},{5,7},{7,5},{8,10},{10,8},{9,1... | collective-permute-start | bytes 208904 | tf_op jit(solution)/shard_map/ppermute | solution.py:22
  24.1 2.7 %collective-permute-start.3 = (f32[2,4,2,8,128]{4,3,2,1,0:T(8,128)S(1)}, f32[2,4,2,8,128]{4,3,2,1,0:T(8,128)S(1)}, u32[]{:S(2)}, u32[]{:S(2)}) collective-permute-start(f32[2,4,2,8,128]{4,3,2,1,0:T(8,128)S(1)} %get-tuple-element.64.hxf_ref), channel_id=1, source_target_pairs={{0,4},{4,8},{8,12},{12,16},{16,20},{20,24},{24,28},{1,5},{5,9},{9,... | collective-permute-start | bytes 196616 | tf_op jit(solution)/shard_map/ppermute | solution.py:28

commit v20 on v13

--- a/solution.py
+++ b/solution.py
@@ -20,6 +20,12 @@
 def passed_round(value, axis, steps):
     count = lax.axis_size(axis)
     return lax.ppermute(value, axis, [(source, (source + steps) % count) for source in range(count)])
+
+
+def passed_along(value, axis, steps):
+    count = lax.axis_size(axis)
+    leading, last = (max(0, -steps), min(count, count - steps))
+    return lax.ppermute(value, axis, [(source, source + steps) for source in range(leading, last)])
 
 
 def inverse_stretch(places, length, low_width, high_width):
@@ -29,6 +35,13 @@
     absorb = SIGMA_TOP * inside_depth * inside_depth
     scaled = 1.0 / (1.0 + absorb * absorb)
     return scaled, -absorb * scaled
+
+
+def tree_sum(values):
+    while len(values) > 1:
+        pairs = [values[place] + values[place + 1] for place in range(0, len(values) - 1, 2)]
+        values = pairs + ([values[-1]] if len(values) % 2 else [])
+    return values[0]
 
 
 def cmul(left, right):
@@ -122,7 +135,7 @@
 
 def prepare_kernel(
     pml_ref, eps_real_ref, eps_loss_ref, coeffs_ref, fields_ref, material_ref,
-    basis_ref, loss_ref, h_ref, packed_ref, table_ref, sz_ref,
+    basis_ref, eps_ref, h_ref, packed_ref, table_ref, sz_ref,
 ):
     _, vectors, _, nz, nx, ny = fields_ref.shape
     plane = (nx, ny)
@@ -141,20 +154,22 @@
     @pl.loop(0, nz)
     def _(z):
         material = material_ref[z]
-        eps = []
-        for source in (eps_real_ref, eps_loss_ref):
+        for part, source in enumerate((eps_real_ref, eps_loss_ref)):
             value = jnp.zeros(plane, jnp.float32)
             for number in range(source.shape[0]):
                 value = jnp.where(material == number, -OMEGA_SQ * source[number], value)
-            eps.append(value)
+            eps_ref[part, z] = value
         for comp in range(3):
-            old = [(fields_ref[0, a, comp, z], fields_ref[1, a, comp, z]) for a in range(vectors)]
+            real = [fields_ref[0, a, comp, z] for a in range(vectors)]
+            imag = [fields_ref[1, a, comp, z] for a in range(vectors)]
+            both = [first + second for first, second in zip(real, imag)]
             for b in range(vectors):
-                new = rotated(coeffs_ref, old, b)
-                loss = cmul(eps, new)
-                for part in parts:
-                    basis_ref[part, b, comp, z] = new[part]
-                    loss_ref[part, b, comp, z] = loss[part]
+                turns = [(coeffs_ref[0, a, b], coeffs_ref[1, a, b]) for a in range(vectors)]
+                shared = tree_sum([turn[0] * value for turn, value in zip(turns, both)])
+                less = tree_sum([(turn[0] + turn[1]) * value for turn, value in zip(turns, imag)])
+                more = tree_sum([(turn[1] - turn[0]) * value for turn, value in zip(turns, real)])
+                basis_ref[0, b, comp, z] = shared - less
+                basis_ref[1, b, comp, z] = shared + more
         packed_ref[z] = jnp.zeros(plane, jnp.float32)
 
     tile = (SUB, ny)
@@ -306,7 +321,7 @@
 
 
 def plane_step(
-    b, z, before, sums, ritz_ref, basis_ref, loss_ref, table_ref, sz_ref, h_ref, left_ref, halos=None
+    b, z, before, sums, ritz_ref, basis_ref, eps_ref, table_ref, sz_ref, h_ref, left_ref, halos=None
 ):
     _, vectors, _, _, nx, ny = basis_ref.shape
     rows = lax.broadcasted_iota(jnp.int32, (SUB, ny), 0)
@@ -344,9 +359,11 @@
         byz, byx = (cmul(sey, back_y(value)) for value in (hz, hx))
         bzx, bzy = (cmul(sez, sub(value, past)) for value, past in zip((hx, hy), before[t]))
         curl = (sub(byz, bzy), sub(bzx, bxz), sub(bxy, byx))
-        w = [add(curl[comp], field_of(loss_ref, b, comp, z, cut)) for comp in range(3)]
+        u = [field_of(basis_ref, b, comp, z, cut) for comp in range(3)]
+        eps = tuple(eps_ref[part, z, cut] for part in parts)
+        w = [add(curl[comp], cmul(eps, u[comp])) for comp in range(3)]
         for comp in range(3):
-            left = sub(w[comp], cmul((ritz_ref[0, b], ritz_ref[1, b]), field_of(basis_ref, b, comp, z, cut)))
+            left = sub(w[comp], cmul((ritz_ref[0, b], ritz_ref[1, b]), u[comp]))
             for part in parts:
                 left_ref[part, b, comp, z, cut] = left[part]
         for a in range(vectors):
@@ -358,7 +375,7 @@
 
 
 def inner_kernel(
-    ritz_ref, basis_ref, loss_ref, table_ref, sz_ref, h_in, packed_in, xadd_ref, yadd_ref,
+    ritz_ref, basis_ref, eps_ref, table_ref, sz_ref, h_in, packed_in, xadd_ref, yadd_ref,
     h_ref, packed_ref, left_ref, acc_ref, before_ref, hxf_ref, basis_hbm, sem,
 ):
     del h_in, packed_in
@@ -390,7 +407,7 @@
             ]
             sums = [(acc_ref[b, a], acc_ref[b, vectors + a]) for a in range(vectors)]
             before, sums = plane_step(
-                b, z, before, sums, ritz_ref, basis_ref, loss_ref, table_ref, sz_ref, h_ref, left_ref, (xadd_ref, yadd_ref)
+                b, z, before, sums, ritz_ref, basis_ref, eps_ref, table_ref, sz_ref, h_ref, left_ref, (xadd_ref, yadd_ref)
             )
             for part in range(2):
                 for a in range(vectors):
@@ -402,8 +419,7 @@
     keep.wait()
 
 
-def last_plane_kernel(sz_ref, zf_ref, h_in, packed_in, hxf_in, h_ref, hxf_ref, hyf_ref):
-    del h_in, hxf_in
+def close_last_plane(sz_ref, zf_ref, packed_in, h_ref, hxf_ref, hyf_ref):
     _, vectors, _, nz, nx, ny = h_ref.shape
     parts = range(2)
     last = nz - 1
@@ -427,10 +443,11 @@
 
 
 def outer_kernel(
-    pml_ref, ritz_ref, basis_ref, loss_ref, table_ref, sz_ref, h_ref, zf_ref, xf_ref, yt_ref, hxf_ref, hyf_ref,
-    left_in, acc_ref, before_ref, left_ref, gram_ref,
+    pml_ref, ritz_ref, basis_ref, eps_ref, table_ref, sz_ref, h_in, zf_ref, xf_ref, yt_ref, hxf_in, packed_in,
+    left_in, acc_ref, before_ref, left_ref, gram_ref, h_ref, hxf_ref, hyf_ref,
 ):
-    del left_in
+    del left_in, h_in, hxf_in
+    close_last_plane(sz_ref, zf_ref, packed_in, h_ref, hxf_ref, hyf_ref)
     _, vectors, _, nz, nx, ny = basis_ref.shape
     parts = range(2)
     cuts = tiles_of(nx)
@@ -453,7 +470,7 @@
         before = [tuple(tile_of(before_ref, slot, cut) for slot in range(2)) for cut in cuts]
         sums = [(acc_ref[b, a], acc_ref[b, vectors + a]) for a in range(vectors)]
         _, sums = plane_step(
-            b, nz - 1, before, sums, ritz_ref, basis_ref, loss_ref, table_ref, sz_ref, h_ref, left_ref
+            b, nz - 1, before, sums, ritz_ref, basis_ref, eps_ref, table_ref, sz_ref, h_ref, left_ref
         )
         for cut in cuts:
             ex, ey = (field_of(basis_ref, b, comp, 0, cut) for comp in range(2))
@@ -495,13 +512,6 @@
         gram_ref[device] = block
 
 
-def tree_sum(values):
-    while len(values) > 1:
-        pairs = [values[place] + values[place + 1] for place in range(0, len(values) - 1, 2)]
-        values = pairs + ([values[-1]] if len(values) % 2 else [])
-    return values[0]
-
-
 def gather_kernel(rows_ref, gram_ref):
     vectors = gram_ref.shape[1]
     total = tree_sum([rows_ref[device] for device in range(rows_ref.shape[0])])[0:1]
@@ -596,9 +606,9 @@
 
     planes = f32(nz, nx, ny)
     face = f32(*xf_shape)
-    basis, loss, h, packed, table, sz = pl.pallas_call(
+    basis, eps, h, packed, table, sz = pl.pallas_call(
         prepare_kernel,
-        out_shape=(whole, whole, whole, planes, f32(8, nx, ny), f32(4, nz, ny)),
+        out_shape=(whole, f32(2, nz, nx, ny), whole, planes, f32(8, nx, ny), f32(4, nz, ny)),
         in_specs=[SMEM] * 4 + [VMEM] * 2,
         out_specs=(VMEM,) * 6,
         compiler_params=params,
@@ -625,30 +635,21 @@
         compiler_params=params,
         cost_estimate=cost(800, 2),
         name="apply_inner",
-    )(ritz, basis, loss, table, sz, h, packed, xadd, yadd)
-    h, hxf, hyf = pl.pallas_call(
-        last_plane_kernel,
-        out_shape=(whole, face, f32(*yf_shape)),
-        in_specs=[VMEM] * 5,
-        out_specs=(VMEM,) * 3,
-        input_output_aliases={2: 0, 4: 1},
-        compiler_params=params,
-        name="last_plane",
-    )(sz, zf, h, packed, hxf)
+    )(ritz, basis, eps, table, sz, h, packed, xadd, yadd)
     devices = lax.axis_size("gx") * lax.axis_size("gy") * lax.axis_size("gz")
-    left, gram = pl.pallas_call(
+    left, gram, _, hxf, hyf = pl.pallas_call(
         outer_kernel,
-        out_shape=(whole, f32(devices, 4, ny)),
+        out_shape=(whole, f32(devices, 4, ny), whole, face, f32(*yf_shape)),
         in_specs=[SMEM] * 2 + [VMEM] * 13,
-        out_specs=(VMEM,) * 2,
-        input_output_aliases={12: 0},
+        out_specs=(VMEM,) * 5,
+        input_output_aliases={12: 0, 6: 2, 10: 3},
         compiler_params=params,
         cost_estimate=cost(300, 1),
         name="apply_outer",
-    )(pml_width, ritz, basis, loss, table, sz, h, zf, xf, yt, hxf, hyf, left, acc, before)
+    )(pml_width, ritz, basis, eps, table, sz, h, zf, xf, yt, hxf, packed, left, acc, before)
     gram, hxf, hyf = lax.optimization_barrier((gram, hxf, hyf))
     rows = lax.all_to_all(gram, ("gx", "gy", "gz"), 0, 0)
-    from_x = passed_round(hxf, "gx", 1)
+    from_x = passed_along(hxf, "gx", 1)
     from_y = passed_round(hyf, "gy", 1)
     _, residual = pl.pallas_call(
         rim_kernel,

time: 31.9 us -> 31.6 us (level); the launches traced: 31.8 us -> 31.1 us
  waiting for transfers between devices: 5.01 us -> 2.47 us
  starting transfers between devices: 12.4 us -> 14.7 us
    ppermute x5 -> x4, waiting for transfers between devices: 5.01 us -> 2.46 us  [passed_round(): lax.ppermute(value, axis, [(source, (source + steps) % count) for source...]
    ppermute x0 -> x1, starting transfers between devices: none -> 2.16 us  [passed_along(): lax.ppermute(value, axis, [(source, source + steps) for source in range(l...]
    pallas_call x3 -> x2, Pallas kernels: 5.09 us -> 4.72 us  [the longest x1 2.87 us: body(): pl.pallas_call(prepare_kernel, out_shape=(whole, f32(2, nz, nx, ny), whol...]
    ppermute x5 -> x4, starting transfers between devices: 9.59 us -> 9.35 us  [passed_round(): lax.ppermute(value, axis, [(source, (source + steps) % count) for source...]
  transfers between devices with their start and end apart: 6 -> 6, of which waited for: 3 -> 2; matrix products, arithmetic and copies ran while one was open for 0% -> 0% of each run, Pallas kernels for 26% -> 26%
where the time goes in v20:
time: 31.6 us; the launch traced here: 31.1 us
  starting transfers between devices  14.7 us (47%)
  Pallas kernels  13.2 us (42%)
  waiting for transfers between devices  2.47 us (8%)
  between operations  0.77 us (2%)
    ppermute x4, starting transfers between devices, passed_round(): lax.ppermute(value, axis, [(source, (source + steps) % count) for source...  9.35 us
    all_to_all x1, starting transfers between devices, body(): rows = lax.all_to_all(gram, ('gx', 'gy', 'gz'), 0, 0)  3.15 us
    pallas_call x1, Pallas kernels, body(): pl.pallas_call(inner_kernel, out_shape=(whole, planes, whole, f32(vectors...  2.99 us
    pallas_call x1, Pallas kernels, body(): pl.pallas_call(prepare_kernel, out_shape=(whole, f32(2, nz, nx, ny), whol...  2.87 us
    ppermute x4, waiting for transfers between devices, passed_round(): lax.ppermute(value, axis, [(source, (source + steps) % count) for source...  2.46 us
    pallas_call x1, Pallas kernels, body(): pl.pallas_call(rim_kernel, out_shape=(whole, whole), in_specs=[SMEM] + [V...  2.25 us
    ppermute x1, starting transfers between devices, passed_along(): lax.ppermute(value, axis, [(source, source + steps) for source in range(l...  2.16 us
    pallas_call x1, Pallas kernels, body(): pl.pallas_call(outer_kernel, out_shape=(whole, f32(devices, 4, ny), whole...  1.85 us
  transfers between devices with their start and end apart: 6, of which 2 were waited for; matrix products, arithmetic and copies ran while one was open for 0% of the time, Pallas kernels for 26%

profile of v20, /device:TPU:0, one launch (start us, length us, event | category | flops | bytes accessed | tf_op | source)
XLA Modules:
  0.0 31.1 jit_solution(14793591762992836337)
XLA Ops:
  0.6 0.0 copy-start.2
  0.6 0.0 copy-start.1
  0.7 0.0 copy-start.5
  0.7 1.6 %take_faces.1 = (f32[2,4,3,8,16,128]{5,4,3,2,1,0:T(8,128)S(1)}, f32[2,4,2,8,128]{4,3,2,1,0:T(8,128)S(1)}, f32[16,128]{1,0:T(8,128)S(1)}) custom-call(f32[2,4,3,8,16,128]{5,4,3,2,1,0:T(8,128)} %fields_hbm.1), custom_call_target="tpu_custom_call" | custom-call | tf_op jit(solution)/shard_map/take_faces/pallas_call | solution.py:591
  2.3 4.5 %collective-permute-start = (f32[2,4,2,8,128]{4,3,2,1,0:T(8,128)S(1)}, f32[2,4,2,8,128]{4,3,2,1,0:T(8,128)S(1)}, u32[]{:S(2)}, u32[]{:S(2)}) collective-permute-start(f32[2,4,2,8,128]{4,3,2,1,0:T(8,128)S(1)} %get-tuple-element.41), channel_id=1, source_target_pairs={{0,28},{4,0},{8,4},{12,8},{16,12},{20,16},{24,20},{28,24},{1,29},{... | collective-permute-start | bytes 196616 | tf_op jit(solution)/shard_map/ppermute | solution.py:22
  6.9 1.5 %collective-permute-start.1 = (f32[16,128]{1,0:T(8,128)S(1)}, f32[16,128]{1,0:T(8,128)S(1)}, u32[]{:S(2)}, u32[]{:S(2)}) collective-permute-start(f32[16,128]{1,0:T(8,128)S(1)} %get-tuple-element.42), channel_id=1, source_target_pairs={{0,2},{2,0},{1,3},{3,1},{4,6},{6,4},{5,7},{7,5},{8,10},{10,8},{9,1... | collective-permute-start | bytes 24584 | tf_op jit(solution)/shard_map/ppermute | solution.py:22
  8.4 0.0 copy-done.5
  8.4 2.9 %prepare.1 = (f32[2,4,3,8,16,128]{5,4,3,2,1,0:T(8,128)S(1)}, f32[2,8,16,128]{3,2,1,0:T(8,128)S(1)}, f32[2,4,3,8,16,128]{5,4,3,2,1,0:T(8,128)S(1)}, f32[8,16,128]...) custom-call(s32[6]{0:T(128)S(1)} %copy-done.2, f32[4]{0:T(128)S(1)} %copy-done.4, ...), custom_call_target="tpu_custom_call" | custom-call | flops 13107200 | bytes 6291456 | tf_op jit(solution)/shard_map/prepare/pallas_call | solution.py:609
  11.3 0.0 collective-permute-done.1.raw_yf_ref
  11.3 0.0 collective-permute-done.raw_xf_ref
  11.3 0.0 copy-start.3
  11.3 0.9 %slab_face.1 = (f32[2,4,3,8,16,128]{5,4,3,2,1,0:T(8,128)S(1)}, f32[2,4,2,8,128]{4,3,2,1,0:T(8,128)S(1)}, f32[16,128]{1,0:T(8,128)S(1)}, f32[2,4,2,8,128]{4,3,2,1...) custom-call(s32[6]{0:T(128)S(1)} %copy-done.2, ...), custom_call_target="tpu_custom_call", output_to_operand_aliasing={{0}: (3, {})} | custom-call | tf_op jit(solution)/shard_map/slab_face/pallas_call | solution.py:618
  12.2 1.6 %collective-permute-start.2 = (f32[2,4,2,16,128]{4,3,2,1,0:T(8,128)S(1)}, f32[2,4,2,16,128]{4,3,2,1,0:T(8,128)S(1)}, u32[]{:S(2)}, u32[]{:S(2)}) collective-permute-start(f32[2,4,2,16,128]{4,3,2,1,0:T(8,128)S(1)} %get-tuple-element.49), channel_id=1, source_target_pairs={{0,1},{1,0},{2,3},{3,2},{4,5},{5,4},{6,7},{7,6},{8,9},{9,8},{10,11... | collective-permute-start | bytes 393224 | tf_op jit(solution)/shard_map/ppermute | solution.py:22
  13.8 3.0 %apply_inner.1 = (f32[2,4,3,8,16,128]{5,4,3,2,1,0:T(8,128)S(1)}, f32[8,16,128]{2,1,0:T(8,128)S(1)}, f32[2,4,3,8,16,128]{5,4,3,2,1,0:T(8,128)S(1)}, f32[4,8,8,128...) custom-call(f32[2,4]{1,0:T(2,128)S(1)} %copy-done.3, ...), custom_call_target="tpu_custom_call", output_to_operand_aliasing={{0}: (5, {}), {1}: (6, {})} | custom-call | flops 13107200 | bytes 3145728 | tf_op jit(solution)/shard_map/apply_inner/pallas_call | solution.py:628
  16.8 0.5 %collective-permute-done.2.zf_ref = f32[2,4,2,16,128]{4,3,2,1,0:T(8,128)S(1)} collective-permute-done((f32[2,4,2,16,128]{4,3,2,1,0:T(8,128)S(1)}, f32[2,4,2,16,128]{4,3,2,1,0:T(8,128)S(1)}, u32[]{:S(2)}, u32[]{:S(2)}) %collective-permute-start.2) | collective-permute-done | bytes 131104 | tf_op jit(solution)/shard_map/ppermute | solution.py:22
  17.3 1.9 %apply_outer.1 = (f32[2,4,3,8,16,128]{5,4,3,2,1,0:T(8,128)S(1)}, f32[32,4,128]{2,1,0:T(4,128)}, f32[2,4,3,8,16,128]{5,4,3,2,1,0:T(8,128)S(1)}, f32[2,4,2,8,128]{4,3,2,1,0:T(8,128)S(1)}, f32[16,128]{1,0:T(8,128)S(1)}) custom-call(s32[6]{0:T(128)S(1)} %copy-done.2, f32[2,4]{1,0:T(2,128)S(1)} %copy-done.3, ...), custom_call_target="tpu_custom_call", output_to_operand_aliasing={{0}: (12, {}), {2}: (6, {}), {3}: (10, {})} | custom-call | flops 4915200 | bytes 1572864 | tf_op jit(solution)/shard_map/apply_outer/pallas_call | solution.py:640
  19.1 3.1 %all-to-all-start = ((f32[32,4,128]{2,1,0:T(4,128)}), f32[32,4,128]{2,1,0:T(4,128)S(1)}, u32[]{:S(2)}, u32[]{:S(2)}) async-start(f32[32,4,128]{2,1,0:T(4,128)} %get-tuple-element.60), calls=%async_computation | async-start | bytes 131072 | tf_op jit(solution)/shard_map/all_to_all | solution.py:651
  22.3 2.2 %collective-permute-start.3 = (f32[2,4,2,8,128]{4,3,2,1,0:T(8,128)S(1)}, f32[2,4,2,8,128]{4,3,2,1,0:T(8,128)S(1)}, u32[]{:S(2)}, u32[]{:S(2)}) collective-permute-start(f32[2,4,2,8,128]{4,3,2,1,0:T(8,128)S(1)} %get-tuple-element.62), channel_id=1, source_target_pairs={{0,4},{4,8},{8,12},{12,16},{16,20},{20,24},{24,28},{1,5},{5,9},{9,... | collective-permute-start | bytes 196616 | tf_op jit(solution)/shard_map/ppermute | solution.py:28
  24.4 1.7 %collective-permute-start.4 = (f32[16,128]{1,0:T(8,128)S(1)}, f32[16,128]{1,0:T(8,128)S(1)}, u32[]{:S(2)}, u32[]{:S(2)}) collective-permute-start(f32[16,128]{1,0:T(8,128)S(1)} %get-tuple-element.63), channel_id=1, source_target_pairs={{0,2},{2,0},{1,3},{3,1},{4,6},{6,4},{5,7},{7,5},{8,10},{10,8},{9,1... | collective-permute-start | bytes 24584 | tf_op jit(solution)/shard_map/ppermute | solution.py:22
  26.2 2.0 %collective-permute-done.4.hyf_ref = f32[16,128]{1,0:T(8,128)S(1)} collective-permute-done((f32[16,128]{1,0:T(8,128)S(1)}, f32[16,128]{1,0:T(8,128)S(1)}, u32[]{:S(2)}, u32[]{:S(2)}) %collective-permute-start.4) | collective-permute-done | bytes 8224 | tf_op jit(solution)/shard_map/ppermute | solution.py:22
  28.2 0.0 collective-permute-done.3.hxf_ref
  28.2 2.3 %add_rims.1 = (f32[2,4,3,8,16,128]{5,4,3,2,1,0:T(8,128)S(1)}, f32[2,4,3,8,16,128]{5,4,3,2,1,0:T(8,128)}) custom-call(s32[6]{0:T(128)S(1)} %copy-done.2, f32[2,4,3,8,16,128]{5,4,3,2,1,0:T(8,128)S(1)} %get-tuple-element.61.left_in, f32[2,4,2,8,128]{4,3,2,1,0:T(8,128)S(1)} %collective-permute-done.3.hxf_ref, ...), custom_call_target="tpu_custom_call", output_to_operand_aliasing={{0}: (1, {})} | custom-call | tf_op jit(solution)/shard_map/add_rims/pallas_call | solution.py:654
  30.4 0.0 all-to-all-done.rows_ref
  30.4 0.7 %sum_rows.1 = f32[2,4,4]{2,1,0:T(4,128)} custom-call(f32[32,4,128]{2,1,0:T(4,128)S(1)} %all-to-all-done.rows_ref), custom_call_target="tpu_custom_call" | custom-call | tf_op jit(solution)/shard_map/sum_rows/pallas_call | solution.py:666
  (7 shorter events, 0.0 us)
Async XLA Ops:
  0.6 7.8 %copy-start.2 = (s32[6]{0:T(128)S(1)}, s32[6]{0:T(128)}, u32[]{:S(2)}) copy-start(s32[6]{0:T(128)} %pml_ref.7) | copy-start | bytes 76
  0.6 7.8 %copy-start.1 = (f32[2,4,4]{2,1,0:T(4,128)S(1)}, f32[2,4,4]{2,1,0:T(4,128)}, u32[]{:S(2)}) copy-start(f32[2,4,4]{2,1,0:T(4,128)} %coeffs_ref.3) | copy-start | bytes 388
  0.7 7.8 %copy-start.5 = (f32[4]{0:T(128)S(1)}, f32[4]{0:T(128)}, u32[]{:S(2)}) copy-start(f32[4]{0:T(128)} %eps_loss_ref.1) | copy-start | bytes 52
  0.7 7.7 %copy-start.4 = (f32[4]{0:T(128)S(1)}, f32[4]{0:T(128)}, u32[]{:S(2)}) copy-start(f32[4]{0:T(128)} %eps_real_ref.1) | copy-start | bytes 52
  0.7 7.7 %copy-start = (s32[8,16,128]{2,1,0:T(8,128)S(1)}, s32[8,16,128]{2,1,0:T(8,128)}, u32[]{:S(2)}) copy-start(s32[8,16,128]{2,1,0:T(8,128)} %material_ref.1) | copy-start | bytes 196612
  2.3 9.0 %collective-permute-start = (f32[2,4,2,8,128]{4,3,2,1,0:T(8,128)S(1)}, f32[2,4,2,8,128]{4,3,2,1,0:T(8,128)S(1)}, u32[]{:S(2)}, u32[]{:S(2)}) collective-permute-start(f32[2,4,2,8,128]{4,3,2,1,0:T(8,128)S(1)} %get-tuple-element.41), channel_id=1, source_target_pairs={{0,28},{4,0},{8,4},{12,8},{16,12},{20,16},{24,20},{28,24},{1,29},{... | collective-permute-start | bytes 196616 | tf_op jit(solution)/shard_map/ppermute | solution.py:22
  6.9 4.4 %collective-permute-start.1 = (f32[16,128]{1,0:T(8,128)S(1)}, f32[16,128]{1,0:T(8,128)S(1)}, u32[]{:S(2)}, u32[]{:S(2)}) collective-permute-start(f32[16,128]{1,0:T(8,128)S(1)} %get-tuple-element.42), channel_id=1, source_target_pairs={{0,2},{2,0},{1,3},{3,1},{4,6},{6,4},{5,7},{7,5},{8,10},{10,8},{9,1... | collective-permute-start | bytes 24584 | tf_op jit(solution)/shard_map/ppermute | solution.py:22
  11.3 2.5 %copy-start.3 = (f32[2,4]{1,0:T(2,128)S(1)}, f32[2,4]{1,0:T(2,128)}, u32[]{:S(2)}) copy-start(f32[2,4]{1,0:T(2,128)} %ritz_ref.3) | copy-start | bytes 100
  12.2 5.0 %collective-permute-start.2 = (f32[2,4,2,16,128]{4,3,2,1,0:T(8,128)S(1)}, f32[2,4,2,16,128]{4,3,2,1,0:T(8,128)S(1)}, u32[]{:S(2)}, u32[]{:S(2)}) collective-permute-start(f32[2,4,2,16,128]{4,3,2,1,0:T(8,128)S(1)} %get-tuple-element.49), channel_id=1, source_target_pairs={{0,1},{1,0},{2,3},{3,2},{4,5},{5,4},{6,7},{7,6},{8,9},{9,8},{10,11... | collective-permute-start | bytes 393224 | tf_op jit(solution)/shard_map/ppermute | solution.py:22
  19.1 11.3 %all-to-all-start = ((f32[32,4,128]{2,1,0:T(4,128)}), f32[32,4,128]{2,1,0:T(4,128)S(1)}, u32[]{:S(2)}, u32[]{:S(2)}) async-start(f32[32,4,128]{2,1,0:T(4,128)} %get-tuple-element.60), calls=%async_computation | async-start | bytes 131072 | tf_op jit(solution)/shard_map/all_to_all | solution.py:651
  22.3 5.9 %collective-permute-start.3 = (f32[2,4,2,8,128]{4,3,2,1,0:T(8,128)S(1)}, f32[2,4,2,8,128]{4,3,2,1,0:T(8,128)S(1)}, u32[]{:S(2)}, u32[]{:S(2)}) collective-permute-start(f32[2,4,2,8,128]{4,3,2,1,0:T(8,128)S(1)} %get-tuple-element.62), channel_id=1, source_target_pairs={{0,4},{4,8},{8,12},{12,16},{16,20},{20,24},{24,28},{1,5},{5,9},{9,... | collective-permute-start | bytes 196616 | tf_op jit(solution)/shard_map/ppermute | solution.py:28
  24.4 3.7 %collective-permute-start.4 = (f32[16,128]{1,0:T(8,128)S(1)}, f32[16,128]{1,0:T(8,128)S(1)}, u32[]{:S(2)}, u32[]{:S(2)}) collective-permute-start(f32[16,128]{1,0:T(8,128)S(1)} %get-tuple-element.63), channel_id=1, source_target_pairs={{0,2},{2,0},{1,3},{3,1},{4,6},{6,4},{5,7},{7,5},{8,10},{10,8},{9,1... | collective-permute-start | bytes 24584 | tf_op jit(solution)/shard_map/ppermute | solution.py:22

commit v21 on v20

--- a/solution.py
+++ b/solution.py
@@ -597,7 +597,7 @@
         compiler_params=params,
         name="take_faces",
     )(pltpu.with_memory_space_constraint(fields, pltpu.HBM))
-    xf = passed_round(xf, "gx", -1)
+    xf = passed_along(xf, "gx", -1)
     yf = passed_round(yf, "gy", -1)
     cells = fields.size // 6 // vectors
 

time: 31.6 us -> 33 us (1.044)
  waiting for transfers between devices: 2.47 us -> 3.75 us
    ppermute x4 -> x3, starting transfers between devices: 9.35 us -> 6.32 us  [passed_round(): lax.ppermute(value, axis, [(source, (source + steps) % count) for source...]
    all_to_all x1, starting transfers between devices: 3.15 us -> 4.89 us  [body(): rows = lax.all_to_all(gram, ('gx', 'gy', 'gz'), 0, 0)]
    ppermute x1 -> x2, starting transfers between devices: 2.16 us -> 3.45 us  [passed_along(): lax.ppermute(value, axis, [(source, source + steps) for source in range(l...]
    ppermute x4 -> x3, waiting for transfers between devices: 2.46 us -> 3.74 us  [passed_round(): lax.ppermute(value, axis, [(source, (source + steps) % count) for source...]
  transfers between devices with their start and end apart: 6 -> 6, of which waited for: 2 -> 2; matrix products, arithmetic and copies ran while one was open for 0% -> 0% of each run, Pallas kernels for 26% -> 25%
where the time goes in v21:
time: 33 us; the launch traced here: 32.4 us
  starting transfers between devices  14.7 us (45%)
  Pallas kernels  13.2 us (40%)
  waiting for transfers between devices  3.75 us (11%)
  between operations  0.78 us (2%)
    ppermute x3, starting transfers between devices, passed_round(): lax.ppermute(value, axis, [(source, (source + steps) % count) for source...  6.32 us
    all_to_all x1, starting transfers between devices, body(): rows = lax.all_to_all(gram, ('gx', 'gy', 'gz'), 0, 0)  4.89 us
    ppermute x3, waiting for transfers between devices, passed_round(): lax.ppermute(value, axis, [(source, (source + steps) % count) for source...  3.74 us
    ppermute x2, starting transfers between devices, passed_along(): lax.ppermute(value, axis, [(source, source + steps) for source in range(l...  3.45 us
    pallas_call x1, Pallas kernels, body(): pl.pallas_call(inner_kernel, out_shape=(whole, planes, whole, f32(vectors...  2.99 us
    pallas_call x1, Pallas kernels, body(): pl.pallas_call(prepare_kernel, out_shape=(whole, f32(2, nz, nx, ny), whol...  2.87 us
    pallas_call x1, Pallas kernels, body(): pl.pallas_call(rim_kernel, out_shape=(whole, whole), in_specs=[SMEM] + [V...  2.25 us
    pallas_call x1, Pallas kernels, body(): pl.pallas_call(outer_kernel, out_shape=(whole, f32(devices, 4, ny), whole...  1.85 us
  transfers between devices with their start and end apart: 6, of which 2 were waited for; matrix products, arithmetic and copies ran while one was open for 0% of the time, Pallas kernels for 25%

profile of v21, /device:TPU:0, one launch (start us, length us, event | category | flops | bytes accessed | tf_op | source)
XLA Modules:
  0.0 32.4 jit_solution(18095622072089837921)
XLA Ops:
  0.6 0.0 copy-start.2
  0.6 0.0 copy-start.1
  0.7 1.6 %take_faces.1 = (f32[2,4,3,8,16,128]{5,4,3,2,1,0:T(8,128)S(1)}, f32[2,4,2,8,128]{4,3,2,1,0:T(8,128)S(1)}, f32[16,128]{1,0:T(8,128)S(1)}) custom-call(f32[2,4,3,8,16,128]{5,4,3,2,1,0:T(8,128)} %fields_hbm.1), custom_call_target="tpu_custom_call" | custom-call | tf_op jit(solution)/shard_map/take_faces/pallas_call | solution.py:591
  2.3 1.3 %collective-permute-start = (f32[2,4,2,8,128]{4,3,2,1,0:T(8,128)S(1)}, f32[2,4,2,8,128]{4,3,2,1,0:T(8,128)S(1)}, u32[]{:S(2)}, u32[]{:S(2)}) collective-permute-start(f32[2,4,2,8,128]{4,3,2,1,0:T(8,128)S(1)} %get-tuple-element.41), channel_id=1, source_target_pairs={{4,0},{8,4},{12,8},{16,12},{20,16},{24,20},{28,24},{5,1},{9,5},{13... | collective-permute-start | bytes 196616 | tf_op jit(solution)/shard_map/ppermute | solution.py:28
  3.6 3.0 %collective-permute-start.1 = (f32[16,128]{1,0:T(8,128)S(1)}, f32[16,128]{1,0:T(8,128)S(1)}, u32[]{:S(2)}, u32[]{:S(2)}) collective-permute-start(f32[16,128]{1,0:T(8,128)S(1)} %get-tuple-element.42), channel_id=1, source_target_pairs={{0,2},{2,0},{1,3},{3,1},{4,6},{6,4},{5,7},{7,5},{8,10},{10,8},{9,1... | collective-permute-start | bytes 24584 | tf_op jit(solution)/shard_map/ppermute | solution.py:22
  6.7 0.0 copy-done.1
  6.7 2.9 %prepare.1 = (f32[2,4,3,8,16,128]{5,4,3,2,1,0:T(8,128)S(1)}, f32[2,8,16,128]{3,2,1,0:T(8,128)S(1)}, f32[2,4,3,8,16,128]{5,4,3,2,1,0:T(8,128)S(1)}, f32[8,16,128]...) custom-call(s32[6]{0:T(128)S(1)} %copy-done.2, f32[4]{0:T(128)S(1)} %copy-done.4, ...), custom_call_target="tpu_custom_call" | custom-call | flops 13107200 | bytes 6291456 | tf_op jit(solution)/shard_map/prepare/pallas_call | solution.py:609
  9.6 0.0 collective-permute-done.1.raw_yf_ref
  9.6 0.0 collective-permute-done.raw_xf_ref
  9.6 0.0 copy-start.3
  9.6 0.9 %slab_face.1 = (f32[2,4,3,8,16,128]{5,4,3,2,1,0:T(8,128)S(1)}, f32[2,4,2,8,128]{4,3,2,1,0:T(8,128)S(1)}, f32[16,128]{1,0:T(8,128)S(1)}, f32[2,4,2,8,128]{4,3,2,1...) custom-call(s32[6]{0:T(128)S(1)} %copy-done.2, ...), custom_call_target="tpu_custom_call", output_to_operand_aliasing={{0}: (3, {})} | custom-call | tf_op jit(solution)/shard_map/slab_face/pallas_call | solution.py:618
  10.5 1.6 %collective-permute-start.2 = (f32[2,4,2,16,128]{4,3,2,1,0:T(8,128)S(1)}, f32[2,4,2,16,128]{4,3,2,1,0:T(8,128)S(1)}, u32[]{:S(2)}, u32[]{:S(2)}) collective-permute-start(f32[2,4,2,16,128]{4,3,2,1,0:T(8,128)S(1)} %get-tuple-element.49), channel_id=1, source_target_pairs={{0,1},{1,0},{2,3},{3,2},{4,5},{5,4},{6,7},{7,6},{8,9},{9,8},{10,11... | collective-permute-start | bytes 393224 | tf_op jit(solution)/shard_map/ppermute | solution.py:22
  12.1 0.0 copy-done.3
  12.1 3.0 %apply_inner.1 = (f32[2,4,3,8,16,128]{5,4,3,2,1,0:T(8,128)S(1)}, f32[8,16,128]{2,1,0:T(8,128)S(1)}, f32[2,4,3,8,16,128]{5,4,3,2,1,0:T(8,128)S(1)}, f32[4,8,8,128...) custom-call(f32[2,4]{1,0:T(2,128)S(1)} %copy-done.3, ...), custom_call_target="tpu_custom_call", output_to_operand_aliasing={{0}: (5, {}), {1}: (6, {})} | custom-call | flops 13107200 | bytes 3145728 | tf_op jit(solution)/shard_map/apply_inner/pallas_call | solution.py:628
  15.1 1.8 %collective-permute-done.2.zf_ref = f32[2,4,2,16,128]{4,3,2,1,0:T(8,128)S(1)} collective-permute-done((f32[2,4,2,16,128]{4,3,2,1,0:T(8,128)S(1)}, f32[2,4,2,16,128]{4,3,2,1,0:T(8,128)S(1)}, u32[]{:S(2)}, u32[]{:S(2)}) %collective-permute-start.2) | collective-permute-done | bytes 131104 | tf_op jit(solution)/shard_map/ppermute | solution.py:22
  16.8 1.9 %apply_outer.1 = (f32[2,4,3,8,16,128]{5,4,3,2,1,0:T(8,128)S(1)}, f32[32,4,128]{2,1,0:T(4,128)}, f32[2,4,3,8,16,128]{5,4,3,2,1,0:T(8,128)S(1)}, f32[2,4,2,8,128]{4,3,2,1,0:T(8,128)S(1)}, f32[16,128]{1,0:T(8,128)S(1)}) custom-call(s32[6]{0:T(128)S(1)} %copy-done.2, f32[2,4]{1,0:T(2,128)S(1)} %copy-done.3, ...), custom_call_target="tpu_custom_call", output_to_operand_aliasing={{0}: (12, {}), {2}: (6, {}), {3}: (10, {})} | custom-call | flops 4915200 | bytes 1572864 | tf_op jit(solution)/shard_map/apply_outer/pallas_call | solution.py:640
  18.7 4.9 %all-to-all-start = ((f32[32,4,128]{2,1,0:T(4,128)}), f32[32,4,128]{2,1,0:T(4,128)S(1)}, u32[]{:S(2)}, u32[]{:S(2)}) async-start(f32[32,4,128]{2,1,0:T(4,128)} %get-tuple-element.60), calls=%async_computation | async-start | bytes 131072 | tf_op jit(solution)/shard_map/all_to_all | solution.py:651
  23.6 2.2 %collective-permute-start.3 = (f32[2,4,2,8,128]{4,3,2,1,0:T(8,128)S(1)}, f32[2,4,2,8,128]{4,3,2,1,0:T(8,128)S(1)}, u32[]{:S(2)}, u32[]{:S(2)}) collective-permute-start(f32[2,4,2,8,128]{4,3,2,1,0:T(8,128)S(1)} %get-tuple-element.62), channel_id=1, source_target_pairs={{0,4},{4,8},{8,12},{12,16},{16,20},{20,24},{24,28},{1,5},{5,9},{9,... | collective-permute-start | bytes 196616 | tf_op jit(solution)/shard_map/ppermute | solution.py:28
  25.7 1.7 %collective-permute-start.4 = (f32[16,128]{1,0:T(8,128)S(1)}, f32[16,128]{1,0:T(8,128)S(1)}, u32[]{:S(2)}, u32[]{:S(2)}) collective-permute-start(f32[16,128]{1,0:T(8,128)S(1)} %get-tuple-element.63), channel_id=1, source_target_pairs={{0,2},{2,0},{1,3},{3,1},{4,6},{6,4},{5,7},{7,5},{8,10},{10,8},{9,1... | collective-permute-start | bytes 24584 | tf_op jit(solution)/shard_map/ppermute | solution.py:22
  27.5 2.0 %collective-permute-done.4.hyf_ref = f32[16,128]{1,0:T(8,128)S(1)} collective-permute-done((f32[16,128]{1,0:T(8,128)S(1)}, f32[16,128]{1,0:T(8,128)S(1)}, u32[]{:S(2)}, u32[]{:S(2)}) %collective-permute-start.4) | collective-permute-done | bytes 8224 | tf_op jit(solution)/shard_map/ppermute | solution.py:22
  29.4 0.0 collective-permute-done.3.hxf_ref
  29.5 2.3 %add_rims.1 = (f32[2,4,3,8,16,128]{5,4,3,2,1,0:T(8,128)S(1)}, f32[2,4,3,8,16,128]{5,4,3,2,1,0:T(8,128)}) custom-call(s32[6]{0:T(128)S(1)} %copy-done.2, f32[2,4,3,8,16,128]{5,4,3,2,1,0:T(8,128)S(1)} %get-tuple-element.61.left_in, f32[2,4,2,8,128]{4,3,2,1,0:T(8,128)S(1)} %collective-permute-done.3.hxf_ref, ...), custom_call_target="tpu_custom_call", output_to_operand_aliasing={{0}: (1, {})} | custom-call | tf_op jit(solution)/shard_map/add_rims/pallas_call | solution.py:654
  31.7 0.0 all-to-all-done.rows_ref
  31.7 0.7 %sum_rows.1 = f32[2,4,4]{2,1,0:T(4,128)} custom-call(f32[32,4,128]{2,1,0:T(4,128)S(1)} %all-to-all-done.rows_ref), custom_call_target="tpu_custom_call" | custom-call | tf_op jit(solution)/shard_map/sum_rows/pallas_call | solution.py:666
  (7 shorter events, 0.0 us)
Async XLA Ops:
  0.6 6.0 %copy-start.2 = (s32[6]{0:T(128)S(1)}, s32[6]{0:T(128)}, u32[]{:S(2)}) copy-start(s32[6]{0:T(128)} %pml_ref.7) | copy-start | bytes 76
  0.6 6.0 %copy-start.1 = (f32[2,4,4]{2,1,0:T(4,128)S(1)}, f32[2,4,4]{2,1,0:T(4,128)}, u32[]{:S(2)}) copy-start(f32[2,4,4]{2,1,0:T(4,128)} %coeffs_ref.3) | copy-start | bytes 388
  0.7 6.0 %copy-start.5 = (f32[4]{0:T(128)S(1)}, f32[4]{0:T(128)}, u32[]{:S(2)}) copy-start(f32[4]{0:T(128)} %eps_loss_ref.1) | copy-start | bytes 52
  0.7 6.0 %copy-start.4 = (f32[4]{0:T(128)S(1)}, f32[4]{0:T(128)}, u32[]{:S(2)}) copy-start(f32[4]{0:T(128)} %eps_real_ref.1) | copy-start | bytes 52
  0.7 6.0 %copy-start = (s32[8,16,128]{2,1,0:T(8,128)S(1)}, s32[8,16,128]{2,1,0:T(8,128)}, u32[]{:S(2)}) copy-start(s32[8,16,128]{2,1,0:T(8,128)} %material_ref.1) | copy-start | bytes 196612
  2.3 7.2 %collective-permute-start = (f32[2,4,2,8,128]{4,3,2,1,0:T(8,128)S(1)}, f32[2,4,2,8,128]{4,3,2,1,0:T(8,128)S(1)}, u32[]{:S(2)}, u32[]{:S(2)}) collective-permute-start(f32[2,4,2,8,128]{4,3,2,1,0:T(8,128)S(1)} %get-tuple-element.41), channel_id=1, source_target_pairs={{4,0},{8,4},{12,8},{16,12},{20,16},{24,20},{28,24},{5,1},{9,5},{13... | collective-permute-start | bytes 196616 | tf_op jit(solution)/shard_map/ppermute | solution.py:28
  3.6 5.9 %collective-permute-start.1 = (f32[16,128]{1,0:T(8,128)S(1)}, f32[16,128]{1,0:T(8,128)S(1)}, u32[]{:S(2)}, u32[]{:S(2)}) collective-permute-start(f32[16,128]{1,0:T(8,128)S(1)} %get-tuple-element.42), channel_id=1, source_target_pairs={{0,2},{2,0},{1,3},{3,1},{4,6},{6,4},{5,7},{7,5},{8,10},{10,8},{9,1... | collective-permute-start | bytes 24584 | tf_op jit(solution)/shard_map/ppermute | solution.py:22
  9.6 2.5 %copy-start.3 = (f32[2,4]{1,0:T(2,128)S(1)}, f32[2,4]{1,0:T(2,128)}, u32[]{:S(2)}) copy-start(f32[2,4]{1,0:T(2,128)} %ritz_ref.3) | copy-start | bytes 100
  10.5 6.3 %collective-permute-start.2 = (f32[2,4,2,16,128]{4,3,2,1,0:T(8,128)S(1)}, f32[2,4,2,16,128]{4,3,2,1,0:T(8,128)S(1)}, u32[]{:S(2)}, u32[]{:S(2)}) collective-permute-start(f32[2,4,2,16,128]{4,3,2,1,0:T(8,128)S(1)} %get-tuple-element.49), channel_id=1, source_target_pairs={{0,1},{1,0},{2,3},{3,2},{4,5},{5,4},{6,7},{7,6},{8,9},{9,8},{10,11... | collective-permute-start | bytes 393224 | tf_op jit(solution)/shard_map/ppermute | solution.py:22
  18.7 13.0 %all-to-all-start = ((f32[32,4,128]{2,1,0:T(4,128)}), f32[32,4,128]{2,1,0:T(4,128)S(1)}, u32[]{:S(2)}, u32[]{:S(2)}) async-start(f32[32,4,128]{2,1,0:T(4,128)} %get-tuple-element.60), calls=%async_computation | async-start | bytes 131072 | tf_op jit(solution)/shard_map/all_to_all | solution.py:651
  23.6 5.9 %collective-permute-start.3 = (f32[2,4,2,8,128]{4,3,2,1,0:T(8,128)S(1)}, f32[2,4,2,8,128]{4,3,2,1,0:T(8,128)S(1)}, u32[]{:S(2)}, u32[]{:S(2)}) collective-permute-start(f32[2,4,2,8,128]{4,3,2,1,0:T(8,128)S(1)} %get-tuple-element.62), channel_id=1, source_target_pairs={{0,4},{4,8},{8,12},{12,16},{16,20},{20,24},{24,28},{1,5},{5,9},{9,... | collective-permute-start | bytes 196616 | tf_op jit(solution)/shard_map/ppermute | solution.py:28
  25.7 3.7 %collective-permute-start.4 = (f32[16,128]{1,0:T(8,128)S(1)}, f32[16,128]{1,0:T(8,128)S(1)}, u32[]{:S(2)}, u32[]{:S(2)}) collective-permute-start(f32[16,128]{1,0:T(8,128)S(1)} %get-tuple-element.63), channel_id=1, source_target_pairs={{0,2},{2,0},{1,3},{3,1},{4,6},{6,4},{5,7},{7,5},{8,10},{10,8},{9,1... | collective-permute-start | bytes 24584 | tf_op jit(solution)/shard_map/ppermute | solution.py:22

commit v22 on v21

--- a/solution.py
+++ b/solution.py
@@ -20,6 +20,16 @@
 def passed_round(value, axis, steps):
     count = lax.axis_size(axis)
     return lax.ppermute(value, axis, [(source, (source + steps) % count) for source in range(count)])
+
+
+def passed_over(value, axis, across, steps):
+    count, rows = lax.axis_size(axis), lax.axis_size(across)
+    pairs = []
+    for place in range(count):
+        for row in range(rows):
+            turns, target = divmod(place + steps, count)
+            pairs.append((place * rows + row, target * rows + (row + turns) % rows))
+    return lax.ppermute(value, (axis, across), pairs)
 
 
 def passed_along(value, axis, steps):
@@ -597,7 +607,7 @@
         compiler_params=params,
         name="take_faces",
     )(pltpu.with_memory_space_constraint(fields, pltpu.HBM))
-    xf = passed_along(xf, "gx", -1)
+    xf = passed_over(xf, "gx", "gz", -1)
     yf = passed_round(yf, "gy", -1)
     cells = fields.size // 6 // vectors
 

time: 33 us -> 31.9 us (0.967)
  starting transfers between devices: 14.7 us -> 13.9 us
  waiting for transfers between devices: 3.75 us -> 3.41 us
    ppermute x0 -> x1, starting transfers between devices: none -> 5.47 us  [passed_over(): return lax.ppermute(value, (axis, across), pairs)]
    ppermute x3, starting transfers between devices: 6.32 us -> 3.88 us  [passed_round(): lax.ppermute(value, axis, [(source, (source + steps) % count) for source...]
    all_to_all x1, starting transfers between devices: 4.89 us -> 2.56 us  [body(): rows = lax.all_to_all(gram, ('gx', 'gy', 'gz'), 0, 0)]
    ppermute x2 -> x1, starting transfers between devices: 3.45 us -> 2.02 us  [passed_along(): lax.ppermute(value, axis, [(source, source + steps) for source in range(l...]
    ppermute x3, waiting for transfers between devices: 3.74 us -> 3.4 us  [passed_round(): lax.ppermute(value, axis, [(source, (source + steps) % count) for source...]
  transfers between devices with their start and end apart: 6 -> 6, of which waited for: 2 -> 2; matrix products, arithmetic and copies ran while one was open for 0% -> 0% of each run, Pallas kernels for 25% -> 26%
where the time goes in v22:
time: 31.9 us; the launch traced here: 31.3 us
  starting transfers between devices  13.9 us (44%)
  Pallas kernels  13.2 us (41%)
  waiting for transfers between devices  3.41 us (11%)
  between operations  0.77 us (2%)
    ppermute x1, starting transfers between devices, passed_over(): return lax.ppermute(value, (axis, across), pairs)  5.47 us
    ppermute x3, starting transfers between devices, passed_round(): lax.ppermute(value, axis, [(source, (source + steps) % count) for source...  3.88 us
    ppermute x3, waiting for transfers between devices, passed_round(): lax.ppermute(value, axis, [(source, (source + steps) % count) for source...  3.4 us
    pallas_call x1, Pallas kernels, body(): pl.pallas_call(inner_kernel, out_shape=(whole, planes, whole, f32(vectors...  2.99 us
    pallas_call x1, Pallas kernels, body(): pl.pallas_call(prepare_kernel, out_shape=(whole, f32(2, nz, nx, ny), whol...  2.87 us
    all_to_all x1, starting transfers between devices, body(): rows = lax.all_to_all(gram, ('gx', 'gy', 'gz'), 0, 0)  2.56 us
    pallas_call x1, Pallas kernels, body(): pl.pallas_call(rim_kernel, out_shape=(whole, whole), in_specs=[SMEM] + [V...  2.25 us
    ppermute x1, starting transfers between devices, passed_along(): lax.ppermute(value, axis, [(source, source + steps) for source in range(l...  2.02 us
  transfers between devices with their start and end apart: 6, of which 2 were waited for; matrix products, arithmetic and copies ran while one was open for 0% of the time, Pallas kernels for 26%

profile of v22, /device:TPU:0, one launch (start us, length us, event | category | flops | bytes accessed | tf_op | source)
XLA Modules:
  0.0 31.3 jit_solution(13097745018149074403)
XLA Ops:
  0.6 0.0 copy-start.2
  0.6 0.0 copy-start.1
  0.7 0.0 copy-start.5
  0.7 0.0 copy-start.4
  0.7 1.6 %take_faces.1 = (f32[2,4,3,8,16,128]{5,4,3,2,1,0:T(8,128)S(1)}, f32[2,4,2,8,128]{4,3,2,1,0:T(8,128)S(1)}, f32[16,128]{1,0:T(8,128)S(1)}) custom-call(f32[2,4,3,8,16,128]{5,4,3,2,1,0:T(8,128)} %fields_hbm.1), custom_call_target="tpu_custom_call" | custom-call | tf_op jit(solution)/shard_map/take_faces/pallas_call | solution.py:601
  2.3 5.5 %collective-permute-start = (f32[2,4,2,8,128]{4,3,2,1,0:T(8,128)S(1)}, f32[2,4,2,8,128]{4,3,2,1,0:T(8,128)S(1)}, u32[]{:S(2)}, u32[]{:S(2)}) collective-permute-start(f32[2,4,2,8,128]{4,3,2,1,0:T(8,128)S(1)} %get-tuple-element.41), channel_id=1, source_target_pairs={{0,29},{1,28},{4,0},{5,1},{8,4},{9,5},{12,8},{13,9},{16,12},{17,13... | collective-permute-start | bytes 196616 | tf_op jit(solution)/shard_map/ppermute | solution.py:32
  7.8 1.5 %collective-permute-start.1 = (f32[16,128]{1,0:T(8,128)S(1)}, f32[16,128]{1,0:T(8,128)S(1)}, u32[]{:S(2)}, u32[]{:S(2)}) collective-permute-start(f32[16,128]{1,0:T(8,128)S(1)} %get-tuple-element.42), channel_id=1, source_target_pairs={{0,2},{2,0},{1,3},{3,1},{4,6},{6,4},{5,7},{7,5},{8,10},{10,8},{9,1... | collective-permute-start | bytes 24584 | tf_op jit(solution)/shard_map/ppermute | solution.py:22
  9.3 2.9 %prepare.1 = (f32[2,4,3,8,16,128]{5,4,3,2,1,0:T(8,128)S(1)}, f32[2,8,16,128]{3,2,1,0:T(8,128)S(1)}, f32[2,4,3,8,16,128]{5,4,3,2,1,0:T(8,128)S(1)}, f32[8,16,128]...) custom-call(s32[6]{0:T(128)S(1)} %copy-done.2, f32[4]{0:T(128)S(1)} %copy-done.4, ...), custom_call_target="tpu_custom_call" | custom-call | flops 13107200 | bytes 6291456 | tf_op jit(solution)/shard_map/prepare/pallas_call | solution.py:619
  12.2 0.0 collective-permute-done.1.raw_yf_ref
  12.2 0.0 collective-permute-done.raw_xf_ref
  12.2 0.0 copy-start.3
  12.3 0.9 %slab_face.1 = (f32[2,4,3,8,16,128]{5,4,3,2,1,0:T(8,128)S(1)}, f32[2,4,2,8,128]{4,3,2,1,0:T(8,128)S(1)}, f32[16,128]{1,0:T(8,128)S(1)}, f32[2,4,2,8,128]{4,3,2,1...) custom-call(s32[6]{0:T(128)S(1)} %copy-done.2, ...), custom_call_target="tpu_custom_call", output_to_operand_aliasing={{0}: (3, {})} | custom-call | tf_op jit(solution)/shard_map/slab_face/pallas_call | solution.py:628
  13.2 0.6 %collective-permute-start.2 = (f32[2,4,2,16,128]{4,3,2,1,0:T(8,128)S(1)}, f32[2,4,2,16,128]{4,3,2,1,0:T(8,128)S(1)}, u32[]{:S(2)}, u32[]{:S(2)}) collective-permute-start(f32[2,4,2,16,128]{4,3,2,1,0:T(8,128)S(1)} %get-tuple-element.49), channel_id=1, source_target_pairs={{0,1},{1,0},{2,3},{3,2},{4,5},{5,4},{6,7},{7,6},{8,9},{9,8},{10,11... | collective-permute-start | bytes 393224 | tf_op jit(solution)/shard_map/ppermute | solution.py:22
  13.8 3.0 %apply_inner.1 = (f32[2,4,3,8,16,128]{5,4,3,2,1,0:T(8,128)S(1)}, f32[8,16,128]{2,1,0:T(8,128)S(1)}, f32[2,4,3,8,16,128]{5,4,3,2,1,0:T(8,128)S(1)}, f32[4,8,8,128...) custom-call(f32[2,4]{1,0:T(2,128)S(1)} %copy-done.3, ...), custom_call_target="tpu_custom_call", output_to_operand_aliasing={{0}: (5, {}), {1}: (6, {})} | custom-call | flops 13107200 | bytes 3145728 | tf_op jit(solution)/shard_map/apply_inner/pallas_call | solution.py:638
  16.8 1.4 %collective-permute-done.2.zf_ref = f32[2,4,2,16,128]{4,3,2,1,0:T(8,128)S(1)} collective-permute-done((f32[2,4,2,16,128]{4,3,2,1,0:T(8,128)S(1)}, f32[2,4,2,16,128]{4,3,2,1,0:T(8,128)S(1)}, u32[]{:S(2)}, u32[]{:S(2)}) %collective-permute-start.2) | collective-permute-done | bytes 131104 | tf_op jit(solution)/shard_map/ppermute | solution.py:22
  18.2 1.9 %apply_outer.1 = (f32[2,4,3,8,16,128]{5,4,3,2,1,0:T(8,128)S(1)}, f32[32,4,128]{2,1,0:T(4,128)}, f32[2,4,3,8,16,128]{5,4,3,2,1,0:T(8,128)S(1)}, f32[2,4,2,8,128]{4,3,2,1,0:T(8,128)S(1)}, f32[16,128]{1,0:T(8,128)S(1)}) custom-call(s32[6]{0:T(128)S(1)} %copy-done.2, f32[2,4]{1,0:T(2,128)S(1)} %copy-done.3, ...), custom_call_target="tpu_custom_call", output_to_operand_aliasing={{0}: (12, {}), {2}: (6, {}), {3}: (10, {})} | custom-call | flops 4915200 | bytes 1572864 | tf_op jit(solution)/shard_map/apply_outer/pallas_call | solution.py:650
  20.0 2.6 %all-to-all-start = ((f32[32,4,128]{2,1,0:T(4,128)}), f32[32,4,128]{2,1,0:T(4,128)S(1)}, u32[]{:S(2)}, u32[]{:S(2)}) async-start(f32[32,4,128]{2,1,0:T(4,128)} %get-tuple-element.60), calls=%async_computation | async-start | bytes 131072 | tf_op jit(solution)/shard_map/all_to_all | solution.py:661
  22.6 2.0 %collective-permute-start.3 = (f32[2,4,2,8,128]{4,3,2,1,0:T(8,128)S(1)}, f32[2,4,2,8,128]{4,3,2,1,0:T(8,128)S(1)}, u32[]{:S(2)}, u32[]{:S(2)}) collective-permute-start(f32[2,4,2,8,128]{4,3,2,1,0:T(8,128)S(1)} %get-tuple-element.62), channel_id=1, source_target_pairs={{0,4},{4,8},{8,12},{12,16},{16,20},{20,24},{24,28},{1,5},{5,9},{9,... | collective-permute-start | bytes 196616 | tf_op jit(solution)/shard_map/ppermute | solution.py:38
  24.6 1.8 %collective-permute-start.4 = (f32[16,128]{1,0:T(8,128)S(1)}, f32[16,128]{1,0:T(8,128)S(1)}, u32[]{:S(2)}, u32[]{:S(2)}) collective-permute-start(f32[16,128]{1,0:T(8,128)S(1)} %get-tuple-element.63), channel_id=1, source_target_pairs={{0,2},{2,0},{1,3},{3,1},{4,6},{6,4},{5,7},{7,5},{8,10},{10,8},{9,1... | collective-permute-start | bytes 24584 | tf_op jit(solution)/shard_map/ppermute | solution.py:22
  26.4 2.0 %collective-permute-done.4.hyf_ref = f32[16,128]{1,0:T(8,128)S(1)} collective-permute-done((f32[16,128]{1,0:T(8,128)S(1)}, f32[16,128]{1,0:T(8,128)S(1)}, u32[]{:S(2)}, u32[]{:S(2)}) %collective-permute-start.4) | collective-permute-done | bytes 8224 | tf_op jit(solution)/shard_map/ppermute | solution.py:22
  28.4 0.0 collective-permute-done.3.hxf_ref
  28.4 2.3 %add_rims.1 = (f32[2,4,3,8,16,128]{5,4,3,2,1,0:T(8,128)S(1)}, f32[2,4,3,8,16,128]{5,4,3,2,1,0:T(8,128)}) custom-call(s32[6]{0:T(128)S(1)} %copy-done.2, f32[2,4,3,8,16,128]{5,4,3,2,1,0:T(8,128)S(1)} %get-tuple-element.61.left_in, f32[2,4,2,8,128]{4,3,2,1,0:T(8,128)S(1)} %collective-permute-done.3.hxf_ref, ...), custom_call_target="tpu_custom_call", output_to_operand_aliasing={{0}: (1, {})} | custom-call | tf_op jit(solution)/shard_map/add_rims/pallas_call | solution.py:664
  30.6 0.0 all-to-all-done.rows_ref
  30.6 0.7 %sum_rows.1 = f32[2,4,4]{2,1,0:T(4,128)} custom-call(f32[32,4,128]{2,1,0:T(4,128)S(1)} %all-to-all-done.rows_ref), custom_call_target="tpu_custom_call" | custom-call | tf_op jit(solution)/shard_map/sum_rows/pallas_call | solution.py:676
  (7 shorter events, 0.0 us)
Async XLA Ops:
  0.6 8.7 %copy-start.2 = (s32[6]{0:T(128)S(1)}, s32[6]{0:T(128)}, u32[]{:S(2)}) copy-start(s32[6]{0:T(128)} %pml_ref.7) | copy-start | bytes 76
  0.6 8.7 %copy-start.1 = (f32[2,4,4]{2,1,0:T(4,128)S(1)}, f32[2,4,4]{2,1,0:T(4,128)}, u32[]{:S(2)}) copy-start(f32[2,4,4]{2,1,0:T(4,128)} %coeffs_ref.3) | copy-start | bytes 388
  0.7 8.7 %copy-start.5 = (f32[4]{0:T(128)S(1)}, f32[4]{0:T(128)}, u32[]{:S(2)}) copy-start(f32[4]{0:T(128)} %eps_loss_ref.1) | copy-start | bytes 52
  0.7 8.7 %copy-start.4 = (f32[4]{0:T(128)S(1)}, f32[4]{0:T(128)}, u32[]{:S(2)}) copy-start(f32[4]{0:T(128)} %eps_real_ref.1) | copy-start | bytes 52
  0.7 8.7 %copy-start = (s32[8,16,128]{2,1,0:T(8,128)S(1)}, s32[8,16,128]{2,1,0:T(8,128)}, u32[]{:S(2)}) copy-start(s32[8,16,128]{2,1,0:T(8,128)} %material_ref.1) | copy-start | bytes 196612
  2.3 9.9 %collective-permute-start = (f32[2,4,2,8,128]{4,3,2,1,0:T(8,128)S(1)}, f32[2,4,2,8,128]{4,3,2,1,0:T(8,128)S(1)}, u32[]{:S(2)}, u32[]{:S(2)}) collective-permute-start(f32[2,4,2,8,128]{4,3,2,1,0:T(8,128)S(1)} %get-tuple-element.41), channel_id=1, source_target_pairs={{0,29},{1,28},{4,0},{5,1},{8,4},{9,5},{12,8},{13,9},{16,12},{17,13... | collective-permute-start | bytes 196616 | tf_op jit(solution)/shard_map/ppermute | solution.py:32
  7.8 4.4 %collective-permute-start.1 = (f32[16,128]{1,0:T(8,128)S(1)}, f32[16,128]{1,0:T(8,128)S(1)}, u32[]{:S(2)}, u32[]{:S(2)}) collective-permute-start(f32[16,128]{1,0:T(8,128)S(1)} %get-tuple-element.42), channel_id=1, source_target_pairs={{0,2},{2,0},{1,3},{3,1},{4,6},{6,4},{5,7},{7,5},{8,10},{10,8},{9,1... | collective-permute-start | bytes 24584 | tf_op jit(solution)/shard_map/ppermute | solution.py:22
  12.2 1.5 %copy-start.3 = (f32[2,4]{1,0:T(2,128)S(1)}, f32[2,4]{1,0:T(2,128)}, u32[]{:S(2)}) copy-start(f32[2,4]{1,0:T(2,128)} %ritz_ref.3) | copy-start | bytes 100
  13.2 5.0 %collective-permute-start.2 = (f32[2,4,2,16,128]{4,3,2,1,0:T(8,128)S(1)}, f32[2,4,2,16,128]{4,3,2,1,0:T(8,128)S(1)}, u32[]{:S(2)}, u32[]{:S(2)}) collective-permute-start(f32[2,4,2,16,128]{4,3,2,1,0:T(8,128)S(1)} %get-tuple-element.49), channel_id=1, source_target_pairs={{0,1},{1,0},{2,3},{3,2},{4,5},{5,4},{6,7},{7,6},{8,9},{9,8},{10,11... | collective-permute-start | bytes 393224 | tf_op jit(solution)/shard_map/ppermute | solution.py:22
  20.0 10.6 %all-to-all-start = ((f32[32,4,128]{2,1,0:T(4,128)}), f32[32,4,128]{2,1,0:T(4,128)S(1)}, u32[]{:S(2)}, u32[]{:S(2)}) async-start(f32[32,4,128]{2,1,0:T(4,128)} %get-tuple-element.60), calls=%async_computation | async-start | bytes 131072 | tf_op jit(solution)/shard_map/all_to_all | solution.py:661
  22.6 5.8 %collective-permute-start.3 = (f32[2,4,2,8,128]{4,3,2,1,0:T(8,128)S(1)}, f32[2,4,2,8,128]{4,3,2,1,0:T(8,128)S(1)}, u32[]{:S(2)}, u32[]{:S(2)}) collective-permute-start(f32[2,4,2,8,128]{4,3,2,1,0:T(8,128)S(1)} %get-tuple-element.62), channel_id=1, source_target_pairs={{0,4},{4,8},{8,12},{12,16},{16,20},{20,24},{24,28},{1,5},{5,9},{9,... | collective-permute-start | bytes 196616 | tf_op jit(solution)/shard_map/ppermute | solution.py:38
  24.6 3.7 %collective-permute-start.4 = (f32[16,128]{1,0:T(8,128)S(1)}, f32[16,128]{1,0:T(8,128)S(1)}, u32[]{:S(2)}, u32[]{:S(2)}) collective-permute-start(f32[16,128]{1,0:T(8,128)S(1)} %get-tuple-element.63), channel_id=1, source_target_pairs={{0,2},{2,0},{1,3},{3,1},{4,6},{6,4},{5,7},{7,5},{8,10},{10,8},{9,1... | collective-permute-start | bytes 24584 | tf_op jit(solution)/shard_map/ppermute | solution.py:22

commit v23 on v20

--- a/solution.py
+++ b/solution.py
@@ -20,12 +20,6 @@
 def passed_round(value, axis, steps):
     count = lax.axis_size(axis)
     return lax.ppermute(value, axis, [(source, (source + steps) % count) for source in range(count)])
-
-
-def passed_along(value, axis, steps):
-    count = lax.axis_size(axis)
-    leading, last = (max(0, -steps), min(count, count - steps))
-    return lax.ppermute(value, axis, [(source, source + steps) for source in range(leading, last)])
 
 
 def inverse_stretch(places, length, low_width, high_width):
@@ -523,20 +517,13 @@
             gram_ref[part, a:a + 1] = turned[:, :vectors]
 
 
-def rim_kernel(pml_ref, left_in, hxf_ref, hyf_ref, left_ref, residual_hbm, xadd_ref, yadd_ref, sems):
+def rim_y_kernel(pml_ref, left_in, hyf_ref, left_ref, residual_hbm, yadd_ref, sems):
     del left_in
     _, vectors, _, nz, nx, ny = left_ref.shape
     parts = range(2)
     both = 2 * vectors
-    sex = axis_stretch(pml_ref, 1, nx, one_place(1, nx, 0, (nz, ny)))
-    sex = tuple(part * has_neighbour(1, -1) for part in sex)
     sey = axis_stretch(pml_ref, 2, ny, one_place(2, ny, 0, (vectors, nz * nx)))
     sey = tuple(part * has_neighbour(2, -1) for part in sey)
-    for b in range(vectors):
-        for slot in range(2):
-            value = cmul(sex, tuple(hxf_ref[part, b, slot] for part in parts))
-            for part in parts:
-                xadd_ref[part, b, slot] = value[part] if slot else -value[part]
     added = []
     for slot in range(2):
         first = slot * both
@@ -544,11 +531,15 @@
         added += [part if slot else -part for part in value]
     rest = jnp.zeros((ny - 2 * both, nz * nx), jnp.float32)
     yadd_ref[...] = jnp.concatenate(added + [rest], axis=0).T.reshape(nz, nx, ny)
-    rows = lax.broadcasted_iota(jnp.int32, (SUB, ny), 0)
     lanes = lax.broadcasted_iota(jnp.int32, (SUB, ny), 1)
 
     def kept(z):
-        return pltpu.make_async_copy(left_ref.at[:, :, :, z], residual_hbm.at[:, :, :, z], sems.at[z])
+        blocks = [(slice(None), slice(None), 0, z)]
+        blocks += [(slice(None), slice(None), comp, z, slice(SUB, nx)) for comp in (1, 2)]
+        return [
+            pltpu.make_async_copy(left_ref.at[block], residual_hbm.at[block], sems.at[place, z])
+            for place, block in enumerate(blocks)
+        ]
 
     @pl.loop(0, nz)
     def _(z):
@@ -556,27 +547,45 @@
             column = yadd_ref[z, cut]
             for b in range(vectors):
                 for part in parts:
-
-                    def turned(slot, b=b, part=part):
+                    for slot, comp in enumerate((0, 2)):
                         row = packed_row(slot, part, b, vectors)
                         value = pltpu.roll(column, ny - row, 1) if row else column
-                        return jnp.where(lanes == 0, value, 0.0)
-
-                    def row_of(slot, b=b, part=part):
-                        return jnp.where(rows == 0, xadd_ref[part, b, slot, pl.ds(z, 1)], 0.0)
-
-                    ex = left_ref[part, b, 0, z, cut] + turned(0)
-                    ez = left_ref[part, b, 2, z, cut] + turned(1)
-                    if cut.start == 0:
-                        left_ref[part, b, 1, z, cut] = left_ref[part, b, 1, z, cut] + row_of(1)
-                        ez = ez + row_of(0)
-                    left_ref[part, b, 0, z, cut] = ex
-                    left_ref[part, b, 2, z, cut] = ez
-        kept(z).start()
+                        value = jnp.where(lanes == 0, value, 0.0)
+                        left_ref[part, b, comp, z, cut] = left_ref[part, b, comp, z, cut] + value
+        for copy in kept(z):
+            copy.start()
 
     @pl.loop(0, nz)
     def _(z):
-        kept(z).wait()
+        for copy in kept(z):
+            copy.wait()
+
+
+def rim_x_kernel(pml_ref, left_in, residual_in, hxf_ref, left_ref, residual_hbm, xadd_ref, sems):
+    del left_in, residual_in
+    _, vectors, _, nz, nx, ny = left_ref.shape
+    parts = range(2)
+    sex = axis_stretch(pml_ref, 1, nx, one_place(1, nx, 0, (nz, ny)))
+    sex = tuple(part * has_neighbour(1, -1) for part in sex)
+    for b in range(vectors):
+        for slot in range(2):
+            value = cmul(sex, tuple(hxf_ref[part, b, slot] for part in parts))
+            for part in parts:
+                xadd_ref[part, b, slot] = value[part] if slot else -value[part]
+    rows = lax.broadcasted_iota(jnp.int32, (SUB, ny), 0)
+    first = slice(0, SUB)
+    copies = []
+    for z in range(nz):
+        for b in range(vectors):
+            for part in parts:
+                for slot, comp in ((1, 1), (0, 2)):
+                    value = jnp.where(rows == 0, xadd_ref[part, b, slot, z:z + 1], 0.0)
+                    left_ref[part, b, comp, z, first] = left_ref[part, b, comp, z, first] + value
+        block = (slice(None), slice(None), slice(1, 3), z, first)
+        copies.append(pltpu.make_async_copy(left_ref.at[block], residual_hbm.at[block], sems.at[z]))
+        copies[-1].start()
+    for copy in copies:
+        copy.wait()
 
 
 def body(fields, material, pml_width, eps_real, eps_loss, coeffs, ritz):
@@ -649,19 +658,31 @@
     )(pml_width, ritz, basis, eps, table, sz, h, zf, xf, yt, hxf, packed, left, acc, before)
     gram, hxf, hyf = lax.optimization_barrier((gram, hxf, hyf))
     rows = lax.all_to_all(gram, ("gx", "gy", "gz"), 0, 0)
-    from_x = passed_along(hxf, "gx", 1)
+    from_x = passed_round(hxf, "gx", 1)
     from_y = passed_round(hyf, "gy", 1)
-    _, residual = pl.pallas_call(
-        rim_kernel,
+    free = pl.CostEstimate(flops=0, bytes_accessed=0, transcendentals=0)
+    left, residual = pl.pallas_call(
+        rim_y_kernel,
         out_shape=(whole, whole),
-        in_specs=[SMEM] + [VMEM] * 3,
+        in_specs=[SMEM] + [VMEM] * 2,
         out_specs=(VMEM, HBM),
-        scratch_shapes=[scratch(*xf_shape), scratch(nz, nx, ny), pltpu.SemaphoreType.DMA((nz,))],
+        scratch_shapes=[scratch(nz, nx, ny), pltpu.SemaphoreType.DMA((3, nz))],
         input_output_aliases={1: 0},
         compiler_params=params,
-        cost_estimate=pl.CostEstimate(flops=0, bytes_accessed=0, transcendentals=0),
-        name="add_rims",
-    )(pml_width, left, from_x, from_y)
+        cost_estimate=free,
+        name="add_y_rims",
+    )(pml_width, left, from_y)
+    _, residual = pl.pallas_call(
+        rim_x_kernel,
+        out_shape=(whole, whole),
+        in_specs=[SMEM, VMEM, HBM, VMEM],
+        out_specs=(VMEM, HBM),
+        scratch_shapes=[scratch(*xf_shape), pltpu.SemaphoreType.DMA((nz,))],
+        input_output_aliases={1: 0, 2: 1},
+        compiler_params=params,
+        cost_estimate=free,
+        name="add_x_rims",
+    )(pml_width, left, residual, from_x)
     rows, residual = lax.optimization_barrier((rows, residual))
     gram = pl.pallas_call(
         gather_kernel,

time: 31.6 us -> 31.2 us (0.987)
  starting transfers between devices: 14.7 us -> 12.7 us
  Pallas kernels: 13.2 us -> 14.7 us
    ppermute x1 -> x0, starting transfers between devices: 2.16 us -> none  [passed_along(): lax.ppermute(value, axis, [(source, source + steps) for source in range(l...]
    pallas_call x1 -> x2, Pallas kernels: 2.25 us -> 3.8 us  [the longest x1 2.36 us: body(): pl.pallas_call(rim_y_kernel, out_shape=(whole, whole), in_specs=[SMEM] +...]
    ppermute x4 -> x5, starting transfers between devices: 9.35 us -> 9.59 us  [passed_round(): lax.ppermute(value, axis, [(source, (source + steps) % count) for source...]
    ppermute x4 -> x5, waiting for transfers between devices: 2.46 us -> 2.61 us  [passed_round(): lax.ppermute(value, axis, [(source, (source + steps) % count) for source...]
  transfers between devices with their start and end apart: 6 -> 6, of which waited for: 2 -> 3; matrix products, arithmetic and copies ran while one was open for 0% -> 0% of each run, Pallas kernels for 26% -> 31%
where the time goes in v23:
time: 31.2 us; the launch traced here: 30.9 us
  Pallas kernels  14.7 us (47%)
  starting transfers between devices  12.7 us (41%)
  waiting for transfers between devices  2.61 us (8%)
  between operations  0.77 us (2%)
    ppermute x5, starting transfers between devices, passed_round(): lax.ppermute(value, axis, [(source, (source + steps) % count) for source...  9.59 us
    all_to_all x1, starting transfers between devices, body(): rows = lax.all_to_all(gram, ('gx', 'gy', 'gz'), 0, 0)  3.15 us
    pallas_call x1, Pallas kernels, body(): pl.pallas_call(inner_kernel, out_shape=(whole, planes, whole, f32(vectors...  2.99 us
    pallas_call x1, Pallas kernels, body(): pl.pallas_call(prepare_kernel, out_shape=(whole, f32(2, nz, nx, ny), whol...  2.87 us
    ppermute x5, waiting for transfers between devices, passed_round(): lax.ppermute(value, axis, [(source, (source + steps) % count) for source...  2.61 us
    pallas_call x1, Pallas kernels, body(): pl.pallas_call(rim_y_kernel, out_shape=(whole, whole), in_specs=[SMEM] +...  2.36 us
    pallas_call x1, Pallas kernels, body(): pl.pallas_call(outer_kernel, out_shape=(whole, f32(devices, 4, ny), whole...  1.85 us
    pallas_call x1, Pallas kernels, body(): pl.pallas_call(face_kernel, out_shape=(whole, f32(*xf_shape), f32(*yf_sha...  1.64 us
  transfers between devices with their start and end apart: 6, of which 3 were waited for; matrix products, arithmetic and copies ran while one was open for 0% of the time, Pallas kernels for 31%

profile of v23, /device:TPU:0, one launch (start us, length us, event | category | flops | bytes accessed | tf_op | source)
XLA Modules:
  0.0 30.9 jit_solution(3913323564231632284)
XLA Ops:
  0.6 0.0 copy-start.2
  0.7 1.6 %take_faces.1 = (f32[2,4,3,8,16,128]{5,4,3,2,1,0:T(8,128)S(1)}, f32[2,4,2,8,128]{4,3,2,1,0:T(8,128)S(1)}, f32[16,128]{1,0:T(8,128)S(1)}) custom-call(f32[2,4,3,8,16,128]{5,4,3,2,1,0:T(8,128)} %fields_hbm.1), custom_call_target="tpu_custom_call" | custom-call | tf_op jit(solution)/shard_map/take_faces/pallas_call | solution.py:600
  2.3 4.5 %collective-permute-start = (f32[2,4,2,8,128]{4,3,2,1,0:T(8,128)S(1)}, f32[2,4,2,8,128]{4,3,2,1,0:T(8,128)S(1)}, u32[]{:S(2)}, u32[]{:S(2)}) collective-permute-start(f32[2,4,2,8,128]{4,3,2,1,0:T(8,128)S(1)} %get-tuple-element.43), channel_id=1, source_target_pairs={{0,28},{4,0},{8,4},{12,8},{16,12},{20,16},{24,20},{28,24},{1,29},{... | collective-permute-start | bytes 196616 | tf_op jit(solution)/shard_map/ppermute | solution.py:22
  6.9 1.5 %collective-permute-start.1 = (f32[16,128]{1,0:T(8,128)S(1)}, f32[16,128]{1,0:T(8,128)S(1)}, u32[]{:S(2)}, u32[]{:S(2)}) collective-permute-start(f32[16,128]{1,0:T(8,128)S(1)} %get-tuple-element.44), channel_id=1, source_target_pairs={{0,2},{2,0},{1,3},{3,1},{4,6},{6,4},{5,7},{7,5},{8,10},{10,8},{9,1... | collective-permute-start | bytes 24584 | tf_op jit(solution)/shard_map/ppermute | solution.py:22
  8.4 0.0 copy-done.4
  8.4 0.0 copy-done
  8.4 2.9 %prepare.1 = (f32[2,4,3,8,16,128]{5,4,3,2,1,0:T(8,128)S(1)}, f32[2,8,16,128]{3,2,1,0:T(8,128)S(1)}, f32[2,4,3,8,16,128]{5,4,3,2,1,0:T(8,128)S(1)}, f32[8,16,128]...) custom-call(s32[6]{0:T(128)S(1)} %copy-done.2, f32[4]{0:T(128)S(1)} %copy-done.4, ...), custom_call_target="tpu_custom_call" | custom-call | flops 13107200 | bytes 6291456 | tf_op jit(solution)/shard_map/prepare/pallas_call | solution.py:618
  11.3 0.0 collective-permute-done.1.raw_yf_ref
  11.3 0.0 collective-permute-done.raw_xf_ref
  11.3 0.0 copy-start.3
  11.3 0.9 %slab_face.1 = (f32[2,4,3,8,16,128]{5,4,3,2,1,0:T(8,128)S(1)}, f32[2,4,2,8,128]{4,3,2,1,0:T(8,128)S(1)}, f32[16,128]{1,0:T(8,128)S(1)}, f32[2,4,2,8,128]{4,3,2,1...) custom-call(s32[6]{0:T(128)S(1)} %copy-done.2, ...), custom_call_target="tpu_custom_call", output_to_operand_aliasing={{0}: (3, {})} | custom-call | tf_op jit(solution)/shard_map/slab_face/pallas_call | solution.py:627
  12.2 1.6 %collective-permute-start.2 = (f32[2,4,2,16,128]{4,3,2,1,0:T(8,128)S(1)}, f32[2,4,2,16,128]{4,3,2,1,0:T(8,128)S(1)}, u32[]{:S(2)}, u32[]{:S(2)}) collective-permute-start(f32[2,4,2,16,128]{4,3,2,1,0:T(8,128)S(1)} %get-tuple-element.51), channel_id=1, source_target_pairs={{0,1},{1,0},{2,3},{3,2},{4,5},{5,4},{6,7},{7,6},{8,9},{9,8},{10,11... | collective-permute-start | bytes 393224 | tf_op jit(solution)/shard_map/ppermute | solution.py:22
  13.8 3.0 %apply_inner.1 = (f32[2,4,3,8,16,128]{5,4,3,2,1,0:T(8,128)S(1)}, f32[8,16,128]{2,1,0:T(8,128)S(1)}, f32[2,4,3,8,16,128]{5,4,3,2,1,0:T(8,128)S(1)}, f32[4,8,8,128...) custom-call(f32[2,4]{1,0:T(2,128)S(1)} %copy-done.3, ...), custom_call_target="tpu_custom_call", output_to_operand_aliasing={{0}: (5, {}), {1}: (6, {})} | custom-call | flops 13107200 | bytes 3145728 | tf_op jit(solution)/shard_map/apply_inner/pallas_call | solution.py:637
  16.8 0.5 %collective-permute-done.2.zf_ref = f32[2,4,2,16,128]{4,3,2,1,0:T(8,128)S(1)} collective-permute-done((f32[2,4,2,16,128]{4,3,2,1,0:T(8,128)S(1)}, f32[2,4,2,16,128]{4,3,2,1,0:T(8,128)S(1)}, u32[]{:S(2)}, u32[]{:S(2)}) %collective-permute-start.2) | collective-permute-done | bytes 131104 | tf_op jit(solution)/shard_map/ppermute | solution.py:22
  17.3 1.8 %apply_outer.1 = (f32[2,4,3,8,16,128]{5,4,3,2,1,0:T(8,128)S(1)}, f32[32,4,128]{2,1,0:T(4,128)}, f32[2,4,3,8,16,128]{5,4,3,2,1,0:T(8,128)S(1)}, f32[2,4,2,8,128]{4,3,2,1,0:T(8,128)S(1)}, f32[16,128]{1,0:T(8,128)S(1)}) custom-call(s32[6]{0:T(128)S(1)} %copy-done.2, f32[2,4]{1,0:T(2,128)S(1)} %copy-done.3, ...), custom_call_target="tpu_custom_call", output_to_operand_aliasing={{0}: (12, {}), {2}: (6, {}), {3}: (10, {})} | custom-call | flops 4915200 | bytes 1572864 | tf_op jit(solution)/shard_map/apply_outer/pallas_call | solution.py:649
  19.1 3.1 %all-to-all-start = ((f32[32,4,128]{2,1,0:T(4,128)}), f32[32,4,128]{2,1,0:T(4,128)S(1)}, u32[]{:S(2)}, u32[]{:S(2)}) async-start(f32[32,4,128]{2,1,0:T(4,128)} %get-tuple-element.62), calls=%async_computation | async-start | bytes 131072 | tf_op jit(solution)/shard_map/all_to_all | solution.py:660
  22.3 0.3 collective-permute-start.4
  22.6 1.7 %collective-permute-start.3 = (f32[16,128]{1,0:T(8,128)S(1)}, f32[16,128]{1,0:T(8,128)S(1)}, u32[]{:S(2)}, u32[]{:S(2)}) collective-permute-start(f32[16,128]{1,0:T(8,128)S(1)} %get-tuple-element.64), channel_id=1, source_target_pairs={{0,2},{2,0},{1,3},{3,1},{4,6},{6,4},{5,7},{7,5},{8,10},{10,8},{9,1... | collective-permute-start | bytes 24584 | tf_op jit(solution)/shard_map/ppermute | solution.py:22
  24.2 2.0 %collective-permute-done.3.hyf_ref = f32[16,128]{1,0:T(8,128)S(1)} collective-permute-done((f32[16,128]{1,0:T(8,128)S(1)}, f32[16,128]{1,0:T(8,128)S(1)}, u32[]{:S(2)}, u32[]{:S(2)}) %collective-permute-start.3) | collective-permute-done | bytes 8224 | tf_op jit(solution)/shard_map/ppermute | solution.py:22
  26.2 2.4 %add_y_rims.1 = (f32[2,4,3,8,16,128]{5,4,3,2,1,0:T(8,128)S(1)}, f32[2,4,3,8,16,128]{5,4,3,2,1,0:T(8,128)}) custom-call(s32[6]{0:T(128)S(1)} %copy-done.2, f32[2,4,3,8,16,128]{5,4,3,2,1,0:T(8,128)S(1)} %get-tuple-element.63.left_in, f32[16,128]{1,0:T(8,128)S(1)} %collective-permute-done.3.hyf_ref), custom_call_target="tpu_custom_call", output_to_operand_aliasing={{0}: (1, {})} | custom-call | tf_op jit(solution)/shard_map/add_y_rims/pallas_call | solution.py:664
  28.6 0.1 collective-permute-done.4.hxf_ref
  28.7 1.4 %add_x_rims.1 = (f32[2,4,3,8,16,128]{5,4,3,2,1,0:T(8,128)S(1)}, f32[2,4,3,8,16,128]{5,4,3,2,1,0:T(8,128)}) custom-call(s32[6]{0:T(128)S(1)} %copy-done.2, f32[2,4,3,8,16,128]{5,4,3,2,1,0:T(8,128)S(1)} %get-tuple-element.65.left_in, f32[2,4,3,8,16,128]{5,4,3,2,1,0:T(8,128)} %get-tuple-element.66.residual_in, ...), custom_call_target="tpu_custom_call", output_to_operand_aliasing={{0}: (1, {}), {1}: (2, {})} | custom-call | tf_op jit(solution)/shard_map/add_x_rims/pallas_call | solution.py:675
  30.2 0.0 all-to-all-done.rows_ref
  30.2 0.7 %sum_rows.1 = f32[2,4,4]{2,1,0:T(4,128)} custom-call(f32[32,4,128]{2,1,0:T(4,128)S(1)} %all-to-all-done.rows_ref), custom_call_target="tpu_custom_call" | custom-call | tf_op jit(solution)/shard_map/sum_rows/pallas_call | solution.py:687
  (8 shorter events, 0.0 us)
Async XLA Ops:
  0.6 7.8 %copy-start.2 = (s32[6]{0:T(128)S(1)}, s32[6]{0:T(128)}, u32[]{:S(2)}) copy-start(s32[6]{0:T(128)} %pml_ref.9) | copy-start | bytes 76
  0.6 7.8 %copy-start.1 = (f32[2,4,4]{2,1,0:T(4,128)S(1)}, f32[2,4,4]{2,1,0:T(4,128)}, u32[]{:S(2)}) copy-start(f32[2,4,4]{2,1,0:T(4,128)} %coeffs_ref.3) | copy-start | bytes 388
  0.7 7.8 %copy-start.5 = (f32[4]{0:T(128)S(1)}, f32[4]{0:T(128)}, u32[]{:S(2)}) copy-start(f32[4]{0:T(128)} %eps_loss_ref.1) | copy-start | bytes 52
  0.7 7.7 %copy-start.4 = (f32[4]{0:T(128)S(1)}, f32[4]{0:T(128)}, u32[]{:S(2)}) copy-start(f32[4]{0:T(128)} %eps_real_ref.1) | copy-start | bytes 52
  0.7 7.7 %copy-start = (s32[8,16,128]{2,1,0:T(8,128)S(1)}, s32[8,16,128]{2,1,0:T(8,128)}, u32[]{:S(2)}) copy-start(s32[8,16,128]{2,1,0:T(8,128)} %material_ref.1) | copy-start | bytes 196612
  2.3 9.0 %collective-permute-start = (f32[2,4,2,8,128]{4,3,2,1,0:T(8,128)S(1)}, f32[2,4,2,8,128]{4,3,2,1,0:T(8,128)S(1)}, u32[]{:S(2)}, u32[]{:S(2)}) collective-permute-start(f32[2,4,2,8,128]{4,3,2,1,0:T(8,128)S(1)} %get-tuple-element.43), channel_id=1, source_target_pairs={{0,28},{4,0},{8,4},{12,8},{16,12},{20,16},{24,20},{28,24},{1,29},{... | collective-permute-start | bytes 196616 | tf_op jit(solution)/shard_map/ppermute | solution.py:22
  6.9 4.4 %collective-permute-start.1 = (f32[16,128]{1,0:T(8,128)S(1)}, f32[16,128]{1,0:T(8,128)S(1)}, u32[]{:S(2)}, u32[]{:S(2)}) collective-permute-start(f32[16,128]{1,0:T(8,128)S(1)} %get-tuple-element.44), channel_id=1, source_target_pairs={{0,2},{2,0},{1,3},{3,1},{4,6},{6,4},{5,7},{7,5},{8,10},{10,8},{9,1... | collective-permute-start | bytes 24584 | tf_op jit(solution)/shard_map/ppermute | solution.py:22
  11.3 2.5 %copy-start.3 = (f32[2,4]{1,0:T(2,128)S(1)}, f32[2,4]{1,0:T(2,128)}, u32[]{:S(2)}) copy-start(f32[2,4]{1,0:T(2,128)} %ritz_ref.3) | copy-start | bytes 100
  12.2 5.0 %collective-permute-start.2 = (f32[2,4,2,16,128]{4,3,2,1,0:T(8,128)S(1)}, f32[2,4,2,16,128]{4,3,2,1,0:T(8,128)S(1)}, u32[]{:S(2)}, u32[]{:S(2)}) collective-permute-start(f32[2,4,2,16,128]{4,3,2,1,0:T(8,128)S(1)} %get-tuple-element.51), channel_id=1, source_target_pairs={{0,1},{1,0},{2,3},{3,2},{4,5},{5,4},{6,7},{7,6},{8,9},{9,8},{10,11... | collective-permute-start | bytes 393224 | tf_op jit(solution)/shard_map/ppermute | solution.py:22
  19.1 11.1 %all-to-all-start = ((f32[32,4,128]{2,1,0:T(4,128)}), f32[32,4,128]{2,1,0:T(4,128)S(1)}, u32[]{:S(2)}, u32[]{:S(2)}) async-start(f32[32,4,128]{2,1,0:T(4,128)} %get-tuple-element.62), calls=%async_computation | async-start | bytes 131072 | tf_op jit(solution)/shard_map/all_to_all | solution.py:660
  22.3 6.5 %collective-permute-start.4 = (f32[2,4,2,8,128]{4,3,2,1,0:T(8,128)S(1)}, f32[2,4,2,8,128]{4,3,2,1,0:T(8,128)S(1)}, u32[]{:S(2)}, u32[]{:S(2)}) collective-permute-start(f32[2,4,2,8,128]{4,3,2,1,0:T(8,128)S(1)} %get-tuple-element.67), channel_id=1, source_target_pairs={{0,4},{4,8},{8,12},{12,16},{16,20},{20,24},{24,28},{28,0},{1,5},{5... | collective-permute-start | bytes 196616 | tf_op jit(solution)/shard_map/ppermute | solution.py:22
  22.6 3.7 %collective-permute-start.3 = (f32[16,128]{1,0:T(8,128)S(1)}, f32[16,128]{1,0:T(8,128)S(1)}, u32[]{:S(2)}, u32[]{:S(2)}) collective-permute-start(f32[16,128]{1,0:T(8,128)S(1)} %get-tuple-element.64), channel_id=1, source_target_pairs={{0,2},{2,0},{1,3},{3,1},{4,6},{6,4},{5,7},{7,5},{8,10},{10,8},{9,1... | collective-permute-start | bytes 24584 | tf_op jit(solution)/shard_map/ppermute | solution.py:22

commit v24 on v23

--- a/solution.py
+++ b/solution.py
@@ -119,6 +119,37 @@
 SHX, SEX, SHY, SEY = range(0, 8, 2)
 
 
+class Splats:
+    def __init__(self, ref, first, shape):
+        self.ref, self.first, self.shape = ref, first, shape
+
+    def __getitem__(self, place):
+        row = 0
+        for index, size in zip(place, self.shape):
+            row = row * size + index
+        return self.ref[self.first + row:self.first + row + 1]
+
+
+ENDS = ("under", "next_x", "next_y", "first_x", "first_y", "last_x", "last_y")
+
+
+def end_value(splat_ref, name, width=None):
+    row = 2 * ENDS.index(name)
+    return tuple(splat_ref[row + part:row + part + 1, :width] for part in range(2))
+
+
+def ritz_rows(splat_ref, vectors):
+    return Splats(splat_ref, 2 * len(ENDS), (2, vectors))
+
+
+def coeff_rows(splat_ref, vectors):
+    return Splats(splat_ref, 2 * len(ENDS) + 2 * vectors, (2, vectors, vectors))
+
+
+def splat_count(vectors):
+    return -(-(2 * len(ENDS) + 2 * vectors * (vectors + 1)) // SUB) * SUB
+
+
 def field_of(ref, b, comp, z, cut):
     return tuple(ref[part, b, comp, z, cut] for part in range(2))
 
@@ -128,8 +159,8 @@
 
 
 def prepare_kernel(
-    pml_ref, eps_real_ref, eps_loss_ref, coeffs_ref, fields_ref, material_ref,
-    basis_ref, eps_ref, h_ref, packed_ref, table_ref, sz_ref,
+    pml_ref, eps_real_ref, eps_loss_ref, coeffs_ref, ritz_ref, fields_ref, material_ref,
+    basis_ref, eps_ref, h_ref, packed_ref, table_ref, sz_ref, splat_ref,
 ):
     _, vectors, _, nz, nx, ny = fields_ref.shape
     plane = (nx, ny)
@@ -140,6 +171,29 @@
         values = axis_stretch(pml_ref, direction, count, local_places(direction, count, plane, dim) + half)
         for part in parts:
             table_ref[slot + part] = values[part]
+    line = (1, ny)
+    ends = {
+        "under": (0, nz, -1, 0.5, 1.0),
+        "next_x": (1, nx, nx, 0.0, 1.0),
+        "next_y": (2, ny, ny, 0.0, 1.0),
+        "first_x": (1, nx, 0, 0.0, has_neighbour(1, -1)),
+        "first_y": (2, ny, 0, 0.0, has_neighbour(2, -1)),
+        "last_x": (1, nx, nx - 1, 0.5, 1.0),
+        "last_y": (2, ny, ny - 1, 0.5, 1.0),
+    }
+    lines = []
+    for name in ENDS:
+        direction, count, offset, half, factor = ends[name]
+        values = axis_stretch(pml_ref, direction, count, one_place(direction, count, offset, line) + half)
+        lines += [value * factor for value in values]
+    lines += [jnp.full(line, ritz_ref[part, b], jnp.float32) for part in parts for b in range(vectors)]
+    lines += [
+        jnp.full(line, coeffs_ref[part, a, b], jnp.float32)
+        for part in parts for a in range(vectors) for b in range(vectors)
+    ]
+    for row, value in enumerate(lines):
+        splat_ref[row:row + 1] = value
+    splat_ref[len(lines):] = jnp.zeros((splat_ref.shape[0] - len(lines), ny), jnp.float32)
     for slot, half in ((0, 0.0), (2, 0.5)):
         values = axis_stretch(pml_ref, 0, nz, local_places(0, nz, (nz, ny), 0) + half)
         for part in parts:
@@ -240,7 +294,7 @@
         for a in range(vectors):
             column = jnp.zeros(shape, jnp.float32)
             for b in range(vectors):
-                first, second = coeffs_ref[0, a, b] * inside, coeffs_ref[1, a, b] * inside
+                first, second = (coeffs_ref[0, a, b] * inside)[:, :shape[1]], (coeffs_ref[1, a, b] * inside)[:, :shape[1]]
                 if part:
                     first, second = -second, first
                 column = jnp.where(which == b, first, column)
@@ -278,7 +332,7 @@
 
 
 def slab_kernel(
-    pml_ref, coeffs_ref, basis_ref, h_in, raw_xf_ref, raw_yf_ref,
+    splat_ref, basis_ref, h_in, raw_xf_ref, raw_yf_ref,
     h_ref, xf_ref, yt_ref, xadd_ref, yadd_ref, zf_ref,
 ):
     del h_in
@@ -286,10 +340,11 @@
     parts = range(2)
     cells = nz * nx
     both = 2 * vectors
-    turn_face(coeffs_ref, 1, raw_xf_ref, xf_ref)
-    turn_column(coeffs_ref, raw_yf_ref, yt_ref)
-    shx = axis_stretch(pml_ref, 1, nx, one_place(1, nx, nx - 1, (1, ny)) + 0.5)
-    shy = axis_stretch(pml_ref, 2, ny, one_place(2, ny, ny - 1, (1, cells)) + 0.5)
+    coeffs = coeff_rows(splat_ref, vectors)
+    turn_face(coeffs, 1, raw_xf_ref, xf_ref)
+    turn_column(coeffs, raw_yf_ref, yt_ref)
+    shx = end_value(splat_ref, "last_x")
+    shy = end_value(splat_ref, "last_y", cells)
     for b in range(vectors):
         for slot in range(2):
             value = cmul(shx, tuple(xf_ref[part, b, 1 - slot] for part in parts))
@@ -369,7 +424,7 @@
 
 
 def inner_kernel(
-    ritz_ref, basis_ref, eps_ref, table_ref, sz_ref, h_in, packed_in, xadd_ref, yadd_ref,
+    splat_ref, basis_ref, eps_ref, table_ref, sz_ref, h_in, packed_in, xadd_ref, yadd_ref,
     h_ref, packed_ref, left_ref, acc_ref, before_ref, hxf_ref, basis_hbm, sem,
 ):
     del h_in, packed_in
@@ -401,7 +456,7 @@
             ]
             sums = [(acc_ref[b, a], acc_ref[b, vectors + a]) for a in range(vectors)]
             before, sums = plane_step(
-                b, z, before, sums, ritz_ref, basis_ref, eps_ref, table_ref, sz_ref, h_ref, left_ref, (xadd_ref, yadd_ref)
+                b, z, before, sums, ritz_rows(splat_ref, vectors), basis_ref, eps_ref, table_ref, sz_ref, h_ref, left_ref, (xadd_ref, yadd_ref)
             )
             for part in range(2):
                 for a in range(vectors):
@@ -437,7 +492,7 @@
 
 
 def outer_kernel(
-    pml_ref, ritz_ref, basis_ref, eps_ref, table_ref, sz_ref, h_in, zf_ref, xf_ref, yt_ref, hxf_in, packed_in,
+    splat_ref, basis_ref, eps_ref, table_ref, sz_ref, h_in, zf_ref, xf_ref, yt_ref, hxf_in, packed_in,
     left_in, acc_ref, before_ref, left_ref, gram_ref, h_ref, hxf_ref, hyf_ref,
 ):
     del left_in, h_in, hxf_in
@@ -445,10 +500,10 @@
     _, vectors, _, nz, nx, ny = basis_ref.shape
     parts = range(2)
     cuts = tiles_of(nx)
-    under = axis_stretch(pml_ref, 0, nz, one_place(0, nz, -1, (1, ny)) + 0.5)
+    under = end_value(splat_ref, "under")
     sez = tuple(sz_ref[part, 0:1] * has_neighbour(0, -1) for part in parts)
-    sx_next = axis_stretch(pml_ref, 1, nx, one_place(1, nx, nx, (1, ny)))
-    sy_next = axis_stretch(pml_ref, 2, ny, one_place(2, ny, ny, (1, nz * nx)))
+    sx_next = end_value(splat_ref, "next_x")
+    sy_next = end_value(splat_ref, "next_y", nz * nx)
     both = 2 * vectors
     ends = [
         cmul(sy_next, (yt_ref[slot * both:slot * both + vectors], yt_ref[slot * both + vectors:(slot + 1) * both]))
@@ -464,7 +519,7 @@
         before = [tuple(tile_of(before_ref, slot, cut) for slot in range(2)) for cut in cuts]
         sums = [(acc_ref[b, a], acc_ref[b, vectors + a]) for a in range(vectors)]
         _, sums = plane_step(
-            b, nz - 1, before, sums, ritz_ref, basis_ref, eps_ref, table_ref, sz_ref, h_ref, left_ref
+            b, nz - 1, before, sums, ritz_rows(splat_ref, vectors), basis_ref, eps_ref, table_ref, sz_ref, h_ref, left_ref
         )
         for cut in cuts:
             ex, ey = (field_of(basis_ref, b, comp, 0, cut) for comp in range(2))
@@ -517,13 +572,12 @@
             gram_ref[part, a:a + 1] = turned[:, :vectors]
 
 
-def rim_y_kernel(pml_ref, left_in, hyf_ref, left_ref, residual_hbm, yadd_ref, sems):
+def rim_y_kernel(splat_ref, left_in, hyf_ref, left_ref, residual_hbm, yadd_ref, sems):
     del left_in
     _, vectors, _, nz, nx, ny = left_ref.shape
     parts = range(2)
     both = 2 * vectors
-    sey = axis_stretch(pml_ref, 2, ny, one_place(2, ny, 0, (vectors, nz * nx)))
-    sey = tuple(part * has_neighbour(2, -1) for part in sey)
+    sey = end_value(splat_ref, "first_y", nz * nx)
     added = []
     for slot in range(2):
         first = slot * both
@@ -561,12 +615,11 @@
             copy.wait()
 
 
-def rim_x_kernel(pml_ref, left_in, residual_in, hxf_ref, left_ref, residual_hbm, xadd_ref, sems):
+def rim_x_kernel(splat_ref, left_in, residual_in, hxf_ref, left_ref, residual_hbm, xadd_ref, sems):
     del left_in, residual_in
     _, vectors, _, nz, nx, ny = left_ref.shape
     parts = range(2)
-    sex = axis_stretch(pml_ref, 1, nx, one_place(1, nx, 0, (nz, ny)))
-    sex = tuple(part * has_neighbour(1, -1) for part in sex)
+    sex = end_value(splat_ref, "first_x")
     for b in range(vectors):
         for slot in range(2):
             value = cmul(sex, tuple(hxf_ref[part, b, slot] for part in parts))
@@ -615,47 +668,47 @@
 
     planes = f32(nz, nx, ny)
     face = f32(*xf_shape)
-    basis, eps, h, packed, table, sz = pl.pallas_call(
+    basis, eps, h, packed, table, sz, splats = pl.pallas_call(
         prepare_kernel,
-        out_shape=(whole, f32(2, nz, nx, ny), whole, planes, f32(8, nx, ny), f32(4, nz, ny)),
-        in_specs=[SMEM] * 4 + [VMEM] * 2,
-        out_specs=(VMEM,) * 6,
+        out_shape=(whole, f32(2, nz, nx, ny), whole, planes, f32(8, nx, ny), f32(4, nz, ny), f32(splat_count(vectors), ny)),
+        in_specs=[SMEM] * 5 + [VMEM] * 2,
+        out_specs=(VMEM,) * 7,
         compiler_params=params,
         cost_estimate=cost(800, 4),
         name="prepare",
-    )(pml_width, eps_real, eps_loss, coeffs, near, material)
+    )(pml_width, eps_real, eps_loss, coeffs, ritz, near, material)
     h, xf, yt, xadd, yadd, zf = pl.pallas_call(
         slab_kernel,
         out_shape=(whole, face, f32(*yf_shape), face, planes, f32(*zf_shape)),
-        in_specs=[SMEM] * 2 + [VMEM] * 4,
+        in_specs=[VMEM] * 5,
         out_specs=(VMEM,) * 6,
-        input_output_aliases={3: 0},
+        input_output_aliases={2: 0},
         compiler_params=params,
         name="slab_face",
-    )(pml_width, coeffs, basis, h, xf, yf)
+    )(splats, basis, h, xf, yf)
     zf = passed_round(zf, "gz", 1)
     h, packed, left, acc, before, hxf, basis_new = pl.pallas_call(
         inner_kernel,
         out_shape=(whole, planes, whole, f32(vectors, 2 * vectors, SUB, ny), f32(*zf_shape), face, whole),
-        in_specs=[SMEM] + [VMEM] * 8,
+        in_specs=[VMEM] * 9,
         out_specs=(VMEM,) * 6 + (HBM,),
         scratch_shapes=[pltpu.SemaphoreType.DMA],
         input_output_aliases={5: 0, 6: 1},
         compiler_params=params,
         cost_estimate=cost(800, 2),
         name="apply_inner",
-    )(ritz, basis, eps, table, sz, h, packed, xadd, yadd)
+    )(splats, basis, eps, table, sz, h, packed, xadd, yadd)
     devices = lax.axis_size("gx") * lax.axis_size("gy") * lax.axis_size("gz")
     left, gram, _, hxf, hyf = pl.pallas_call(
         outer_kernel,
         out_shape=(whole, f32(devices, 4, ny), whole, face, f32(*yf_shape)),
-        in_specs=[SMEM] * 2 + [VMEM] * 13,
+        in_specs=[VMEM] * 14,
         out_specs=(VMEM,) * 5,
-        input_output_aliases={12: 0, 6: 2, 10: 3},
+        input_output_aliases={11: 0, 5: 2, 9: 3},
         compiler_params=params,
         cost_estimate=cost(300, 1),
         name="apply_outer",
-    )(pml_width, ritz, basis, eps, table, sz, h, zf, xf, yt, hxf, packed, left, acc, before)
+    )(splats, basis, eps, table, sz, h, zf, xf, yt, hxf, packed, left, acc, before)
     gram, hxf, hyf = lax.optimization_barrier((gram, hxf, hyf))
     rows = lax.all_to_all(gram, ("gx", "gy", "gz"), 0, 0)
     from_x = passed_round(hxf, "gx", 1)
@@ -664,25 +717,25 @@
     left, residual = pl.pallas_call(
         rim_y_kernel,
         out_shape=(whole, whole),
-        in_specs=[SMEM] + [VMEM] * 2,
+        in_specs=[VMEM] * 3,
         out_specs=(VMEM, HBM),
         scratch_shapes=[scratch(nz, nx, ny), pltpu.SemaphoreType.DMA((3, nz))],
         input_output_aliases={1: 0},
         compiler_params=params,
         cost_estimate=free,
         name="add_y_rims",
-    )(pml_width, left, from_y)
+    )(splats, left, from_y)
     _, residual = pl.pallas_call(
         rim_x_kernel,
         out_shape=(whole, whole),
-        in_specs=[SMEM, VMEM, HBM, VMEM],
+        in_specs=[VMEM, VMEM, HBM, VMEM],
         out_specs=(VMEM, HBM),
         scratch_shapes=[scratch(*xf_shape), pltpu.SemaphoreType.DMA((nz,))],
         input_output_aliases={1: 0, 2: 1},
         compiler_params=params,
         cost_estimate=free,
         name="add_x_rims",
-    )(pml_width, left, residual, from_x)
+    )(splats, left, residual, from_x)
     rows, residual = lax.optimization_barrier((rows, residual))
     gram = pl.pallas_call(
         gather_kernel,

time: 31.2 us -> 29.8 us (0.955)
  Pallas kernels: 14.7 us -> 12 us
  waiting for transfers between devices: 2.61 us -> 4.12 us
    pallas_call x2, Pallas kernels: 3.8 us -> 2.66 us  [the longest x1 1.79 us: body(): pl.pallas_call(rim_y_kernel, out_shape=(whole, whole), in_specs=[VMEM] *...]
    ppermute x5, waiting for transfers between devices: 2.61 us -> 3.64 us  [passed_round(): lax.ppermute(value, axis, [(source, (source + steps) % count) for source...]
    pallas_call x1, Pallas kernels: 0.89 us -> 0.28 us  [body(): pl.pallas_call(slab_kernel, out_shape=(whole, face, f32(*yf_shape), face,...]
    pallas_call x1, Pallas kernels: 1.85 us -> 1.27 us  [body(): pl.pallas_call(outer_kernel, out_shape=(whole, f32(devices, 4, ny), whole...]
    all_to_all x1, waiting for transfers between devices: 0.01 us -> 0.48 us  [body(): rows = lax.all_to_all(gram, ('gx', 'gy', 'gz'), 0, 0)]
    pallas_call x1, Pallas kernels: 2.99 us -> 2.53 us  [body(): pl.pallas_call(inner_kernel, out_shape=(whole, planes, whole, f32(vectors...]
  transfers between devices with their start and end apart: 6 -> 6, of which waited for: 3 -> 4; matrix products, arithmetic and copies ran while one was open for 0% -> 0% of each run, Pallas kernels for 31% -> 27%
where the time goes in v24:
time: 29.8 us; the launch traced here: 29.6 us
  starting transfers between devices  12.7 us (43%)
  Pallas kernels  12 us (40%)
  waiting for transfers between devices  4.12 us (14%)
  between operations  0.77 us (3%)
    ppermute x5, starting transfers between devices, passed_round(): lax.ppermute(value, axis, [(source, (source + steps) % count) for source...  9.59 us
    ppermute x5, waiting for transfers between devices, passed_round(): lax.ppermute(value, axis, [(source, (source + steps) % count) for source...  3.64 us
    all_to_all x1, starting transfers between devices, body(): rows = lax.all_to_all(gram, ('gx', 'gy', 'gz'), 0, 0)  3.09 us
    pallas_call x1, Pallas kernels, body(): pl.pallas_call(prepare_kernel, out_shape=(whole, f32(2, nz, nx, ny), whol...  2.93 us
    pallas_call x1, Pallas kernels, body(): pl.pallas_call(inner_kernel, out_shape=(whole, planes, whole, f32(vectors...  2.53 us
    pallas_call x1, Pallas kernels, body(): pl.pallas_call(rim_y_kernel, out_shape=(whole, whole), in_specs=[VMEM] *...  1.79 us
    pallas_call x1, Pallas kernels, body(): pl.pallas_call(face_kernel, out_shape=(whole, f32(*xf_shape), f32(*yf_sha...  1.65 us
    pallas_call x1, Pallas kernels, body(): pl.pallas_call(outer_kernel, out_shape=(whole, f32(devices, 4, ny), whole...  1.27 us
  transfers between devices with their start and end apart: 6, of which 4 were waited for; matrix products, arithmetic and copies ran while one was open for 0% of the time, Pallas kernels for 27%

profile of v24, /device:TPU:0, one launch (start us, length us, event | category | flops | bytes accessed | tf_op | source)
XLA Modules:
  0.0 29.6 jit_solution(11250762293342302614)
XLA Ops:
  0.6 0.0 copy-start.2
  0.6 0.0 copy-start.1
  0.7 0.0 copy-start.5
  0.7 1.6 %take_faces.1 = (f32[2,4,3,8,16,128]{5,4,3,2,1,0:T(8,128)S(1)}, f32[2,4,2,8,128]{4,3,2,1,0:T(8,128)S(1)}, f32[16,128]{1,0:T(8,128)S(1)}) custom-call(f32[2,4,3,8,16,128]{5,4,3,2,1,0:T(8,128)} %fields_hbm.1), custom_call_target="tpu_custom_call" | custom-call | tf_op jit(solution)/shard_map/take_faces/pallas_call | solution.py:653
  2.3 4.5 %collective-permute-start = (f32[2,4,2,8,128]{4,3,2,1,0:T(8,128)S(1)}, f32[2,4,2,8,128]{4,3,2,1,0:T(8,128)S(1)}, u32[]{:S(2)}, u32[]{:S(2)}) collective-permute-start(f32[2,4,2,8,128]{4,3,2,1,0:T(8,128)S(1)} %get-tuple-element.45), channel_id=1, source_target_pairs={{0,28},{4,0},{8,4},{12,8},{16,12},{20,16},{24,20},{28,24},{1,29},{... | collective-permute-start | bytes 196616 | tf_op jit(solution)/shard_map/ppermute | solution.py:22
  6.9 1.5 %collective-permute-start.1 = (f32[16,128]{1,0:T(8,128)S(1)}, f32[16,128]{1,0:T(8,128)S(1)}, u32[]{:S(2)}, u32[]{:S(2)}) collective-permute-start(f32[16,128]{1,0:T(8,128)S(1)} %get-tuple-element.46), channel_id=1, source_target_pairs={{0,2},{2,0},{1,3},{3,1},{4,6},{6,4},{5,7},{7,5},{8,10},{10,8},{9,1... | collective-permute-start | bytes 24584 | tf_op jit(solution)/shard_map/ppermute | solution.py:22
  8.4 0.0 copy-done.1
  8.4 2.9 %prepare.1 = (f32[2,4,3,8,16,128]{5,4,3,2,1,0:T(8,128)S(1)}, f32[2,8,16,128]{3,2,1,0:T(8,128)S(1)}, f32[2,4,3,8,16,128]{5,4,3,2,1,0:T(8,128)S(1)}, f32[8,16,128]...) custom-call(s32[6]{0:T(128)S(1)} %copy-done.3, f32[4]{0:T(128)S(1)} %copy-done.4, ...), custom_call_target="tpu_custom_call" | custom-call | flops 13107200 | bytes 6291456 | tf_op jit(solution)/shard_map/prepare/pallas_call | solution.py:671
  11.4 0.0 collective-permute-done.1.raw_yf_ref
  11.4 0.0 collective-permute-done.raw_xf_ref
  11.4 0.3 slab_face.1
  11.7 1.6 %collective-permute-start.2 = (f32[2,4,2,16,128]{4,3,2,1,0:T(8,128)S(1)}, f32[2,4,2,16,128]{4,3,2,1,0:T(8,128)S(1)}, u32[]{:S(2)}, u32[]{:S(2)}) collective-permute-start(f32[2,4,2,16,128]{4,3,2,1,0:T(8,128)S(1)} %get-tuple-element.53), channel_id=1, source_target_pairs={{0,1},{1,0},{2,3},{3,2},{4,5},{5,4},{6,7},{7,6},{8,9},{9,8},{10,11... | collective-permute-start | bytes 393224 | tf_op jit(solution)/shard_map/ppermute | solution.py:22
  13.2 2.5 %apply_inner.1 = (f32[2,4,3,8,16,128]{5,4,3,2,1,0:T(8,128)S(1)}, f32[8,16,128]{2,1,0:T(8,128)S(1)}, f32[2,4,3,8,16,128]{5,4,3,2,1,0:T(8,128)S(1)}, f32[4,8,8,128...) custom-call(f32[56,128]{1,0:T(8,128)S(1)} %get-tuple-element.39.spla, ...), custom_call_target="tpu_custom_call", output_to_operand_aliasing={{0}: (5, {}), {1}: (6, {})} | custom-call | flops 13107200 | bytes 3145728 | tf_op jit(solution)/shard_map/apply_inner/pallas_call | solution.py:690
  15.8 0.9 %collective-permute-done.2.zf_ref = f32[2,4,2,16,128]{4,3,2,1,0:T(8,128)S(1)} collective-permute-done((f32[2,4,2,16,128]{4,3,2,1,0:T(8,128)S(1)}, f32[2,4,2,16,128]{4,3,2,1,0:T(8,128)S(1)}, u32[]{:S(2)}, u32[]{:S(2)}) %collective-permute-start.2) | collective-permute-done | bytes 131104 | tf_op jit(solution)/shard_map/ppermute | solution.py:22
  16.7 1.3 %apply_outer.1 = (f32[2,4,3,8,16,128]{5,4,3,2,1,0:T(8,128)S(1)}, f32[32,4,128]{2,1,0:T(4,128)}, f32[2,4,3,8,16,128]{5,4,3,2,1,0:T(8,128)S(1)}, f32[2,4,2,8,128]{4,3,2,1,0:T(8,128)S(1)}, f32[16,128]{1,0:T(8,128)S(1)}) custom-call(f32[56,128]{1,0:T(8,128)S(1)} %get-tuple-element.39.splat_ref, ...), custom_call_target="tpu_custom_call", output_to_operand_aliasing={{0}: (11, {}), {2}: (5, {}), {3}: (9, {})} | custom-call | flops 4915200 | bytes 1572864 | tf_op jit(solution)/shard_map/apply_outer/pallas_call | solution.py:702
  18.0 3.1 %all-to-all-start = ((f32[32,4,128]{2,1,0:T(4,128)}), f32[32,4,128]{2,1,0:T(4,128)S(1)}, u32[]{:S(2)}, u32[]{:S(2)}) async-start(f32[32,4,128]{2,1,0:T(4,128)} %get-tuple-element.64), calls=%async_computation | async-start | bytes 131072 | tf_op jit(solution)/shard_map/all_to_all | solution.py:713
  21.1 0.3 %collective-permute-start.4 = (f32[2,4,2,8,128]{4,3,2,1,0:T(8,128)S(1)}, f32[2,4,2,8,128]{4,3,2,1,0:T(8,128)S(1)}, u32[]{:S(2)}, u32[]{:S(2)}) collective-permute-start(f32[2,4,2,8,128]{4,3,2,1,0:T(8,128)S(1)} %get-tuple-element.69), channel_id=1, source_target_pairs={{0,4},{4,8},{8,12},{12,16},{16,20},{20,24},{24,28},{28,0},{1,5},{5... | collective-permute-start | bytes 196616 | tf_op jit(solution)/shard_map/ppermute | solution.py:22
  21.4 1.7 %collective-permute-start.3 = (f32[16,128]{1,0:T(8,128)S(1)}, f32[16,128]{1,0:T(8,128)S(1)}, u32[]{:S(2)}, u32[]{:S(2)}) collective-permute-start(f32[16,128]{1,0:T(8,128)S(1)} %get-tuple-element.66), channel_id=1, source_target_pairs={{0,2},{2,0},{1,3},{3,1},{4,6},{6,4},{5,7},{7,5},{8,10},{10,8},{9,1... | collective-permute-start | bytes 24584 | tf_op jit(solution)/shard_map/ppermute | solution.py:22
  23.1 2.0 %collective-permute-done.3.hyf_ref = f32[16,128]{1,0:T(8,128)S(1)} collective-permute-done((f32[16,128]{1,0:T(8,128)S(1)}, f32[16,128]{1,0:T(8,128)S(1)}, u32[]{:S(2)}, u32[]{:S(2)}) %collective-permute-start.3) | collective-permute-done | bytes 8224 | tf_op jit(solution)/shard_map/ppermute | solution.py:22
  25.1 1.8 %add_y_rims.1 = (f32[2,4,3,8,16,128]{5,4,3,2,1,0:T(8,128)S(1)}, f32[2,4,3,8,16,128]{5,4,3,2,1,0:T(8,128)}) custom-call(f32[56,128]{1,0:T(8,128)S(1)} %get-tuple-element.39.splat_ref, f32[2,4,3,8,16,128]{5,4,3,2,1,0:T(8,128)S(1)} %get-tuple-element.65.left_in, f32[16,128]{1,0:T(8,128)S(1)} %collective-permute-done.3.hyf_ref), custom_call_target="tpu_custom_call", output_to_operand_aliasing={{0}: (1, {})} | custom-call | tf_op jit(solution)/shard_map/add_y_rims/pallas_call | solution.py:717
  26.9 0.7 %collective-permute-done.4.hxf_ref = f32[2,4,2,8,128]{4,3,2,1,0:T(8,128)S(1)} collective-permute-done((f32[2,4,2,8,128]{4,3,2,1,0:T(8,128)S(1)}, f32[2,4,2,8,128]{4,3,2,1,0:T(8,128)S(1)}, u32[]{:S(2)}, u32[]{:S(2)}) %collective-permute-start.4) | collective-permute-done | bytes 65568 | tf_op jit(solution)/shard_map/ppermute | solution.py:22
  27.6 0.9 %add_x_rims.1 = (f32[2,4,3,8,16,128]{5,4,3,2,1,0:T(8,128)S(1)}, f32[2,4,3,8,16,128]{5,4,3,2,1,0:T(8,128)}) custom-call(f32[56,128]{1,0:T(8,128)S(1)} %get-tuple-element.39.splat_ref, f32[2,4,3,8,16,128]{5,4,3,2,1,0:T(8,128)S(1)} %get-tuple-element.67.left_in, ...), custom_call_target="tpu_custom_call", output_to_operand_aliasing={{0}: (1, {}), {1}: (2, {})} | custom-call | tf_op jit(solution)/shard_map/add_x_rims/pallas_call | solution.py:728
  28.4 0.5 %all-to-all-done.rows_ref = f32[32,4,128]{2,1,0:T(4,128)S(1)} async-done(((f32[32,4,128]{2,1,0:T(4,128)}), f32[32,4,128]{2,1,0:T(4,128)S(1)}, u32[]{:S(2)}, u32[]{:S(2)}) %all-to-all-start) | async-done | bytes 65568 | tf_op jit(solution)/shard_map/all_to_all | solution.py:713
  28.9 0.7 %sum_rows.1 = f32[2,4,4]{2,1,0:T(4,128)} custom-call(f32[32,4,128]{2,1,0:T(4,128)S(1)} %all-to-all-done.rows_ref), custom_call_target="tpu_custom_call" | custom-call | tf_op jit(solution)/shard_map/sum_rows/pallas_call | solution.py:740
  (8 shorter events, 0.0 us)
Async XLA Ops:
  0.6 7.8 %copy-start.2 = (f32[2,4]{1,0:T(2,128)S(1)}, f32[2,4]{1,0:T(2,128)}, u32[]{:S(2)}) copy-start(f32[2,4]{1,0:T(2,128)} %ritz_ref.1) | copy-start | bytes 100
  0.6 7.8 %copy-start.1 = (f32[2,4,4]{2,1,0:T(4,128)S(1)}, f32[2,4,4]{2,1,0:T(4,128)}, u32[]{:S(2)}) copy-start(f32[2,4,4]{2,1,0:T(4,128)} %coeffs_ref.1) | copy-start | bytes 388
  0.7 7.8 %copy-start.5 = (f32[4]{0:T(128)S(1)}, f32[4]{0:T(128)}, u32[]{:S(2)}) copy-start(f32[4]{0:T(128)} %eps_loss_ref.1) | copy-start | bytes 52
  0.7 7.8 %copy-start.4 = (f32[4]{0:T(128)S(1)}, f32[4]{0:T(128)}, u32[]{:S(2)}) copy-start(f32[4]{0:T(128)} %eps_real_ref.1) | copy-start | bytes 52
  0.7 7.8 %copy-start.3 = (s32[6]{0:T(128)S(1)}, s32[6]{0:T(128)}, u32[]{:S(2)}) copy-start(s32[6]{0:T(128)} %pml_ref.1) | copy-start | bytes 76
  0.7 7.8 %copy-start = (s32[8,16,128]{2,1,0:T(8,128)S(1)}, s32[8,16,128]{2,1,0:T(8,128)}, u32[]{:S(2)}) copy-start(s32[8,16,128]{2,1,0:T(8,128)} %material_ref.1) | copy-start | bytes 196612
  2.3 9.0 %collective-permute-start = (f32[2,4,2,8,128]{4,3,2,1,0:T(8,128)S(1)}, f32[2,4,2,8,128]{4,3,2,1,0:T(8,128)S(1)}, u32[]{:S(2)}, u32[]{:S(2)}) collective-permute-start(f32[2,4,2,8,128]{4,3,2,1,0:T(8,128)S(1)} %get-tuple-element.45), channel_id=1, source_target_pairs={{0,28},{4,0},{8,4},{12,8},{16,12},{20,16},{24,20},{28,24},{1,29},{... | collective-permute-start | bytes 196616 | tf_op jit(solution)/shard_map/ppermute | solution.py:22
  6.9 4.5 %collective-permute-start.1 = (f32[16,128]{1,0:T(8,128)S(1)}, f32[16,128]{1,0:T(8,128)S(1)}, u32[]{:S(2)}, u32[]{:S(2)}) collective-permute-start(f32[16,128]{1,0:T(8,128)S(1)} %get-tuple-element.46), channel_id=1, source_target_pairs={{0,2},{2,0},{1,3},{3,1},{4,6},{6,4},{5,7},{7,5},{8,10},{10,8},{9,1... | collective-permute-start | bytes 24584 | tf_op jit(solution)/shard_map/ppermute | solution.py:22
  11.7 5.0 %collective-permute-start.2 = (f32[2,4,2,16,128]{4,3,2,1,0:T(8,128)S(1)}, f32[2,4,2,16,128]{4,3,2,1,0:T(8,128)S(1)}, u32[]{:S(2)}, u32[]{:S(2)}) collective-permute-start(f32[2,4,2,16,128]{4,3,2,1,0:T(8,128)S(1)} %get-tuple-element.53), channel_id=1, source_target_pairs={{0,1},{1,0},{2,3},{3,2},{4,5},{5,4},{6,7},{7,6},{8,9},{9,8},{10,11... | collective-permute-start | bytes 393224 | tf_op jit(solution)/shard_map/ppermute | solution.py:22
  18.0 10.9 %all-to-all-start = ((f32[32,4,128]{2,1,0:T(4,128)}), f32[32,4,128]{2,1,0:T(4,128)S(1)}, u32[]{:S(2)}, u32[]{:S(2)}) async-start(f32[32,4,128]{2,1,0:T(4,128)} %get-tuple-element.64), calls=%async_computation | async-start | bytes 131072 | tf_op jit(solution)/shard_map/all_to_all | solution.py:713
  21.1 6.5 %collective-permute-start.4 = (f32[2,4,2,8,128]{4,3,2,1,0:T(8,128)S(1)}, f32[2,4,2,8,128]{4,3,2,1,0:T(8,128)S(1)}, u32[]{:S(2)}, u32[]{:S(2)}) collective-permute-start(f32[2,4,2,8,128]{4,3,2,1,0:T(8,128)S(1)} %get-tuple-element.69), channel_id=1, source_target_pairs={{0,4},{4,8},{8,12},{12,16},{16,20},{20,24},{24,28},{28,0},{1,5},{5... | collective-permute-start | bytes 196616 | tf_op jit(solution)/shard_map/ppermute | solution.py:22
  21.4 3.7 %collective-permute-start.3 = (f32[16,128]{1,0:T(8,128)S(1)}, f32[16,128]{1,0:T(8,128)S(1)}, u32[]{:S(2)}, u32[]{:S(2)}) collective-permute-start(f32[16,128]{1,0:T(8,128)S(1)} %get-tuple-element.66), channel_id=1, source_target_pairs={{0,2},{2,0},{1,3},{3,1},{4,6},{6,4},{5,7},{7,5},{8,10},{10,8},{9,1... | collective-permute-start | bytes 24584 | tf_op jit(solution)/shard_map/ppermute | solution.py:22

commit v25 on v24

--- a/solution.py
+++ b/solution.py
@@ -13,7 +13,6 @@
 AXES = ("gz", "gx", "gy")
 
 VMEM = pl.BlockSpec(memory_space=pltpu.VMEM)
-SMEM = pl.BlockSpec(memory_space=pltpu.SMEM)
 HBM = pl.BlockSpec(memory_space=pltpu.HBM)
 
 
@@ -53,8 +52,9 @@
 def axis_stretch(pml_ref, direction, count, places):
     total = count * lax.axis_size(AXES[direction])
     low_slot, high_slot = BOUNDS[direction]
-    low = jnp.full(places.shape, pml_ref[low_slot], jnp.int32).astype(jnp.float32)
-    high = jnp.full(places.shape, pml_ref[high_slot], jnp.int32).astype(jnp.float32)
+    low, high = (
+        jnp.broadcast_to(pml_ref[0:1, slot:slot + 1].astype(jnp.float32), places.shape) for slot in (low_slot, high_slot)
+    )
     return inverse_stretch(places, jnp.float32(total), low, high)
 
 
@@ -146,8 +146,12 @@
     return Splats(splat_ref, 2 * len(ENDS) + 2 * vectors, (2, vectors, vectors))
 
 
+def mixed_rows(splat_ref, vectors):
+    return Splats(splat_ref, 2 * len(ENDS) + 2 * vectors * (vectors + 1), (2, vectors, vectors))
+
+
 def splat_count(vectors):
-    return -(-(2 * len(ENDS) + 2 * vectors * (vectors + 1)) // SUB) * SUB
+    return -(-(2 * len(ENDS) + 2 * vectors * (2 * vectors + 1)) // SUB) * SUB
 
 
 def field_of(ref, b, comp, z, cut):
@@ -186,11 +190,18 @@
         direction, count, offset, half, factor = ends[name]
         values = axis_stretch(pml_ref, direction, count, one_place(direction, count, offset, line) + half)
         lines += [value * factor for value in values]
-    lines += [jnp.full(line, ritz_ref[part, b], jnp.float32) for part in parts for b in range(vectors)]
     lines += [
-        jnp.full(line, coeffs_ref[part, a, b], jnp.float32)
-        for part in parts for a in range(vectors) for b in range(vectors)
+        jnp.broadcast_to(ritz_ref[part:part + 1, b:b + 1], line) for part in parts for b in range(vectors)
     ]
+    real, imag = (
+        [
+            jnp.broadcast_to(coeffs_ref[part, a:a + 1, b:b + 1], line)
+            for a in range(vectors) for b in range(vectors)
+        ]
+        for part in parts
+    )
+    lines += real + imag
+    lines += [second + first for first, second in zip(real, imag)] + [second - first for first, second in zip(real, imag)]
     for row, value in enumerate(lines):
         splat_ref[row:row + 1] = value
     splat_ref[len(lines):] = jnp.zeros((splat_ref.shape[0] - len(lines), ny), jnp.float32)
@@ -199,23 +210,28 @@
         for part in parts:
             sz_ref[slot + part] = values[part]
 
+    coeffs, mixed = coeff_rows(splat_ref, vectors), mixed_rows(splat_ref, vectors)
+    choices = [
+        [jnp.broadcast_to(-OMEGA_SQ * source[0:1, number:number + 1], plane) for number in range(source.shape[1])]
+        for source in (eps_real_ref, eps_loss_ref)
+    ]
+
     @pl.loop(0, nz)
     def _(z):
         material = material_ref[z]
-        for part, source in enumerate((eps_real_ref, eps_loss_ref)):
+        for part in parts:
             value = jnp.zeros(plane, jnp.float32)
-            for number in range(source.shape[0]):
-                value = jnp.where(material == number, -OMEGA_SQ * source[number], value)
+            for number, choice in enumerate(choices[part]):
+                value = jnp.where(material == number, choice, value)
             eps_ref[part, z] = value
         for comp in range(3):
             real = [fields_ref[0, a, comp, z] for a in range(vectors)]
             imag = [fields_ref[1, a, comp, z] for a in range(vectors)]
             both = [first + second for first, second in zip(real, imag)]
             for b in range(vectors):
-                turns = [(coeffs_ref[0, a, b], coeffs_ref[1, a, b]) for a in range(vectors)]
-                shared = tree_sum([turn[0] * value for turn, value in zip(turns, both)])
-                less = tree_sum([(turn[0] + turn[1]) * value for turn, value in zip(turns, imag)])
-                more = tree_sum([(turn[1] - turn[0]) * value for turn, value in zip(turns, real)])
+                shared = tree_sum([coeffs[0, a, b] * both[a] for a in range(vectors)])
+                less = tree_sum([mixed[0, a, b] * imag[a] for a in range(vectors)])
+                more = tree_sum([mixed[1, a, b] * real[a] for a in range(vectors)])
                 basis_ref[0, b, comp, z] = shared - less
                 basis_ref[1, b, comp, z] = shared + more
         packed_ref[z] = jnp.zeros(plane, jnp.float32)
@@ -671,12 +687,12 @@
     basis, eps, h, packed, table, sz, splats = pl.pallas_call(
         prepare_kernel,
         out_shape=(whole, f32(2, nz, nx, ny), whole, planes, f32(8, nx, ny), f32(4, nz, ny), f32(splat_count(vectors), ny)),
-        in_specs=[SMEM] * 5 + [VMEM] * 2,
+        in_specs=[VMEM] * 7,
         out_specs=(VMEM,) * 7,
         compiler_params=params,
         cost_estimate=cost(800, 4),
         name="prepare",
-    )(pml_width, eps_real, eps_loss, coeffs, ritz, near, material)
+    )(pml_width[None], eps_real[None], eps_loss[None], coeffs, ritz, near, material)
     h, xf, yt, xadd, yadd, zf = pl.pallas_call(
         slab_kernel,
         out_shape=(whole, face, f32(*yf_shape), face, planes, f32(*zf_shape)),

time: 29.8 us -> 29.6 us (level)
  Pallas kernels: 12 us -> 11.4 us
  starting transfers between devices: 12.7 us -> 13.1 us
    pallas_call x1, Pallas kernels: 2.93 us -> 2.31 us  [body(): pl.pallas_call(prepare_kernel, out_shape=(whole, f32(2, nz, nx, ny), whol...]
    all_to_all x1, starting transfers between devices: 3.09 us -> 3.51 us  [body(): rows = lax.all_to_all(gram, ('gx', 'gy', 'gz'), 0, 0)]
  transfers between devices with their start and end apart: 6 -> 6, of which waited for: 4 -> 4; matrix products, arithmetic and copies ran while one was open for 0% -> 0% of each run, Pallas kernels for 27% -> 25%
where the time goes in v25:
time: 29.6 us; the launch traced here: 29.4 us
  starting transfers between devices  13.1 us (44%)
  Pallas kernels  11.4 us (39%)
  waiting for transfers between devices  4.12 us (14%)
  between operations  0.77 us (3%)
    ppermute x5, starting transfers between devices, passed_round(): lax.ppermute(value, axis, [(source, (source + steps) % count) for source...  9.59 us
    ppermute x5, waiting for transfers between devices, passed_round(): lax.ppermute(value, axis, [(source, (source + steps) % count) for source...  3.65 us
    all_to_all x1, starting transfers between devices, body(): rows = lax.all_to_all(gram, ('gx', 'gy', 'gz'), 0, 0)  3.51 us
    pallas_call x1, Pallas kernels, body(): pl.pallas_call(inner_kernel, out_shape=(whole, planes, whole, f32(vectors...  2.52 us
    pallas_call x1, Pallas kernels, body(): pl.pallas_call(prepare_kernel, out_shape=(whole, f32(2, nz, nx, ny), whol...  2.31 us
    pallas_call x1, Pallas kernels, body(): pl.pallas_call(rim_y_kernel, out_shape=(whole, whole), in_specs=[VMEM] *...  1.79 us
    pallas_call x1, Pallas kernels, body(): pl.pallas_call(face_kernel, out_shape=(whole, f32(*xf_shape), f32(*yf_sha...  1.65 us
    pallas_call x1, Pallas kernels, body(): pl.pallas_call(outer_kernel, out_shape=(whole, f32(devices, 4, ny), whole...  1.28 us
  transfers between devices with their start and end apart: 6, of which 4 were waited for; matrix products, arithmetic and copies ran while one was open for 0% of the time, Pallas kernels for 25%

profile of v25, /device:TPU:0, one launch (start us, length us, event | category | flops | bytes accessed | tf_op | source)
XLA Modules:
  0.0 29.4 jit_solution(13824779960971823220)
XLA Ops:
  0.6 0.0 copy-start.2
  0.6 0.0 copy-start.1
  0.7 0.0 copy-start.5
  0.7 1.6 %take_faces.1 = (f32[2,4,3,8,16,128]{5,4,3,2,1,0:T(8,128)S(1)}, f32[2,4,2,8,128]{4,3,2,1,0:T(8,128)S(1)}, f32[16,128]{1,0:T(8,128)S(1)}) custom-call(f32[2,4,3,8,16,128]{5,4,3,2,1,0:T(8,128)} %fields_hbm.1), custom_call_target="tpu_custom_call" | custom-call | tf_op jit(solution)/shard_map/take_faces/pallas_call | solution.py:669
  2.3 4.5 %collective-permute-start = (f32[2,4,2,8,128]{4,3,2,1,0:T(8,128)S(1)}, f32[2,4,2,8,128]{4,3,2,1,0:T(8,128)S(1)}, u32[]{:S(2)}, u32[]{:S(2)}) collective-permute-start(f32[2,4,2,8,128]{4,3,2,1,0:T(8,128)S(1)} %get-tuple-element.45), channel_id=1, source_target_pairs={{0,28},{4,0},{8,4},{12,8},{16,12},{20,16},{24,20},{28,24},{1,29},{... | collective-permute-start | bytes 196616 | tf_op jit(solution)/shard_map/ppermute | solution.py:21
  6.9 1.5 %collective-permute-start.1 = (f32[16,128]{1,0:T(8,128)S(1)}, f32[16,128]{1,0:T(8,128)S(1)}, u32[]{:S(2)}, u32[]{:S(2)}) collective-permute-start(f32[16,128]{1,0:T(8,128)S(1)} %get-tuple-element.46), channel_id=1, source_target_pairs={{0,2},{2,0},{1,3},{3,1},{4,6},{6,4},{5,7},{7,5},{8,10},{10,8},{9,1... | collective-permute-start | bytes 24584 | tf_op jit(solution)/shard_map/ppermute | solution.py:21
  8.4 0.0 copy-done.1
  8.4 2.3 %prepare.1 = (f32[2,4,3,8,16,128]{5,4,3,2,1,0:T(8,128)S(1)}, f32[2,8,16,128]{3,2,1,0:T(8,128)S(1)}, f32[2,4,3,8,16,128]{5,4,3,2,1,0:T(8,128)S(1)}, f32[8,16,128]...) custom-call(s32[1,6]{1,0:T(1,128)S(1)} %bitcast.3, ...), custom_call_target="tpu_custom_call" | custom-call | flops 13107200 | bytes 6291456 | tf_op jit(solution)/shard_map/prepare/pallas_call | solution.py:687
  10.8 0.0 collective-permute-done.1.raw_yf_ref
  10.8 0.0 collective-permute-done.raw_xf_ref
  10.8 0.3 slab_face.1
  11.1 1.6 %collective-permute-start.2 = (f32[2,4,2,16,128]{4,3,2,1,0:T(8,128)S(1)}, f32[2,4,2,16,128]{4,3,2,1,0:T(8,128)S(1)}, u32[]{:S(2)}, u32[]{:S(2)}) collective-permute-start(f32[2,4,2,16,128]{4,3,2,1,0:T(8,128)S(1)} %get-tuple-element.53), channel_id=1, source_target_pairs={{0,1},{1,0},{2,3},{3,2},{4,5},{5,4},{6,7},{7,6},{8,9},{9,8},{10,11... | collective-permute-start | bytes 393224 | tf_op jit(solution)/shard_map/ppermute | solution.py:21
  12.6 2.5 %apply_inner.1 = (f32[2,4,3,8,16,128]{5,4,3,2,1,0:T(8,128)S(1)}, f32[8,16,128]{2,1,0:T(8,128)S(1)}, f32[2,4,3,8,16,128]{5,4,3,2,1,0:T(8,128)S(1)}, f32[4,8,8,128...) custom-call(f32[88,128]{1,0:T(8,128)S(1)} %get-tuple-element.39.spla, ...), custom_call_target="tpu_custom_call", output_to_operand_aliasing={{0}: (5, {}), {1}: (6, {})} | custom-call | flops 13107200 | bytes 3145728 | tf_op jit(solution)/shard_map/apply_inner/pallas_call | solution.py:706
  15.2 0.9 %collective-permute-done.2.zf_ref = f32[2,4,2,16,128]{4,3,2,1,0:T(8,128)S(1)} collective-permute-done((f32[2,4,2,16,128]{4,3,2,1,0:T(8,128)S(1)}, f32[2,4,2,16,128]{4,3,2,1,0:T(8,128)S(1)}, u32[]{:S(2)}, u32[]{:S(2)}) %collective-permute-start.2) | collective-permute-done | bytes 131104 | tf_op jit(solution)/shard_map/ppermute | solution.py:21
  16.1 1.3 %apply_outer.1 = (f32[2,4,3,8,16,128]{5,4,3,2,1,0:T(8,128)S(1)}, f32[32,4,128]{2,1,0:T(4,128)}, f32[2,4,3,8,16,128]{5,4,3,2,1,0:T(8,128)S(1)}, f32[2,4,2,8,128]{4,3,2,1,0:T(8,128)S(1)}, f32[16,128]{1,0:T(8,128)S(1)}) custom-call(f32[88,128]{1,0:T(8,128)S(1)} %get-tuple-element.39.splat_ref, ...), custom_call_target="tpu_custom_call", output_to_operand_aliasing={{0}: (11, {}), {2}: (5, {}), {3}: (9, {})} | custom-call | flops 4915200 | bytes 1572864 | tf_op jit(solution)/shard_map/apply_outer/pallas_call | solution.py:718
  17.4 3.5 %all-to-all-start = ((f32[32,4,128]{2,1,0:T(4,128)}), f32[32,4,128]{2,1,0:T(4,128)S(1)}, u32[]{:S(2)}, u32[]{:S(2)}) async-start(f32[32,4,128]{2,1,0:T(4,128)} %get-tuple-element.64), calls=%async_computation | async-start | bytes 131072 | tf_op jit(solution)/shard_map/all_to_all | solution.py:729
  20.9 0.3 %collective-permute-start.4 = (f32[2,4,2,8,128]{4,3,2,1,0:T(8,128)S(1)}, f32[2,4,2,8,128]{4,3,2,1,0:T(8,128)S(1)}, u32[]{:S(2)}, u32[]{:S(2)}) collective-permute-start(f32[2,4,2,8,128]{4,3,2,1,0:T(8,128)S(1)} %get-tuple-element.69), channel_id=1, source_target_pairs={{0,4},{4,8},{8,12},{12,16},{16,20},{20,24},{24,28},{28,0},{1,5},{5... | collective-permute-start | bytes 196616 | tf_op jit(solution)/shard_map/ppermute | solution.py:21
  21.2 1.7 %collective-permute-start.3 = (f32[16,128]{1,0:T(8,128)S(1)}, f32[16,128]{1,0:T(8,128)S(1)}, u32[]{:S(2)}, u32[]{:S(2)}) collective-permute-start(f32[16,128]{1,0:T(8,128)S(1)} %get-tuple-element.66), channel_id=1, source_target_pairs={{0,2},{2,0},{1,3},{3,1},{4,6},{6,4},{5,7},{7,5},{8,10},{10,8},{9,1... | collective-permute-start | bytes 24584 | tf_op jit(solution)/shard_map/ppermute | solution.py:21
  22.9 2.0 %collective-permute-done.3.hyf_ref = f32[16,128]{1,0:T(8,128)S(1)} collective-permute-done((f32[16,128]{1,0:T(8,128)S(1)}, f32[16,128]{1,0:T(8,128)S(1)}, u32[]{:S(2)}, u32[]{:S(2)}) %collective-permute-start.3) | collective-permute-done | bytes 8224 | tf_op jit(solution)/shard_map/ppermute | solution.py:21
  24.9 1.8 %add_y_rims.1 = (f32[2,4,3,8,16,128]{5,4,3,2,1,0:T(8,128)S(1)}, f32[2,4,3,8,16,128]{5,4,3,2,1,0:T(8,128)}) custom-call(f32[88,128]{1,0:T(8,128)S(1)} %get-tuple-element.39.splat_ref, f32[2,4,3,8,16,128]{5,4,3,2,1,0:T(8,128)S(1)} %get-tuple-element.65.left_in, f32[16,128]{1,0:T(8,128)S(1)} %collective-permute-done.3.hyf_ref), custom_call_target="tpu_custom_call", output_to_operand_aliasing={{0}: (1, {})} | custom-call | tf_op jit(solution)/shard_map/add_y_rims/pallas_call | solution.py:733
  26.7 0.7 %collective-permute-done.4.hxf_ref = f32[2,4,2,8,128]{4,3,2,1,0:T(8,128)S(1)} collective-permute-done((f32[2,4,2,8,128]{4,3,2,1,0:T(8,128)S(1)}, f32[2,4,2,8,128]{4,3,2,1,0:T(8,128)S(1)}, u32[]{:S(2)}, u32[]{:S(2)}) %collective-permute-start.4) | collective-permute-done | bytes 65568 | tf_op jit(solution)/shard_map/ppermute | solution.py:21
  27.4 0.9 %add_x_rims.1 = (f32[2,4,3,8,16,128]{5,4,3,2,1,0:T(8,128)S(1)}, f32[2,4,3,8,16,128]{5,4,3,2,1,0:T(8,128)}) custom-call(f32[88,128]{1,0:T(8,128)S(1)} %get-tuple-element.39.splat_ref, f32[2,4,3,8,16,128]{5,4,3,2,1,0:T(8,128)S(1)} %get-tuple-element.67.left_in, ...), custom_call_target="tpu_custom_call", output_to_operand_aliasing={{0}: (1, {}), {1}: (2, {})} | custom-call | tf_op jit(solution)/shard_map/add_x_rims/pallas_call | solution.py:744
  28.2 0.5 %all-to-all-done.rows_ref = f32[32,4,128]{2,1,0:T(4,128)S(1)} async-done(((f32[32,4,128]{2,1,0:T(4,128)}), f32[32,4,128]{2,1,0:T(4,128)S(1)}, u32[]{:S(2)}, u32[]{:S(2)}) %all-to-all-start) | async-done | bytes 65568 | tf_op jit(solution)/shard_map/all_to_all | solution.py:729
  28.7 0.7 %sum_rows.1 = f32[2,4,4]{2,1,0:T(4,128)} custom-call(f32[32,4,128]{2,1,0:T(4,128)S(1)} %all-to-all-done.rows_ref), custom_call_target="tpu_custom_call" | custom-call | tf_op jit(solution)/shard_map/sum_rows/pallas_call | solution.py:756
  (8 shorter events, 0.0 us)
Async XLA Ops:
  0.6 7.8 %copy-start.2 = (f32[2,4]{1,0:T(2,128)S(1)}, f32[2,4]{1,0:T(2,128)}, u32[]{:S(2)}) copy-start(f32[2,4]{1,0:T(2,128)} %ritz_ref.1) | copy-start | bytes 100
  0.6 7.8 %copy-start.1 = (f32[2,4,4]{2,1,0:T(4,128)S(1)}, f32[2,4,4]{2,1,0:T(4,128)}, u32[]{:S(2)}) copy-start(f32[2,4,4]{2,1,0:T(4,128)} %coeffs_ref.1) | copy-start | bytes 388
  0.7 7.8 %copy-start.5 = (f32[4]{0:T(128)S(1)}, f32[4]{0:T(128)}, u32[]{:S(2)}) copy-start(f32[4]{0:T(128)} %param.11) | copy-start | bytes 52
  0.7 7.8 %copy-start.4 = (f32[4]{0:T(128)S(1)}, f32[4]{0:T(128)}, u32[]{:S(2)}) copy-start(f32[4]{0:T(128)} %param.10) | copy-start | bytes 52
  0.7 7.8 %copy-start.3 = (s32[6]{0:T(128)S(1)}, s32[6]{0:T(128)}, u32[]{:S(2)}) copy-start(s32[6]{0:T(128)} %param.9) | copy-start | bytes 76
  0.7 7.8 %copy-start = (s32[8,16,128]{2,1,0:T(8,128)S(1)}, s32[8,16,128]{2,1,0:T(8,128)}, u32[]{:S(2)}) copy-start(s32[8,16,128]{2,1,0:T(8,128)} %material_ref.1) | copy-start | bytes 196612
  2.3 8.4 %collective-permute-start = (f32[2,4,2,8,128]{4,3,2,1,0:T(8,128)S(1)}, f32[2,4,2,8,128]{4,3,2,1,0:T(8,128)S(1)}, u32[]{:S(2)}, u32[]{:S(2)}) collective-permute-start(f32[2,4,2,8,128]{4,3,2,1,0:T(8,128)S(1)} %get-tuple-element.45), channel_id=1, source_target_pairs={{0,28},{4,0},{8,4},{12,8},{16,12},{20,16},{24,20},{28,24},{1,29},{... | collective-permute-start | bytes 196616 | tf_op jit(solution)/shard_map/ppermute | solution.py:21
  6.9 3.9 %collective-permute-start.1 = (f32[16,128]{1,0:T(8,128)S(1)}, f32[16,128]{1,0:T(8,128)S(1)}, u32[]{:S(2)}, u32[]{:S(2)}) collective-permute-start(f32[16,128]{1,0:T(8,128)S(1)} %get-tuple-element.46), channel_id=1, source_target_pairs={{0,2},{2,0},{1,3},{3,1},{4,6},{6,4},{5,7},{7,5},{8,10},{10,8},{9,1... | collective-permute-start | bytes 24584 | tf_op jit(solution)/shard_map/ppermute | solution.py:21
  11.1 5.0 %collective-permute-start.2 = (f32[2,4,2,16,128]{4,3,2,1,0:T(8,128)S(1)}, f32[2,4,2,16,128]{4,3,2,1,0:T(8,128)S(1)}, u32[]{:S(2)}, u32[]{:S(2)}) collective-permute-start(f32[2,4,2,16,128]{4,3,2,1,0:T(8,128)S(1)} %get-tuple-element.53), channel_id=1, source_target_pairs={{0,1},{1,0},{2,3},{3,2},{4,5},{5,4},{6,7},{7,6},{8,9},{9,8},{10,11... | collective-permute-start | bytes 393224 | tf_op jit(solution)/shard_map/ppermute | solution.py:21
  17.4 11.3 %all-to-all-start = ((f32[32,4,128]{2,1,0:T(4,128)}), f32[32,4,128]{2,1,0:T(4,128)S(1)}, u32[]{:S(2)}, u32[]{:S(2)}) async-start(f32[32,4,128]{2,1,0:T(4,128)} %get-tuple-element.64), calls=%async_computation | async-start | bytes 131072 | tf_op jit(solution)/shard_map/all_to_all | solution.py:729
  20.9 6.5 %collective-permute-start.4 = (f32[2,4,2,8,128]{4,3,2,1,0:T(8,128)S(1)}, f32[2,4,2,8,128]{4,3,2,1,0:T(8,128)S(1)}, u32[]{:S(2)}, u32[]{:S(2)}) collective-permute-start(f32[2,4,2,8,128]{4,3,2,1,0:T(8,128)S(1)} %get-tuple-element.69), channel_id=1, source_target_pairs={{0,4},{4,8},{8,12},{12,16},{16,20},{20,24},{24,28},{28,0},{1,5},{5... | collective-permute-start | bytes 196616 | tf_op jit(solution)/shard_map/ppermute | solution.py:21
  21.2 3.7 %collective-permute-start.3 = (f32[16,128]{1,0:T(8,128)S(1)}, f32[16,128]{1,0:T(8,128)S(1)}, u32[]{:S(2)}, u32[]{:S(2)}) collective-permute-start(f32[16,128]{1,0:T(8,128)S(1)} %get-tuple-element.66), channel_id=1, source_target_pairs={{0,2},{2,0},{1,3},{3,1},{4,6},{6,4},{5,7},{7,5},{8,10},{10,8},{9,1... | collective-permute-start | bytes 24584 | tf_op jit(solution)/shard_map/ppermute | solution.py:21

commit v26 on v25

--- a/solution.py
+++ b/solution.py
@@ -160,6 +160,55 @@
 
 def tiles_of(nx):
     return [slice(SUB * t, SUB * (t + 1)) for t in range(nx // SUB)]
+
+
+def open_magnetic(basis_ref, table_ref, sz_ref, h_ref, packed_ref):
+    _, vectors, _, nz, nx, ny = basis_ref.shape
+    parts = range(2)
+    tile = (SUB, ny)
+    rows = lax.broadcasted_iota(jnp.int32, tile, 0)
+    lanes = lax.broadcasted_iota(jnp.int32, tile, 1)
+    cuts = tiles_of(nx)
+
+    def magnetic(b, z, last):
+        shz = tuple(sz_ref[2 + part, pl.ds(z, 1)] for part in parts)
+        for cut in cuts:
+            u = [field_of(basis_ref, b, comp, z, cut) for comp in range(3)]
+
+            def step_z(comp):
+                if last:
+                    return tuple(-value for value in u[comp])
+                return sub(field_of(basis_ref, b, comp, z + 1, cut), u[comp])
+
+            def step_x(comp):
+                if cut.stop < nx:
+                    ahead = field_of(basis_ref, b, comp, z, slice(cut.start + 1, cut.stop + 1))
+                else:
+                    ahead = tuple(jnp.where(rows == SUB - 1, 0.0, pltpu.roll(value, SUB - 1, 0)) for value in u[comp])
+                return sub(ahead, u[comp])
+
+            def step_y(comp):
+                ahead = tuple(jnp.where(lanes == ny - 1, 0.0, pltpu.roll(value, ny - 1, 1)) for value in u[comp])
+                return sub(ahead, u[comp])
+
+            shx = tuple(table_ref[SHX + part, cut] for part in parts)
+            shy = tuple(table_ref[SHY + part, cut] for part in parts)
+            h = (
+                sub(cmul(shy, step_y(2)), cmul(shz, step_z(1))),
+                sub(cmul(shz, step_z(0)), cmul(shx, step_x(2))),
+                sub(cmul(shx, step_x(1)), cmul(shy, step_y(0))),
+            )
+            for comp in range(3):
+                for part in parts:
+                    h_ref[part, b, comp, z, cut] = h[comp][part]
+            packed = packed_ref[z, cut]
+            for slot, value in enumerate((h[2], h[0])):
+                for part in parts:
+                    row = packed_row(slot, part, b, vectors)
+                    packed = jnp.where(lanes == row, pltpu.roll(value[part], (row + 1) % ny, 1), packed)
+            packed_ref[z, cut] = packed
+
+    return magnetic
 
 
 def prepare_kernel(
@@ -236,54 +285,7 @@
                 basis_ref[1, b, comp, z] = shared + more
         packed_ref[z] = jnp.zeros(plane, jnp.float32)
 
-    tile = (SUB, ny)
-    rows = lax.broadcasted_iota(jnp.int32, tile, 0)
-    lanes = lax.broadcasted_iota(jnp.int32, tile, 1)
-    cuts = tiles_of(nx)
-
-    def magnetic(b, z, last):
-        shz = tuple(sz_ref[2 + part, pl.ds(z, 1)] for part in parts)
-        for cut in cuts:
-            u = [field_of(basis_ref, b, comp, z, cut) for comp in range(3)]
-
-            def step_z(comp):
-                if last:
-                    return tuple(-value for value in u[comp])
-                return sub(field_of(basis_ref, b, comp, z + 1, cut), u[comp])
-
-            def step_x(comp):
-                if cut.stop < nx:
-                    ahead = field_of(basis_ref, b, comp, z, slice(cut.start + 1, cut.stop + 1))
-                else:
-                    ahead = tuple(jnp.where(rows == SUB - 1, 0.0, pltpu.roll(value, SUB - 1, 0)) for value in u[comp])
-                return sub(ahead, u[comp])
-
-            def step_y(comp):
-                ahead = tuple(jnp.where(lanes == ny - 1, 0.0, pltpu.roll(value, ny - 1, 1)) for value in u[comp])
-                return sub(ahead, u[comp])
-
-            shx = tuple(table_ref[SHX + part, cut] for part in parts)
-            shy = tuple(table_ref[SHY + part, cut] for part in parts)
-            h = (
-                sub(cmul(shy, step_y(2)), cmul(shz, step_z(1))),
-                sub(cmul(shz, step_z(0)), cmul(shx, step_x(2))),
-                sub(cmul(shx, step_x(1)), cmul(shy, step_y(0))),
-            )
-            for comp in range(3):
-                for part in parts:
-                    h_ref[part, b, comp, z, cut] = h[comp][part]
-            packed = packed_ref[z, cut]
-            for slot, value in enumerate((h[2], h[0])):
-                for part in parts:
-                    row = packed_row(slot, part, b, vectors)
-                    packed = jnp.where(lanes == row, pltpu.roll(value[part], (row + 1) % ny, 1), packed)
-            packed_ref[z, cut] = packed
-
-    @pl.loop(0, nz - 1)
-    def _(z):
-        for b in range(vectors):
-            magnetic(b, z, False)
-
+    magnetic = open_magnetic(basis_ref, table_ref, sz_ref, h_ref, packed_ref)
     for b in range(vectors):
         magnetic(b, nz - 1, True)
 
@@ -448,6 +450,13 @@
     keep = pltpu.make_async_copy(basis_ref, basis_hbm, sem)
     keep.start()
     cuts = tiles_of(nx)
+    magnetic = open_magnetic(basis_ref, table_ref, sz_ref, h_ref, packed_ref)
+
+    @pl.loop(0, nz - 1)
+    def _(z):
+        for b in range(vectors):
+            magnetic(b, z, False)
+
     lanes = lax.broadcasted_iota(jnp.int32, (nz, ny), 1)
     open_plane = lax.broadcasted_iota(jnp.int32, (nz, ny), 0) < nz - 1
     packed_ref[...] = packed_ref[...] + yadd_ref[...]

time: 29.6 us -> 29.6 us (level)
    pallas_call x1, Pallas kernels: 2.52 us -> 3.77 us  [body(): pl.pallas_call(inner_kernel, out_shape=(whole, planes, whole, f32(vectors...]
    pallas_call x1, Pallas kernels: 2.31 us -> 1.07 us  [body(): pl.pallas_call(prepare_kernel, out_shape=(whole, f32(2, nz, nx, ny), whol...]
  transfers between devices with their start and end apart: 6 -> 6, of which waited for: 4 -> 4; matrix products, arithmetic and copies ran while one was open for 0% -> 0% of each run, Pallas kernels for 25% -> 26%
where the time goes in v26:
time: 29.6 us; the launch traced here: 29.4 us
  starting transfers between devices  13 us (44%)
  Pallas kernels  11.4 us (39%)
  waiting for transfers between devices  4.2 us (14%)
  between operations  0.77 us (3%)
    ppermute x5, starting transfers between devices, passed_round(): lax.ppermute(value, axis, [(source, (source + steps) % count) for source...  9.59 us
    pallas_call x1, Pallas kernels, body(): pl.pallas_call(inner_kernel, out_shape=(whole, planes, whole, f32(vectors...  3.77 us
    ppermute x5, waiting for transfers between devices, passed_round(): lax.ppermute(value, axis, [(source, (source + steps) % count) for source...  3.72 us
    all_to_all x1, starting transfers between devices, body(): rows = lax.all_to_all(gram, ('gx', 'gy', 'gz'), 0, 0)  3.43 us
    pallas_call x1, Pallas kernels, body(): pl.pallas_call(rim_y_kernel, out_shape=(whole, whole), in_specs=[VMEM] *...  1.79 us
    pallas_call x1, Pallas kernels, body(): pl.pallas_call(face_kernel, out_shape=(whole, f32(*xf_shape), f32(*yf_sha...  1.65 us
    pallas_call x1, Pallas kernels, body(): pl.pallas_call(outer_kernel, out_shape=(whole, f32(devices, 4, ny), whole...  1.28 us
    pallas_call x1, Pallas kernels, body(): pl.pallas_call(prepare_kernel, out_shape=(whole, f32(2, nz, nx, ny), whol...  1.07 us
  transfers between devices with their start and end apart: 6, of which 4 were waited for; matrix products, arithmetic and copies ran while one was open for 0% of the time, Pallas kernels for 26%

profile of v26, /device:TPU:0, one launch (start us, length us, event | category | flops | bytes accessed | tf_op | source)
XLA Modules:
  0.0 29.4 jit_solution(17413853030532422624)
XLA Ops:
  0.6 0.0 copy-start.2
  0.6 0.0 copy-start.1
  0.7 0.0 copy-start.5
  0.7 1.6 %take_faces.1 = (f32[2,4,3,8,16,128]{5,4,3,2,1,0:T(8,128)S(1)}, f32[2,4,2,8,128]{4,3,2,1,0:T(8,128)S(1)}, f32[16,128]{1,0:T(8,128)S(1)}) custom-call(f32[2,4,3,8,16,128]{5,4,3,2,1,0:T(8,128)} %fields_hbm.1), custom_call_target="tpu_custom_call" | custom-call | tf_op jit(solution)/shard_map/take_faces/pallas_call | solution.py:678
  2.3 4.5 %collective-permute-start = (f32[2,4,2,8,128]{4,3,2,1,0:T(8,128)S(1)}, f32[2,4,2,8,128]{4,3,2,1,0:T(8,128)S(1)}, u32[]{:S(2)}, u32[]{:S(2)}) collective-permute-start(f32[2,4,2,8,128]{4,3,2,1,0:T(8,128)S(1)} %get-tuple-element.45), channel_id=1, source_target_pairs={{0,28},{4,0},{8,4},{12,8},{16,12},{20,16},{24,20},{28,24},{1,29},{... | collective-permute-start | bytes 196616 | tf_op jit(solution)/shard_map/ppermute | solution.py:21
  6.9 1.5 %collective-permute-start.1 = (f32[16,128]{1,0:T(8,128)S(1)}, f32[16,128]{1,0:T(8,128)S(1)}, u32[]{:S(2)}, u32[]{:S(2)}) collective-permute-start(f32[16,128]{1,0:T(8,128)S(1)} %get-tuple-element.46), channel_id=1, source_target_pairs={{0,2},{2,0},{1,3},{3,1},{4,6},{6,4},{5,7},{7,5},{8,10},{10,8},{9,1... | collective-permute-start | bytes 24584 | tf_op jit(solution)/shard_map/ppermute | solution.py:21
  8.4 0.0 copy-done.1
  8.4 1.1 %prepare.1 = (f32[2,4,3,8,16,128]{5,4,3,2,1,0:T(8,128)S(1)}, f32[2,8,16,128]{3,2,1,0:T(8,128)S(1)}, f32[2,4,3,8,16,128]{5,4,3,2,1,0:T(8,128)S(1)}, f32[8,16,128]...) custom-call(s32[1,6]{1,0:T(1,128)S(1)} %bitcast.3, ...), custom_call_target="tpu_custom_call" | custom-call | flops 13107200 | bytes 6291456 | tf_op jit(solution)/shard_map/prepare/pallas_call | solution.py:696
  9.5 1.0 %collective-permute-done.1.raw_yf_ref = f32[16,128]{1,0:T(8,128)S(1)} collective-permute-done((f32[16,128]{1,0:T(8,128)S(1)}, f32[16,128]{1,0:T(8,128)S(1)}, u32[]{:S(2)}, u32[]{:S(2)}) %collective-permute-start.1) | collective-permute-done | bytes 8224 | tf_op jit(solution)/shard_map/ppermute | solution.py:21
  10.5 0.0 collective-permute-done.raw_xf_ref
  10.5 0.3 slab_face.1
  10.8 1.6 %collective-permute-start.2 = (f32[2,4,2,16,128]{4,3,2,1,0:T(8,128)S(1)}, f32[2,4,2,16,128]{4,3,2,1,0:T(8,128)S(1)}, u32[]{:S(2)}, u32[]{:S(2)}) collective-permute-start(f32[2,4,2,16,128]{4,3,2,1,0:T(8,128)S(1)} %get-tuple-element.53), channel_id=1, source_target_pairs={{0,1},{1,0},{2,3},{3,2},{4,5},{5,4},{6,7},{7,6},{8,9},{9,8},{10,11... | collective-permute-start | bytes 393224 | tf_op jit(solution)/shard_map/ppermute | solution.py:21
  12.4 3.8 %apply_inner.1 = (f32[2,4,3,8,16,128]{5,4,3,2,1,0:T(8,128)S(1)}, f32[8,16,128]{2,1,0:T(8,128)S(1)}, f32[2,4,3,8,16,128]{5,4,3,2,1,0:T(8,128)S(1)}, f32[4,8,8,128...) custom-call(f32[88,128]{1,0:T(8,128)S(1)} %get-tuple-element.39.spla, ...), custom_call_target="tpu_custom_call", output_to_operand_aliasing={{0}: (5, {}), {1}: (6, {})} | custom-call | flops 13107200 | bytes 3145728 | tf_op jit(solution)/shard_map/apply_inner/pallas_call | solution.py:715
  16.2 0.0 collective-permute-done.2.zf_ref
  16.2 1.3 %apply_outer.1 = (f32[2,4,3,8,16,128]{5,4,3,2,1,0:T(8,128)S(1)}, f32[32,4,128]{2,1,0:T(4,128)}, f32[2,4,3,8,16,128]{5,4,3,2,1,0:T(8,128)S(1)}, f32[2,4,2,8,128]{4,3,2,1,0:T(8,128)S(1)}, f32[16,128]{1,0:T(8,128)S(1)}) custom-call(f32[88,128]{1,0:T(8,128)S(1)} %get-tuple-element.39.splat_ref, ...), custom_call_target="tpu_custom_call", output_to_operand_aliasing={{0}: (11, {}), {2}: (5, {}), {3}: (9, {})} | custom-call | flops 4915200 | bytes 1572864 | tf_op jit(solution)/shard_map/apply_outer/pallas_call | solution.py:727
  17.5 3.4 %all-to-all-start = ((f32[32,4,128]{2,1,0:T(4,128)}), f32[32,4,128]{2,1,0:T(4,128)S(1)}, u32[]{:S(2)}, u32[]{:S(2)}) async-start(f32[32,4,128]{2,1,0:T(4,128)} %get-tuple-element.64), calls=%async_computation | async-start | bytes 131072 | tf_op jit(solution)/shard_map/all_to_all | solution.py:738
  20.9 0.3 %collective-permute-start.4 = (f32[2,4,2,8,128]{4,3,2,1,0:T(8,128)S(1)}, f32[2,4,2,8,128]{4,3,2,1,0:T(8,128)S(1)}, u32[]{:S(2)}, u32[]{:S(2)}) collective-permute-start(f32[2,4,2,8,128]{4,3,2,1,0:T(8,128)S(1)} %get-tuple-element.69), channel_id=1, source_target_pairs={{0,4},{4,8},{8,12},{12,16},{16,20},{20,24},{24,28},{28,0},{1,5},{5... | collective-permute-start | bytes 196616 | tf_op jit(solution)/shard_map/ppermute | solution.py:21
  21.2 1.7 %collective-permute-start.3 = (f32[16,128]{1,0:T(8,128)S(1)}, f32[16,128]{1,0:T(8,128)S(1)}, u32[]{:S(2)}, u32[]{:S(2)}) collective-permute-start(f32[16,128]{1,0:T(8,128)S(1)} %get-tuple-element.66), channel_id=1, source_target_pairs={{0,2},{2,0},{1,3},{3,1},{4,6},{6,4},{5,7},{7,5},{8,10},{10,8},{9,1... | collective-permute-start | bytes 24584 | tf_op jit(solution)/shard_map/ppermute | solution.py:21
  22.9 2.0 %collective-permute-done.3.hyf_ref = f32[16,128]{1,0:T(8,128)S(1)} collective-permute-done((f32[16,128]{1,0:T(8,128)S(1)}, f32[16,128]{1,0:T(8,128)S(1)}, u32[]{:S(2)}, u32[]{:S(2)}) %collective-permute-start.3) | collective-permute-done | bytes 8224 | tf_op jit(solution)/shard_map/ppermute | solution.py:21
  24.9 1.8 %add_y_rims.1 = (f32[2,4,3,8,16,128]{5,4,3,2,1,0:T(8,128)S(1)}, f32[2,4,3,8,16,128]{5,4,3,2,1,0:T(8,128)}) custom-call(f32[88,128]{1,0:T(8,128)S(1)} %get-tuple-element.39.splat_ref, f32[2,4,3,8,16,128]{5,4,3,2,1,0:T(8,128)S(1)} %get-tuple-element.65.left_in, f32[16,128]{1,0:T(8,128)S(1)} %collective-permute-done.3.hyf_ref), custom_call_target="tpu_custom_call", output_to_operand_aliasing={{0}: (1, {})} | custom-call | tf_op jit(solution)/shard_map/add_y_rims/pallas_call | solution.py:742
  26.7 0.7 %collective-permute-done.4.hxf_ref = f32[2,4,2,8,128]{4,3,2,1,0:T(8,128)S(1)} collective-permute-done((f32[2,4,2,8,128]{4,3,2,1,0:T(8,128)S(1)}, f32[2,4,2,8,128]{4,3,2,1,0:T(8,128)S(1)}, u32[]{:S(2)}, u32[]{:S(2)}) %collective-permute-start.4) | collective-permute-done | bytes 65568 | tf_op jit(solution)/shard_map/ppermute | solution.py:21
  27.4 0.9 %add_x_rims.1 = (f32[2,4,3,8,16,128]{5,4,3,2,1,0:T(8,128)S(1)}, f32[2,4,3,8,16,128]{5,4,3,2,1,0:T(8,128)}) custom-call(f32[88,128]{1,0:T(8,128)S(1)} %get-tuple-element.39.splat_ref, f32[2,4,3,8,16,128]{5,4,3,2,1,0:T(8,128)S(1)} %get-tuple-element.67.left_in, ...), custom_call_target="tpu_custom_call", output_to_operand_aliasing={{0}: (1, {}), {1}: (2, {})} | custom-call | tf_op jit(solution)/shard_map/add_x_rims/pallas_call | solution.py:753
  28.2 0.5 %all-to-all-done.rows_ref = f32[32,4,128]{2,1,0:T(4,128)S(1)} async-done(((f32[32,4,128]{2,1,0:T(4,128)}), f32[32,4,128]{2,1,0:T(4,128)S(1)}, u32[]{:S(2)}, u32[]{:S(2)}) %all-to-all-start) | async-done | bytes 65568 | tf_op jit(solution)/shard_map/all_to_all | solution.py:738
  28.7 0.7 %sum_rows.1 = f32[2,4,4]{2,1,0:T(4,128)} custom-call(f32[32,4,128]{2,1,0:T(4,128)S(1)} %all-to-all-done.rows_ref), custom_call_target="tpu_custom_call" | custom-call | tf_op jit(solution)/shard_map/sum_rows/pallas_call | solution.py:765
  (8 shorter events, 0.0 us)
Async XLA Ops:
  0.6 7.8 %copy-start.2 = (f32[2,4]{1,0:T(2,128)S(1)}, f32[2,4]{1,0:T(2,128)}, u32[]{:S(2)}) copy-start(f32[2,4]{1,0:T(2,128)} %ritz_ref.1) | copy-start | bytes 100
  0.6 7.8 %copy-start.1 = (f32[2,4,4]{2,1,0:T(4,128)S(1)}, f32[2,4,4]{2,1,0:T(4,128)}, u32[]{:S(2)}) copy-start(f32[2,4,4]{2,1,0:T(4,128)} %coeffs_ref.1) | copy-start | bytes 388
  0.7 7.8 %copy-start.5 = (f32[4]{0:T(128)S(1)}, f32[4]{0:T(128)}, u32[]{:S(2)}) copy-start(f32[4]{0:T(128)} %param.11) | copy-start | bytes 52
  0.7 7.8 %copy-start.4 = (f32[4]{0:T(128)S(1)}, f32[4]{0:T(128)}, u32[]{:S(2)}) copy-start(f32[4]{0:T(128)} %param.10) | copy-start | bytes 52
  0.7 7.8 %copy-start.3 = (s32[6]{0:T(128)S(1)}, s32[6]{0:T(128)}, u32[]{:S(2)}) copy-start(s32[6]{0:T(128)} %param.9) | copy-start | bytes 76
  0.7 7.8 %copy-start = (s32[8,16,128]{2,1,0:T(8,128)S(1)}, s32[8,16,128]{2,1,0:T(8,128)}, u32[]{:S(2)}) copy-start(s32[8,16,128]{2,1,0:T(8,128)} %material_ref.1) | copy-start | bytes 196612
  2.3 8.2 %collective-permute-start = (f32[2,4,2,8,128]{4,3,2,1,0:T(8,128)S(1)}, f32[2,4,2,8,128]{4,3,2,1,0:T(8,128)S(1)}, u32[]{:S(2)}, u32[]{:S(2)}) collective-permute-start(f32[2,4,2,8,128]{4,3,2,1,0:T(8,128)S(1)} %get-tuple-element.45), channel_id=1, source_target_pairs={{0,28},{4,0},{8,4},{12,8},{16,12},{20,16},{24,20},{28,24},{1,29},{... | collective-permute-start | bytes 196616 | tf_op jit(solution)/shard_map/ppermute | solution.py:21
  6.9 3.7 %collective-permute-start.1 = (f32[16,128]{1,0:T(8,128)S(1)}, f32[16,128]{1,0:T(8,128)S(1)}, u32[]{:S(2)}, u32[]{:S(2)}) collective-permute-start(f32[16,128]{1,0:T(8,128)S(1)} %get-tuple-element.46), channel_id=1, source_target_pairs={{0,2},{2,0},{1,3},{3,1},{4,6},{6,4},{5,7},{7,5},{8,10},{10,8},{9,1... | collective-permute-start | bytes 24584 | tf_op jit(solution)/shard_map/ppermute | solution.py:21
  10.8 5.3 %collective-permute-start.2 = (f32[2,4,2,16,128]{4,3,2,1,0:T(8,128)S(1)}, f32[2,4,2,16,128]{4,3,2,1,0:T(8,128)S(1)}, u32[]{:S(2)}, u32[]{:S(2)}) collective-permute-start(f32[2,4,2,16,128]{4,3,2,1,0:T(8,128)S(1)} %get-tuple-element.53), channel_id=1, source_target_pairs={{0,1},{1,0},{2,3},{3,2},{4,5},{5,4},{6,7},{7,6},{8,9},{9,8},{10,11... | collective-permute-start | bytes 393224 | tf_op jit(solution)/shard_map/ppermute | solution.py:21
  17.5 11.3 %all-to-all-start = ((f32[32,4,128]{2,1,0:T(4,128)}), f32[32,4,128]{2,1,0:T(4,128)S(1)}, u32[]{:S(2)}, u32[]{:S(2)}) async-start(f32[32,4,128]{2,1,0:T(4,128)} %get-tuple-element.64), calls=%async_computation | async-start | bytes 131072 | tf_op jit(solution)/shard_map/all_to_all | solution.py:738
  20.9 6.5 %collective-permute-start.4 = (f32[2,4,2,8,128]{4,3,2,1,0:T(8,128)S(1)}, f32[2,4,2,8,128]{4,3,2,1,0:T(8,128)S(1)}, u32[]{:S(2)}, u32[]{:S(2)}) collective-permute-start(f32[2,4,2,8,128]{4,3,2,1,0:T(8,128)S(1)} %get-tuple-element.69), channel_id=1, source_target_pairs={{0,4},{4,8},{8,12},{12,16},{16,20},{20,24},{24,28},{28,0},{1,5},{5... | collective-permute-start | bytes 196616 | tf_op jit(solution)/shard_map/ppermute | solution.py:21
  21.2 3.7 %collective-permute-start.3 = (f32[16,128]{1,0:T(8,128)S(1)}, f32[16,128]{1,0:T(8,128)S(1)}, u32[]{:S(2)}, u32[]{:S(2)}) collective-permute-start(f32[16,128]{1,0:T(8,128)S(1)} %get-tuple-element.66), channel_id=1, source_target_pairs={{0,2},{2,0},{1,3},{3,1},{4,6},{6,4},{5,7},{7,5},{8,10},{10,8},{9,1... | collective-permute-start | bytes 24584 | tf_op jit(solution)/shard_map/ppermute | solution.py:21

commit v27 on v26

--- a/solution.py
+++ b/solution.py
@@ -160,6 +160,10 @@
 
 def tiles_of(nx):
     return [slice(SUB * t, SUB * (t + 1)) for t in range(nx // SUB)]
+
+
+def early_planes(nz):
+    return (nz - 1) // 2
 
 
 def open_magnetic(basis_ref, table_ref, sz_ref, h_ref, packed_ref):
@@ -286,6 +290,12 @@
         packed_ref[z] = jnp.zeros(plane, jnp.float32)
 
     magnetic = open_magnetic(basis_ref, table_ref, sz_ref, h_ref, packed_ref)
+
+    @pl.loop(0, early_planes(nz))
+    def _(z):
+        for b in range(vectors):
+            magnetic(b, z, False)
+
     for b in range(vectors):
         magnetic(b, nz - 1, True)
 
@@ -452,7 +462,7 @@
     cuts = tiles_of(nx)
     magnetic = open_magnetic(basis_ref, table_ref, sz_ref, h_ref, packed_ref)
 
-    @pl.loop(0, nz - 1)
+    @pl.loop(early_planes(nz), nz - 1)
     def _(z):
         for b in range(vectors):
             magnetic(b, z, False)

time: 29.6 us -> 29.6 us (level)
  starting transfers between devices: 13 us -> 13.3 us
    pallas_call x1, Pallas kernels: 3.77 us -> 3.24 us  [body(): pl.pallas_call(inner_kernel, out_shape=(whole, planes, whole, f32(vectors...]
    pallas_call x1, Pallas kernels: 1.07 us -> 1.59 us  [body(): pl.pallas_call(prepare_kernel, out_shape=(whole, f32(2, nz, nx, ny), whol...]
    all_to_all x1, starting transfers between devices: 3.43 us -> 3.75 us  [body(): rows = lax.all_to_all(gram, ('gx', 'gy', 'gz'), 0, 0)]
  transfers between devices with their start and end apart: 6 -> 6, of which waited for: 4 -> 5; matrix products, arithmetic and copies ran while one was open for 0% -> 0% of each run, Pallas kernels for 26% -> 25%
where the time goes in v27:
time: 29.6 us; the launch traced here: 29.4 us
  starting transfers between devices  13.3 us (45%)
  Pallas kernels  11.4 us (39%)
  waiting for transfers between devices  3.91 us (13%)
  between operations  0.76 us (3%)
    ppermute x5, starting transfers between devices, passed_round(): lax.ppermute(value, axis, [(source, (source + steps) % count) for source...  9.59 us
    all_to_all x1, starting transfers between devices, body(): rows = lax.all_to_all(gram, ('gx', 'gy', 'gz'), 0, 0)  3.75 us
    ppermute x5, waiting for transfers between devices, passed_round(): lax.ppermute(value, axis, [(source, (source + steps) % count) for source...  3.43 us
    pallas_call x1, Pallas kernels, body(): pl.pallas_call(inner_kernel, out_shape=(whole, planes, whole, f32(vectors...  3.24 us
    pallas_call x1, Pallas kernels, body(): pl.pallas_call(rim_y_kernel, out_shape=(whole, whole), in_specs=[VMEM] *...  1.79 us
    pallas_call x1, Pallas kernels, body(): pl.pallas_call(face_kernel, out_shape=(whole, f32(*xf_shape), f32(*yf_sha...  1.65 us
    pallas_call x1, Pallas kernels, body(): pl.pallas_call(prepare_kernel, out_shape=(whole, f32(2, nz, nx, ny), whol...  1.59 us
    pallas_call x1, Pallas kernels, body(): pl.pallas_call(outer_kernel, out_shape=(whole, f32(devices, 4, ny), whole...  1.28 us
  transfers between devices with their start and end apart: 6, of which 5 were waited for; matrix products, arithmetic and copies ran while one was open for 0% of the time, Pallas kernels for 25%

profile of v27, /device:TPU:0, one launch (start us, length us, event | category | flops | bytes accessed | tf_op | source)
XLA Modules:
  0.0 29.4 jit_solution(4538153968228635761)
XLA Ops:
  0.6 0.0 copy-start.2
  0.6 0.0 copy-start.1
  0.7 0.0 copy-start.5
  0.7 1.6 %take_faces.1 = (f32[2,4,3,8,16,128]{5,4,3,2,1,0:T(8,128)S(1)}, f32[2,4,2,8,128]{4,3,2,1,0:T(8,128)S(1)}, f32[16,128]{1,0:T(8,128)S(1)}) custom-call(f32[2,4,3,8,16,128]{5,4,3,2,1,0:T(8,128)} %fields_hbm.1), custom_call_target="tpu_custom_call" | custom-call | tf_op jit(solution)/shard_map/take_faces/pallas_call | solution.py:688
  2.3 4.5 %collective-permute-start = (f32[2,4,2,8,128]{4,3,2,1,0:T(8,128)S(1)}, f32[2,4,2,8,128]{4,3,2,1,0:T(8,128)S(1)}, u32[]{:S(2)}, u32[]{:S(2)}) collective-permute-start(f32[2,4,2,8,128]{4,3,2,1,0:T(8,128)S(1)} %get-tuple-element.45), channel_id=1, source_target_pairs={{0,28},{4,0},{8,4},{12,8},{16,12},{20,16},{24,20},{28,24},{1,29},{... | collective-permute-start | bytes 196616 | tf_op jit(solution)/shard_map/ppermute | solution.py:21
  6.9 1.5 %collective-permute-start.1 = (f32[16,128]{1,0:T(8,128)S(1)}, f32[16,128]{1,0:T(8,128)S(1)}, u32[]{:S(2)}, u32[]{:S(2)}) collective-permute-start(f32[16,128]{1,0:T(8,128)S(1)} %get-tuple-element.46), channel_id=1, source_target_pairs={{0,2},{2,0},{1,3},{3,1},{4,6},{6,4},{5,7},{7,5},{8,10},{10,8},{9,1... | collective-permute-start | bytes 24584 | tf_op jit(solution)/shard_map/ppermute | solution.py:21
  8.4 0.0 copy-done.1
  8.4 1.6 %prepare.1 = (f32[2,4,3,8,16,128]{5,4,3,2,1,0:T(8,128)S(1)}, f32[2,8,16,128]{3,2,1,0:T(8,128)S(1)}, f32[2,4,3,8,16,128]{5,4,3,2,1,0:T(8,128)S(1)}, f32[8,16,128]...) custom-call(s32[1,6]{1,0:T(1,128)S(1)} %bitcast.3, ...), custom_call_target="tpu_custom_call" | custom-call | flops 13107200 | bytes 6291456 | tf_op jit(solution)/shard_map/prepare/pallas_call | solution.py:706
  10.0 0.5 %collective-permute-done.1.raw_yf_ref = f32[16,128]{1,0:T(8,128)S(1)} collective-permute-done((f32[16,128]{1,0:T(8,128)S(1)}, f32[16,128]{1,0:T(8,128)S(1)}, u32[]{:S(2)}, u32[]{:S(2)}) %collective-permute-start.1) | collective-permute-done | bytes 8224 | tf_op jit(solution)/shard_map/ppermute | solution.py:21
  10.5 0.0 collective-permute-done.raw_xf_ref
  10.5 0.3 slab_face.1
  10.8 1.6 %collective-permute-start.2 = (f32[2,4,2,16,128]{4,3,2,1,0:T(8,128)S(1)}, f32[2,4,2,16,128]{4,3,2,1,0:T(8,128)S(1)}, u32[]{:S(2)}, u32[]{:S(2)}) collective-permute-start(f32[2,4,2,16,128]{4,3,2,1,0:T(8,128)S(1)} %get-tuple-element.53), channel_id=1, source_target_pairs={{0,1},{1,0},{2,3},{3,2},{4,5},{5,4},{6,7},{7,6},{8,9},{9,8},{10,11... | collective-permute-start | bytes 393224 | tf_op jit(solution)/shard_map/ppermute | solution.py:21
  12.4 3.2 %apply_inner.1 = (f32[2,4,3,8,16,128]{5,4,3,2,1,0:T(8,128)S(1)}, f32[8,16,128]{2,1,0:T(8,128)S(1)}, f32[2,4,3,8,16,128]{5,4,3,2,1,0:T(8,128)S(1)}, f32[4,8,8,128...) custom-call(f32[88,128]{1,0:T(8,128)S(1)} %get-tuple-element.39.spla, ...), custom_call_target="tpu_custom_call", output_to_operand_aliasing={{0}: (5, {}), {1}: (6, {})} | custom-call | flops 13107200 | bytes 3145728 | tf_op jit(solution)/shard_map/apply_inner/pallas_call | solution.py:725
  15.6 0.2 collective-permute-done.2.zf_ref
  15.9 1.3 %apply_outer.1 = (f32[2,4,3,8,16,128]{5,4,3,2,1,0:T(8,128)S(1)}, f32[32,4,128]{2,1,0:T(4,128)}, f32[2,4,3,8,16,128]{5,4,3,2,1,0:T(8,128)S(1)}, f32[2,4,2,8,128]{4,3,2,1,0:T(8,128)S(1)}, f32[16,128]{1,0:T(8,128)S(1)}) custom-call(f32[88,128]{1,0:T(8,128)S(1)} %get-tuple-element.39.splat_ref, ...), custom_call_target="tpu_custom_call", output_to_operand_aliasing={{0}: (11, {}), {2}: (5, {}), {3}: (9, {})} | custom-call | flops 4915200 | bytes 1572864 | tf_op jit(solution)/shard_map/apply_outer/pallas_call | solution.py:737
  17.1 3.8 %all-to-all-start = ((f32[32,4,128]{2,1,0:T(4,128)}), f32[32,4,128]{2,1,0:T(4,128)S(1)}, u32[]{:S(2)}, u32[]{:S(2)}) async-start(f32[32,4,128]{2,1,0:T(4,128)} %get-tuple-element.64), calls=%async_computation | async-start | bytes 131072 | tf_op jit(solution)/shard_map/all_to_all | solution.py:748
  20.9 0.3 %collective-permute-start.4 = (f32[2,4,2,8,128]{4,3,2,1,0:T(8,128)S(1)}, f32[2,4,2,8,128]{4,3,2,1,0:T(8,128)S(1)}, u32[]{:S(2)}, u32[]{:S(2)}) collective-permute-start(f32[2,4,2,8,128]{4,3,2,1,0:T(8,128)S(1)} %get-tuple-element.69), channel_id=1, source_target_pairs={{0,4},{4,8},{8,12},{12,16},{16,20},{20,24},{24,28},{28,0},{1,5},{5... | collective-permute-start | bytes 196616 | tf_op jit(solution)/shard_map/ppermute | solution.py:21
  21.2 1.7 %collective-permute-start.3 = (f32[16,128]{1,0:T(8,128)S(1)}, f32[16,128]{1,0:T(8,128)S(1)}, u32[]{:S(2)}, u32[]{:S(2)}) collective-permute-start(f32[16,128]{1,0:T(8,128)S(1)} %get-tuple-element.66), channel_id=1, source_target_pairs={{0,2},{2,0},{1,3},{3,1},{4,6},{6,4},{5,7},{7,5},{8,10},{10,8},{9,1... | collective-permute-start | bytes 24584 | tf_op jit(solution)/shard_map/ppermute | solution.py:21
  22.9 2.0 %collective-permute-done.3.hyf_ref = f32[16,128]{1,0:T(8,128)S(1)} collective-permute-done((f32[16,128]{1,0:T(8,128)S(1)}, f32[16,128]{1,0:T(8,128)S(1)}, u32[]{:S(2)}, u32[]{:S(2)}) %collective-permute-start.3) | collective-permute-done | bytes 8224 | tf_op jit(solution)/shard_map/ppermute | solution.py:21
  24.9 1.8 %add_y_rims.1 = (f32[2,4,3,8,16,128]{5,4,3,2,1,0:T(8,128)S(1)}, f32[2,4,3,8,16,128]{5,4,3,2,1,0:T(8,128)}) custom-call(f32[88,128]{1,0:T(8,128)S(1)} %get-tuple-element.39.splat_ref, f32[2,4,3,8,16,128]{5,4,3,2,1,0:T(8,128)S(1)} %get-tuple-element.65.left_in, f32[16,128]{1,0:T(8,128)S(1)} %collective-permute-done.3.hyf_ref), custom_call_target="tpu_custom_call", output_to_operand_aliasing={{0}: (1, {})} | custom-call | tf_op jit(solution)/shard_map/add_y_rims/pallas_call | solution.py:752
  26.7 0.7 %collective-permute-done.4.hxf_ref = f32[2,4,2,8,128]{4,3,2,1,0:T(8,128)S(1)} collective-permute-done((f32[2,4,2,8,128]{4,3,2,1,0:T(8,128)S(1)}, f32[2,4,2,8,128]{4,3,2,1,0:T(8,128)S(1)}, u32[]{:S(2)}, u32[]{:S(2)}) %collective-permute-start.4) | collective-permute-done | bytes 65568 | tf_op jit(solution)/shard_map/ppermute | solution.py:21
  27.4 0.9 %add_x_rims.1 = (f32[2,4,3,8,16,128]{5,4,3,2,1,0:T(8,128)S(1)}, f32[2,4,3,8,16,128]{5,4,3,2,1,0:T(8,128)}) custom-call(f32[88,128]{1,0:T(8,128)S(1)} %get-tuple-element.39.splat_ref, f32[2,4,3,8,16,128]{5,4,3,2,1,0:T(8,128)S(1)} %get-tuple-element.67.left_in, ...), custom_call_target="tpu_custom_call", output_to_operand_aliasing={{0}: (1, {}), {1}: (2, {})} | custom-call | tf_op jit(solution)/shard_map/add_x_rims/pallas_call | solution.py:763
  28.2 0.5 %all-to-all-done.rows_ref = f32[32,4,128]{2,1,0:T(4,128)S(1)} async-done(((f32[32,4,128]{2,1,0:T(4,128)}), f32[32,4,128]{2,1,0:T(4,128)S(1)}, u32[]{:S(2)}, u32[]{:S(2)}) %all-to-all-start) | async-done | bytes 65568 | tf_op jit(solution)/shard_map/all_to_all | solution.py:748
  28.7 0.7 %sum_rows.1 = f32[2,4,4]{2,1,0:T(4,128)} custom-call(f32[32,4,128]{2,1,0:T(4,128)S(1)} %all-to-all-done.rows_ref), custom_call_target="tpu_custom_call" | custom-call | tf_op jit(solution)/shard_map/sum_rows/pallas_call | solution.py:775
  (8 shorter events, 0.0 us)
Async XLA Ops:
  0.6 7.8 %copy-start.2 = (f32[2,4]{1,0:T(2,128)S(1)}, f32[2,4]{1,0:T(2,128)}, u32[]{:S(2)}) copy-start(f32[2,4]{1,0:T(2,128)} %ritz_ref.1) | copy-start | bytes 100
  0.6 7.8 %copy-start.1 = (f32[2,4,4]{2,1,0:T(4,128)S(1)}, f32[2,4,4]{2,1,0:T(4,128)}, u32[]{:S(2)}) copy-start(f32[2,4,4]{2,1,0:T(4,128)} %coeffs_ref.1) | copy-start | bytes 388
  0.7 7.8 %copy-start.5 = (f32[4]{0:T(128)S(1)}, f32[4]{0:T(128)}, u32[]{:S(2)}) copy-start(f32[4]{0:T(128)} %param.11) | copy-start | bytes 52
  0.7 7.8 %copy-start.4 = (f32[4]{0:T(128)S(1)}, f32[4]{0:T(128)}, u32[]{:S(2)}) copy-start(f32[4]{0:T(128)} %param.10) | copy-start | bytes 52
  0.7 7.8 %copy-start.3 = (s32[6]{0:T(128)S(1)}, s32[6]{0:T(128)}, u32[]{:S(2)}) copy-start(s32[6]{0:T(128)} %param.9) | copy-start | bytes 76
  0.7 7.8 %copy-start = (s32[8,16,128]{2,1,0:T(8,128)S(1)}, s32[8,16,128]{2,1,0:T(8,128)}, u32[]{:S(2)}) copy-start(s32[8,16,128]{2,1,0:T(8,128)} %material_ref.1) | copy-start | bytes 196612
  2.3 8.2 %collective-permute-start = (f32[2,4,2,8,128]{4,3,2,1,0:T(8,128)S(1)}, f32[2,4,2,8,128]{4,3,2,1,0:T(8,128)S(1)}, u32[]{:S(2)}, u32[]{:S(2)}) collective-permute-start(f32[2,4,2,8,128]{4,3,2,1,0:T(8,128)S(1)} %get-tuple-element.45), channel_id=1, source_target_pairs={{0,28},{4,0},{8,4},{12,8},{16,12},{20,16},{24,20},{28,24},{1,29},{... | collective-permute-start | bytes 196616 | tf_op jit(solution)/shard_map/ppermute | solution.py:21
  6.9 3.7 %collective-permute-start.1 = (f32[16,128]{1,0:T(8,128)S(1)}, f32[16,128]{1,0:T(8,128)S(1)}, u32[]{:S(2)}, u32[]{:S(2)}) collective-permute-start(f32[16,128]{1,0:T(8,128)S(1)} %get-tuple-element.46), channel_id=1, source_target_pairs={{0,2},{2,0},{1,3},{3,1},{4,6},{6,4},{5,7},{7,5},{8,10},{10,8},{9,1... | collective-permute-start | bytes 24584 | tf_op jit(solution)/shard_map/ppermute | solution.py:21
  10.8 5.0 %collective-permute-start.2 = (f32[2,4,2,16,128]{4,3,2,1,0:T(8,128)S(1)}, f32[2,4,2,16,128]{4,3,2,1,0:T(8,128)S(1)}, u32[]{:S(2)}, u32[]{:S(2)}) collective-permute-start(f32[2,4,2,16,128]{4,3,2,1,0:T(8,128)S(1)} %get-tuple-element.53), channel_id=1, source_target_pairs={{0,1},{1,0},{2,3},{3,2},{4,5},{5,4},{6,7},{7,6},{8,9},{9,8},{10,11... | collective-permute-start | bytes 393224 | tf_op jit(solution)/shard_map/ppermute | solution.py:21
  17.1 11.6 %all-to-all-start = ((f32[32,4,128]{2,1,0:T(4,128)}), f32[32,4,128]{2,1,0:T(4,128)S(1)}, u32[]{:S(2)}, u32[]{:S(2)}) async-start(f32[32,4,128]{2,1,0:T(4,128)} %get-tuple-element.64), calls=%async_computation | async-start | bytes 131072 | tf_op jit(solution)/shard_map/all_to_all | solution.py:748
  20.9 6.5 %collective-permute-start.4 = (f32[2,4,2,8,128]{4,3,2,1,0:T(8,128)S(1)}, f32[2,4,2,8,128]{4,3,2,1,0:T(8,128)S(1)}, u32[]{:S(2)}, u32[]{:S(2)}) collective-permute-start(f32[2,4,2,8,128]{4,3,2,1,0:T(8,128)S(1)} %get-tuple-element.69), channel_id=1, source_target_pairs={{0,4},{4,8},{8,12},{12,16},{16,20},{20,24},{24,28},{28,0},{1,5},{5... | collective-permute-start | bytes 196616 | tf_op jit(solution)/shard_map/ppermute | solution.py:21
  21.2 3.7 %collective-permute-start.3 = (f32[16,128]{1,0:T(8,128)S(1)}, f32[16,128]{1,0:T(8,128)S(1)}, u32[]{:S(2)}, u32[]{:S(2)}) collective-permute-start(f32[16,128]{1,0:T(8,128)S(1)} %get-tuple-element.66), channel_id=1, source_target_pairs={{0,2},{2,0},{1,3},{3,1},{4,6},{6,4},{5,7},{7,5},{8,10},{10,8},{9,1... | collective-permute-start | bytes 24584 | tf_op jit(solution)/shard_map/ppermute | solution.py:21

commit v28 on v27

--- a/solution.py
+++ b/solution.py
@@ -81,17 +81,20 @@
 def face_kernel(fields_hbm, fields_ref, xf_ref, yf_ref, sems):
     _, vectors, _, nz, nx, ny = fields_ref.shape
     lanes = lax.broadcasted_iota(jnp.int32, (nx, ny), 1)
-    copies = [
-        pltpu.make_async_copy(fields_hbm.at[part, :, comp], fields_ref.at[part, :, comp], sems.at[part, comp])
-        for comp in (0, 2, 1) for part in range(2)
-    ]
-    for copy in copies:
-        copy.start()
+    copies = {}
+    for comp in (0, 2, 1):
+        for part in range(2):
+            for a in range(vectors):
+                copy = pltpu.make_async_copy(
+                    fields_hbm.at[part, a, comp], fields_ref.at[part, a, comp], sems.at[part, comp, a]
+                )
+                copy.start()
+                copies[comp, part, a] = copy
     packed = [jnp.zeros((nx, ny), jnp.float32)] * nz
-    for place, comp in enumerate((0, 2)):
+    for comp in (0, 2):
         for part in range(2):
-            copies[2 * place + part].wait()
             for a in range(vectors):
+                copies[comp, part, a].wait()
                 row = packed_row(comp // 2, part, a, vectors)
                 for z in range(nz):
                     value = fields_ref[part, a, comp, z]
@@ -102,8 +105,8 @@
         for a in range(vectors):
             xf_ref[part, a, 1] = fields_ref[part, a, 2, :, 0, :]
     for part in range(2):
-        copies[4 + part].wait()
         for a in range(vectors):
+            copies[1, part, a].wait()
             xf_ref[part, a, 0] = fields_ref[part, a, 1, :, 0, :]
 
 
@@ -690,7 +693,7 @@
         out_shape=(whole, f32(*xf_shape), f32(*yf_shape)),
         in_specs=[HBM],
         out_specs=(VMEM,) * 3,
-        scratch_shapes=[pltpu.SemaphoreType.DMA((2, 3))],
+        scratch_shapes=[pltpu.SemaphoreType.DMA((2, 3, vectors))],
         compiler_params=params,
         name="take_faces",
     )(pltpu.with_memory_space_constraint(fields, pltpu.HBM))

time: 29.6 us -> 30.5 us (1.030)
  Pallas kernels: 11.4 us -> 12.2 us
    pallas_call x1, Pallas kernels: 1.65 us -> 2.51 us  [body(): pl.pallas_call(face_kernel, out_shape=(whole, f32(*xf_shape), f32(*yf_sha...]
where the time goes in v28:
time: 30.5 us; the launch traced here: 30.3 us
  starting transfers between devices  13.3 us (44%)
  Pallas kernels  12.2 us (40%)
  waiting for transfers between devices  3.91 us (13%)
  between operations  0.76 us (2%)
    ppermute x5, starting transfers between devices, passed_round(): lax.ppermute(value, axis, [(source, (source + steps) % count) for source...  9.59 us
    all_to_all x1, starting transfers between devices, body(): rows = lax.all_to_all(gram, ('gx', 'gy', 'gz'), 0, 0)  3.75 us
    ppermute x5, waiting for transfers between devices, passed_round(): lax.ppermute(value, axis, [(source, (source + steps) % count) for source...  3.43 us
    pallas_call x1, Pallas kernels, body(): pl.pallas_call(inner_kernel, out_shape=(whole, planes, whole, f32(vectors...  3.24 us
    pallas_call x1, Pallas kernels, body(): pl.pallas_call(face_kernel, out_shape=(whole, f32(*xf_shape), f32(*yf_sha...  2.51 us
    pallas_call x1, Pallas kernels, body(): pl.pallas_call(rim_y_kernel, out_shape=(whole, whole), in_specs=[VMEM] *...  1.79 us
    pallas_call x1, Pallas kernels, body(): pl.pallas_call(prepare_kernel, out_shape=(whole, f32(2, nz, nx, ny), whol...  1.59 us
    pallas_call x1, Pallas kernels, body(): pl.pallas_call(outer_kernel, out_shape=(whole, f32(devices, 4, ny), whole...  1.28 us
  transfers between devices with their start and end apart: 6, of which 5 were waited for; matrix products, arithmetic and copies ran while one was open for 0% of the time, Pallas kernels for 25%

profile of v28, /device:TPU:0, one launch (start us, length us, event | category | flops | bytes accessed | tf_op | source)
XLA Modules:
  0.0 30.3 jit_solution(2519123945634413140)
XLA Ops:
  0.6 0.0 copy-start.2
  0.6 0.0 copy-start.1
  0.7 2.5 %take_faces.1 = (f32[2,4,3,8,16,128]{5,4,3,2,1,0:T(8,128)S(1)}, f32[2,4,2,8,128]{4,3,2,1,0:T(8,128)S(1)}, f32[16,128]{1,0:T(8,128)S(1)}) custom-call(f32[2,4,3,8,16,128]{5,4,3,2,1,0:T(8,128)} %fields_hbm.1), custom_call_target="tpu_custom_call" | custom-call | tf_op jit(solution)/shard_map/take_faces/pallas_call | solution.py:691
  3.2 4.5 %collective-permute-start = (f32[2,4,2,8,128]{4,3,2,1,0:T(8,128)S(1)}, f32[2,4,2,8,128]{4,3,2,1,0:T(8,128)S(1)}, u32[]{:S(2)}, u32[]{:S(2)}) collective-permute-start(f32[2,4,2,8,128]{4,3,2,1,0:T(8,128)S(1)} %get-tuple-element.45), channel_id=1, source_target_pairs={{0,28},{4,0},{8,4},{12,8},{16,12},{20,16},{24,20},{28,24},{1,29},{... | collective-permute-start | bytes 196616 | tf_op jit(solution)/shard_map/ppermute | solution.py:21
  7.8 1.5 %collective-permute-start.1 = (f32[16,128]{1,0:T(8,128)S(1)}, f32[16,128]{1,0:T(8,128)S(1)}, u32[]{:S(2)}, u32[]{:S(2)}) collective-permute-start(f32[16,128]{1,0:T(8,128)S(1)} %get-tuple-element.46), channel_id=1, source_target_pairs={{0,2},{2,0},{1,3},{3,1},{4,6},{6,4},{5,7},{7,5},{8,10},{10,8},{9,1... | collective-permute-start | bytes 24584 | tf_op jit(solution)/shard_map/ppermute | solution.py:21
  9.3 0.0 copy-done.1
  9.3 0.0 copy-done.4
  9.3 1.6 %prepare.1 = (f32[2,4,3,8,16,128]{5,4,3,2,1,0:T(8,128)S(1)}, f32[2,8,16,128]{3,2,1,0:T(8,128)S(1)}, f32[2,4,3,8,16,128]{5,4,3,2,1,0:T(8,128)S(1)}, f32[8,16,128]...) custom-call(s32[1,6]{1,0:T(1,128)S(1)} %bitcast.3, ...), custom_call_target="tpu_custom_call" | custom-call | flops 13107200 | bytes 6291456 | tf_op jit(solution)/shard_map/prepare/pallas_call | solution.py:709
  10.9 0.5 %collective-permute-done.1.raw_yf_ref = f32[16,128]{1,0:T(8,128)S(1)} collective-permute-done((f32[16,128]{1,0:T(8,128)S(1)}, f32[16,128]{1,0:T(8,128)S(1)}, u32[]{:S(2)}, u32[]{:S(2)}) %collective-permute-start.1) | collective-permute-done | bytes 8224 | tf_op jit(solution)/shard_map/ppermute | solution.py:21
  11.4 0.0 collective-permute-done.raw_xf_ref
  11.4 0.3 slab_face.1
  11.7 1.6 %collective-permute-start.2 = (f32[2,4,2,16,128]{4,3,2,1,0:T(8,128)S(1)}, f32[2,4,2,16,128]{4,3,2,1,0:T(8,128)S(1)}, u32[]{:S(2)}, u32[]{:S(2)}) collective-permute-start(f32[2,4,2,16,128]{4,3,2,1,0:T(8,128)S(1)} %get-tuple-element.53), channel_id=1, source_target_pairs={{0,1},{1,0},{2,3},{3,2},{4,5},{5,4},{6,7},{7,6},{8,9},{9,8},{10,11... | collective-permute-start | bytes 393224 | tf_op jit(solution)/shard_map/ppermute | solution.py:21
  13.2 3.2 %apply_inner.1 = (f32[2,4,3,8,16,128]{5,4,3,2,1,0:T(8,128)S(1)}, f32[8,16,128]{2,1,0:T(8,128)S(1)}, f32[2,4,3,8,16,128]{5,4,3,2,1,0:T(8,128)S(1)}, f32[4,8,8,128...) custom-call(f32[88,128]{1,0:T(8,128)S(1)} %get-tuple-element.39.spla, ...), custom_call_target="tpu_custom_call", output_to_operand_aliasing={{0}: (5, {}), {1}: (6, {})} | custom-call | flops 13107200 | bytes 3145728 | tf_op jit(solution)/shard_map/apply_inner/pallas_call | solution.py:728
  16.5 0.2 collective-permute-done.2.zf_ref
  16.7 1.3 %apply_outer.1 = (f32[2,4,3,8,16,128]{5,4,3,2,1,0:T(8,128)S(1)}, f32[32,4,128]{2,1,0:T(4,128)}, f32[2,4,3,8,16,128]{5,4,3,2,1,0:T(8,128)S(1)}, f32[2,4,2,8,128]{4,3,2,1,0:T(8,128)S(1)}, f32[16,128]{1,0:T(8,128)S(1)}) custom-call(f32[88,128]{1,0:T(8,128)S(1)} %get-tuple-element.39.splat_ref, ...), custom_call_target="tpu_custom_call", output_to_operand_aliasing={{0}: (11, {}), {2}: (5, {}), {3}: (9, {})} | custom-call | flops 4915200 | bytes 1572864 | tf_op jit(solution)/shard_map/apply_outer/pallas_call | solution.py:740
  18.0 3.8 %all-to-all-start = ((f32[32,4,128]{2,1,0:T(4,128)}), f32[32,4,128]{2,1,0:T(4,128)S(1)}, u32[]{:S(2)}, u32[]{:S(2)}) async-start(f32[32,4,128]{2,1,0:T(4,128)} %get-tuple-element.64), calls=%async_computation | async-start | bytes 131072 | tf_op jit(solution)/shard_map/all_to_all | solution.py:751
  21.8 0.3 %collective-permute-start.4 = (f32[2,4,2,8,128]{4,3,2,1,0:T(8,128)S(1)}, f32[2,4,2,8,128]{4,3,2,1,0:T(8,128)S(1)}, u32[]{:S(2)}, u32[]{:S(2)}) collective-permute-start(f32[2,4,2,8,128]{4,3,2,1,0:T(8,128)S(1)} %get-tuple-element.69), channel_id=1, source_target_pairs={{0,4},{4,8},{8,12},{12,16},{16,20},{20,24},{24,28},{28,0},{1,5},{5... | collective-permute-start | bytes 196616 | tf_op jit(solution)/shard_map/ppermute | solution.py:21
  22.1 1.7 %collective-permute-start.3 = (f32[16,128]{1,0:T(8,128)S(1)}, f32[16,128]{1,0:T(8,128)S(1)}, u32[]{:S(2)}, u32[]{:S(2)}) collective-permute-start(f32[16,128]{1,0:T(8,128)S(1)} %get-tuple-element.66), channel_id=1, source_target_pairs={{0,2},{2,0},{1,3},{3,1},{4,6},{6,4},{5,7},{7,5},{8,10},{10,8},{9,1... | collective-permute-start | bytes 24584 | tf_op jit(solution)/shard_map/ppermute | solution.py:21
  23.7 2.0 %collective-permute-done.3.hyf_ref = f32[16,128]{1,0:T(8,128)S(1)} collective-permute-done((f32[16,128]{1,0:T(8,128)S(1)}, f32[16,128]{1,0:T(8,128)S(1)}, u32[]{:S(2)}, u32[]{:S(2)}) %collective-permute-start.3) | collective-permute-done | bytes 8224 | tf_op jit(solution)/shard_map/ppermute | solution.py:21
  25.7 1.8 %add_y_rims.1 = (f32[2,4,3,8,16,128]{5,4,3,2,1,0:T(8,128)S(1)}, f32[2,4,3,8,16,128]{5,4,3,2,1,0:T(8,128)}) custom-call(f32[88,128]{1,0:T(8,128)S(1)} %get-tuple-element.39.splat_ref, f32[2,4,3,8,16,128]{5,4,3,2,1,0:T(8,128)S(1)} %get-tuple-element.65.left_in, f32[16,128]{1,0:T(8,128)S(1)} %collective-permute-done.3.hyf_ref), custom_call_target="tpu_custom_call", output_to_operand_aliasing={{0}: (1, {})} | custom-call | tf_op jit(solution)/shard_map/add_y_rims/pallas_call | solution.py:755
  27.5 0.7 %collective-permute-done.4.hxf_ref = f32[2,4,2,8,128]{4,3,2,1,0:T(8,128)S(1)} collective-permute-done((f32[2,4,2,8,128]{4,3,2,1,0:T(8,128)S(1)}, f32[2,4,2,8,128]{4,3,2,1,0:T(8,128)S(1)}, u32[]{:S(2)}, u32[]{:S(2)}) %collective-permute-start.4) | collective-permute-done | bytes 65568 | tf_op jit(solution)/shard_map/ppermute | solution.py:21
  28.2 0.9 %add_x_rims.1 = (f32[2,4,3,8,16,128]{5,4,3,2,1,0:T(8,128)S(1)}, f32[2,4,3,8,16,128]{5,4,3,2,1,0:T(8,128)}) custom-call(f32[88,128]{1,0:T(8,128)S(1)} %get-tuple-element.39.splat_ref, f32[2,4,3,8,16,128]{5,4,3,2,1,0:T(8,128)S(1)} %get-tuple-element.67.left_in, ...), custom_call_target="tpu_custom_call", output_to_operand_aliasing={{0}: (1, {}), {1}: (2, {})} | custom-call | tf_op jit(solution)/shard_map/add_x_rims/pallas_call | solution.py:766
  29.1 0.5 %all-to-all-done.rows_ref = f32[32,4,128]{2,1,0:T(4,128)S(1)} async-done(((f32[32,4,128]{2,1,0:T(4,128)}), f32[32,4,128]{2,1,0:T(4,128)S(1)}, u32[]{:S(2)}, u32[]{:S(2)}) %all-to-all-start) | async-done | bytes 65568 | tf_op jit(solution)/shard_map/all_to_all | solution.py:751
  29.6 0.7 %sum_rows.1 = f32[2,4,4]{2,1,0:T(4,128)} custom-call(f32[32,4,128]{2,1,0:T(4,128)S(1)} %all-to-all-done.rows_ref), custom_call_target="tpu_custom_call" | custom-call | tf_op jit(solution)/shard_map/sum_rows/pallas_call | solution.py:778
  (8 shorter events, 0.0 us)
Async XLA Ops:
  0.6 8.6 %copy-start.2 = (f32[2,4]{1,0:T(2,128)S(1)}, f32[2,4]{1,0:T(2,128)}, u32[]{:S(2)}) copy-start(f32[2,4]{1,0:T(2,128)} %ritz_ref.1) | copy-start | bytes 100
  0.6 8.6 %copy-start.1 = (f32[2,4,4]{2,1,0:T(4,128)S(1)}, f32[2,4,4]{2,1,0:T(4,128)}, u32[]{:S(2)}) copy-start(f32[2,4,4]{2,1,0:T(4,128)} %coeffs_ref.1) | copy-start | bytes 388
  0.7 8.6 %copy-start.5 = (f32[4]{0:T(128)S(1)}, f32[4]{0:T(128)}, u32[]{:S(2)}) copy-start(f32[4]{0:T(128)} %param.11) | copy-start | bytes 52
  0.7 8.6 %copy-start.4 = (f32[4]{0:T(128)S(1)}, f32[4]{0:T(128)}, u32[]{:S(2)}) copy-start(f32[4]{0:T(128)} %param.10) | copy-start | bytes 52
  0.7 8.6 %copy-start.3 = (s32[6]{0:T(128)S(1)}, s32[6]{0:T(128)}, u32[]{:S(2)}) copy-start(s32[6]{0:T(128)} %param.9) | copy-start | bytes 76
  0.7 8.6 %copy-start = (s32[8,16,128]{2,1,0:T(8,128)S(1)}, s32[8,16,128]{2,1,0:T(8,128)}, u32[]{:S(2)}) copy-start(s32[8,16,128]{2,1,0:T(8,128)} %material_ref.1) | copy-start | bytes 196612
  3.2 8.2 %collective-permute-start = (f32[2,4,2,8,128]{4,3,2,1,0:T(8,128)S(1)}, f32[2,4,2,8,128]{4,3,2,1,0:T(8,128)S(1)}, u32[]{:S(2)}, u32[]{:S(2)}) collective-permute-start(f32[2,4,2,8,128]{4,3,2,1,0:T(8,128)S(1)} %get-tuple-element.45), channel_id=1, source_target_pairs={{0,28},{4,0},{8,4},{12,8},{16,12},{20,16},{24,20},{28,24},{1,29},{... | collective-permute-start | bytes 196616 | tf_op jit(solution)/shard_map/ppermute | solution.py:21
  7.8 3.7 %collective-permute-start.1 = (f32[16,128]{1,0:T(8,128)S(1)}, f32[16,128]{1,0:T(8,128)S(1)}, u32[]{:S(2)}, u32[]{:S(2)}) collective-permute-start(f32[16,128]{1,0:T(8,128)S(1)} %get-tuple-element.46), channel_id=1, source_target_pairs={{0,2},{2,0},{1,3},{3,1},{4,6},{6,4},{5,7},{7,5},{8,10},{10,8},{9,1... | collective-permute-start | bytes 24584 | tf_op jit(solution)/shard_map/ppermute | solution.py:21
  11.7 5.0 %collective-permute-start.2 = (f32[2,4,2,16,128]{4,3,2,1,0:T(8,128)S(1)}, f32[2,4,2,16,128]{4,3,2,1,0:T(8,128)S(1)}, u32[]{:S(2)}, u32[]{:S(2)}) collective-permute-start(f32[2,4,2,16,128]{4,3,2,1,0:T(8,128)S(1)} %get-tuple-element.53), channel_id=1, source_target_pairs={{0,1},{1,0},{2,3},{3,2},{4,5},{5,4},{6,7},{7,6},{8,9},{9,8},{10,11... | collective-permute-start | bytes 393224 | tf_op jit(solution)/shard_map/ppermute | solution.py:21
  18.0 11.6 %all-to-all-start = ((f32[32,4,128]{2,1,0:T(4,128)}), f32[32,4,128]{2,1,0:T(4,128)S(1)}, u32[]{:S(2)}, u32[]{:S(2)}) async-start(f32[32,4,128]{2,1,0:T(4,128)} %get-tuple-element.64), calls=%async_computation | async-start | bytes 131072 | tf_op jit(solution)/shard_map/all_to_all | solution.py:751
  21.8 6.5 %collective-permute-start.4 = (f32[2,4,2,8,128]{4,3,2,1,0:T(8,128)S(1)}, f32[2,4,2,8,128]{4,3,2,1,0:T(8,128)S(1)}, u32[]{:S(2)}, u32[]{:S(2)}) collective-permute-start(f32[2,4,2,8,128]{4,3,2,1,0:T(8,128)S(1)} %get-tuple-element.69), channel_id=1, source_target_pairs={{0,4},{4,8},{8,12},{12,16},{16,20},{20,24},{24,28},{28,0},{1,5},{5... | collective-permute-start | bytes 196616 | tf_op jit(solution)/shard_map/ppermute | solution.py:21
  22.1 3.7 %collective-permute-start.3 = (f32[16,128]{1,0:T(8,128)S(1)}, f32[16,128]{1,0:T(8,128)S(1)}, u32[]{:S(2)}, u32[]{:S(2)}) collective-permute-start(f32[16,128]{1,0:T(8,128)S(1)} %get-tuple-element.66), channel_id=1, source_target_pairs={{0,2},{2,0},{1,3},{3,1},{4,6},{6,4},{5,7},{7,5},{8,10},{10,8},{9,1... | collective-permute-start | bytes 24584 | tf_op jit(solution)/shard_map/ppermute | solution.py:21
